TPU v7x, 32 devices: a whole 2x2x4 slice. The times are simulated.
32 devices in a mesh: inst: 4 (over y, x), space: 8 (over z, core).
Axes of the slice: x: 2, y: 2, z: 4, core: 2. Of those that a mesh axis runs over, the one named last changes fastest.
Arguments:
- adjoint: float32 [4, 5, 256, 64, 128], P('inst', None, 'space'), may hold values from -6 to 6
- source: float32 [4, 5, 256, 64, 128], P('inst', None, 'space'), may hold values from -6 to 6
- viscosity: float32 [256, 64, 128], P('space'), may hold values from 0.2 to 2
- kappa: float32 [5], replicated, may hold values from 0.5 to 2
- coupling: float32 [5, 5], replicated, may hold values from -2.4 to 2.4
- bc_flags: int32 [5, 3], replicated, may hold values 0 or 1
- inst_map: int32 [4], replicated, may hold values from 0 to 3, each once
Outputs:
- residual: float32 [4, 5, 256, 64, 128], P('inst', None, 'space')
Inputs may be any that keep to these rules, and one draw needn't show every extreme that they name: `inst_map`: a permutation of 0 to 3. `bc_flags`: 1 marks a face of zero normal flux, 0 a face held at zero.
All inputs are finite; a program needn't handle non-finite values.
Results may differ from a plain program's by a relative error of at most 0.0001.
Values sent between devices are 32-bit elements; how exact they have to be, the bound alone decides.
No kernel may reach another device: no remote copies, remote signals or barrier semaphores. Data moves between devices by JAX's collectives and lax.ppermute only.
A program may use at most 128 MiB of HBM per device.

v0:
```python
import jax
import jax.numpy as jnp
from jax import lax
from jax.sharding import PartitionSpec as P


def with_halo(block, sides, width):
    for axis, dim in sides:
        count = lax.axis_size(axis)
        forward = [(i, i + 1) for i in range(count - 1)]
        forward.append((count - 1, 0))
        backward = [(target, source) for source, target in forward]
        low = lax.ppermute(
            lax.slice_in_dim(block, block.shape[dim] - width, None, axis=dim), axis, forward
        )
        high = lax.ppermute(lax.slice_in_dim(block, 0, width, axis=dim), axis, backward)
        block = jnp.concatenate([low, block, high], axis=dim)
    return block


def spectral_matrix(labels, slots):
    offset = labels[:, None] - labels[None, :]
    parity = (1 - 2 * (jnp.abs(offset) % 2)).astype(jnp.float32)
    sines = jnp.sin(jnp.pi * offset.astype(jnp.float32) / slots)
    safe = jnp.where(offset == 0, jnp.float32(1.0), sines)
    return jnp.where(offset == 0, jnp.float32(0.0), 0.5 * parity / safe)


def mode_tables(points):
    indices = jnp.arange(points, dtype=jnp.int32)
    product = indices[:, None] * indices[None, :] % points
    angles = 2.0 * jnp.pi * product.astype(jnp.float32) / points
    return (jnp.cos(angles), jnp.sin(angles))


def cycle_response(points, cycle_index, near):
    indices = jnp.arange(points, dtype=jnp.int32)
    wave_number = jnp.minimum(indices, points - indices)
    cutoff = jnp.maximum(4, points * (cycle_index + 1) // (2 * near))
    return (wave_number[None, :] < cutoff[:, None]).astype(jnp.float32)


def smooth_cycles(pencil, first_cycle, near):
    points = pencil.shape[1]
    cycles = pencil.shape[2]
    cosines, sines_table = mode_tables(points)
    cycle_index = first_cycle + jnp.arange(cycles, dtype=jnp.int32)
    response = (cycle_response(points, cycle_index, near).T / points)[None, :, :, None]
    coef_cos = jnp.einsum("tk,ftrx->fkrx", cosines, pencil, precision=lax.Precision.HIGHEST)
    coef_sin = jnp.einsum("tk,ftrx->fkrx", sines_table, pencil, precision=lax.Precision.HIGHEST)
    smoothed = jnp.einsum(
        "tk,fkrx->ftrx", cosines, coef_cos * response, precision=lax.Precision.HIGHEST
    )
    smoothed = smoothed + jnp.einsum(
        "tk,fkrx->ftrx", sines_table, coef_sin * response, precision=lax.Precision.HIGHEST
    )
    weights = jnp.maximum(1.0 - cycle_index.astype(jnp.float32) / near, 0.0)[None, None, :, None]
    return pencil + weights * (smoothed - pencil)


def viscous(center, nbr_up, nbr_dn, visc, visc_up, visc_dn, kappa, flags):
    cycles = center.shape[2]
    cells_x = center.shape[3]
    cycle_weight = (1.0 / (jnp.arange(cycles, dtype=jnp.float32) + 1.0))[None, :, None]
    theta = cycle_weight * (
        0.5 * (visc + visc_up) * (center - nbr_up) + 0.5 * (visc + visc_dn) * (center - nbr_dn)
    )
    face_r = 0.5 * (visc[:, :-1, :] + visc[:, 1:, :])
    flux_r = face_r * (center[:, :, :-1, :] - center[:, :, 1:, :])
    radial = jnp.pad(flux_r, ((0, 0), (0, 0), (0, 1), (0, 0))) - jnp.pad(
        flux_r, ((0, 0), (0, 0), (1, 0), (0, 0))
    )
    face_x = 0.5 * (visc[:, :, :-1] + visc[:, :, 1:])
    flux_x = face_x * (center[:, :, :, :-1] - center[:, :, :, 1:])
    axial = jnp.pad(flux_x, ((0, 0), (0, 0), (0, 0), (0, 1))) - jnp.pad(
        flux_x, ((0, 0), (0, 0), (0, 0), (1, 0))
    )
    open_faces = (1 - flags).astype(jnp.float32)
    outer = open_faces[:, 2][:, None, None, None] * visc[None, :, -1:, :] * center[:, :, -1:, :]
    outer = jnp.pad(outer, ((0, 0), (0, 0), (cycles - 1, 0), (0, 0)))
    inflow = open_faces[:, 0][:, None, None, None] * visc[None, :, :, :1] * center[:, :, :, :1]
    inflow = jnp.pad(inflow, ((0, 0), (0, 0), (0, 0), (0, cells_x - 1)))
    outflow = open_faces[:, 1][:, None, None, None] * visc[None, :, :, -1:] * center[:, :, :, -1:]
    outflow = jnp.pad(outflow, ((0, 0), (0, 0), (0, 0), (cells_x - 1, 0)))
    return kappa[:, None, None, None] * (theta + radial + axial + outer + inflow + outflow)


def body(adjoint, source, viscosity, kappa, coupling, bc_flags, inst_map):
    slots = lax.axis_size("inst")
    own_slot = lax.axis_index("inst")
    matrix = spectral_matrix(inst_map, slots)
    center = adjoint[0]
    column = lax.dynamic_slice_in_dim(matrix, own_slot, 1, 1)[:, 0]
    spectral = jnp.tensordot(
        column,
        lax.all_gather(adjoint, "inst", axis=0, tiled=True),
        axes=1,
        precision=lax.Precision.HIGHEST,
    )
    stacked = jnp.concatenate([center, viscosity[None]], axis=0)
    padded = with_halo(stacked, (("space", 1),), 1)
    fields = center.shape[0]
    diffused = viscous(
        center,
        padded[:fields, 2:],
        padded[:fields, :-2],
        viscosity,
        padded[fields, 2:],
        padded[fields, :-2],
        kappa,
        bc_flags,
    )
    coupled = jnp.einsum("gf,gtrx->ftrx", coupling, center, precision=lax.Precision.HIGHEST)
    pre = source[0] + coupled + diffused + spectral
    total_cycles = pre.shape[2]
    near = total_cycles // 2
    pencil = lax.all_to_all(pre[:, :, :near, :], "space", split_axis=2, concat_axis=1, tiled=True)
    first_cycle = lax.axis_index("space") * pencil.shape[2]
    result = smooth_cycles(pencil, first_cycle, near)
    inner = lax.all_to_all(result, "space", split_axis=1, concat_axis=2, tiled=True)
    residual = jnp.concatenate([inner, pre[:, :, near:, :]], axis=2)
    return residual[None]


def solution(mesh):
    return jax.shard_map(
        body,
        mesh=mesh,
        in_specs=(
            P("inst", None, "space", None, None),
            P("inst", None, "space", None, None),
            P("space", None, None),
            P(),
            P(),
            P(),
            P(),
        ),
        out_specs=P("inst", None, "space", None, None),
        check_vma=False,
    )
```

profile of v0, /device:TPU:0, one launch (start us, length us, event | category | flops | bytes accessed | tf_op | source)
XLA Modules:
  0.0 479.7 jit_solution(10881192963398426203)
XLA Ops:
  9.1 4.5 collective-permute-start
  14.2 9.8 %copy.101 = f32[1,5,32,64,128]{4,1,3,2,0:T(8,128)} copy(f32[1,5,32,64,128]{4,3,2,1,0:T(8,128)S(1)} %copy-done.2) | data formatting | bytes 10485760 | tf_op args[0]
  27.0 5.1 %pad_maximum_fusion = f32[6,32,64,128]{3,2,1,0:T(8,128)S(1)} fusion(f32[1,32,64,128]{3,2,1,0:T(8,128)S(1)} %bitcast.95, f32[5,32,64,128]{3,2,1,0:T(8,128)} %bitcast.89), kind=kLoop, calls=%fused_computation.4 | loop fusion | flops 1572864 | bytes 12582912 | tf_op jit(solution)/shard_map/concatenate | solution.py:100
  32.6 4.2 fusion.14
  36.8 4.5 fusion.2
  41.3 8.5 %slice_multiply_fusion.1 = (f32[5,32,64,1]{3,0,2,1:T(8,128)}, f32[5,32,64,1]{3,0,2,1:T(8,128)}) fusion(f32[5,32,64,128]{3,0,2,1:T(8,128)S(1)} %bitcast.87, f32[32,64]{1,0:T(8,128)S(1)} %bitcast.105, f32[5]{0:T(128)S(1)} %get-tuple-element.17, f32[32,64]{1,0:T(8,128)S(1)} %bitcast.106, f32[5]{0:T(128)S(1)} %get-tuple-element.16), kind=kLoop, calls=%fused_computation.6 | loop fusion | flops 40960 | bytes 180264 | tf_op jit(solution)/shard_map/mul | solution.py:81
  51.0 5.6 %copy_dynamic-update-slice_fusion = f32[6,33,64,128]{3,0,2,1:T(8,128)S(1)} fusion(f32[6,33,64,128]{3,0,2,1:T(8,128)S(1)} %copy_dynamic-update-slice_fusion.1, f32[6,32,64,128]{3,2,1,0:T(8,128)S(1)} %pad_maximum_fusion), kind=kLoop, calls=%fused_computation.23 | loop fusion | bytes 14680064 | tf_op jit(solution)/shard_map/concatenate | solution.py:17
  56.6 3.4 copy-done.5
  61.5 3.2 fusion.16
  64.7 140.4 %all-gather.2.cloned.1.call-done = f32[4,5,32,64,128]{4,3,2,1,0:T(8,128)} async-done(((f32[1,5,32,64,128]{4,3,2,1,0:T(8,128)}), f32[4,5,32,64,128]{4,3,2,1,0:T(8,128)}) %all-gather.2.cloned.1.call-update) | async-done | bytes 20971536 | tf_op jit(solution)/shard_map/all_gather | solution.py:96
  205.2 57.2 %fusion = f32[1,5,32,64,128]{4,0,3,2,1:T(1,128)S(1)} fusion(f32[4,5,32,64,128]{4,3,2,1,0:T(8,128)} %all-gather.2.cloned.1.call-done, f32[4,4]{0,1:T(4,128)S(1)} %fusion.58, s32[]{:T(128)S(6)} %select_n.41), kind=kOutput, calls=%fused_computation | convolution fusion | flops 62914560 | bytes 26214916 | tf_op jit(solution)/shard_map/dot_general | solution.py:94
  262.4 39.9 %fusion.13 = f32[5,32,64,128]{3,0,2,1:T(8,128)S(1)} fusion(f32[6,33,64,128]{3,0,2,1:T(8,128)} %copy-done.5, f32[1,5,32,64,128]{4,0,3,2,1:T(1,128)S(1)} %fusion, f32[5,32,64,128]{3,2,1,0:T(8,128)S(1)} %copy-done.4, f32[1,5,32,64,128]{4,3,2,1,0:T(8,128)} %param.8, f32[5,32,64,1]{3,0,2,1:T(8,128)} %get-tuple-element.8, f32[5,32,64,1]{3,0,2,1:T(8,128)} %get-tuple-element.7, ...), kind=kOutput, calls=%fused_computation.20 | convolution fusion | flops 98304000 | bytes 74400120 | tf_op jit(solution)/shard_map/gf,gtrx->ftrx/dot_general | solution.py:113
  302.3 2.8 fusion.79
  305.1 3.0 copy.64
  308.1 4.6 all-to-all-start
  312.8 60.2 %all-to-all-done = f32[5,32,32,128]{3,1,0,2:T(8,128)S(1)} async-done(((f32[5,32,32,128]{3,1,0,2:T(8,128)}), f32[5,32,32,128]{3,1,0,2:T(8,128)S(1)}, u32[]{:S(2)}, u32[]{:S(2)}) %all-to-all-start) | async-done | bytes 2621472 | tf_op jit(solution)/shard_map/all_to_all | solution.py:117
  378.9 5.4 %fusion.29 = f32[5,4,128,256]{3,2,1,0:T(8,128)S(1)} fusion(f32[5,256,4,128]{3,1,2,0:T(8,128)S(1)} %bitcast.99), kind=kOutput, calls=%fused_computation.55 | convolution fusion | flops 2014183424 | bytes 5242880 | tf_op jit(solution)/shard_map/tk,ftrx->fkrx/dot_general | solution.py:50
  384.3 5.5 %fusion.32 = f32[5,4,128,256]{3,2,1,0:T(8,128)S(1)} fusion(f32[5,256,4,128]{3,1,2,0:T(8,128)S(1)} %bitcast.100), kind=kOutput, calls=%fused_computation.58 | convolution fusion | flops 2014183424 | bytes 5242880 | tf_op jit(solution)/shard_map/tk,ftrx->fkrx/dot_general | solution.py:49
  389.8 3.5 fusion.19
  393.3 4.9 %fusion.18 = f32[5,256,4,128]{1,3,2,0:T(8,128)} fusion(f32[5,256,4,128]{1,3,2,0:T(8,128)S(1)} %copy-done.7, f32[5,4,128,256]{3,2,1,0:T(8,128)S(1)} %fusion.19, f32[5,4,128,256]{3,2,1,0:T(8,128)S(1)} %fusion.32, f32[256,4]{0,1:T(4,128)S(1)} %compare_select_fusion, f32[4]{0:T(128)S(1)} %subtract_maximum_fusion), kind=kOutput, calls=%fused_computation.35 | convolution fusion | flops 2017460224 | bytes 10489872 | tf_op jit(solution)/shard_map/tk,fkrx->ftrx/dot_general | solution.py:51
  398.2 3.3 copy.71
  401.4 62.8 %all_to_all.36 = f32[5,256,4,128]{3,2,0,1:T(4,128)S(1)} all-to-all(f32[5,256,4,128]{3,2,0,1:T(4,128)S(1)} %copy.71), channel_id=1, replica_groups=mesh['inst'=4,'space'=8] {'space'}, dimensions={1} | all-to-all | bytes 5242880 | tf_op jit(solution)/shard_map/all_to_all | solution.py:120
  466.1 3.2 maximum_bitcast_fusion
  469.3 3.3 copy.74
  (61 shorter events, 17.2 us)
Async XLA Ops:
  6.5 255.8 %copy-start = (f32[5,5]{1,0:T(8,128)S(1)}, f32[5,5]{1,0:T(8,128)}, u32[]{:S(2)}) copy-start(f32[5,5]{1,0:T(8,128)} %param.11) | copy-start | bytes 304
  6.5 7.1 %copy-start.3 = (f32[32,64,128]{2,1,0:T(8,128)S(1)}, f32[32,64,128]{2,1,0:T(8,128)}, u32[]{:S(2)}) copy-start(f32[32,64,128]{2,1,0:T(8,128)} %param.9) | copy-start | bytes 3145732
  6.5 198.6 %all-gather.2.cloned.1.call-start = ((), (), s32[]{:S(2)}) async-start(), calls=%async_computation.2 | async-start | bytes 26214400 | tf_op jit(solution)/shard_map/all_gather | solution.py:96
  7.3 7.0 %copy-start.2 = (f32[1,5,32,64,128]{4,3,2,1,0:T(8,128)S(1)}, f32[1,5,32,64,128]{4,3,2,1,0:T(8,128)}, u32[]{:S(2)}) copy-start(f32[1,5,32,64,128]{4,3,2,1,0:T(8,128)} %param.7) | copy-start | bytes 15728644
  9.1 52.0 %collective-permute-start = (f32[6,1,64,128]{3,2,1,0:T(8,128)S(1)}, f32[6,1,64,128]{3,2,1,0:T(8,128)S(1)}, u32[]{:S(2)}, u32[]{:S(2)}) collective-permute-start(f32[6,1,64,128]{3,2,1,0:T(8,128)S(1)} %get-tuple-element.9), channel_id=1, source_target_pairs={{1,0},{2,1},{3,2},{4,3},{5,4},{6,5},{7,6},{0,7},{9,8},{10,9},{11,1... | collective-permute-start | bytes 589832 | tf_op jit(solution)/shard_map/ppermute | solution.py:16
  13.6 36.3 %collective-permute-start.1 = (f32[6,1,64,128]{3,2,1,0:T(8,128)}, f32[6,1,64,128]{3,2,1,0:T(8,128)}, u32[]{:S(2)}, u32[]{:S(2)}) collective-permute-start(f32[6,1,64,128]{3,2,1,0:T(8,128)} %get-tuple-element.10), channel_id=1, source_target_pairs={{0,1},{1,2},{2,3},{3,4},{4,5},{5,6},{6,7},{7,0},{8,9},{9,10},{10,1... | collective-permute-start | bytes 589832 | tf_op jit(solution)/shard_map/ppermute | solution.py:13
  14.2 11.5 %copy-start.10 = (s32[5,3]{0,1:T(4,128)S(1)}, s32[5,3]{0,1:T(4,128)}, u32[]{:S(2)}) copy-start(s32[5,3]{0,1:T(4,128)} %param.12) | copy-start | bytes 184
  25.8 6.8 %slice-start = ((s8[8388608]{0:T(1024)(128)(4,1)}), s8[4194304]{0:T(1024)(128)(4,1)S(1)}, s32[]{:S(2)}) async-start(s8[8388608]{0:T(1024)(128)(4,1)} %bitcast.83), calls=%async_computation.3 | async-start | bytes 8388608
  26.9 5.7 %slice-start.1 = ((s8[8388608]{0:T(1024)(128)(4,1)}), s8[4194304]{0:T(1024)(128)(4,1)S(1)}, s32[]{:S(2)}) async-start(s8[8388608]{0:T(1024)(128)(4,1)} %bitcast.83), calls=%async_computation.4 | async-start | bytes 8388608
  36.8 4.5 copy-start.8
  36.8 24.3 %slice-start.2 = ((s8[5242880]{0:T(1024)(128)(4,1)}), s8[4194304]{0:T(1024)(128)(4,1)S(1)}, s32[]{:S(2)}) async-start(s8[5242880]{0:T(1024)(128)(4,1)} %bitcast.90), calls=%async_computation.5 | async-start | bytes 8388608
  41.3 8.5 %copy-start.9 = (s32[4]{0:T(128)S(1)}, s32[4]{0:T(128)}, u32[]{:S(2)}) copy-start(s32[4]{0:T(128)} %param.13) | copy-start | bytes 52
  41.3 19.8 %slice-start.3 = ((s8[5242880]{0:T(1024)(128)(4,1)}), s8[1048576]{0:T(1024)(128)(4,1)S(1)}, s32[]{:S(2)}) async-start(s8[5242880]{0:T(1024)(128)(4,1)} %bitcast.90), calls=%async_computation.6 | async-start | bytes 2097152
  56.6 3.4 copy-start.5
  64.7 197.7 %copy-start.11 = (f32[5]{0:T(128)S(1)}, f32[5]{0:T(128)}, u32[]{:S(2)}) copy-start(f32[5]{0:T(128)} %param.10) | copy-start | bytes 64
  205.2 57.2 %copy-start.4 = (f32[5,32,64,128]{3,2,1,0:T(8,128)S(1)}, f32[5,32,64,128]{3,2,1,0:T(8,128)}, u32[]{:S(2)}) copy-start(f32[5,32,64,128]{3,2,1,0:T(8,128)} %fusion.16) | copy-start | bytes 15728644
  308.1 64.9 %all-to-all-start = ((f32[5,32,32,128]{3,1,0,2:T(8,128)}), f32[5,32,32,128]{3,1,0,2:T(8,128)S(1)}, u32[]{:S(2)}, u32[]{:S(2)}) async-start(f32[5,32,32,128]{3,1,0,2:T(8,128)} %copy.64), calls=%async_computation | async-start | bytes 5242880 | tf_op jit(solution)/shard_map/all_to_all | solution.py:117
  373.0 1.5 copy-start.6
  378.9 14.4 %copy-start.7 = (f32[5,256,4,128]{1,3,2,0:T(8,128)S(1)}, f32[5,256,4,128]{1,3,2,0:T(8,128)}, u32[]{:S(2)}) copy-start(f32[5,256,4,128]{1,3,2,0:T(8,128)} %copy.70) | copy-start | bytes 7864324
  466.1 6.5 %copy-start.1 = (f32[5,5]{1,0:T(8,128)S(1)}, f32[5,5]{1,0:T(8,128)}, u32[]{:S(2)}) copy-start(f32[5,5]{1,0:T(8,128)} %param.11) | copy-start | bytes 304
Sparse Core Ops, SparseCore 0:
  9.2 195.8 all-gather.1
where the time goes:
time: 485 us; the launch traced here: 480 us
  waiting for transfers between devices  201 us (41%)
  matrix products  116 us (24%)
  blocking collectives  62.8 us (13%)
  local copies, waits for them, and re-layouts  43.5 us (9%)
  other arithmetic  32.7 us (7%)
  between operations  13.9 us (3%)
  starting transfers between devices  9.1 us (2%)
    all_gather x1, waiting for transfers between devices, body(): lax.all_gather(adjoint, 'inst', axis=0, tiled=True)  140 us
    all_to_all x1, blocking collectives, body(): lax.all_to_all(result, 'space', split_axis=1, concat_axis=2, tiled=True)  62.8 us
    all_to_all x1, waiting for transfers between devices, body(): lax.all_to_all(pre[:, :, :near, :], 'space', split_axis=2, concat_axis=1,...  60.2 us
    dot_general x1, matrix products, body(): jnp.tensordot(column, lax.all_gather(adjoint, 'inst', axis=0, tiled=True)...  57.2 us
    dot_general x1, matrix products, body(): jnp.einsum('gf,gtrx->ftrx', coupling, center, precision=lax.Precision.HIG...  39.9 us
    unnamed x36, local copies, waits for them, and re-layouts  17.2 us
  transfers between devices with their start and end apart: 4, of which 2 were waited for; matrix products, arithmetic and copies ran while one was open for 10% of the time, Pallas kernels for 0%

commit v1 on v0

v1 whole, which is shorter than its diff:
```python
import functools

import jax
import jax.numpy as jnp
import numpy as np
from jax import lax
from jax.experimental import pallas as pl
from jax.experimental.pallas import tpu as pltpu
from jax.sharding import PartitionSpec as P

GROUP = 4
NEAR_SIZES = (2, 2, 1)
FAR_SIZES = (3, 2)
SMEM = pl.BlockSpec(memory_space=pltpu.SMEM)
VMEM_LIMIT = 48 * 1024 * 1024


def spectral_matrix(labels, slots):
    offset = labels[:, None] - labels[None, :]
    parity = (1 - 2 * (jnp.abs(offset) % 2)).astype(jnp.float32)
    sines = jnp.sin(jnp.pi * offset.astype(jnp.float32) / slots)
    safe = jnp.where(offset == 0, jnp.float32(1.0), sines)
    return jnp.where(offset == 0, jnp.float32(0.0), 0.5 * parity / safe)


def mode_layout(points, near):
    half = points // 2
    pairs = near // 2
    bases, base, scale = [], np.zeros(near, np.float32), np.zeros(near, np.float32)
    for r in range(near):
        cutoff = max(4, points * (r + 1) // (2 * near))
        weight = max(1.0 - r / near, 0.0)
        kept = [m for m in range(half + 1) if m < cutoff]
        out = [m for m in range(half + 1) if m >= cutoff]
        count = [sum(1 if m in (0, half) else 2 for m in modes) for modes in (kept, out)]
        low = count[0] <= count[1]
        rows = []
        for m in kept if low else out:
            norm = np.sqrt((1.0 if m in (0, half) else 2.0) / points)
            rows.append((m, 0, norm))
            if m not in (0, half):
                rows.append((m, points // 4, norm))
        bases.append(rows)
        base[r] = 1.0 - weight if low else 1.0
        scale[r] = weight if low else -weight
    depth = max(len(bases[p]) + len(bases[p + pairs]) for p in range(pairs))
    depth = -(-depth // 8) * 8
    mode = np.zeros((pairs, depth), np.int32)
    phase = np.zeros((pairs, depth), np.int32)
    which = np.zeros((pairs, depth), np.int32)
    norm = np.zeros((pairs, depth), np.float32)
    for p in range(pairs):
        rows = [(0,) + row for row in bases[p]] + [(1,) + row for row in bases[p + pairs]]
        for i, (a, m, ph, nm) in enumerate(rows):
            mode[p, i], phase[p, i], which[p, i], norm[p, i] = m, ph, a, nm
    pair_base = np.stack([base[:pairs], base[pairs:]], axis=1)
    pair_scale = np.stack([scale[:pairs], scale[pairs:]], axis=1)
    return mode, phase, which, norm, pair_base, pair_scale


def filter_tables(points, near, block, place):
    mode, phase, which, norm, base, scale = mode_layout(points, near)
    owned = mode.shape[0] // GROUP
    depth = mode.shape[1]
    rank = place % GROUP
    mine = lambda table: lax.dynamic_slice_in_dim(jnp.asarray(table), rank * owned, owned, 0)
    mode, phase, which, norm, base, scale = map(mine, (mode, phase, which, norm, base, scale))
    sector = (place - rank) + (rank ^ jnp.arange(GROUP, dtype=jnp.int32))
    theta = sector[:, None] * block + jnp.arange(block, dtype=jnp.int32)[None, :]
    theta = theta.reshape(-1)
    index = (mode[:, :, None] * theta[None, None, :] - phase[:, :, None] + points) % points
    wave = norm[:, :, None] * jnp.cos(index.astype(jnp.float32) * np.float32(2.0 * np.pi / points))
    side = which[:, :, None, None] == jnp.arange(2, dtype=jnp.int32)[None, None, :, None]
    table = jnp.where(side, wave[:, :, None, :], jnp.float32(0.0))
    back = jnp.transpose(table * scale[:, None, :, None], (0, 2, 3, 1))
    width = 2 * GROUP * block
    return (
        table.reshape(owned, depth, width),
        back.reshape(owned, width, depth),
        base.reshape(-1),
    )


def local_kernel(
    coupling, kappa, flags, adj, before, after, src, mu, mu_before, mu_after, low, high, out
):
    fields, planes, rows, cells = adj.shape
    step = pl.program_id(0)
    first = step == 0
    last = step == pl.num_programs(0) - 1
    row = lax.broadcasted_iota(jnp.int32, (rows, cells), 0)
    col = lax.broadcasted_iota(jnp.int32, (rows, cells), 1)
    ring = 0.5 / (row.astype(jnp.float32) + 1.0)

    def pick(source, behind, ahead, f, k):
        if k < 0:
            return jnp.where(first, low[f, 0], behind)
        if k >= planes:
            return jnp.where(last, high[f, 0], ahead)
        return source

    def visc(k):
        return pick(mu[max(0, min(k, planes - 1))], mu_before[0], mu_after[0], fields, k)

    def cell(f, k):
        return pick(adj[f, max(0, min(k, planes - 1))], before[f, 0], after[f, 0], f, k)

    for k in range(planes):
        m = visc(k)
        up = ring * (m + visc(k + 1))
        down = ring * (m + visc(k - 1))
        outer = jnp.where(row < rows - 1, 0.5 * (m + pltpu.roll(m, rows - 1, 0)), 0.0)
        inner = jnp.where(row > 0, 0.5 * (m + pltpu.roll(m, 1, 0)), 0.0)
        east = jnp.where(col < cells - 1, 0.5 * (m + pltpu.roll(m, cells - 1, 1)), 0.0)
        west = jnp.where(col > 0, 0.5 * (m + pltpu.roll(m, 1, 1)), 0.0)
        diag = up + down + outer + inner + east + west
        for f in range(fields):
            p = adj[f, k]
            opens = [(1 - flags[f, i]).astype(jnp.float32) for i in range(3)]
            wall = jnp.where(col == 0, opens[0], 0.0)
            wall = wall + jnp.where(col == cells - 1, opens[1], 0.0)
            wall = wall + jnp.where(row == rows - 1, opens[2], 0.0)
            flux = (diag + wall * m) * p
            flux = flux - up * cell(f, k + 1) - down * cell(f, k - 1)
            flux = flux - outer * pltpu.roll(p, rows - 1, 0) - inner * pltpu.roll(p, 1, 0)
            flux = flux - east * pltpu.roll(p, cells - 1, 1) - west * pltpu.roll(p, 1, 1)
            total = src[f, k] + kappa[f] * flux
            for g in range(fields):
                total = total + coupling[g, f] * adj[g, k]
            out[f, k] = total


def local_part(center, source, viscosity, kappa, coupling, flags, low, high):
    fields, block, rows, cells = center.shape
    planes = min(4, block)
    steps = block // planes
    whole = lambda width, index: pl.BlockSpec((fields, width, rows, cells), lambda i: (0, index(i), 0, 0))
    plane = lambda width, index: pl.BlockSpec((width, rows, cells), lambda i: (index(i), 0, 0))
    behind = lambda i: jnp.maximum(i * planes - 1, 0)
    ahead = lambda i: jnp.minimum(i * planes + planes, block - 1)
    here = lambda i: i
    halo = pl.BlockSpec((fields + 1, 1, rows, cells), lambda i: (0, 0, 0, 0))
    return pl.pallas_call(
        local_kernel,
        grid=(steps,),
        in_specs=[
            SMEM,
            SMEM,
            SMEM,
            whole(planes, here),
            whole(1, behind),
            whole(1, ahead),
            whole(planes, here),
            plane(planes, here),
            plane(1, behind),
            plane(1, ahead),
            halo,
            halo,
        ],
        out_specs=whole(planes, here),
        out_shape=jax.ShapeDtypeStruct(center.shape, jnp.float32),
        compiler_params=pltpu.CompilerParams(vmem_limit_bytes=VMEM_LIMIT),
        cost_estimate=pl.CostEstimate(
            flops=40 * center.size, bytes_accessed=16 * center.size, transcendentals=0
        ),
        name="local_part",
    )(coupling, kappa, flags, center, center, center, source, viscosity, viscosity, viscosity, low, high)


def sums(coef, local, others):
    steps = (len(others) - 2) // 2
    half = local.shape[1] // 2
    far_hi, mix_lo = others[:steps], others[steps]
    far_lo, mix_hi = others[steps + 1], others[steps + 2 :]
    top = local[0, :half] + mix_lo[0]
    for s in range(steps):
        top = top + coef[s] * far_hi[s][0]
    bottom = local[0, half:] + coef[steps] * far_lo[0]
    for s in range(steps):
        bottom = bottom + mix_hi[s][0]
    return top, bottom


def spread_kernel(count, rank, coef, local, *refs):
    others, outs, (flat, stage) = refs[:count], refs[count : count + GROUP], refs[count + GROUP :]
    top, bottom = sums(coef, local, others)
    block, near, cells = local.shape[1:]
    size = top.shape[0] * near
    flat[:size] = top.reshape(size, cells)
    flat[size:] = bottom.reshape(size, cells)
    pairs = near // 2
    owned = pairs // GROUP
    for o in range(GROUP):
        for j in range(owned):
            for a in range(2):
                r = o * owned + j + a * pairs
                stage[o, 2 * j + a] = flat[pl.ds(r, block, stride=near), :]
    for k in range(GROUP):
        outs[k][0] = stage[rank[0] ^ k]


def spread(rank, coef, local, others, first, fields, near):
    block, rows, cells = local.shape[1:]
    cycles = near // GROUP
    part = lambda width: pl.BlockSpec((1, width, near, cells), lambda i: (i, 0, 0, 0))
    return pl.pallas_call(
        functools.partial(spread_kernel, len(others)),
        grid=(fields,),
        in_specs=[SMEM, SMEM, pl.BlockSpec((1, block, near, cells), lambda i: (first + i, 0, 0, 0))]
        + [part(block // 2)] * len(others),
        out_specs=[pl.BlockSpec((1, cycles, block, cells), lambda i: (i, 0, 0, 0))] * GROUP,
        out_shape=[jax.ShapeDtypeStruct((fields, cycles, block, cells), jnp.float32)] * GROUP,
        scratch_shapes=[
            pltpu.VMEM((block * near, cells), jnp.float32),
            pltpu.VMEM((GROUP, cycles, block, cells), jnp.float32),
        ],
        compiler_params=pltpu.CompilerParams(vmem_limit_bytes=VMEM_LIMIT),
        cost_estimate=pl.CostEstimate(
            flops=4 * fields * block * near * cells,
            bytes_accessed=16 * fields * block * near * cells,
            transcendentals=0,
        ),
        name="spread",
    )(rank, coef, local, *others)


def coefficient_kernel(table, *refs):
    parts, out = refs[:GROUP], refs[GROUP]
    for j in range(table.shape[0]):
        column = jnp.concatenate([parts[k][0, 2 * j + a] for a in range(2) for k in range(GROUP)], axis=0)
        out[0, j] = jnp.dot(
            table[j], column, precision=lax.Precision.HIGHEST, preferred_element_type=jnp.float32
        )


def coefficients(table, parts):
    fields, cycles, block, cells = parts[0].shape
    owned, depth, width = table.shape
    return pl.pallas_call(
        coefficient_kernel,
        grid=(fields,),
        in_specs=[pl.BlockSpec(table.shape, lambda i: (0, 0, 0))]
        + [pl.BlockSpec((1, cycles, block, cells), lambda i: (i, 0, 0, 0))] * GROUP,
        out_specs=pl.BlockSpec((1, owned, depth, cells), lambda i: (i, 0, 0, 0)),
        out_shape=jax.ShapeDtypeStruct((fields, owned, depth, cells), jnp.float32),
        compiler_params=pltpu.CompilerParams(vmem_limit_bytes=VMEM_LIMIT),
        cost_estimate=pl.CostEstimate(
            flops=12 * fields * owned * depth * width * cells,
            bytes_accessed=4 * (table.size + fields * owned * (depth + width) * cells),
            transcendentals=0,
        ),
        name="coefficients",
    )(table, *parts)


def filtered_kernel(base, back, own, other, *refs):
    parts, outs = refs[:GROUP], refs[GROUP:]
    block = parts[0].shape[2]
    for j in range(back.shape[0]):
        total = own[0, j] + other[0, j]
        waves = jnp.dot(
            back[j], total, precision=lax.Precision.HIGHEST, preferred_element_type=jnp.float32
        )
        for a in range(2):
            for k in range(GROUP):
                start = (a * GROUP + k) * block
                outs[k][0, 2 * j + a] = (
                    base[2 * j + a] * parts[k][0, 2 * j + a] + waves[start : start + block]
                )


def filtered(base, back, own, other, parts):
    fields, cycles, block, cells = parts[0].shape
    owned, width, depth = back.shape
    part = pl.BlockSpec((1, cycles, block, cells), lambda i: (i, 0, 0, 0))
    modes = pl.BlockSpec((1, owned, depth, cells), lambda i: (i, 0, 0, 0))
    return pl.pallas_call(
        filtered_kernel,
        grid=(fields,),
        in_specs=[SMEM, pl.BlockSpec(back.shape, lambda i: (0, 0, 0)), modes, modes] + [part] * GROUP,
        out_specs=[part] * GROUP,
        out_shape=[jax.ShapeDtypeStruct(parts[0].shape, jnp.float32)] * GROUP,
        compiler_params=pltpu.CompilerParams(vmem_limit_bytes=VMEM_LIMIT),
        cost_estimate=pl.CostEstimate(
            flops=12 * fields * owned * depth * width * cells,
            bytes_accessed=4 * (back.size + 2 * fields * owned * (depth + width) * cells),
            transcendentals=0,
        ),
        name="filtered",
    )(base, back, own, other, *parts)


def near_kernel(rank, *refs):
    parts, out, stage = refs[:GROUP], refs[-2], refs[-1]
    near = out.shape[2]
    pairs = near // 2
    owned = pairs // GROUP
    for k in range(GROUP):
        stage[rank[0] ^ k] = parts[k][0]
    for o in range(GROUP):
        for j in range(owned):
            for a in range(2):
                out[0, :, o * owned + j + a * pairs, :] = stage[o, 2 * j + a]


def place_near(rank, parts, held, first, shape, near):
    fields, cycles, block, cells = parts[0].shape
    carried = [] if held is None else [held]
    return pl.pallas_call(
        near_kernel,
        grid=(fields,),
        in_specs=[SMEM]
        + [pl.BlockSpec((1, cycles, block, cells), lambda i: (i, 0, 0, 0))] * GROUP
        + [pl.BlockSpec(memory_space=pl.ANY)] * len(carried),
        out_specs=pl.BlockSpec((1, block, near, cells), lambda i: (first + i, 0, 0, 0)),
        out_shape=jax.ShapeDtypeStruct(shape, jnp.float32),
        scratch_shapes=[pltpu.VMEM((GROUP, cycles, block, cells), jnp.float32)],
        input_output_aliases={1 + GROUP: 0} if carried else {},
        compiler_params=pltpu.CompilerParams(vmem_limit_bytes=VMEM_LIMIT),
        cost_estimate=pl.CostEstimate(
            flops=0, bytes_accessed=8 * fields * block * near * cells, transcendentals=0
        ),
        name="place_near",
    )(rank, *parts, *carried)


def far_kernel(coef, local, *refs):
    others, out = refs[:-2], refs[-1]
    half = local.shape[1] // 2
    top, bottom = sums(coef, local, others)
    out[0, :half] = top
    out[0, half:] = bottom


def place_far(coef, local, others, held, first, fields, near):
    block, rows, cells = local.shape[1:]
    side = pl.BlockSpec((1, block, near, cells), lambda i: (first + i, 0, 1, 0))
    return pl.pallas_call(
        far_kernel,
        grid=(fields,),
        in_specs=[SMEM, side]
        + [pl.BlockSpec((1, block // 2, near, cells), lambda i: (i, 0, 0, 0))] * len(others)
        + [pl.BlockSpec(memory_space=pl.ANY)],
        out_specs=side,
        out_shape=jax.ShapeDtypeStruct(held.shape, jnp.float32),
        input_output_aliases={2 + len(others): 0},
        compiler_params=pltpu.CompilerParams(vmem_limit_bytes=VMEM_LIMIT),
        cost_estimate=pl.CostEstimate(
            flops=4 * fields * block * near * cells,
            bytes_accessed=16 * fields * block * near * cells,
            transcendentals=0,
        ),
        name="place_far",
    )(coef, local, *others, held)


def spans(sizes, total):
    ends = np.minimum(np.cumsum(sizes), total)
    ends[-1] = total
    starts = np.concatenate([[0], ends[:-1]])
    return [(int(s), int(e)) for s, e in zip(starts, ends) if e > s]


def body(adjoint, source, viscosity, kappa, coupling, bc_flags, inst_map):
    slots = lax.axis_size("inst")
    sectors = lax.axis_size("space")
    center = adjoint[0]
    fields, block, cycles, cells = center.shape
    near = cycles // 2
    half = block // 2
    span = slots // 2

    def turned(i, s):
        return ((i // 2 + s) % span) * 2 + i % 2

    def to_pair(x):
        return lax.ppermute(x, "inst", [(i, i ^ 1) for i in range(slots)])

    def to_turned(x, s):
        return lax.ppermute(x, "inst", [(i, turned(i, s)) for i in range(slots)])

    def to_sector(x, k):
        return lax.ppermute(x, "space", [(i, i ^ k) for i in range(sectors)])

    matrix = spectral_matrix(inst_map, slots)
    slot = lax.axis_index("inst")
    pair = slot ^ 1
    weight = lambda i, j: matrix[i, j]
    shifts = range(1, span)
    coef = jnp.stack([weight(turned(slot, span - s), slot) for s in shifts] + [weight(pair, slot)])

    def first_step(lo, hi, base):
        top = center[lo:hi, :half, base : base + near]
        bottom = center[lo:hi, half:, base : base + near]
        return top, bottom, [to_turned(top, s) for s in shifts], to_pair(bottom)

    def second_step(top, bottom, hi_parts, lo_part):
        mix = weight(slot, pair) * top
        for s, part in zip(shifts, hi_parts):
            mix = mix + weight(turned(slot, span - s), pair) * part
        mix_lo = to_pair(mix)
        mix_hi = []
        for s in shifts:
            target = turned(slot, s)
            mix_hi.append(
                to_turned(weight(slot, target) * bottom + weight(pair, target) * lo_part, s)
            )
        return hi_parts + [mix_lo, lo_part] + mix_hi

    near_spans = spans(NEAR_SIZES, fields)
    far_spans = spans(FAR_SIZES, fields)

    def edge(start):
        return jnp.concatenate(
            [center[:, start : start + 1], viscosity[None, start : start + 1]], axis=0
        )

    ring = lambda step: [(i, (i + step) % sectors) for i in range(sectors)]
    low = lax.ppermute(edge(block - 1), "space", ring(1))
    high = lax.ppermute(edge(0), "space", ring(-1))

    local = local_part(center, source[0], viscosity, kappa, coupling, bc_flags, low, high)

    place = lax.axis_index("space")
    rank = (place % GROUP).reshape(1)
    points = block * sectors
    table, back, base = filter_tables(points, near, block, place)

    result = None
    for lo, hi in near_spans:
        others = second_step(*first_step(lo, hi, 0))
        mine = spread(rank, coef, local, others, lo, hi - lo, near)
        parts = [mine[0]] + [to_sector(mine[k], k) for k in range(1, GROUP)]
        own = coefficients(table, parts)
        stride = GROUP
        while 2 * stride < sectors:
            own = own + to_sector(own, stride)
            stride = 2 * stride
        other = to_sector(own, stride) if stride < sectors else jnp.zeros_like(own)
        done = filtered(base, back, own, other, parts)
        done = [done[0]] + [to_sector(done[k], k) for k in range(1, GROUP)]
        result = place_near(rank, done, result, lo, center.shape, near)
    for lo, hi in far_spans:
        others = second_step(*first_step(lo, hi, near))
        result = place_far(coef, local, others, result, lo, hi - lo, near)
    return result[None]


def solution(mesh):
    return jax.shard_map(
        body,
        mesh=mesh,
        in_specs=(
            P("inst", None, "space", None, None),
            P("inst", None, "space", None, None),
            P("space", None, None),
            P(),
            P(),
            P(),
            P(),
        ),
        out_specs=P("inst", None, "space", None, None),
        check_vma=False,
    )
```

time: 485 us -> 231 us (0.48)
  matrix products: 116 us -> 0 us
  waiting for transfers between devices: 201 us -> 95.5 us
  blocking collectives: 62.8 us -> 0 us
  Pallas kernels: 0 us -> 42.3 us
  starting transfers between devices: 9.1 us -> 40.8 us
  local copies, waits for them, and re-layouts: 43.5 us -> 22.5 us
  between operations: 13.9 us -> 0.41 us
    all_gather x1 -> x0, waiting for transfers between devices: 140 us -> none  [body(): lax.all_gather(adjoint, 'inst', axis=0, tiled=True)]
    dot_general x6 -> x0, matrix products: 116 us -> none  [the longest x1 57.2 us: body(): jnp.tensordot(column, lax.all_gather(adjoint, 'inst', axis=0, tiled=True)...]
    ppermute x2 -> x43, waiting for transfers between devices: 0.01 us -> 95.5 us  [the longest x21 62 us: to_sector(): return lax.ppermute(x, 'space', [(i, i ^ k) for i in range(sectors)])]
    all_to_all x1 -> x0, blocking collectives: 62.8 us -> none  [body(): lax.all_to_all(result, 'space', split_axis=1, concat_axis=2, tiled=True)]
    all_to_all x1 -> x0, waiting for transfers between devices: 60.2 us -> none  [body(): lax.all_to_all(pre[:, :, :near, :], 'space', split_axis=2, concat_axis=1,...]
    pallas_call x0 -> x15, Pallas kernels: none -> 42.3 us  [the longest x1 12.4 us: local_part(): pl.pallas_call(local_kernel, grid=(steps,), in_specs=[SMEM, SMEM, SMEM, w...]
    ppermute x2 -> x43, starting transfers between devices: 4.49 us -> 40.8 us  [the longest x10 14.2 us: to_pair(): return lax.ppermute(x, 'inst', [(i, i ^ 1) for i in range(slots)])]
    mul x8 -> x3, other arithmetic: 22.3 us -> 3.02 us  [the longest x1 2.81 us: filter_tables(): norm[:, :, None]]
  transfers between devices with their start and end apart: 4 -> 43, of which waited for: 2 -> 15; matrix products, arithmetic and copies ran while one was open for 10% -> 17% of each run, Pallas kernels for 0% -> 17%
where the time goes in v1:
time: 231 us; the launch traced here: 230 us
  waiting for transfers between devices  95.5 us (41%)
  Pallas kernels  42.3 us (18%)
  starting transfers between devices  40.8 us (18%)
  other arithmetic  28.3 us (12%)
  local copies, waits for them, and re-layouts  22.5 us (10%)
    ppermute x21, waiting for transfers between devices, to_sector(): return lax.ppermute(x, 'space', [(i, i ^ k) for i in range(sectors)])  62 us
    ppermute x10, waiting for transfers between devices, to_turned(): return lax.ppermute(x, 'inst', [(i, turned(i, s)) for i in range(slots)])  18.4 us
    add x4, other arithmetic, second_step(): weight(slot, target) * bottom + weight(pair, target) * lo_part  18.2 us
    ppermute x10, waiting for transfers between devices, to_pair(): return lax.ppermute(x, 'inst', [(i, i ^ 1) for i in range(slots)])  15 us
    ppermute x10, starting transfers between devices, to_pair(): return lax.ppermute(x, 'inst', [(i, i ^ 1) for i in range(slots)])  14.2 us
    ppermute x21, starting transfers between devices, to_sector(): return lax.ppermute(x, 'space', [(i, i ^ k) for i in range(sectors)])  12.9 us
    ppermute x10, starting transfers between devices, to_turned(): return lax.ppermute(x, 'inst', [(i, turned(i, s)) for i in range(slots)])  12.8 us
    pallas_call x1, Pallas kernels, local_part(): pl.pallas_call(local_kernel, grid=(steps,), in_specs=[SMEM, SMEM, SMEM, w...  12.4 us
  transfers between devices with their start and end apart: 43, of which 15 were waited for; matrix products, arithmetic and copies ran while one was open for 17% of the time, Pallas kernels for 17%

profile of v1, /device:TPU:0, one launch (start us, length us, event | category | flops | bytes accessed | tf_op | source)
XLA Modules:
  0.0 229.7 jit_solution(17629118746807393151)
XLA Ops:
  0.0 2.7 %fusion.23 = (f32[2,16,32,128]{3,2,1,0:T(8,128)S(1)}, f32[2,16,32,128]{3,2,1,0:T(8,128)}, f32[2,16,32,128]{3,2,1,0:T(8,128)}, f32[2,16,32,128]{3,2,1,0:T(8,128)}) fusion(f32[5,32,64,128]{3,2,1,0:T(8,128)} %bitcast.21), kind=kLoop, calls=%fused_computation.64 | loop fusion | bytes 4194304 | tf_op jit(solution)/shard_map/slice | solution.py:394
  2.7 3.0 %collective-permute-start.2 = (f32[2,16,32,128]{3,2,1,0:T(8,128)}, f32[2,16,32,128]{3,2,1,0:T(8,128)S(1)}, u32[]{:S(2)}, u32[]{:S(2)}) collective-permute-start(f32[2,16,32,128]{3,2,1,0:T(8,128)} %get-tuple-element.62), channel_id=1, source_target_pairs={{0,16},{8,24},{16,0},{24,8},{1,17},{9,25},{17,1},{25,9},{2,18},{10... | collective-permute-start | bytes 1572872 | tf_op jit(solution)/shard_map/ppermute | solution.py:380
  16.2 2.8 %fusion.9 = (f32[4,128,128]{2,1,0:T(8,128)S(1)}, f32[4,128,128]{2,1,0:T(8,128)}) fusion(s32[4,128]{1,0:T(4,128)S(1)} %get-tuple-element.85, s32[128]{0:T(128)S(1)} %add.227, s32[4,128]{1,0:T(4,128)S(1)} %get-tuple-element.86, f32[4,128]{1,0:T(4,128)S(1)} %constant_dynamic-slice_fusion.3), kind=kLoop, calls=%fused_computation.25 | loop fusion | flops 2228224 | bytes 530944 | tf_op jit(solution)/shard_map/mul | solution.py:72
  20.7 9.2 %collective-permute-done.21.refs_0_ = f32[2,16,32,128]{3,2,1,0:T(8,128)S(1)} collective-permute-done((f32[2,16,32,128]{3,2,1,0:T(8,128)}, f32[2,16,32,128]{3,2,1,0:T(8,128)S(1)}, u32[]{:S(2)}, u32[]{:S(2)}) %collective-permute-start.21) | collective-permute-done | bytes 524320 | tf_op jit(solution)/shard_map/ppermute | solution.py:380
  31.9 9.2 %collective-permute-done.32.refs_0_ = f32[2,16,32,128]{3,2,1,0:T(8,128)S(1)} collective-permute-done((f32[2,16,32,128]{3,2,1,0:T(8,128)}, f32[2,16,32,128]{3,2,1,0:T(8,128)S(1)}, u32[]{:S(2)}, u32[]{:S(2)}) %collective-permute-start.32) | collective-permute-done | bytes 524320 | tf_op jit(solution)/shard_map/ppermute | solution.py:380
  41.1 5.9 %multiply_add_fusion.2 = (f32[2,16,32,128]{3,2,1,0:T(8,128)}, f32[2,16,32,128]{3,2,1,0:T(8,128)}, f32[2,16,32,128]{3,2,1,0:T(8,128)}, f32[2,16,32,128]{3,2,1,0:T...) fusion(f32[2,16,32,128]{3,2,1,0:T(8,128)S(1)} %collective-permute-done.34.refs_2_, f32[]{:T(128)} %bitcast.9, ...), kind=kLoop, calls=%fused_computation.3 | loop fusion | flops 1572864 | bytes 8388624 | tf_op jit(solution)/shard_map/add | solution.py:406
  50.9 2.7 %fusion.25 = (f32[3,16,32,128]{3,2,1,0:T(8,128)}, f32[3,16,32,128]{3,2,1,0:T(8,128)}) fusion(f32[5,32,64,128]{3,2,1,0:T(8,128)} %bitcast.25), kind=kLoop, calls=%fused_computation.66 | loop fusion | bytes 3145728 | tf_op jit(solution)/shard_map/slice | solution.py:394
  56.0 4.4 %multiply_add_fusion.8 = (f32[1,16,32,128]{3,2,1,0:T(8,128)}, f32[1,16,32,128]{3,2,1,0:T(8,128)}) fusion(f32[1,16,32,128]{3,2,1,0:T(8,128)S(1)} %collective-permute-done.12.refs_2_, f32[]{:T(128)} %bitcast.9, f32[]{:T(128)} %bitcast.8, f32[5,32,64,128]{3,2,1,0:T(8,128)} %bitcast.26, f32[1,16,32,128]{3,2,1,0:T(8,128)S(1)} %collective-permute-done.10.refs_0_, ...), kind=kLoop, calls=%fused_computation.26 | loop fusion | flops 393216 | bytes 1572880 | tf_op jit(solution)/shard_map/add | solution.py:406
  60.4 3.2 %collective-permute-done.23.refs_2_ = f32[2,16,32,128]{3,2,1,0:T(8,128)S(1)} collective-permute-done((f32[2,16,32,128]{3,2,1,0:T(8,128)S(1)}, f32[2,16,32,128]{3,2,1,0:T(8,128)S(1)}, u32[]{:S(2)}, u32[]{:S(2)}) %collective-permute-start.23) | collective-permute-done | bytes 524320 | tf_op jit(solution)/shard_map/ppermute | solution.py:377
  65.7 9.2 %collective-permute-done.4.refs_2_ = f32[2,16,32,128]{3,2,1,0:T(8,128)S(1)} collective-permute-done((f32[2,16,32,128]{3,2,1,0:T(8,128)S(1)}, f32[2,16,32,128]{3,2,1,0:T(8,128)S(1)}, u32[]{:S(2)}, u32[]{:S(2)}) %collective-permute-start.4) | collective-permute-done | bytes 524320 | tf_op jit(solution)/shard_map/ppermute | solution.py:377
  76.9 3.7 %multiply_add_fusion.4 = (f32[2,16,32,128]{3,2,1,0:T(8,128)}, f32[2,16,32,128]{3,2,1,0:T(8,128)}) fusion(f32[2,16,32,128]{3,2,1,0:T(8,128)S(1)} %collective-permute-done.23.refs_2_, f32[]{:T(128)} %bitcast.9, f32[]{:T(128)} %bitcast.8, f32[5,32,64,128]{3,2,1,0:T(8,128)} %bitcast.27, f32[2,16,32,128]{3,2,1,0:T(8,128)S(1)} %collective-permute-done.4.refs_2_), kind=kLoop, calls=%fused_computation.5 | loop fusion | flops 786432 | bytes 3145736 | tf_op jit(solution)/shard_map/add | solution.py:406
  92.2 12.4 %local_part.1.local = f32[5,32,64,128]{3,2,1,0:T(8,128)} custom-call(f32[5,5]{1,0:T(8,128)S(1)} %copy-done.18, f32[5]{0:T(128)S(1)} %copy-done.19, s32[5,3]{1,0:T(8,128)S(1)} %copy.19.flags, f32[5,32,64,128]{3,2,1,0:T(8,128)} %bitcast.28, f32[5,32,64,128]{3,2,1,0:T(8,128)} %bitcast.29, f32[5,32,64,128]{3,2,1,0:T(8,128)} %bitcast.30, ...), custom_call_target="tpu_custom_call" | custom-call | flops 52428800 | bytes 20971520 | tf_op jit(solution)/shard_map/local_part/pallas_call | solution.py:143
  104.7 2.9 %spread.5 = (f32[2,8,32,128]{3,2,1,0:T(8,128)S(1)}, f32[2,8,32,128]{3,2,1,0:T(8,128)S(1)}, f32[2,8,32,128]{3,2,1,0:T(8,128)}, f32[2,8,32,128]{3,2,1,0:T(8,128)}) custom-call(s32[1]{0:T(128)} %bitcast.10.rank, f32[2]{0:T(128)S(1)} %pad_maximum_fusion.2.coef, f32[5,32,64,128]{3,2,1,0:T(8,128)} %local_part.1.local, f32[2,16,32,128]{3,2,1,0:T(8,128)S(1)} %copy-done.2, ...), custom_call_target="tpu_custom_call" | custom-call | flops 1048576 | bytes 4194304 | tf_op jit(solution)/shard_map/spread/pallas_call | solution.py:206
  112.7 2.8 %spread.4 = (f32[2,8,32,128]{3,2,1,0:T(8,128)S(1)}, f32[2,8,32,128]{3,2,1,0:T(8,128)}, f32[2,8,32,128]{3,2,1,0:T(8,128)S(1)}, f32[2,8,32,128]{3,2,1,0:T(8,128)S(1)}) custom-call(s32[1]{0:T(128)} %bitcast.10.rank, f32[2]{0:T(128)S(1)} %pad_maximum_fusion.2.coef, f32[5,32,64,128]{3,2,1,0:T(8,128)} %local_part.1.local, ...), custom_call_target="tpu_custom_call" | custom-call | flops 1048576 | bytes 4194304 | tf_op jit(solution)/shard_map/spread/pallas_call | solution.py:206
  130.1 2.7 %collective-permute-start.39 = (f32[2,4,128,128]{3,2,1,0:T(8,128)S(1)}, f32[2,4,128,128]{3,2,1,0:T(8,128)S(1)}, u32[]{:S(2)}, u32[]{:S(2)}) collective-permute-start(f32[2,4,128,128]{3,2,1,0:T(8,128)S(1)} %coefficients.5.own), channel_id=1, source_target_pairs={{0,4},{1,5},{2,6},{3,7},{4,0},{5,1},{6,2},{7,3},{8,12},{9,13},{10,... | collective-permute-start | bytes 1572872 | tf_op jit(solution)/shard_map/ppermute | solution.py:383
  136.7 14.1 %collective-permute-done.26.refs_2_ = f32[2,8,32,128]{3,2,1,0:T(8,128)S(1)} collective-permute-done((f32[2,8,32,128]{3,2,1,0:T(8,128)}, f32[2,8,32,128]{3,2,1,0:T(8,128)S(1)}, u32[]{:S(2)}, u32[]{:S(2)}) %collective-permute-start.26) | collective-permute-done | bytes 262176 | tf_op jit(solution)/shard_map/ppermute | solution.py:383
  151.8 4.7 %collective-permute-done.27.refs_3_ = f32[2,8,32,128]{3,2,1,0:T(8,128)S(1)} collective-permute-done((f32[2,8,32,128]{3,2,1,0:T(8,128)}, f32[2,8,32,128]{3,2,1,0:T(8,128)S(1)}, u32[]{:S(2)}, u32[]{:S(2)}) %collective-permute-start.27) | collective-permute-done | bytes 262176 | tf_op jit(solution)/shard_map/ppermute | solution.py:383
  159.8 18.8 %collective-permute-done.17.other = f32[1,4,128,128]{3,2,1,0:T(8,128)S(1)} collective-permute-done((f32[1,4,128,128]{3,2,1,0:T(8,128)S(1)}, f32[1,4,128,128]{3,2,1,0:T(8,128)S(1)}, u32[]{:S(2)}, u32[]{:S(2)}) %collective-permute-start.17) | collective-permute-done | bytes 262176 | tf_op jit(solution)/shard_map/ppermute | solution.py:383
  184.9 4.2 %multiply_add_fusion = (f32[3,16,32,128]{3,2,1,0:T(8,128)S(1)}, f32[3,16,32,128]{3,2,1,0:T(8,128)S(1)}) fusion(f32[3,16,32,128]{3,2,1,0:T(8,128)S(1)} %collective-permute-done.8.refs_2_, f32[]{:T(128)} %bitcast.9, f32[]{:T(128)} %bitcast.8, f32[5,32,64,128]{3,2,1,0:T(8,128)} %bitcast.31, f32[3,16,32,128]{3,2,1,0:T(8,128)S(1)} %collective-permute-done.6.refs_0_, ...), kind=kLoop, calls=%fused_computation | loop fusion | flops 1179648 | bytes 4718608 | tf_op jit(solution)/shard_map/add | solution.py:406
  194.1 3.7 %collective-permute-done.41.refs_2_ = f32[2,8,32,128]{3,2,1,0:T(8,128)S(1)} collective-permute-done((f32[2,8,32,128]{3,2,1,0:T(8,128)S(1)}, f32[2,8,32,128]{3,2,1,0:T(8,128)S(1)}, u32[]{:S(2)}, u32[]{:S(2)}) %collective-permute-start.41) | collective-permute-done | bytes 262176 | tf_op jit(solution)/shard_map/ppermute | solution.py:383
  197.8 5.5 %collective-permute-done.42.refs_3_ = f32[2,8,32,128]{3,2,1,0:T(8,128)S(1)} collective-permute-done((f32[2,8,32,128]{3,2,1,0:T(8,128)S(1)}, f32[2,8,32,128]{3,2,1,0:T(8,128)S(1)}, u32[]{:S(2)}, u32[]{:S(2)}) %collective-permute-start.42) | collective-permute-done | bytes 262176 | tf_op jit(solution)/shard_map/ppermute | solution.py:383
  205.3 3.7 %collective-permute-done.30.refs_2_ = f32[2,8,32,128]{3,2,1,0:T(8,128)S(1)} collective-permute-done((f32[2,8,32,128]{3,2,1,0:T(8,128)S(1)}, f32[2,8,32,128]{3,2,1,0:T(8,128)S(1)}, u32[]{:S(2)}, u32[]{:S(2)}) %collective-permute-start.30) | collective-permute-done | bytes 262176 | tf_op jit(solution)/shard_map/ppermute | solution.py:383
  209.0 8.4 %collective-permute-done.31.refs_3_ = f32[2,8,32,128]{3,2,1,0:T(8,128)S(1)} collective-permute-done((f32[2,8,32,128]{3,2,1,0:T(8,128)S(1)}, f32[2,8,32,128]{3,2,1,0:T(8,128)S(1)}, u32[]{:S(2)}, u32[]{:S(2)}) %collective-permute-start.31) | collective-permute-done | bytes 262176 | tf_op jit(solution)/shard_map/ppermute | solution.py:383
  224.0 3.5 %place_far.2.refs_4_ = f32[5,32,64,128]{3,2,1,0:T(8,128)} custom-call(f32[2]{0:T(128)S(1)} %pad_maximum_fusion.2.coef, f32[5,32,64,128]{3,2,1,0:T(8,128)} %local_part.1.local, f32[3,16,32,128]{3,2,1,0:T(8,128)S(1)} %collective-permute-done.6.refs_0_, f32[3,16,32,128]{3,2,1,0:T(8,128)S(1)} %collective-permute-done.7.refs_1_, ...), custom_call_target="tpu_custom_call", output_to_operand_aliasing={{}: (6, {})} | custom-call | flops 1572864 | bytes 6291456 | tf_op jit(solution)/shard_map/place_far/pallas_call | solution.py:338
  (174 shorter events, 86.0 us)
Async XLA Ops:
  5.7 24.2 %collective-permute-start.21 = (f32[2,16,32,128]{3,2,1,0:T(8,128)}, f32[2,16,32,128]{3,2,1,0:T(8,128)S(1)}, u32[]{:S(2)}, u32[]{:S(2)}) collective-permute-start(f32[2,16,32,128]{3,2,1,0:T(8,128)} %get-tuple-element.61), channel_id=1, source_target_pairs={{0,16},{8,24},{16,0},{24,8},{1,17},{9,25},{17,1},{25,9},{2,18},{10... | collective-permute-start | bytes 1572872 | tf_op jit(solution)/shard_map/ppermute | solution.py:380
  5.7 35.4 %collective-permute-start.32 = (f32[2,16,32,128]{3,2,1,0:T(8,128)}, f32[2,16,32,128]{3,2,1,0:T(8,128)S(1)}, u32[]{:S(2)}, u32[]{:S(2)}) collective-permute-start(f32[2,16,32,128]{3,2,1,0:T(8,128)} %get-tuple-element.60), channel_id=1, source_target_pairs={{0,16},{8,24},{16,0},{24,8},{1,17},{9,25},{17,1},{25,9},{2,18},{10... | collective-permute-start | bytes 1572872 | tf_op jit(solution)/shard_map/ppermute | solution.py:380
  7.7 33.4 %collective-permute-start.34 = (f32[2,16,32,128]{3,2,1,0:T(8,128)S(1)}, f32[2,16,32,128]{3,2,1,0:T(8,128)S(1)}, u32[]{:S(2)}, u32[]{:S(2)}) collective-permute-start(f32[2,16,32,128]{3,2,1,0:T(8,128)S(1)} %get-tuple-element.59), channel_id=1, source_target_pairs={{0,8},{8,0},{16,24},{24,16},{1,9},{9,1},{17,25},{25,17},{2,10},{10... | collective-permute-start | bytes 1572872 | tf_op jit(solution)/shard_map/ppermute | solution.py:377
  11.7 69.7 %collective-permute-start = (f32[6,1,64,128]{3,2,1,0:T(8,128)}, f32[6,1,64,128]{3,2,1,0:T(8,128)S(1)}, u32[]{:S(2)}, u32[]{:S(2)}) collective-permute-start(f32[6,1,64,128]{3,2,1,0:T(8,128)} %pad_maximum_fusion), channel_id=1, source_target_pairs={{0,1},{1,2},{2,3},{3,4},{4,5},{5,6},{6,7},{7,0},{8,9},{9,10},{10,1... | collective-permute-start | bytes 589832 | tf_op jit(solution)/shard_map/ppermute | solution.py:419
  20.1 33.5 %collective-permute-start.10 = (f32[1,16,32,128]{3,2,1,0:T(8,128)S(1)}, f32[1,16,32,128]{3,2,1,0:T(8,128)S(1)}, u32[]{:S(2)}, u32[]{:S(2)}) collective-permute-start(f32[1,16,32,128]{3,2,1,0:T(8,128)S(1)} %get-tuple-element.68), channel_id=1, source_target_pairs={{0,16},{8,24},{16,0},{24,8},{1,17},{9,25},{17,1},{25,9},{2,18},{10... | collective-permute-start | bytes 786440 | tf_op jit(solution)/shard_map/ppermute | solution.py:380
  29.9 24.7 %collective-permute-start.12 = (f32[1,16,32,128]{3,2,1,0:T(8,128)S(1)}, f32[1,16,32,128]{3,2,1,0:T(8,128)S(1)}, u32[]{:S(2)}, u32[]{:S(2)}) collective-permute-start(f32[1,16,32,128]{3,2,1,0:T(8,128)S(1)} %get-tuple-element.67), channel_id=1, source_target_pairs={{0,8},{8,0},{16,24},{24,16},{1,9},{9,1},{17,25},{25,17},{2,10},{10... | collective-permute-start | bytes 786440 | tf_op jit(solution)/shard_map/ppermute | solution.py:377
  50.8 24.1 %collective-permute-start.4 = (f32[2,16,32,128]{3,2,1,0:T(8,128)S(1)}, f32[2,16,32,128]{3,2,1,0:T(8,128)S(1)}, u32[]{:S(2)}, u32[]{:S(2)}) collective-permute-start(f32[2,16,32,128]{3,2,1,0:T(8,128)S(1)} %get-tuple-element.58), channel_id=1, source_target_pairs={{0,8},{8,0},{16,24},{24,16},{1,9},{9,1},{17,25},{25,17},{2,10},{10... | collective-permute-start | bytes 1572872 | tf_op jit(solution)/shard_map/ppermute | solution.py:377
  53.6 27.8 %collective-permute-start.1 = (f32[6,1,64,128]{3,2,1,0:T(8,128)S(1)}, f32[6,1,64,128]{3,2,1,0:T(8,128)S(1)}, u32[]{:S(2)}, u32[]{:S(2)}) collective-permute-start(f32[6,1,64,128]{3,2,1,0:T(8,128)S(1)} %copy-done.27), channel_id=1, source_target_pairs={{0,7},{1,0},{2,1},{3,2},{4,3},{5,4},{6,5},{7,6},{8,15},{9,8},{10,9... | collective-permute-start | bytes 589832 | tf_op jit(solution)/shard_map/ppermute | solution.py:420
  54.5 31.6 %collective-permute-start.33 = (f32[2,16,32,128]{3,2,1,0:T(8,128)S(1)}, f32[2,16,32,128]{3,2,1,0:T(8,128)S(1)}, u32[]{:S(2)}, u32[]{:S(2)}) collective-permute-start(f32[2,16,32,128]{3,2,1,0:T(8,128)S(1)} %get-tuple-element.56), channel_id=1, source_target_pairs={{0,8},{8,0},{16,24},{24,16},{1,9},{9,1},{17,25},{25,17},{2,10},{10... | collective-permute-start | bytes 1572872 | tf_op jit(solution)/shard_map/ppermute | solution.py:377
  63.6 41.0 %collective-permute-start.35 = (f32[2,16,32,128]{3,2,1,0:T(8,128)}, f32[2,16,32,128]{3,2,1,0:T(8,128)}, u32[]{:S(2)}, u32[]{:S(2)}) collective-permute-start(f32[2,16,32,128]{3,2,1,0:T(8,128)} %get-tuple-element.53), channel_id=1, source_target_pairs={{0,16},{8,24},{16,0},{24,8},{1,17},{9,25},{17,1},{25,9},{2,18},{10... | collective-permute-start | bytes 1572872 | tf_op jit(solution)/shard_map/ppermute | solution.py:380
  74.9 37.2 %collective-permute-start.22 = (f32[2,16,32,128]{3,2,1,0:T(8,128)}, f32[2,16,32,128]{3,2,1,0:T(8,128)}, u32[]{:S(2)}, u32[]{:S(2)}) collective-permute-start(f32[2,16,32,128]{3,2,1,0:T(8,128)} %get-tuple-element.55), channel_id=1, source_target_pairs={{0,8},{8,0},{16,24},{24,16},{1,9},{9,1},{17,25},{25,17},{2,10},{10... | collective-permute-start | bytes 1572872 | tf_op jit(solution)/shard_map/ppermute | solution.py:377
  81.4 26.8 %collective-permute-start.11 = (f32[1,16,32,128]{3,2,1,0:T(8,128)}, f32[1,16,32,128]{3,2,1,0:T(8,128)}, u32[]{:S(2)}, u32[]{:S(2)}) collective-permute-start(f32[1,16,32,128]{3,2,1,0:T(8,128)} %get-tuple-element.66), channel_id=1, source_target_pairs={{0,8},{8,0},{16,24},{24,16},{1,9},{9,1},{17,25},{25,17},{2,10},{10... | collective-permute-start | bytes 786440 | tf_op jit(solution)/shard_map/ppermute | solution.py:377
  81.4 26.8 %collective-permute-start.13 = (f32[1,16,32,128]{3,2,1,0:T(8,128)}, f32[1,16,32,128]{3,2,1,0:T(8,128)}, u32[]{:S(2)}, u32[]{:S(2)}) collective-permute-start(f32[1,16,32,128]{3,2,1,0:T(8,128)} %get-tuple-element.65), channel_id=1, source_target_pairs={{0,16},{8,24},{16,0},{24,8},{1,17},{9,25},{17,1},{25,9},{2,18},{10... | collective-permute-start | bytes 786440 | tf_op jit(solution)/shard_map/ppermute | solution.py:380
  86.9 25.2 %collective-permute-start.24 = (f32[2,16,32,128]{3,2,1,0:T(8,128)}, f32[2,16,32,128]{3,2,1,0:T(8,128)}, u32[]{:S(2)}, u32[]{:S(2)}) collective-permute-start(f32[2,16,32,128]{3,2,1,0:T(8,128)} %get-tuple-element.63), channel_id=1, source_target_pairs={{0,16},{8,24},{16,0},{24,8},{1,17},{9,25},{17,1},{25,9},{2,18},{10... | collective-permute-start | bytes 1572872 | tf_op jit(solution)/shard_map/ppermute | solution.py:380
  112.2 70.6 %collective-permute-start.6 = (f32[3,16,32,128]{3,2,1,0:T(8,128)}, f32[3,16,32,128]{3,2,1,0:T(8,128)S(1)}, u32[]{:S(2)}, u32[]{:S(2)}) collective-permute-start(f32[3,16,32,128]{3,2,1,0:T(8,128)} %get-tuple-element.72), channel_id=1, source_target_pairs={{0,16},{8,24},{16,0},{24,8},{1,17},{9,25},{17,1},{25,9},{2,18},{10... | collective-permute-start | bytes 2359304 | tf_op jit(solution)/shard_map/ppermute | solution.py:380
  116.9 66.3 %collective-permute-start.8 = (f32[3,16,32,128]{3,2,1,0:T(8,128)}, f32[3,16,32,128]{3,2,1,0:T(8,128)S(1)}, u32[]{:S(2)}, u32[]{:S(2)}) collective-permute-start(f32[3,16,32,128]{3,2,1,0:T(8,128)} %get-tuple-element.71), channel_id=1, source_target_pairs={{0,8},{8,0},{16,24},{24,16},{1,9},{9,1},{17,25},{25,17},{2,10},{10... | collective-permute-start | bytes 2359304 | tf_op jit(solution)/shard_map/ppermute | solution.py:377
  130.1 50.2 %collective-permute-start.39 = (f32[2,4,128,128]{3,2,1,0:T(8,128)S(1)}, f32[2,4,128,128]{3,2,1,0:T(8,128)S(1)}, u32[]{:S(2)}, u32[]{:S(2)}) collective-permute-start(f32[2,4,128,128]{3,2,1,0:T(8,128)S(1)} %coefficients.5.own), channel_id=1, source_target_pairs={{0,4},{1,5},{2,6},{3,7},{4,0},{5,1},{6,2},{7,3},{8,12},{9,13},{10,... | collective-permute-start | bytes 1572872 | tf_op jit(solution)/shard_map/ppermute | solution.py:383
  133.0 23.4 %collective-permute-start.27 = (f32[2,8,32,128]{3,2,1,0:T(8,128)}, f32[2,8,32,128]{3,2,1,0:T(8,128)S(1)}, u32[]{:S(2)}, u32[]{:S(2)}) collective-permute-start(f32[2,8,32,128]{3,2,1,0:T(8,128)} %copy-done.20), channel_id=1, source_target_pairs={{0,3},{1,2},{2,1},{3,0},{4,7},{5,6},{6,5},{7,4},{8,11},{9,10},{10,... | collective-permute-start | bytes 786440 | tf_op jit(solution)/shard_map/ppermute | solution.py:383
  150.8 27.8 %collective-permute-start.17 = (f32[1,4,128,128]{3,2,1,0:T(8,128)S(1)}, f32[1,4,128,128]{3,2,1,0:T(8,128)S(1)}, u32[]{:S(2)}, u32[]{:S(2)}) collective-permute-start(f32[1,4,128,128]{3,2,1,0:T(8,128)S(1)} %coefficients.3.own), channel_id=1, source_target_pairs={{0,4},{1,5},{2,6},{3,7},{4,0},{5,1},{6,2},{7,3},{8,12},{9,13},{10,... | collective-permute-start | bytes 786440 | tf_op jit(solution)/shard_map/ppermute | solution.py:383
  159.5 29.9 %collective-permute-start.28 = (f32[2,4,128,128]{3,2,1,0:T(8,128)S(1)}, f32[2,4,128,128]{3,2,1,0:T(8,128)S(1)}, u32[]{:S(2)}, u32[]{:S(2)}) collective-permute-start(f32[2,4,128,128]{3,2,1,0:T(8,128)S(1)} %coefficients.4.own), channel_id=1, source_target_pairs={{0,4},{1,5},{2,6},{3,7},{4,0},{5,1},{6,2},{7,3},{8,12},{9,13},{10,... | collective-permute-start | bytes 1572872 | tf_op jit(solution)/shard_map/ppermute | solution.py:383
  189.4 34.6 %collective-permute-start.7 = (f32[3,16,32,128]{3,2,1,0:T(8,128)S(1)}, f32[3,16,32,128]{3,2,1,0:T(8,128)S(1)}, u32[]{:S(2)}, u32[]{:S(2)}) collective-permute-start(f32[3,16,32,128]{3,2,1,0:T(8,128)S(1)} %get-tuple-element.70), channel_id=1, source_target_pairs={{0,8},{8,0},{16,24},{24,16},{1,9},{9,1},{17,25},{25,17},{2,10},{10... | collective-permute-start | bytes 2359304 | tf_op jit(solution)/shard_map/ppermute | solution.py:377
  193.5 30.5 %collective-permute-start.9 = (f32[3,16,32,128]{3,2,1,0:T(8,128)S(1)}, f32[3,16,32,128]{3,2,1,0:T(8,128)S(1)}, u32[]{:S(2)}, u32[]{:S(2)}) collective-permute-start(f32[3,16,32,128]{3,2,1,0:T(8,128)S(1)} %get-tuple-element.69), channel_id=1, source_target_pairs={{0,16},{8,24},{16,0},{24,8},{1,17},{9,25},{17,1},{25,9},{2,18},{10... | collective-permute-start | bytes 2359304 | tf_op jit(solution)/shard_map/ppermute | solution.py:380
  203.3 24.2 %collective-permute-start.3 = (f32[2,16,32,128]{3,2,1,0:T(8,128)S(1)}, f32[2,16,32,128]{3,2,1,0:T(8,128)S(1)}, u32[]{:S(2)}, u32[]{:S(2)}) collective-permute-start(f32[2,16,32,128]{3,2,1,0:T(8,128)S(1)} %copy-done.24), channel_id=1, source_target_pairs={{0,8},{8,0},{16,24},{24,16},{1,9},{9,1},{17,25},{25,17},{2,10},{10... | collective-permute-start | bytes 1572872 | tf_op jit(solution)/shard_map/ppermute | solution.py:377
  204.9 22.7 %collective-permute-start.5 = (f32[2,16,32,128]{3,2,1,0:T(8,128)S(1)}, f32[2,16,32,128]{3,2,1,0:T(8,128)S(1)}, u32[]{:S(2)}, u32[]{:S(2)}) collective-permute-start(f32[2,16,32,128]{3,2,1,0:T(8,128)S(1)} %copy-done.25), channel_id=1, source_target_pairs={{0,16},{8,24},{16,0},{24,8},{1,17},{9,25},{17,1},{25,9},{2,18},{10... | collective-permute-start | bytes 1572872 | tf_op jit(solution)/shard_map/ppermute | solution.py:380
  (51 other events, 727.3 us)

commit v2 on v0

v2 whole, which is shorter than its diff:
```python
import functools

import jax
import jax.numpy as jnp
import numpy as np
from jax import lax
from jax.experimental import pallas as pl
from jax.experimental.pallas import tpu as pltpu
from jax.sharding import PartitionSpec as P

QUAD = 4
NEAR_SIZES = (2, 2, 1)
FAR_SIZES = (3, 2)
ORDER = (
    ("pack", 0),
    ("pack", 1),
    ("local", 0),
    ("mix", 0),
    ("mix", 1),
    ("spread", 0),
    ("pack", 2),
    ("coef", 0),
    ("spread", 1),
    ("pack", 3),
    ("mix", 2),
    ("spread", 2),
    ("pack", 4),
    ("coef", 1),
    ("filter", 0),
    ("mix", 3),
    ("coef", 2),
    ("near", 0),
    ("filter", 1),
    ("mix", 4),
    ("near", 1),
    ("filter", 2),
    ("far", 3),
    ("near", 2),
    ("far", 4),
)
SMEM = pl.BlockSpec(memory_space=pltpu.SMEM)
ANY = pl.BlockSpec(memory_space=pl.ANY)
PARAMS = pltpu.CompilerParams(vmem_limit_bytes=48 * 1024 * 1024)


def spectral_values(slots):
    offset = np.arange(1 - slots, slots)
    safe = np.where(offset == 0, 1.0, np.sin(np.pi * offset / slots))
    return np.where(offset == 0, 0.0, 0.5 * (1.0 - 2.0 * (np.abs(offset) % 2)) / safe)


def mode_layout(points, near):
    half = points // 2
    pairs = near // 2
    theta = np.arange(points)
    bases, base, scale = [], np.zeros(near), np.zeros(near)
    for r in range(near):
        cutoff = max(4, points * (r + 1) // (2 * near))
        weight = max(1.0 - r / near, 0.0)
        kept = [m for m in range(half + 1) if m < cutoff]
        out = [m for m in range(half + 1) if m >= cutoff]
        count = [sum(1 if m in (0, half) else 2 for m in modes) for modes in (kept, out)]
        low = count[0] <= count[1]
        rows = []
        for m in kept if low else out:
            angle = 2.0 * np.pi * (m * theta % points) / points
            if m in (0, half):
                rows.append(np.cos(angle) / np.sqrt(points))
            else:
                rows.append(np.cos(angle) * np.sqrt(2.0 / points))
                rows.append(np.sin(angle) * np.sqrt(2.0 / points))
        bases.append(rows)
        base[r] = 1.0 - weight if low else 1.0
        scale[r] = weight if low else -weight
    depth = max(len(bases[p]) + len(bases[p + pairs]) for p in range(pairs))
    depth = -(-depth // 8) * 8
    table = np.zeros((pairs, depth, points), np.float32)
    split = np.zeros(pairs, np.int32)
    for p in range(pairs):
        rows = bases[p] + bases[p + pairs]
        table[p, : len(rows)] = np.stack(rows)
        split[p] = len(bases[p])
    return table, split, base, scale


class Scalars:
    def __init__(self, ints, reals, slots, near):
        self.ints, self.reals, self.slots, self.near = ints, reals, slots, near
        self.slot, self.place = ints[0], ints[1]
        self.rank = self.place % QUAD

    def weight(self, i, j):
        return self.reals[self.ints[2 + i] - self.ints[2 + j] + self.slots - 1]

    def split(self, pair):
        return self.ints[2 + self.slots + pair]

    def base(self, r):
        return self.reals[2 * self.slots - 1 + r]

    def scale(self, r):
        return self.reals[2 * self.slots - 1 + self.near + r]

    def first(self):
        return first_partner(self.slot, self.place % 2, self.slots)

    def target(self, s):
        return later_partner(self.slot, self.place % 2, self.slots, s)


def first_partner(slot, core, slots):
    if slots == 4:
        return slot ^ (2 - core)
    return slot ^ 1


def later_partner(slot, core, slots, s):
    if slots == 4:
        return slot ^ (1 + core)
    return (slot // 2 + s) % (slots // 2) * 2 + slot % 2


def call(kernel, name, token, grid, inputs, in_specs, out_specs, out_shape, scratch=(), cost=(0, 0), alias=None):
    extra = [] if token is None else [token]
    return pl.pallas_call(
        lambda *refs: kernel(*refs[: len(inputs)], *refs[len(inputs) + len(extra) :]),
        grid=grid,
        in_specs=list(in_specs) + [ANY] * len(extra),
        out_specs=out_specs,
        out_shape=out_shape,
        scratch_shapes=list(scratch),
        input_output_aliases=alias or {},
        compiler_params=PARAMS,
        cost_estimate=pl.CostEstimate(flops=cost[0], bytes_accessed=cost[1], transcendentals=0),
        name=name,
    )(*inputs, *extra)


def shaped(*shape):
    return jax.ShapeDtypeStruct(shape, jnp.float32)


def pack(center, viscosity, lo, hi, base, near, edges, token):
    fields, block, rows, cells = center.shape

    def kernel(center, viscosity, *refs):
        outs, sem = refs[:-1], refs[-1]
        moves = [(center.at[pl.ds(lo, hi - lo), :, pl.ds(base, near)], outs[0])]
        if edges:
            for out, start in zip(outs[1:], (block - 1, 0)):
                moves.append((center.at[:, pl.ds(start, 1)], out.at[pl.ds(0, fields)]))
                moves.append((viscosity.at[pl.ds(start, 1)], out.at[fields]))
        copies = [pltpu.make_async_copy(a, b, sem.at[i]) for i, (a, b) in enumerate(moves)]
        for copy in copies:
            copy.start()
        for copy in copies:
            copy.wait()

    shapes = [shaped(hi - lo, block, near, cells)]
    if edges:
        shapes += [shaped(fields + 1, 1, rows, cells)] * 2
    return call(
        kernel,
        "pack",
        token,
        (),
        [center, viscosity],
        [ANY, ANY],
        [ANY] * len(shapes),
        shapes,
        [pltpu.SemaphoreType.DMA((5,))],
        (0, 8 * (hi - lo) * block * near * cells),
    )


def local_kernel(
    coupling, kappa, flags, adj, before, after, src, mu, mu_before, mu_after, low, high, out
):
    fields, planes, rows, cells = adj.shape
    step = pl.program_id(0)
    first = step == 0
    last = step == pl.num_programs(0) - 1
    row = lax.broadcasted_iota(jnp.int32, (rows, cells), 0)
    col = lax.broadcasted_iota(jnp.int32, (rows, cells), 1)
    ring = 0.5 / (row.astype(jnp.float32) + 1.0)

    def pick(source, behind, ahead, f, k):
        if k < 0:
            return jnp.where(first, low[f, 0], behind)
        if k >= planes:
            return jnp.where(last, high[f, 0], ahead)
        return source

    def visc(k):
        return pick(mu[max(0, min(k, planes - 1))], mu_before[0], mu_after[0], fields, k)

    def cell(f, k):
        return pick(adj[f, max(0, min(k, planes - 1))], before[f, 0], after[f, 0], f, k)

    for k in range(planes):
        m = visc(k)
        up = ring * (m + visc(k + 1))
        down = ring * (m + visc(k - 1))
        outer = jnp.where(row < rows - 1, 0.5 * (m + pltpu.roll(m, rows - 1, 0)), 0.0)
        inner = jnp.where(row > 0, 0.5 * (m + pltpu.roll(m, 1, 0)), 0.0)
        east = jnp.where(col < cells - 1, 0.5 * (m + pltpu.roll(m, cells - 1, 1)), 0.0)
        west = jnp.where(col > 0, 0.5 * (m + pltpu.roll(m, 1, 1)), 0.0)
        diag = up + down + outer + inner + east + west
        for f in range(fields):
            p = adj[f, k]
            opens = [(1 - flags[f, i]).astype(jnp.float32) for i in range(3)]
            wall = jnp.where(col == 0, opens[0], 0.0)
            wall = wall + jnp.where(col == cells - 1, opens[1], 0.0)
            wall = wall + jnp.where(row == rows - 1, opens[2], 0.0)
            flux = (diag + wall * m) * p
            flux = flux - up * cell(f, k + 1) - down * cell(f, k - 1)
            flux = flux - outer * pltpu.roll(p, rows - 1, 0) - inner * pltpu.roll(p, 1, 0)
            flux = flux - east * pltpu.roll(p, cells - 1, 1) - west * pltpu.roll(p, 1, 1)
            total = src[f, k] + kappa[f] * flux
            for g in range(fields):
                total = total + coupling[g, f] * adj[g, k]
            out[f, k] = total


def local_part(center, source, viscosity, kappa, coupling, flags, low, high, token):
    fields, block, rows, cells = center.shape
    planes = min(4, block)

    def whole(width, index):
        return pl.BlockSpec((fields, width, rows, cells), lambda i: (0, index(i), 0, 0))

    def plane(width, index):
        return pl.BlockSpec((width, rows, cells), lambda i: (index(i), 0, 0))

    behind = lambda i: jnp.maximum(i * planes - 1, 0)
    ahead = lambda i: jnp.minimum(i * planes + planes, block - 1)
    here = lambda i: i
    halo = pl.BlockSpec((fields + 1, 1, rows, cells), lambda i: (0, 0, 0, 0))
    return call(
        local_kernel,
        "local_part",
        token,
        (block // planes,),
        [coupling, kappa, flags, center, center, center, source, viscosity, viscosity, viscosity, low, high],
        [
            SMEM,
            SMEM,
            SMEM,
            whole(planes, here),
            whole(1, behind),
            whole(1, ahead),
            whole(planes, here),
            plane(planes, here),
            plane(1, behind),
            plane(1, ahead),
            halo,
            halo,
        ],
        whole(planes, here),
        shaped(*center.shape),
        cost=(40 * center.size, 16 * center.size),
    )


def sums(scalars, local, others):
    total = local[0] + scalars.weight(scalars.first(), scalars.slot) * others[0][0]
    for part in others[1:]:
        total = total + part[0]
    return total


class Plan:
    def __init__(self, ints, reals, slots, shape, near, table, back):
        self.ints, self.reals, self.slots, self.near = ints, reals, slots, near
        self.shape, self.table, self.back = shape, table, back
        self.fields, self.block, self.rows, self.cells = shape
        self.pairs = near // 2
        self.owned = self.pairs // QUAD
        self.cycles = near // QUAD
        self.depth = table.shape[2]

    def scalars(self, ints, reals):
        return Scalars(ints, reals, self.slots, self.near)

    def side(self, first, index):
        return pl.BlockSpec((1, self.block, self.near, self.cells), lambda i: (first + i, 0, index, 0))

    def part(self):
        return pl.BlockSpec((1, self.cycles, self.block, self.cells), lambda i: (i, 0, 0, 0))

    def size(self, fields):
        return fields * self.block * self.near * self.cells

    def mix(self, center, first, lo, hi, index, token):
        count = max(1, self.slots // 2 - 1)

        def kernel(ints, reals, own, got, *outs):
            scalars = self.scalars(ints, reals)
            for s in range(count):
                target = scalars.target(s + 1)
                outs[s][0] = (
                    scalars.weight(scalars.slot, target) * own[0]
                    + scalars.weight(scalars.first(), target) * got[0]
                )

        return call(
            kernel,
            "mix",
            token,
            (hi - lo,),
            [self.ints, self.reals, center, first],
            [SMEM, SMEM, self.side(lo, index), self.side(0, 0)],
            [self.side(0, 0)] * count,
            [shaped(hi - lo, self.block, self.near, self.cells)] * count,
            cost=(3 * self.size(hi - lo), 12 * self.size(hi - lo)),
        )

    def spread(self, local, others, lo, hi, token):
        def kernel(ints, reals, local, *refs):
            others, outs = refs[: len(refs) - QUAD - 2], refs[-QUAD - 2 : -2]
            flat, stage = refs[-2:]
            scalars = self.scalars(ints, reals)
            flat[...] = sums(scalars, local, others).reshape(flat.shape)
            for o in range(QUAD):
                for j in range(self.owned):
                    for a in range(2):
                        r = o * self.owned + j + a * self.pairs
                        stage[o, 2 * j + a] = flat[pl.ds(r, self.block, stride=self.near), :]
            for k in range(QUAD):
                outs[k][0] = stage[scalars.rank ^ k]

        return call(
            kernel,
            "spread",
            token,
            (hi - lo,),
            [self.ints, self.reals, local] + others,
            [SMEM, SMEM, self.side(lo, 0)] + [self.side(0, 0)] * len(others),
            [self.part()] * QUAD,
            [shaped(hi - lo, self.cycles, self.block, self.cells)] * QUAD,
            [
                pltpu.VMEM((self.block * self.near, self.cells), jnp.float32),
                pltpu.VMEM((QUAD, self.cycles, self.block, self.cells), jnp.float32),
            ],
            (4 * self.size(hi - lo), 16 * self.size(hi - lo)),
        )

    def own_rows(self, shape):
        return pl.BlockSpec(
            (1, self.owned) + shape, lambda i, ints: (ints[1] // QUAD, ints[1] % QUAD, 0, 0)
        )

    def table_call(self, kernel, name, fields, inputs, in_specs, out_specs, out_shape, scratch, token):
        extra = [] if token is None else [token]
        count = len(inputs)
        return pl.pallas_call(
            lambda *refs: kernel(*refs[: count + 1], *refs[count + 1 + len(extra) :]),
            grid_spec=pltpu.PrefetchScalarGridSpec(
                num_scalar_prefetch=1,
                grid=(fields,),
                in_specs=in_specs + [ANY] * len(extra),
                out_specs=out_specs,
                scratch_shapes=scratch,
            ),
            out_shape=out_shape,
            compiler_params=PARAMS,
            cost_estimate=pl.CostEstimate(
                flops=12 * self.size(fields) * self.depth,
                bytes_accessed=16 * self.size(fields),
                transcendentals=0,
            ),
            name=name,
        )(self.ints, *inputs, *extra)

    def block4(self, *shape):
        return pl.BlockSpec((1,) + shape, lambda i, ints: (i, 0, 0, 0))

    def coefficients(self, parts, token):
        fields = parts[0].shape[0]

        def kernel(ints, reals, table, *refs):
            parts, out, column = refs[:QUAD], refs[QUAD], refs[QUAD + 1]
            scalars = self.scalars(ints, reals)
            row = lax.broadcasted_iota(jnp.int32, (self.depth, self.cells), 0)
            for k in range(QUAD):
                column[:, scalars.rank ^ k] = parts[k][0]
            for j in range(self.owned):
                modes = [
                    jnp.dot(
                        table[0, j],
                        column[2 * j + a].reshape(QUAD * self.block, self.cells),
                        precision=lax.Precision.HIGHEST,
                        preferred_element_type=jnp.float32,
                    )
                    for a in range(2)
                ]
                split = scalars.split(scalars.rank * self.owned + j)
                out[0, j] = jnp.where(row < split, modes[0], modes[1])

        return self.table_call(
            kernel,
            "coefficients",
            fields,
            [self.reals, self.table] + parts,
            [SMEM, self.own_rows(self.table.shape[2:])]
            + [self.block4(self.cycles, self.block, self.cells)] * QUAD,
            self.block4(self.owned, self.depth, self.cells),
            shaped(fields, self.owned, self.depth, self.cells),
            [pltpu.VMEM((self.cycles, QUAD, self.block, self.cells), jnp.float32)],
            token,
        )

    def filtered(self, own, other, parts, token):
        fields = parts[0].shape[0]

        def kernel(ints, reals, back, own, other, *refs):
            parts, outs, waves = refs[:QUAD], refs[QUAD : 2 * QUAD], refs[2 * QUAD]
            scalars = self.scalars(ints, reals)
            row = lax.broadcasted_iota(jnp.int32, (self.depth, self.cells), 0)
            for j in range(self.owned):
                pair = scalars.rank * self.owned + j
                total = own[0, j] + other[0, j]
                keep = row < scalars.split(pair)
                for a in range(2):
                    waves[2 * j + a] = jnp.dot(
                        back[0, j],
                        jnp.where(keep if a == 0 else jnp.logical_not(keep), total, 0.0),
                        precision=lax.Precision.HIGHEST,
                        preferred_element_type=jnp.float32,
                    ).reshape(QUAD, self.block, self.cells)
                    r = pair + a * self.pairs
                    for k in range(QUAD):
                        outs[k][0, 2 * j + a] = (
                            scalars.base(r) * parts[k][0, 2 * j + a]
                            + scalars.scale(r) * waves[2 * j + a, scalars.rank ^ k]
                        )

        part = self.block4(self.cycles, self.block, self.cells)
        modes = self.block4(self.owned, self.depth, self.cells)
        return self.table_call(
            kernel,
            "filtered",
            fields,
            [self.reals, self.back, own, other] + parts,
            [SMEM, self.own_rows(self.back.shape[2:]), modes, modes] + [part] * QUAD,
            [part] * QUAD,
            [shaped(*parts[0].shape)] * QUAD,
            [pltpu.VMEM((self.cycles, QUAD, self.block, self.cells), jnp.float32)],
            token,
        )

    def place_near(self, parts, held, lo, hi, token):
        def kernel(ints, reals, *refs):
            parts, out, stage = refs[:QUAD], refs[-2], refs[-1]
            scalars = self.scalars(ints, reals)
            for k in range(QUAD):
                stage[scalars.rank ^ k] = parts[k][0]
            for o in range(QUAD):
                for j in range(self.owned):
                    for a in range(2):
                        out[0, :, o * self.owned + j + a * self.pairs, :] = stage[o, 2 * j + a]

        carried = [] if held is None else [held]
        return call(
            kernel,
            "place_near",
            token,
            (hi - lo,),
            [self.ints, self.reals] + parts + carried,
            [SMEM, SMEM] + [self.part()] * QUAD + [ANY] * len(carried),
            self.side(lo, 0),
            shaped(*self.shape),
            [pltpu.VMEM((QUAD, self.cycles, self.block, self.cells), jnp.float32)],
            (0, 8 * self.size(hi - lo)),
            {2 + QUAD: 0} if carried else None,
        )

    def place_far(self, local, others, held, lo, hi, token):
        def kernel(ints, reals, local, *refs):
            others, out = refs[: len(refs) - 1 - len(carried)], refs[-1]
            out[0] = sums(self.scalars(ints, reals), local, others)

        carried = [] if held is None else [held]
        return call(
            kernel,
            "place_far",
            token,
            (hi - lo,),
            [self.ints, self.reals, local] + others + carried,
            [SMEM, SMEM, self.side(lo, 1)]
            + [self.side(0, 0)] * len(others)
            + [ANY] * len(carried),
            self.side(lo, 1),
            shaped(*self.shape),
            (),
            (4 * self.size(hi - lo), 16 * self.size(hi - lo)),
            {3 + len(others): 0} if carried else None,
        )


def spans(sizes, total):
    ends = np.cumsum(sizes)
    return [(int(end - size), int(end)) for size, end in zip(sizes, ends)]


def body(adjoint, source, viscosity, kappa, coupling, bc_flags, inst_map):
    slots = lax.axis_size("inst")
    sectors = lax.axis_size("space")
    center = adjoint[0]
    fields, block, cycles, cells = center.shape
    near = cycles // 2
    points = block * sectors
    quads = sectors // QUAD

    def to_partner(x, pick):
        pairs = []
        for i in range(slots):
            for p in range(sectors):
                pairs.append((i * sectors + p, pick(i, p % 2) * sectors + p))
        return lax.ppermute(x, ("inst", "space"), pairs)

    def to_first(x):
        return to_partner(x, lambda i, core: first_partner(i, core, slots))

    def to_later(x, s):
        return to_partner(x, lambda i, core: later_partner(i, core, slots, s))

    def to_sector(x, k):
        return lax.ppermute(x, "space", [(i, i ^ k) for i in range(sectors)])

    def ring(x, step):
        return lax.ppermute(x, "space", [(i, (i + step) % sectors) for i in range(sectors)])

    table, split, base, scale = mode_layout(points, near)
    table = table.reshape(table.shape[0], table.shape[1], quads, QUAD * block).transpose(2, 0, 1, 3)
    here = jnp.stack([lax.axis_index("inst"), lax.axis_index("space")])
    ints = jnp.concatenate([here, inst_map, jnp.asarray(split)])
    reals = jnp.asarray(np.concatenate([spectral_values(slots), base, scale]).astype(np.float32))
    plan = Plan(
        ints,
        reals,
        slots,
        center.shape,
        near,
        jnp.asarray(np.ascontiguousarray(table)),
        jnp.asarray(np.ascontiguousarray(table.transpose(0, 1, 3, 2))),
    )

    groups = [(lo, hi, 0) for lo, hi in spans(NEAR_SIZES, fields)]
    groups += [(lo, hi, 1) for lo, hi in spans(FAR_SIZES, fields)]
    first, others, parts, own, done = {}, {}, {}, {}, {}
    token, local, held, halos = None, None, None, None
    for step, g in ORDER:
        lo, hi, index = groups[g]
        if step == "pack":
            packed = pack(center, viscosity, lo, hi, index * near, near, halos is None, token)
            token = packed[0]
            first[g] = to_first(packed[0])
            if halos is None:
                halos = ring(packed[1], 1), ring(packed[2], -1)
        elif step == "local":
            local = token = local_part(
                center, source[0], viscosity, kappa, coupling, bc_flags, *halos, token
            )
        elif step == "mix":
            mixed = plan.mix(center, first[g], lo, hi, index, token)
            token = mixed[0]
            others[g] = [first[g]] + [to_later(x, s + 1) for s, x in enumerate(mixed)]
        elif step == "spread":
            mine = plan.spread(local, others[g], lo, hi, token)
            token = mine[0]
            parts[g] = [mine[0]] + [to_sector(mine[k], k) for k in range(1, QUAD)]
        elif step == "coef":
            part = token = plan.coefficients(parts[g], token)
            stride = QUAD
            while 2 * stride < sectors:
                part = part + to_sector(part, stride)
                stride = 2 * stride
            other = to_sector(part, stride) if stride < sectors else jnp.zeros_like(part)
            own[g] = part, other
        elif step == "filter":
            mine = plan.filtered(*own[g], parts[g], token)
            token = mine[0]
            done[g] = [mine[0]] + [to_sector(mine[k], k) for k in range(1, QUAD)]
        elif step == "near":
            held = token = plan.place_near(done[g], held, lo, hi, None if token is held else token)
        else:
            held = token = plan.place_far(
                local, others[g], held, lo, hi, None if token is held else token
            )
    return held[None]


def solution(mesh):
    return jax.shard_map(
        body,
        mesh=mesh,
        in_specs=(
            P("inst", None, "space", None, None),
            P("inst", None, "space", None, None),
            P("space", None, None),
            P(),
            P(),
            P(),
            P(),
        ),
        out_specs=P("inst", None, "space", None, None),
        check_vma=False,
    )
```

time: 485 us -> 280 us (0.58)
  Pallas kernels: 0 us -> 121 us
  matrix products: 116 us -> 0 us
  waiting for transfers between devices: 201 us -> 121 us
  blocking collectives: 62.8 us -> 0 us
  local copies, waits for them, and re-layouts: 43.5 us -> 1.38 us
  other arithmetic: 32.7 us -> 0.08 us
  starting transfers between devices: 9.1 us -> 34.6 us
  between operations: 13.9 us -> 0.33 us
    all_gather x1 -> x0, waiting for transfers between devices: 140 us -> none  [body(): lax.all_gather(adjoint, 'inst', axis=0, tiled=True)]
    pallas_call x0 -> x25, Pallas kernels: none -> 121 us  [the longest x19 108 us: call(): pl.pallas_call(lambda *refs: kernel(*refs[:len(inputs)], *refs[len(inputs...]
    ppermute x2 -> x33, waiting for transfers between devices: 0.01 us -> 121 us  [the longest x21 75.8 us: to_sector(): return lax.ppermute(x, 'space', [(i, i ^ k) for i in range(sectors)])]
    dot_general x6 -> x0, matrix products: 116 us -> none  [the longest x1 57.2 us: body(): jnp.tensordot(column, lax.all_gather(adjoint, 'inst', axis=0, tiled=True)...]
    all_to_all x1 -> x0, blocking collectives: 62.8 us -> none  [body(): lax.all_to_all(result, 'space', split_axis=1, concat_axis=2, tiled=True)]
    all_to_all x1 -> x0, waiting for transfers between devices: 60.2 us -> none  [body(): lax.all_to_all(pre[:, :, :near, :], 'space', split_axis=2, concat_axis=1,...]
    ppermute x2 -> x33, starting transfers between devices: 4.49 us -> 34.6 us  [the longest x21 17 us: to_sector(): return lax.ppermute(x, 'space', [(i, i ^ k) for i in range(sectors)])]
    mul x8 -> x0, other arithmetic: 22.3 us -> none  [the longest x1 8.49 us: viscous(): open_faces[:, 0][:, None, None, None] * visc[None, :, :, :1]]
  transfers between devices with their start and end apart: 4 -> 33, of which waited for: 2 -> 15; matrix products, arithmetic and copies ran while one was open for 10% -> 0% of each run, Pallas kernels for 0% -> 30%
where the time goes in v2:
time: 280 us; the launch traced here: 279 us
  Pallas kernels  121 us (43%)
  waiting for transfers between devices  121 us (43%)
  starting transfers between devices  34.6 us (12%)
    pallas_call x19, Pallas kernels, call(): pl.pallas_call(lambda *refs: kernel(*refs[:len(inputs)], *refs[len(inputs...  108 us
    ppermute x21, waiting for transfers between devices, to_sector(): return lax.ppermute(x, 'space', [(i, i ^ k) for i in range(sectors)])  75.8 us
    ppermute x10, waiting for transfers between devices, to_partner(): return lax.ppermute(x, ('inst', 'space'), pairs)  41.8 us
    ppermute x21, starting transfers between devices, to_sector(): return lax.ppermute(x, 'space', [(i, i ^ k) for i in range(sectors)])  17 us
    ppermute x10, starting transfers between devices, to_partner(): return lax.ppermute(x, ('inst', 'space'), pairs)  14 us
    pallas_call x6, Pallas kernels, table_call(): pl.pallas_call(lambda *refs: kernel(*refs[:count + 1], *refs[count + 1 +...  13 us
  transfers between devices with their start and end apart: 33, of which 15 were waited for; matrix products, arithmetic and copies ran while one was open for 0% of the time, Pallas kernels for 30%

profile of v2, /device:TPU:0, one launch (start us, length us, event | category | flops | bytes accessed | tf_op | source)
XLA Modules:
  0.0 278.7 jit_solution(13189957310717874581)
XLA Ops:
  1.2 32.9 %pack.5 = (f32[2,32,32,128]{3,2,1,0:T(8,128)}, f32[6,1,64,128]{3,2,1,0:T(8,128)S(1)}, f32[6,1,64,128]{3,2,1,0:T(8,128)S(1)}) custom-call(f32[5,32,64,128]{3,2,1,0:T(8,128)} %bitcast.5, f32[32,64,128]{2,1,0:T(8,128)S(1)} %copy-done), custom_call_target="tpu_custom_call" | custom-call | bytes 2097152 | tf_op jit(solution)/shard_map/pack/pallas_call | solution.py:125
  34.2 3.0 %collective-permute-start.2 = (f32[2,32,32,128]{3,2,1,0:T(8,128)}, f32[2,32,32,128]{3,2,1,0:T(8,128)}, u32[]{:S(2)}, u32[]{:S(2)}) collective-permute-start(f32[2,32,32,128]{3,2,1,0:T(8,128)} %get-tuple-element.34.refs_2_), channel_id=1, source_target_pairs={{0,16},{1,9},{2,18},{3,11},{4,20},{5,13},{6,22},{7,15},{8,24},{9,1... | collective-permute-start | bytes 3145736 | tf_op jit(solution)/shard_map/ppermute | solution.py:520
  37.3 32.9 %pack.6.refs_12_ = f32[2,32,32,128]{3,2,1,0:T(8,128)} custom-call(f32[5,32,64,128]{3,2,1,0:T(8,128)} %bitcast.6, f32[32,64,128]{2,1,0:T(8,128)S(1)} %copy-done, f32[2,32,32,128]{3,2,1,0:T(8,128)} %get-tuple-element.34.refs_2_), custom_call_target="tpu_custom_call" | custom-call | bytes 2097152 | tf_op jit(solution)/shard_map/pack/pallas_call | solution.py:125
  70.3 3.5 %collective-permute-start.1 = (f32[6,1,64,128]{3,2,1,0:T(8,128)S(1)}, f32[6,1,64,128]{3,2,1,0:T(8,128)S(1)}, u32[]{:S(2)}, u32[]{:S(2)}) collective-permute-start(f32[6,1,64,128]{3,2,1,0:T(8,128)S(1)} %get-tuple-element.33), channel_id=1, source_target_pairs={{0,7},{1,0},{2,1},{3,2},{4,3},{5,4},{6,5},{7,6},{8,15},{9,8},{10,9... | collective-permute-start | bytes 589832 | tf_op jit(solution)/shard_map/ppermute | solution.py:532
  74.0 3.3 %collective-permute-done.refs_10_ = f32[6,1,64,128]{3,2,1,0:T(8,128)S(1)} collective-permute-done((f32[6,1,64,128]{3,2,1,0:T(8,128)S(1)}, f32[6,1,64,128]{3,2,1,0:T(8,128)S(1)}, u32[]{:S(2)}, u32[]{:S(2)}) %collective-permute-start) | collective-permute-done | bytes 196640 | tf_op jit(solution)/shard_map/ppermute | solution.py:532
  77.3 12.3 %local_part.1.refs_4_.refs_2_ = f32[5,32,64,128]{3,2,1,0:T(8,128)} custom-call(f32[5,5]{1,0:T(8,128)S(1)} %copy-done.5, f32[5]{0:T(128)S(1)} %copy-done.6, s32[5,3]{1,0:T(8,128)S(1)} %copy.16.refs_2_, f32[5,32,64,128]{3,2,1,0:T(8,128)} %bitcast.7, f32[5,32,64,128]{3,2,1,0:T(8,128)} %bitcast.8, f32[5,32,64,128]{3,2,1,0:T(8,128)} %bitcast.9, ...), custom_call_target="tpu_custom_call" | custom-call | flops 52428800 | bytes 20971520 | tf_op jit(solution)/shard_map/local_part/pallas_call | solution.py:125
  94.8 11.4 %collective-permute-done.3.refs_4_ = f32[2,32,32,128]{3,2,1,0:T(8,128)S(1)} collective-permute-done((f32[2,32,32,128]{3,2,1,0:T(8,128)S(1)}, f32[2,32,32,128]{3,2,1,0:T(8,128)S(1)}, u32[]{:S(2)}, u32[]{:S(2)}) %collective-permute-start.3) | collective-permute-done | bytes 1048608 | tf_op jit(solution)/shard_map/ppermute | solution.py:520
  112.5 6.6 %collective-permute-done.8.refs_5_.refs_7_ = f32[2,8,32,128]{3,2,1,0:T(8,128)S(1)} collective-permute-done((f32[2,8,32,128]{3,2,1,0:T(8,128)S(1)}, f32[2,8,32,128]{3,2,1,0:T(8,128)S(1)}, u32[]{:S(2)}, u32[]{:S(2)}) %collective-permute-start.8) | collective-permute-done | bytes 262176 | tf_op jit(solution)/shard_map/ppermute | solution.py:529
  119.1 3.8 %collective-permute-done.9.refs_6_.refs_8_ = f32[2,8,32,128]{3,2,1,0:T(8,128)S(1)} collective-permute-done((f32[2,8,32,128]{3,2,1,0:T(8,128)S(1)}, f32[2,8,32,128]{3,2,1,0:T(8,128)S(1)}, u32[]{:S(2)}, u32[]{:S(2)}) %collective-permute-start.9) | collective-permute-done | bytes 262176 | tf_op jit(solution)/shard_map/ppermute | solution.py:529
  122.9 2.4 coefficients.3.refs_5_.refs_3_
  131.0 24.0 %collective-permute-done.5.refs_3_ = f32[1,32,32,128]{3,2,1,0:T(8,128)S(1)} collective-permute-done((f32[1,32,32,128]{3,2,1,0:T(8,128)S(1)}, f32[1,32,32,128]{3,2,1,0:T(8,128)S(1)}, u32[]{:S(2)}, u32[]{:S(2)}) %collective-permute-start.5) | collective-permute-done | bytes 524320 | tf_op jit(solution)/shard_map/ppermute | solution.py:520
  159.0 6.4 %collective-permute-done.10.refs_4_ = f32[1,32,32,128]{3,2,1,0:T(8,128)S(1)} collective-permute-done((f32[1,32,32,128]{3,2,1,0:T(8,128)S(1)}, f32[1,32,32,128]{3,2,1,0:T(8,128)S(1)}, u32[]{:S(2)}, u32[]{:S(2)}) %collective-permute-start.10) | collective-permute-done | bytes 524320 | tf_op jit(solution)/shard_map/ppermute | solution.py:520
  171.0 18.9 %collective-permute-done.13.refs_5_.refs_7_ = f32[2,8,32,128]{3,2,1,0:T(8,128)S(1)} collective-permute-done((f32[2,8,32,128]{3,2,1,0:T(8,128)S(1)}, f32[2,8,32,128]{3,2,1,0:T(8,128)S(1)}, u32[]{:S(2)}, u32[]{:S(2)}) %collective-permute-start.13) | collective-permute-done | bytes 262176 | tf_op jit(solution)/shard_map/ppermute | solution.py:529
  195.4 2.4 filtered.3
  198.2 2.5 collective-permute-start.15
  204.8 10.2 %collective-permute-done.22.refs_6_.refs_8_ = f32[1,8,32,128]{3,2,1,0:T(8,128)S(1)} collective-permute-done((f32[1,8,32,128]{3,2,1,0:T(8,128)S(1)}, f32[1,8,32,128]{3,2,1,0:T(8,128)S(1)}, u32[]{:S(2)}, u32[]{:S(2)}) %collective-permute-start.22) | collective-permute-done | bytes 131104 | tf_op jit(solution)/shard_map/ppermute | solution.py:529
  219.0 11.0 %collective-permute-done.18.refs_4_ = f32[2,8,32,128]{3,2,1,0:T(8,128)S(1)} collective-permute-done((f32[2,8,32,128]{3,2,1,0:T(8,128)S(1)}, f32[2,8,32,128]{3,2,1,0:T(8,128)S(1)}, u32[]{:S(2)}, u32[]{:S(2)}) %collective-permute-start.18) | collective-permute-done | bytes 262176 | tf_op jit(solution)/shard_map/ppermute | solution.py:529
  230.0 5.6 %collective-permute-done.19.refs_5_ = f32[2,8,32,128]{3,2,1,0:T(8,128)S(1)} collective-permute-done((f32[2,8,32,128]{3,2,1,0:T(8,128)S(1)}, f32[2,8,32,128]{3,2,1,0:T(8,128)S(1)}, u32[]{:S(2)}, u32[]{:S(2)}) %collective-permute-start.19) | collective-permute-done | bytes 262176 | tf_op jit(solution)/shard_map/ppermute | solution.py:529
  235.7 2.4 place_near.3.refs_9_.refs_6_
  238.1 2.4 filtered.4
  246.5 11.5 %collective-permute-done.27.refs_4_ = f32[2,8,32,128]{3,2,1,0:T(8,128)S(1)} collective-permute-done((f32[2,8,32,128]{3,2,1,0:T(8,128)S(1)}, f32[2,8,32,128]{3,2,1,0:T(8,128)S(1)}, u32[]{:S(2)}, u32[]{:S(2)}) %collective-permute-start.27) | collective-permute-done | bytes 262176 | tf_op jit(solution)/shard_map/ppermute | solution.py:529
  258.1 4.5 %collective-permute-done.28.refs_5_ = f32[2,8,32,128]{3,2,1,0:T(8,128)S(1)} collective-permute-done((f32[2,8,32,128]{3,2,1,0:T(8,128)S(1)}, f32[2,8,32,128]{3,2,1,0:T(8,128)S(1)}, u32[]{:S(2)}, u32[]{:S(2)}) %collective-permute-start.28) | collective-permute-done | bytes 262176 | tf_op jit(solution)/shard_map/ppermute | solution.py:529
  262.5 2.4 place_near.4.refs_9_.refs_5_
  268.6 3.9 %place_far.2.refs_6_ = f32[5,32,64,128]{3,2,1,0:T(8,128)} custom-call(s32[22]{0:T(128)S(1)} %pad_add_fusion.refs_0_, f32[71]{0:T(128)S(1)} %copy-done.4, f32[5,32,64,128]{3,2,1,0:T(8,128)} %local_part.1.refs_4_.refs_2_, f32[3,32,32,128]{3,2,1,0:T(8,128)S(1)} %collective-permute-done.23.refs_3_, ...), custom_call_target="tpu_custom_call", output_to_operand_aliasing={{}: (5, {})} | custom-call | flops 1572864 | bytes 6291456 | tf_op jit(solution)/shard_map/place_far/pallas_call | solution.py:125
  (89 shorter events, 57.9 us)
Async XLA Ops:
  34.2 55.4 %collective-permute-start.2 = (f32[2,32,32,128]{3,2,1,0:T(8,128)}, f32[2,32,32,128]{3,2,1,0:T(8,128)}, u32[]{:S(2)}, u32[]{:S(2)}) collective-permute-start(f32[2,32,32,128]{3,2,1,0:T(8,128)} %get-tuple-element.34.refs_2_), channel_id=1, source_target_pairs={{0,16},{1,9},{2,18},{3,11},{4,20},{5,13},{6,22},{7,15},{8,24},{9,1... | collective-permute-start | bytes 3145736 | tf_op jit(solution)/shard_map/ppermute | solution.py:520
  70.2 23.2 %collective-permute-start.4 = (f32[2,32,32,128]{3,2,1,0:T(8,128)}, f32[2,32,32,128]{3,2,1,0:T(8,128)S(1)}, u32[]{:S(2)}, u32[]{:S(2)}) collective-permute-start(f32[2,32,32,128]{3,2,1,0:T(8,128)} %pack.6.refs_12_), channel_id=1, source_target_pairs={{0,16},{1,9},{2,18},{3,11},{4,20},{5,13},{6,22},{7,15},{8,24},{9,1... | collective-permute-start | bytes 3145736 | tf_op jit(solution)/shard_map/ppermute | solution.py:520
  91.3 14.9 %collective-permute-start.3 = (f32[2,32,32,128]{3,2,1,0:T(8,128)S(1)}, f32[2,32,32,128]{3,2,1,0:T(8,128)S(1)}, u32[]{:S(2)}, u32[]{:S(2)}) collective-permute-start(f32[2,32,32,128]{3,2,1,0:T(8,128)S(1)} %mix.5.refs_4_), channel_id=1, source_target_pairs={{0,8},{1,17},{2,10},{3,19},{4,12},{5,21},{6,14},{7,23},{8,0},{9,25... | collective-permute-start | bytes 3145736 | tf_op jit(solution)/shard_map/ppermute | solution.py:520
  94.7 30.7 %collective-permute-start.6 = (f32[2,32,32,128]{3,2,1,0:T(8,128)S(1)}, f32[2,32,32,128]{3,2,1,0:T(8,128)S(1)}, u32[]{:S(2)}, u32[]{:S(2)}) collective-permute-start(f32[2,32,32,128]{3,2,1,0:T(8,128)S(1)} %mix.6.refs_5_), channel_id=1, source_target_pairs={{0,8},{1,17},{2,10},{3,19},{4,12},{5,21},{6,14},{7,23},{8,0},{9,25... | collective-permute-start | bytes 3145736 | tf_op jit(solution)/shard_map/ppermute | solution.py:520
  110.5 12.4 %collective-permute-start.9 = (f32[2,8,32,128]{3,2,1,0:T(8,128)S(1)}, f32[2,8,32,128]{3,2,1,0:T(8,128)S(1)}, u32[]{:S(2)}, u32[]{:S(2)}) collective-permute-start(f32[2,8,32,128]{3,2,1,0:T(8,128)S(1)} %get-tuple-element.38), channel_id=1, source_target_pairs={{0,3},{1,2},{2,1},{3,0},{4,7},{5,6},{6,5},{7,4},{8,11},{9,10},{10,... | collective-permute-start | bytes 786440 | tf_op jit(solution)/shard_map/ppermute | solution.py:529
  128.9 69.4 %collective-permute-start.23 = (f32[3,32,32,128]{3,2,1,0:T(8,128)S(1)}, f32[3,32,32,128]{3,2,1,0:T(8,128)S(1)}, u32[]{:S(2)}, u32[]{:S(2)}) collective-permute-start(f32[3,32,32,128]{3,2,1,0:T(8,128)S(1)} %pack.8.refs_4_), channel_id=1, source_target_pairs={{0,16},{1,9},{2,18},{3,11},{4,20},{5,13},{6,22},{7,15},{8,24},{9,1... | collective-permute-start | bytes 4718600 | tf_op jit(solution)/shard_map/ppermute | solution.py:520
  130.7 24.3 %collective-permute-start.5 = (f32[1,32,32,128]{3,2,1,0:T(8,128)S(1)}, f32[1,32,32,128]{3,2,1,0:T(8,128)S(1)}, u32[]{:S(2)}, u32[]{:S(2)}) collective-permute-start(f32[1,32,32,128]{3,2,1,0:T(8,128)S(1)} %pack.7.refs_7_), channel_id=1, source_target_pairs={{0,16},{1,9},{2,18},{3,11},{4,20},{5,13},{6,22},{7,15},{8,24},{9,1... | collective-permute-start | bytes 1572872 | tf_op jit(solution)/shard_map/ppermute | solution.py:520
  157.9 13.1 %collective-permute-start.12 = (f32[2,8,32,128]{3,2,1,0:T(8,128)S(1)}, f32[2,8,32,128]{3,2,1,0:T(8,128)S(1)}, u32[]{:S(2)}, u32[]{:S(2)}) collective-permute-start(f32[2,8,32,128]{3,2,1,0:T(8,128)S(1)} %get-tuple-element.41), channel_id=1, source_target_pairs={{0,1},{1,0},{2,3},{3,2},{4,5},{5,4},{6,7},{7,6},{8,9},{9,8},{10,11... | collective-permute-start | bytes 786440 | tf_op jit(solution)/shard_map/ppermute | solution.py:529
  157.9 37.5 %collective-permute-start.16 = (f32[2,4,128,128]{3,2,1,0:T(8,128)S(1)}, f32[2,4,128,128]{3,2,1,0:T(8,128)S(1)}, u32[]{:S(2)}, u32[]{:S(2)}) collective-permute-start(f32[2,4,128,128]{3,2,1,0:T(8,128)S(1)} %coefficients.3.refs_5_.refs_3_), channel_id=1, source_target_pairs={{0,4},{1,5},{2,6},{3,7},{4,0},{5,1},{6,2},{7,3},{8,12},{9,13},{10,... | collective-permute-start | bytes 1572872 | tf_op jit(solution)/shard_map/ppermute | solution.py:529
  168.3 72.2 %collective-permute-start.11 = (f32[2,32,32,128]{3,2,1,0:T(8,128)S(1)}, f32[2,32,32,128]{3,2,1,0:T(8,128)S(1)}, u32[]{:S(2)}, u32[]{:S(2)}) collective-permute-start(f32[2,32,32,128]{3,2,1,0:T(8,128)S(1)} %pack.9.refs_7_), channel_id=1, source_target_pairs={{0,16},{1,9},{2,18},{3,11},{4,20},{5,13},{6,22},{7,15},{8,24},{9,1... | collective-permute-start | bytes 3145736 | tf_op jit(solution)/shard_map/ppermute | solution.py:520
  170.2 19.8 %collective-permute-start.13 = (f32[2,8,32,128]{3,2,1,0:T(8,128)S(1)}, f32[2,8,32,128]{3,2,1,0:T(8,128)S(1)}, u32[]{:S(2)}, u32[]{:S(2)}) collective-permute-start(f32[2,8,32,128]{3,2,1,0:T(8,128)S(1)} %get-tuple-element.42), channel_id=1, source_target_pairs={{0,2},{1,3},{2,0},{3,1},{4,6},{5,7},{6,4},{7,5},{8,10},{9,11},{10,... | collective-permute-start | bytes 786440 | tf_op jit(solution)/shard_map/ppermute | solution.py:529
  171.0 20.3 %collective-permute-start.14 = (f32[2,8,32,128]{3,2,1,0:T(8,128)S(1)}, f32[2,8,32,128]{3,2,1,0:T(8,128)S(1)}, u32[]{:S(2)}, u32[]{:S(2)}) collective-permute-start(f32[2,8,32,128]{3,2,1,0:T(8,128)S(1)} %get-tuple-element.43), channel_id=1, source_target_pairs={{0,3},{1,2},{2,1},{3,0},{4,7},{5,6},{6,5},{7,4},{8,11},{9,10},{10,... | collective-permute-start | bytes 786440 | tf_op jit(solution)/shard_map/ppermute | solution.py:529
  190.0 13.1 %collective-permute-start.20 = (f32[1,8,32,128]{3,2,1,0:T(8,128)S(1)}, f32[1,8,32,128]{3,2,1,0:T(8,128)S(1)}, u32[]{:S(2)}, u32[]{:S(2)}) collective-permute-start(f32[1,8,32,128]{3,2,1,0:T(8,128)S(1)} %get-tuple-element.48), channel_id=1, source_target_pairs={{0,1},{1,0},{2,3},{3,2},{4,5},{5,4},{6,7},{7,6},{8,9},{9,8},{10,11... | collective-permute-start | bytes 393224 | tf_op jit(solution)/shard_map/ppermute | solution.py:529
  191.4 13.4 %collective-permute-start.21 = (f32[1,8,32,128]{3,2,1,0:T(8,128)S(1)}, f32[1,8,32,128]{3,2,1,0:T(8,128)S(1)}, u32[]{:S(2)}, u32[]{:S(2)}) collective-permute-start(f32[1,8,32,128]{3,2,1,0:T(8,128)S(1)} %get-tuple-element.49), channel_id=1, source_target_pairs={{0,2},{1,3},{2,0},{3,1},{4,6},{5,7},{6,4},{7,5},{8,10},{9,11},{10,... | collective-permute-start | bytes 393224 | tf_op jit(solution)/shard_map/ppermute | solution.py:529
  197.9 18.7 %collective-permute-start.17 = (f32[2,8,32,128]{3,2,1,0:T(8,128)S(1)}, f32[2,8,32,128]{3,2,1,0:T(8,128)S(1)}, u32[]{:S(2)}, u32[]{:S(2)}) collective-permute-start(f32[2,8,32,128]{3,2,1,0:T(8,128)S(1)} %get-tuple-element.45), channel_id=1, source_target_pairs={{0,1},{1,0},{2,3},{3,2},{4,5},{5,4},{6,7},{7,6},{8,9},{9,8},{10,11... | collective-permute-start | bytes 786440 | tf_op jit(solution)/shard_map/ppermute | solution.py:529
  198.2 39.8 %collective-permute-start.15 = (f32[2,4,128,128]{3,2,1,0:T(8,128)S(1)}, f32[2,4,128,128]{3,2,1,0:T(8,128)S(1)}, u32[]{:S(2)}, u32[]{:S(2)}) collective-permute-start(f32[2,4,128,128]{3,2,1,0:T(8,128)S(1)} %coefficients.4.refs_9_.refs_3_), channel_id=1, source_target_pairs={{0,4},{1,5},{2,6},{3,7},{4,0},{5,1},{6,2},{7,3},{8,12},{9,13},{10,... | collective-permute-start | bytes 1572872 | tf_op jit(solution)/shard_map/ppermute | solution.py:529
  203.1 65.6 %collective-permute-start.32 = (f32[3,32,32,128]{3,2,1,0:T(8,128)S(1)}, f32[3,32,32,128]{3,2,1,0:T(8,128)}, u32[]{:S(2)}, u32[]{:S(2)}) collective-permute-start(f32[3,32,32,128]{3,2,1,0:T(8,128)S(1)} %mix.8.refs_7_), channel_id=1, source_target_pairs={{0,8},{1,17},{2,10},{3,19},{4,12},{5,21},{6,14},{7,23},{8,0},{9,25... | collective-permute-start | bytes 4718600 | tf_op jit(solution)/shard_map/ppermute | solution.py:520
  204.8 10.2 %collective-permute-start.22 = (f32[1,8,32,128]{3,2,1,0:T(8,128)S(1)}, f32[1,8,32,128]{3,2,1,0:T(8,128)S(1)}, u32[]{:S(2)}, u32[]{:S(2)}) collective-permute-start(f32[1,8,32,128]{3,2,1,0:T(8,128)S(1)} %get-tuple-element.50), channel_id=1, source_target_pairs={{0,3},{1,2},{2,1},{3,0},{4,7},{5,6},{6,5},{7,4},{8,11},{9,10},{10,... | collective-permute-start | bytes 393224 | tf_op jit(solution)/shard_map/ppermute | solution.py:529
  215.0 15.1 %collective-permute-start.18 = (f32[2,8,32,128]{3,2,1,0:T(8,128)S(1)}, f32[2,8,32,128]{3,2,1,0:T(8,128)S(1)}, u32[]{:S(2)}, u32[]{:S(2)}) collective-permute-start(f32[2,8,32,128]{3,2,1,0:T(8,128)S(1)} %get-tuple-element.46), channel_id=1, source_target_pairs={{0,2},{1,3},{2,0},{3,1},{4,6},{5,7},{6,4},{7,5},{8,10},{9,11},{10,... | collective-permute-start | bytes 786440 | tf_op jit(solution)/shard_map/ppermute | solution.py:529
  216.6 19.1 %collective-permute-start.19 = (f32[2,8,32,128]{3,2,1,0:T(8,128)S(1)}, f32[2,8,32,128]{3,2,1,0:T(8,128)S(1)}, u32[]{:S(2)}, u32[]{:S(2)}) collective-permute-start(f32[2,8,32,128]{3,2,1,0:T(8,128)S(1)} %get-tuple-element.47), channel_id=1, source_target_pairs={{0,3},{1,2},{2,1},{3,0},{4,7},{5,6},{6,5},{7,4},{8,11},{9,10},{10,... | collective-permute-start | bytes 786440 | tf_op jit(solution)/shard_map/ppermute | solution.py:529
  241.9 34.6 %collective-permute-start.24 = (f32[2,32,32,128]{3,2,1,0:T(8,128)S(1)}, f32[2,32,32,128]{3,2,1,0:T(8,128)S(1)}, u32[]{:S(2)}, u32[]{:S(2)}) collective-permute-start(f32[2,32,32,128]{3,2,1,0:T(8,128)S(1)} %mix.9.refs_7_), channel_id=1, source_target_pairs={{0,8},{1,17},{2,10},{3,19},{4,12},{5,21},{6,14},{7,23},{8,0},{9,25... | collective-permute-start | bytes 3145736 | tf_op jit(solution)/shard_map/ppermute | solution.py:520
  243.3 14.8 %collective-permute-start.27 = (f32[2,8,32,128]{3,2,1,0:T(8,128)S(1)}, f32[2,8,32,128]{3,2,1,0:T(8,128)S(1)}, u32[]{:S(2)}, u32[]{:S(2)}) collective-permute-start(f32[2,8,32,128]{3,2,1,0:T(8,128)S(1)} %get-tuple-element.53), channel_id=1, source_target_pairs={{0,2},{1,3},{2,0},{3,1},{4,6},{5,7},{6,4},{7,5},{8,10},{9,11},{10,... | collective-permute-start | bytes 786440 | tf_op jit(solution)/shard_map/ppermute | solution.py:529
  243.3 19.2 %collective-permute-start.28 = (f32[2,8,32,128]{3,2,1,0:T(8,128)S(1)}, f32[2,8,32,128]{3,2,1,0:T(8,128)S(1)}, u32[]{:S(2)}, u32[]{:S(2)}) collective-permute-start(f32[2,8,32,128]{3,2,1,0:T(8,128)S(1)} %get-tuple-element.54), channel_id=1, source_target_pairs={{0,3},{1,2},{2,1},{3,0},{4,7},{5,6},{6,5},{7,4},{8,11},{9,10},{10,... | collective-permute-start | bytes 786440 | tf_op jit(solution)/shard_map/ppermute | solution.py:529
  245.0 19.9 %collective-permute-start.25 = (f32[1,4,128,128]{3,2,1,0:T(8,128)S(1)}, f32[1,4,128,128]{3,2,1,0:T(8,128)S(1)}, u32[]{:S(2)}, u32[]{:S(2)}) collective-permute-start(f32[1,4,128,128]{3,2,1,0:T(8,128)S(1)} %coefficients.5.refs_6_.refs_3_), channel_id=1, source_target_pairs={{0,4},{1,5},{2,6},{3,7},{4,0},{5,1},{6,2},{7,3},{8,12},{9,13},{10,... | collective-permute-start | bytes 786440 | tf_op jit(solution)/shard_map/ppermute | solution.py:529
  (19 other events, 363.2 us)

commit v3 on v2

--- a/solution.py
+++ b/solution.py
@@ -19,27 +19,34 @@
     ("mix", 1),
     ("spread", 0),
     ("pack", 2),
-    ("coef", 0),
+    ("join", 0),
     ("spread", 1),
     ("pack", 3),
+    ("coef", 0),
+    ("join", 1),
     ("mix", 2),
     ("spread", 2),
     ("pack", 4),
+    ("filter", 0),
     ("coef", 1),
-    ("filter", 0),
+    ("join", 2),
     ("mix", 3),
+    ("back", 0),
     ("coef", 2),
     ("near", 0),
     ("filter", 1),
     ("mix", 4),
+    ("back", 1),
     ("near", 1),
     ("filter", 2),
     ("far", 3),
+    ("back", 2),
     ("near", 2),
     ("far", 4),
 )
 SMEM = pl.BlockSpec(memory_space=pltpu.SMEM)
 ANY = pl.BlockSpec(memory_space=pl.ANY)
+COST = pl.CostEstimate(flops=0, bytes_accessed=0, transcendentals=0)
 PARAMS = pltpu.CompilerParams(vmem_limit_bytes=48 * 1024 * 1024)
 
 
@@ -120,7 +127,7 @@
     return (slot // 2 + s) % (slots // 2) * 2 + slot % 2
 
 
-def call(kernel, name, token, grid, inputs, in_specs, out_specs, out_shape, scratch=(), cost=(0, 0), alias=None):
+def call(kernel, name, token, grid, inputs, in_specs, out_specs, out_shape, scratch=(), alias=None):
     extra = [] if token is None else [token]
     return pl.pallas_call(
         lambda *refs: kernel(*refs[: len(inputs)], *refs[len(inputs) + len(extra) :]),
@@ -131,7 +138,7 @@
         scratch_shapes=list(scratch),
         input_output_aliases=alias or {},
         compiler_params=PARAMS,
-        cost_estimate=pl.CostEstimate(flops=cost[0], bytes_accessed=cost[1], transcendentals=0),
+        cost_estimate=COST,
         name=name,
     )(*inputs, *extra)
 
@@ -140,37 +147,27 @@
     return jax.ShapeDtypeStruct(shape, jnp.float32)
 
 
-def pack(center, viscosity, lo, hi, base, near, edges, token):
+def pack(center, viscosity, lo, hi, index, near, edges, token):
     fields, block, rows, cells = center.shape
-
-    def kernel(center, viscosity, *refs):
-        outs, sem = refs[:-1], refs[-1]
-        moves = [(center.at[pl.ds(lo, hi - lo), :, pl.ds(base, near)], outs[0])]
-        if edges:
-            for out, start in zip(outs[1:], (block - 1, 0)):
-                moves.append((center.at[:, pl.ds(start, 1)], out.at[pl.ds(0, fields)]))
-                moves.append((viscosity.at[pl.ds(start, 1)], out.at[fields]))
-        copies = [pltpu.make_async_copy(a, b, sem.at[i]) for i, (a, b) in enumerate(moves)]
-        for copy in copies:
-            copy.start()
-        for copy in copies:
-            copy.wait()
-
+    inputs, in_specs = [center], [pl.BlockSpec((1, block, near, cells), lambda i: (lo + i, 0, index, 0))]
     shapes = [shaped(hi - lo, block, near, cells)]
+    out_specs = [pl.BlockSpec((1, block, near, cells), lambda i: (i, 0, 0, 0))]
     if edges:
-        shapes += [shaped(fields + 1, 1, rows, cells)] * 2
-    return call(
-        kernel,
-        "pack",
-        token,
-        (),
-        [center, viscosity],
-        [ANY, ANY],
-        [ANY] * len(shapes),
-        shapes,
-        [pltpu.SemaphoreType.DMA((5,))],
-        (0, 8 * (hi - lo) * block * near * cells),
-    )
+        for start in (block - 1, 0):
+            inputs += [center, viscosity]
+            in_specs.append(pl.BlockSpec((fields, 1, rows, cells), lambda i, s=start: (0, s, 0, 0)))
+            in_specs.append(pl.BlockSpec((1, rows, cells), lambda i, s=start: (s, 0, 0)))
+            shapes.append(shaped(fields + 1, 1, rows, cells))
+            out_specs.append(pl.BlockSpec((fields + 1, 1, rows, cells), lambda i: (0, 0, 0, 0)))
+
+    def kernel(source, *refs):
+        out, rest = refs[len(inputs) - 1], refs[len(inputs) :]
+        out[...] = source[...]
+        for e, edge in enumerate(rest):
+            edge[:fields] = refs[2 * e][...]
+            edge[fields] = refs[2 * e + 1][...]
+
+    return call(kernel, "pack", token, (hi - lo,), inputs, in_specs, out_specs, shapes)
 
 
 def local_kernel(
@@ -258,7 +255,6 @@
         ],
         whole(planes, here),
         shaped(*center.shape),
-        cost=(40 * center.size, 16 * center.size),
     )
 
 
@@ -286,10 +282,15 @@
         return pl.BlockSpec((1, self.block, self.near, self.cells), lambda i: (first + i, 0, index, 0))
 
     def part(self):
-        return pl.BlockSpec((1, self.cycles, self.block, self.cells), lambda i: (i, 0, 0, 0))
-
-    def size(self, fields):
-        return fields * self.block * self.near * self.cells
+        return pl.BlockSpec((1, self.cycles, self.block, self.cells), lambda i, *_: (i, 0, 0, 0))
+
+    def parts(self, count, first=0):
+        shape = (count, 1, self.cycles, self.block, self.cells)
+        return pl.BlockSpec(shape, lambda i, *_: (first, i, 0, 0, 0))
+
+    def quad_shapes(self, fields):
+        one = (fields, self.cycles, self.block, self.cells)
+        return [shaped(*one), shaped(2, *one), shaped(2, *one)]
 
     def mix(self, center, first, lo, hi, index, token):
         count = max(1, self.slots // 2 - 1)
@@ -312,13 +313,11 @@
             [SMEM, SMEM, self.side(lo, index), self.side(0, 0)],
             [self.side(0, 0)] * count,
             [shaped(hi - lo, self.block, self.near, self.cells)] * count,
-            cost=(3 * self.size(hi - lo), 12 * self.size(hi - lo)),
         )
 
     def spread(self, local, others, lo, hi, token):
         def kernel(ints, reals, local, *refs):
-            others, outs = refs[: len(refs) - QUAD - 2], refs[-QUAD - 2 : -2]
-            flat, stage = refs[-2:]
+            others, (mine, core, chip), (flat, stage) = refs[:-5], refs[-5:-2], refs[-2:]
             scalars = self.scalars(ints, reals)
             flat[...] = sums(scalars, local, others).reshape(flat.shape)
             for o in range(QUAD):
@@ -326,8 +325,10 @@
                     for a in range(2):
                         r = o * self.owned + j + a * self.pairs
                         stage[o, 2 * j + a] = flat[pl.ds(r, self.block, stride=self.near), :]
-            for k in range(QUAD):
-                outs[k][0] = stage[scalars.rank ^ k]
+            mine[0] = stage[scalars.rank]
+            core[0, 0] = stage[scalars.rank ^ 1]
+            core[1, 0] = stage[scalars.rank ^ 3]
+            chip[0, 0] = stage[scalars.rank ^ 2]
 
         return call(
             kernel,
@@ -336,13 +337,28 @@
             (hi - lo,),
             [self.ints, self.reals, local] + others,
             [SMEM, SMEM, self.side(lo, 0)] + [self.side(0, 0)] * len(others),
-            [self.part()] * QUAD,
-            [shaped(hi - lo, self.cycles, self.block, self.cells)] * QUAD,
+            [self.part(), self.parts(2), self.parts(1)],
+            self.quad_shapes(hi - lo),
             [
                 pltpu.VMEM((self.block * self.near, self.cells), jnp.float32),
                 pltpu.VMEM((QUAD, self.cycles, self.block, self.cells), jnp.float32),
             ],
-            (4 * self.size(hi - lo), 16 * self.size(hi - lo)),
+        )
+
+    def join(self, held, new, token):
+        def kernel(held, new, out):
+            out[...] = new[...]
+
+        return call(
+            kernel,
+            "join",
+            token,
+            (held.shape[1],),
+            [held, new],
+            [ANY, self.parts(1, 1)],
+            self.parts(1, 1),
+            shaped(*held.shape),
+            alias={0: 0},
         )
 
     def own_rows(self, shape):
@@ -364,26 +380,21 @@
             ),
             out_shape=out_shape,
             compiler_params=PARAMS,
-            cost_estimate=pl.CostEstimate(
-                flops=12 * self.size(fields) * self.depth,
-                bytes_accessed=16 * self.size(fields),
-                transcendentals=0,
-            ),
+            cost_estimate=COST,
             name=name,
         )(self.ints, *inputs, *extra)
 
     def block4(self, *shape):
         return pl.BlockSpec((1,) + shape, lambda i, ints: (i, 0, 0, 0))
 
-    def coefficients(self, parts, token):
-        fields = parts[0].shape[0]
-
-        def kernel(ints, reals, table, *refs):
-            parts, out, column = refs[:QUAD], refs[QUAD], refs[QUAD + 1]
+    def coefficients(self, mine, core, chip, token):
+        fields = mine.shape[0]
+
+        def kernel(ints, reals, table, mine, core, chip, out, column):
             scalars = self.scalars(ints, reals)
             row = lax.broadcasted_iota(jnp.int32, (self.depth, self.cells), 0)
-            for k in range(QUAD):
-                column[:, scalars.rank ^ k] = parts[k][0]
+            for k, part in enumerate((mine[0], core[0, 0], chip[0, 0], chip[1, 0])):
+                column[:, scalars.rank ^ k] = part
             for j in range(self.owned):
                 modes = [
                     jnp.dot(
@@ -401,22 +412,23 @@
             kernel,
             "coefficients",
             fields,
-            [self.reals, self.table] + parts,
-            [SMEM, self.own_rows(self.table.shape[2:])]
-            + [self.block4(self.cycles, self.block, self.cells)] * QUAD,
+            [self.reals, self.table, mine, core, chip],
+            [SMEM, self.own_rows(self.table.shape[2:]), self.part(), self.parts(1), self.parts(2)],
             self.block4(self.owned, self.depth, self.cells),
             shaped(fields, self.owned, self.depth, self.cells),
             [pltpu.VMEM((self.cycles, QUAD, self.block, self.cells), jnp.float32)],
             token,
         )
 
-    def filtered(self, own, other, parts, token):
-        fields = parts[0].shape[0]
-
-        def kernel(ints, reals, back, own, other, *refs):
-            parts, outs, waves = refs[:QUAD], refs[QUAD : 2 * QUAD], refs[2 * QUAD]
+    def filtered(self, own, other, mine, core, chip, token):
+        fields = mine.shape[0]
+
+        def kernel(ints, reals, back, own, other, mine, core, chip, *refs):
+            (mine_out, core_out, chip_out), waves = refs[:3], refs[3]
             scalars = self.scalars(ints, reals)
             row = lax.broadcasted_iota(jnp.int32, (self.depth, self.cells), 0)
+            source = (mine.at[0], core.at[0, 0], chip.at[0, 0], chip.at[1, 0])
+            result = (mine_out.at[0], core_out.at[0, 0], chip_out.at[0, 0], chip_out.at[1, 0])
             for j in range(self.owned):
                 pair = scalars.rank * self.owned + j
                 total = own[0, j] + other[0, j]
@@ -430,49 +442,49 @@
                     ).reshape(QUAD, self.block, self.cells)
                     r = pair + a * self.pairs
                     for k in range(QUAD):
-                        outs[k][0, 2 * j + a] = (
-                            scalars.base(r) * parts[k][0, 2 * j + a]
+                        result[k][2 * j + a] = (
+                            scalars.base(r) * source[k][2 * j + a]
                             + scalars.scale(r) * waves[2 * j + a, scalars.rank ^ k]
                         )
 
-        part = self.block4(self.cycles, self.block, self.cells)
         modes = self.block4(self.owned, self.depth, self.cells)
         return self.table_call(
             kernel,
             "filtered",
             fields,
-            [self.reals, self.back, own, other] + parts,
-            [SMEM, self.own_rows(self.back.shape[2:]), modes, modes] + [part] * QUAD,
-            [part] * QUAD,
-            [shaped(*parts[0].shape)] * QUAD,
+            [self.reals, self.back, own, other, mine, core, chip],
+            [SMEM, self.own_rows(self.back.shape[2:]), modes, modes]
+            + [self.part(), self.parts(1), self.parts(2)],
+            [self.part(), self.parts(1), self.parts(2)],
+            self.quad_shapes(fields),
             [pltpu.VMEM((self.cycles, QUAD, self.block, self.cells), jnp.float32)],
             token,
         )
 
-    def place_near(self, parts, held, lo, hi, token):
-        def kernel(ints, reals, *refs):
-            parts, out, stage = refs[:QUAD], refs[-2], refs[-1]
-            scalars = self.scalars(ints, reals)
-            for k in range(QUAD):
-                stage[scalars.rank ^ k] = parts[k][0]
+    def place_near(self, mine, core, chip, held, lo, hi, token):
+        carried = [] if held is None else [held]
+
+        def kernel(ints, reals, mine, core, chip, *refs):
+            out, stage = refs[-2:]
+            rank = self.scalars(ints, reals).rank
+            for k, part in enumerate((mine[0], core[0, 0], chip[0, 0], core[1, 0])):
+                stage[rank ^ k] = part
             for o in range(QUAD):
                 for j in range(self.owned):
                     for a in range(2):
                         out[0, :, o * self.owned + j + a * self.pairs, :] = stage[o, 2 * j + a]
 
-        carried = [] if held is None else [held]
         return call(
             kernel,
             "place_near",
             token,
             (hi - lo,),
-            [self.ints, self.reals] + parts + carried,
-            [SMEM, SMEM] + [self.part()] * QUAD + [ANY] * len(carried),
+            [self.ints, self.reals, mine, core, chip] + carried,
+            [SMEM, SMEM, self.part(), self.parts(2), self.parts(1)] + [ANY] * len(carried),
             self.side(lo, 0),
             shaped(*self.shape),
             [pltpu.VMEM((QUAD, self.cycles, self.block, self.cells), jnp.float32)],
-            (0, 8 * self.size(hi - lo)),
-            {2 + QUAD: 0} if carried else None,
+            alias={5: 0} if carried else None,
         )
 
     def place_far(self, local, others, held, lo, hi, token):
@@ -492,9 +504,7 @@
             + [ANY] * len(carried),
             self.side(lo, 1),
             shaped(*self.shape),
-            (),
-            (4 * self.size(hi - lo), 16 * self.size(hi - lo)),
-            {3 + len(others): 0} if carried else None,
+            alias={3 + len(others): 0} if carried else None,
         )
 
 
@@ -553,7 +563,7 @@
     for step, g in ORDER:
         lo, hi, index = groups[g]
         if step == "pack":
-            packed = pack(center, viscosity, lo, hi, index * near, near, halos is None, token)
+            packed = pack(center, viscosity, lo, hi, index, near, halos is None, token)
             token = packed[0]
             first[g] = to_first(packed[0])
             if halos is None:
@@ -567,11 +577,15 @@
             token = mixed[0]
             others[g] = [first[g]] + [to_later(x, s + 1) for s, x in enumerate(mixed)]
         elif step == "spread":
-            mine = plan.spread(local, others[g], lo, hi, token)
-            token = mine[0]
-            parts[g] = [mine[0]] + [to_sector(mine[k], k) for k in range(1, QUAD)]
+            mine, core, chip = plan.spread(local, others[g], lo, hi, token)
+            token = mine
+            parts[g] = mine, to_sector(core, 1), chip
+        elif step == "join":
+            mine, core, chip = parts[g]
+            token = plan.join(chip, core, token)
+            parts[g] = mine, core, to_sector(token, 2)
         elif step == "coef":
-            part = token = plan.coefficients(parts[g], token)
+            part = token = plan.coefficients(*parts[g], token)
             stride = QUAD
             while 2 * stride < sectors:
                 part = part + to_sector(part, stride)
@@ -579,11 +593,15 @@
             other = to_sector(part, stride) if stride < sectors else jnp.zeros_like(part)
             own[g] = part, other
         elif step == "filter":
-            mine = plan.filtered(*own[g], parts[g], token)
-            token = mine[0]
-            done[g] = [mine[0]] + [to_sector(mine[k], k) for k in range(1, QUAD)]
+            mine, core, chip = plan.filtered(*own[g], *parts[g], token)
+            token = mine
+            done[g] = mine, core, to_sector(chip, 2)
+        elif step == "back":
+            mine, core, chip = done[g]
+            token = plan.join(core, chip, token)
+            done[g] = mine, to_sector(token, 1), chip
         elif step == "near":
-            held = token = plan.place_near(done[g], held, lo, hi, None if token is held else token)
+            held = token = plan.place_near(*done[g], held, lo, hi, None if token is held else token)
         else:
             held = token = plan.place_far(
                 local, others[g], held, lo, hi, None if token is held else token

time: 280 us -> 190 us (0.68)
  Pallas kernels: 121 us -> 61.7 us
  waiting for transfers between devices: 121 us -> 96.2 us
  starting transfers between devices: 34.6 us -> 27.4 us
    pallas_call x19 -> x25, Pallas kernels: 108 us -> 48 us  [call(): pl.pallas_call(lambda *refs: kernel(*refs[:len(inputs)], *refs[len(inputs...]
    ppermute x10, waiting for transfers between devices: 41.8 us -> 28.1 us  [to_partner(): return lax.ppermute(x, ('inst', 'space'), pairs)]
    ppermute x21 -> x15, waiting for transfers between devices: 75.8 us -> 64.5 us  [to_sector(): return lax.ppermute(x, 'space', [(i, i ^ k) for i in range(sectors)])]
    ppermute x21 -> x15, starting transfers between devices: 17 us -> 10.1 us  [to_sector(): return lax.ppermute(x, 'space', [(i, i ^ k) for i in range(sectors)])]
  transfers between devices with their start and end apart: 33 -> 27, of which waited for: 15 -> 14; matrix products, arithmetic and copies ran while one was open for 0% -> 0% of each run, Pallas kernels for 30% -> 30%
where the time goes in v3:
time: 190 us
  waiting for transfers between devices  96.2 us (51%)
  Pallas kernels  61.7 us (32%)
  starting transfers between devices  27.4 us (14%)
  local copies, waits for them, and re-layouts  3.89 us (2%)
    ppermute x15, waiting for transfers between devices, to_sector(): return lax.ppermute(x, 'space', [(i, i ^ k) for i in range(sectors)])  64.5 us
    pallas_call x25, Pallas kernels, call(): pl.pallas_call(lambda *refs: kernel(*refs[:len(inputs)], *refs[len(inputs...  48 us
    ppermute x10, waiting for transfers between devices, to_partner(): return lax.ppermute(x, ('inst', 'space'), pairs)  28.1 us
    ppermute x10, starting transfers between devices, to_partner(): return lax.ppermute(x, ('inst', 'space'), pairs)  13.8 us
    pallas_call x6, Pallas kernels, table_call(): pl.pallas_call(lambda *refs: kernel(*refs[:count + 1], *refs[count + 1 +...  13.7 us
    ppermute x15, starting transfers between devices, to_sector(): return lax.ppermute(x, 'space', [(i, i ^ k) for i in range(sectors)])  10.1 us
    unnamed x39, local copies, waits for them, and re-layouts  3.89 us
  transfers between devices with their start and end apart: 27, of which 14 were waited for; matrix products, arithmetic and copies ran while one was open for 0% of the time, Pallas kernels for 30%

profile of v3, /device:TPU:0, one launch (start us, length us, event | category | flops | bytes accessed | tf_op | source)
XLA Modules:
  0.0 189.6 jit_solution(7951723590245147786)
XLA Ops:
  3.6 3.0 %collective-permute-start.2 = (f32[2,32,32,128]{3,2,1,0:T(8,128)}, f32[2,32,32,128]{3,2,1,0:T(8,128)S(1)}, u32[]{:S(2)}, u32[]{:S(2)}) collective-permute-start(f32[2,32,32,128]{3,2,1,0:T(8,128)} %get-tuple-element.28.refs_1_), channel_id=1, source_target_pairs={{0,16},{1,9},{2,18},{3,11},{4,20},{5,13},{6,22},{7,15},{8,24},{9,1... | collective-permute-start | bytes 3145736 | tf_op jit(solution)/shard_map/ppermute | solution.py:530
  8.8 3.5 %collective-permute-start.1 = (f32[6,1,64,128]{3,2,1,0:T(8,128)}, f32[6,1,64,128]{3,2,1,0:T(8,128)}, u32[]{:S(2)}, u32[]{:S(2)}) collective-permute-start(f32[6,1,64,128]{3,2,1,0:T(8,128)} %get-tuple-element.27), channel_id=1, source_target_pairs={{0,7},{1,0},{2,1},{3,2},{4,3},{5,4},{6,5},{7,6},{8,15},{9,8},{10,9... | collective-permute-start | bytes 589832 | tf_op jit(solution)/shard_map/ppermute | solution.py:542
  12.5 3.5 %collective-permute-done.refs_10_ = f32[6,1,64,128]{3,2,1,0:T(8,128)S(1)} collective-permute-done((f32[6,1,64,128]{3,2,1,0:T(8,128)}, f32[6,1,64,128]{3,2,1,0:T(8,128)S(1)}, u32[]{:S(2)}, u32[]{:S(2)}) %collective-permute-start) | collective-permute-done | bytes 196640 | tf_op jit(solution)/shard_map/ppermute | solution.py:542
  16.0 12.3 %local_part.1.refs_4_.refs_2_ = f32[5,32,64,128]{3,2,1,0:T(8,128)} custom-call(f32[5,5]{1,0:T(8,128)S(1)} %copy-done.12, f32[5]{0:T(128)S(1)} %copy-done.13, s32[5,3]{1,0:T(8,128)S(1)} %copy.22.refs_2_, f32[5,32,64,128]{3,2,1,0:T(8,128)} %bitcast.9, f32[5,32,64,128]{3,2,1,0:T(8,128)} %bitcast.10, f32[5,32,64,128]{3,2,1,0:T(8,128)} %bitcast.11, ...), custom_call_target="tpu_custom_call" | custom-call | tf_op jit(solution)/shard_map/local_part/pallas_call | solution.py:132
  34.3 10.2 %collective-permute-done.3.refs_4_ = f32[2,32,32,128]{3,2,1,0:T(8,128)S(1)} collective-permute-done((f32[2,32,32,128]{3,2,1,0:T(8,128)S(1)}, f32[2,32,32,128]{3,2,1,0:T(8,128)S(1)}, u32[]{:S(2)}, u32[]{:S(2)}) %collective-permute-start.3) | collective-permute-done | bytes 1048608 | tf_op jit(solution)/shard_map/ppermute | solution.py:530
  50.4 5.4 %collective-permute-done.6.refs_4_ = f32[2,32,32,128]{3,2,1,0:T(8,128)S(1)} collective-permute-done((f32[2,32,32,128]{3,2,1,0:T(8,128)S(1)}, f32[2,32,32,128]{3,2,1,0:T(8,128)S(1)}, u32[]{:S(2)}, u32[]{:S(2)}) %collective-permute-start.6) | collective-permute-done | bytes 1048608 | tf_op jit(solution)/shard_map/ppermute | solution.py:530
  55.8 2.7 %spread.4 = (f32[2,8,32,128]{3,2,1,0:T(8,128)S(1)}, f32[2,2,8,32,128]{4,3,2,1,0:T(8,128)S(1)}, f32[2,2,8,32,128]{4,3,2,1,0:T(8,128)}) custom-call(s32[22]{0:T(128)S(1)} %pad_add_fusion.refs_0_, f32[71]{0:T(128)S(1)} %copy-done.11, f32[5,32,64,128]{3,2,1,0:T(8,128)} %local_part.1.refs_4_.refs_2_, f32[2,32,32,128]{3,2,1,0:T(8,128)S(1)} %collective-permute-done.4.refs_3_, ...), custom_call_target="tpu_custom_call" | custom-call | tf_op jit(solution)/shard_map/spread/pallas_call | solution.py:132
  64.3 2.4 %coefficients.3.refs_2_.refs_3_ = f32[2,4,128,128]{3,2,1,0:T(8,128)S(1)} custom-call(s32[22]{0:T(128)S(1)} %pad_add_fusion.refs_0_, f32[71]{0:T(128)S(1)} %copy-done.11, f32[2,16,128,128]{3,2,1,0:T(8,128)S(1)} %copy-done.4, f32[2,8,32,128]{3,2,1,0:T(8,128)S(1)} %get-tuple-element.29.refs_1_.refs_3_.refs_5_, ...), custom_call_target="tpu_custom_call" | custom-call | tf_op jit(solution)/shard_map/coefficients/pallas_call | solution.py:372
  74.5 10.8 %collective-permute-done.10.refs_4_ = f32[1,32,32,128]{3,2,1,0:T(8,128)S(1)} collective-permute-done((f32[1,32,32,128]{3,2,1,0:T(8,128)S(1)}, f32[1,32,32,128]{3,2,1,0:T(8,128)S(1)}, u32[]{:S(2)}, u32[]{:S(2)}) %collective-permute-start.10) | collective-permute-done | bytes 524320 | tf_op jit(solution)/shard_map/ppermute | solution.py:530
  88.1 8.9 %collective-permute-done.13.refs_4_ = f32[2,4,128,128]{3,2,1,0:T(8,128)S(1)} collective-permute-done((f32[2,4,128,128]{3,2,1,0:T(8,128)S(1)}, f32[2,4,128,128]{3,2,1,0:T(8,128)S(1)}, u32[]{:S(2)}, u32[]{:S(2)}) %collective-permute-start.13) | collective-permute-done | bytes 524320 | tf_op jit(solution)/shard_map/ppermute | solution.py:539
  97.0 3.0 %filtered.3 = (f32[2,8,32,128]{3,2,1,0:T(8,128)S(1)}, f32[2,2,8,32,128]{4,3,2,1,0:T(8,128)S(1)}, f32[2,2,8,32,128]{4,3,2,1,0:T(8,128)S(1)}) custom-call(s32[22]{0:T(128)S(1)} %pad_add_fusion.refs_0_, f32[71]{0:T(128)S(1)} %copy-done.11, f32[2,16,128,128]{3,2,1,0:T(8,128)} %constant.19.clone.refs_2_, f32[2,4,128,128]{3,2,1,0:T(8,128)S(1)} %coefficients.3.refs_2_.refs_3_, ...), custom_call_target="tpu_custom_call" | custom-call | tf_op jit(solution)/shard_map/filtered/pallas_call | solution.py:372
  100.2 2.4 %coefficients.4.refs_2_.refs_3_ = f32[2,4,128,128]{3,2,1,0:T(8,128)S(1)} custom-call(s32[22]{0:T(128)S(1)} %pad_add_fusion.refs_0_, f32[71]{0:T(128)S(1)} %copy-done.11, f32[2,16,128,128]{3,2,1,0:T(8,128)S(1)} %copy-done.4, f32[2,8,32,128]{3,2,1,0:T(8,128)S(1)} %get-tuple-element.34.refs_1_.refs_3_.refs_5_, ...), custom_call_target="tpu_custom_call" | custom-call | tf_op jit(solution)/shard_map/coefficients/pallas_call | solution.py:372
  102.6 2.4 %mix.8.refs_2_ = f32[3,32,32,128]{3,2,1,0:T(8,128)S(1)} custom-call(s32[22]{0:T(128)S(1)} %pad_add_fusion.refs_0_, f32[71]{0:T(128)S(1)} %copy-done.11, f32[5,32,64,128]{3,2,1,0:T(8,128)} %bitcast.17, f32[3,32,32,128]{3,2,1,0:T(8,128)S(1)} %collective-permute-done.16.refs_3_, f32[2,1,8,32,128]{4,3,2,1,0:T(8,128)S(1)} %join.8.refs_4_), custom_call_target="tpu_custom_call" | custom-call | tf_op jit(solution)/shard_map/mix/pallas_call | solution.py:132
  105.1 8.5 %collective-permute-done.15.refs_1_.refs_4_ = f32[2,2,8,32,128]{4,3,2,1,0:T(8,128)S(1)} collective-permute-done((f32[2,2,8,32,128]{4,3,2,1,0:T(8,128)S(1)}, f32[2,2,8,32,128]{4,3,2,1,0:T(8,128)S(1)}, u32[]{:S(2)}, u32[]{:S(2)}) %collective-permute-start.15) | collective-permute-done | bytes 524320 | tf_op jit(solution)/shard_map/ppermute | solution.py:539
  118.5 13.7 %collective-permute-done.19.refs_5_.refs_7_ = f32[2,1,8,32,128]{4,3,2,1,0:T(8,128)S(1)} collective-permute-done((f32[2,1,8,32,128]{4,3,2,1,0:T(8,128)S(1)}, f32[2,1,8,32,128]{4,3,2,1,0:T(8,128)S(1)}, u32[]{:S(2)}, u32[]{:S(2)}) %collective-permute-start.19) | collective-permute-done | bytes 262176 | tf_op jit(solution)/shard_map/ppermute | solution.py:539
  133.9 2.5 %place_near.3.refs_8_.refs_5_ = f32[5,32,64,128]{3,2,1,0:T(8,128)} custom-call(s32[22]{0:T(128)S(1)} %pad_add_fusion.refs_0_, f32[71]{0:T(128)S(1)} %copy-done.11, f32[2,8,32,128]{3,2,1,0:T(8,128)S(1)} %get-tuple-element.36.refs_6_.refs_2_, f32[2,2,8,32,128]{4,3,2,1,0:T(8,128)S(1)} %collective-permute-done.18.refs_3_, ...), custom_call_target="tpu_custom_call" | custom-call | tf_op jit(solution)/shard_map/place_near/pallas_call | solution.py:132
  136.4 3.5 %collective-permute-done.14.refs_4_ = f32[2,4,128,128]{3,2,1,0:T(8,128)S(1)} collective-permute-done((f32[2,4,128,128]{3,2,1,0:T(8,128)S(1)}, f32[2,4,128,128]{3,2,1,0:T(8,128)S(1)}, u32[]{:S(2)}, u32[]{:S(2)}) %collective-permute-start.14) | collective-permute-done | bytes 524320 | tf_op jit(solution)/shard_map/ppermute | solution.py:539
  139.9 2.5 %filtered.4 = (f32[2,8,32,128]{3,2,1,0:T(8,128)S(1)}, f32[2,2,8,32,128]{4,3,2,1,0:T(8,128)S(1)}, f32[2,2,8,32,128]{4,3,2,1,0:T(8,128)S(1)}) custom-call(s32[22]{0:T(128)S(1)} %pad_add_fusion.refs_0_, f32[71]{0:T(128)S(1)} %copy-done.11, f32[2,16,128,128]{3,2,1,0:T(8,128)S(1)} %copy-done.3, f32[2,4,128,128]{3,2,1,0:T(8,128)S(1)} %coefficients.4.refs_2_.refs_3_, ...), custom_call_target="tpu_custom_call" | custom-call | tf_op jit(solution)/shard_map/filtered/pallas_call | solution.py:372
  143.9 12.5 %collective-permute-done.22.refs_1_.refs_4_ = f32[2,2,8,32,128]{4,3,2,1,0:T(8,128)S(1)} collective-permute-done((f32[2,2,8,32,128]{4,3,2,1,0:T(8,128)S(1)}, f32[2,2,8,32,128]{4,3,2,1,0:T(8,128)S(1)}, u32[]{:S(2)}, u32[]{:S(2)}) %collective-permute-start.22) | collective-permute-done | bytes 524320 | tf_op jit(solution)/shard_map/ppermute | solution.py:539
  159.1 2.5 %place_near.4.refs_8_.refs_5_ = f32[5,32,64,128]{3,2,1,0:T(8,128)} custom-call(s32[22]{0:T(128)S(1)} %pad_add_fusion.refs_0_, f32[71]{0:T(128)S(1)} %copy-done.11, f32[2,8,32,128]{3,2,1,0:T(8,128)S(1)} %get-tuple-element.41.refs_4_.refs_2_, f32[2,2,8,32,128]{4,3,2,1,0:T(8,128)S(1)} %collective-permute-done.23.refs_3_, ...), custom_call_target="tpu_custom_call", output_to_operand_aliasing={{}: (5, {})} | custom-call | tf_op jit(solution)/shard_map/place_near/pallas_call | solution.py:132
  161.5 10.0 %collective-permute-done.21.refs_4_ = f32[1,4,128,128]{3,2,1,0:T(8,128)S(1)} collective-permute-done((f32[1,4,128,128]{3,2,1,0:T(8,128)S(1)}, f32[1,4,128,128]{3,2,1,0:T(8,128)S(1)}, u32[]{:S(2)}, u32[]{:S(2)}) %collective-permute-start.21) | collective-permute-done | bytes 262176 | tf_op jit(solution)/shard_map/ppermute | solution.py:539
  173.3 3.9 %place_far.2.refs_2_.refs_5_ = f32[5,32,64,128]{3,2,1,0:T(8,128)} custom-call(s32[22]{0:T(128)S(1)} %pad_add_fusion.refs_0_, f32[71]{0:T(128)S(1)} %copy-done.11, f32[5,32,64,128]{3,2,1,0:T(8,128)} %local_part.1.refs_4_.refs_2_, f32[3,32,32,128]{3,2,1,0:T(8,128)S(1)} %collective-permute-done.16.refs_3_, ...), custom_call_target="tpu_custom_call", output_to_operand_aliasing={{}: (5, {})} | custom-call | tf_op jit(solution)/shard_map/place_far/pallas_call | solution.py:132
  177.2 4.3 %collective-permute-done.24.refs_1_.refs_4_ = f32[2,1,8,32,128]{4,3,2,1,0:T(8,128)S(1)} collective-permute-done((f32[2,1,8,32,128]{4,3,2,1,0:T(8,128)S(1)}, f32[2,1,8,32,128]{4,3,2,1,0:T(8,128)S(1)}, u32[]{:S(2)}, u32[]{:S(2)}) %collective-permute-start.24) | collective-permute-done | bytes 262176 | tf_op jit(solution)/shard_map/ppermute | solution.py:539
  181.5 2.5 %copy-done = f32[5,32,64,128]{3,2,1,0:T(8,128)S(1)} copy-done((f32[5,32,64,128]{3,2,1,0:T(8,128)S(1)}, f32[5,32,64,128]{3,2,1,0:T(8,128)}, u32[]{:S(2)}) %copy-start) | copy-done | bytes 5242904
  (102 shorter events, 52.1 us)
Async XLA Ops:
  3.6 24.8 %collective-permute-start.2 = (f32[2,32,32,128]{3,2,1,0:T(8,128)}, f32[2,32,32,128]{3,2,1,0:T(8,128)S(1)}, u32[]{:S(2)}, u32[]{:S(2)}) collective-permute-start(f32[2,32,32,128]{3,2,1,0:T(8,128)} %get-tuple-element.28.refs_1_), channel_id=1, source_target_pairs={{0,16},{1,9},{2,18},{3,11},{4,20},{5,13},{6,22},{7,15},{8,24},{9,1... | collective-permute-start | bytes 3145736 | tf_op jit(solution)/shard_map/ppermute | solution.py:530
  8.7 23.1 %collective-permute-start.4 = (f32[2,32,32,128]{3,2,1,0:T(8,128)}, f32[2,32,32,128]{3,2,1,0:T(8,128)S(1)}, u32[]{:S(2)}, u32[]{:S(2)}) collective-permute-start(f32[2,32,32,128]{3,2,1,0:T(8,128)} %pack.6.refs_12_), channel_id=1, source_target_pairs={{0,16},{1,9},{2,18},{3,11},{4,20},{5,13},{6,22},{7,15},{8,24},{9,1... | collective-permute-start | bytes 3145736 | tf_op jit(solution)/shard_map/ppermute | solution.py:530
  8.8 7.2 %collective-permute-start = (f32[6,1,64,128]{3,2,1,0:T(8,128)}, f32[6,1,64,128]{3,2,1,0:T(8,128)S(1)}, u32[]{:S(2)}, u32[]{:S(2)}) collective-permute-start(f32[6,1,64,128]{3,2,1,0:T(8,128)} %get-tuple-element.26), channel_id=1, source_target_pairs={{0,1},{1,2},{2,3},{3,4},{4,5},{5,6},{6,7},{7,0},{8,9},{9,10},{10,1... | collective-permute-start | bytes 589832 | tf_op jit(solution)/shard_map/ppermute | solution.py:542
  8.8 7.2 %collective-permute-start.1 = (f32[6,1,64,128]{3,2,1,0:T(8,128)}, f32[6,1,64,128]{3,2,1,0:T(8,128)}, u32[]{:S(2)}, u32[]{:S(2)}) collective-permute-start(f32[6,1,64,128]{3,2,1,0:T(8,128)} %get-tuple-element.27), channel_id=1, source_target_pairs={{0,7},{1,0},{2,1},{3,2},{4,3},{5,4},{6,5},{7,6},{8,15},{9,8},{10,9... | collective-permute-start | bytes 589832 | tf_op jit(solution)/shard_map/ppermute | solution.py:542
  29.7 14.9 %collective-permute-start.3 = (f32[2,32,32,128]{3,2,1,0:T(8,128)S(1)}, f32[2,32,32,128]{3,2,1,0:T(8,128)S(1)}, u32[]{:S(2)}, u32[]{:S(2)}) collective-permute-start(f32[2,32,32,128]{3,2,1,0:T(8,128)S(1)} %mix.5.refs_4_), channel_id=1, source_target_pairs={{0,8},{1,17},{2,10},{3,19},{4,12},{5,21},{6,14},{7,23},{8,0},{9,25... | collective-permute-start | bytes 3145736 | tf_op jit(solution)/shard_map/ppermute | solution.py:530
  33.2 22.6 %collective-permute-start.6 = (f32[2,32,32,128]{3,2,1,0:T(8,128)S(1)}, f32[2,32,32,128]{3,2,1,0:T(8,128)S(1)}, u32[]{:S(2)}, u32[]{:S(2)}) collective-permute-start(f32[2,32,32,128]{3,2,1,0:T(8,128)S(1)} %mix.6.refs_5_), channel_id=1, source_target_pairs={{0,8},{1,17},{2,10},{3,19},{4,12},{5,21},{6,14},{7,23},{8,0},{9,25... | collective-permute-start | bytes 3145736 | tf_op jit(solution)/shard_map/ppermute | solution.py:530
  46.7 3.0 %collective-permute-start.7 = (f32[2,2,8,32,128]{4,3,2,1,0:T(8,128)S(1)}, f32[2,2,8,32,128]{4,3,2,1,0:T(8,128)S(1)}, u32[]{:S(2)}, u32[]{:S(2)}) collective-permute-start(f32[2,2,8,32,128]{4,3,2,1,0:T(8,128)S(1)} %get-tuple-element.31), channel_id=1, source_target_pairs={{0,1},{1,0},{2,3},{3,2},{4,5},{5,4},{6,7},{7,6},{8,9},{9,8},{10,11... | collective-permute-start | bytes 1572872 | tf_op jit(solution)/shard_map/ppermute | solution.py:539
  49.8 14.5 %collective-permute-start.9 = (f32[2,2,8,32,128]{4,3,2,1,0:T(8,128)S(1)}, f32[2,2,8,32,128]{4,3,2,1,0:T(8,128)S(1)}, u32[]{:S(2)}, u32[]{:S(2)}) collective-permute-start(f32[2,2,8,32,128]{4,3,2,1,0:T(8,128)S(1)} %join.6.refs_5_), channel_id=1, source_target_pairs={{0,2},{1,3},{2,0},{3,1},{4,6},{5,7},{6,4},{7,5},{8,10},{9,11},{10,... | collective-permute-start | bytes 1572872 | tf_op jit(solution)/shard_map/ppermute | solution.py:539
  58.6 8.2 %collective-permute-start.8 = (f32[2,2,8,32,128]{4,3,2,1,0:T(8,128)S(1)}, f32[2,2,8,32,128]{4,3,2,1,0:T(8,128)S(1)}, u32[]{:S(2)}, u32[]{:S(2)}) collective-permute-start(f32[2,2,8,32,128]{4,3,2,1,0:T(8,128)S(1)} %get-tuple-element.33), channel_id=1, source_target_pairs={{0,1},{1,0},{2,3},{3,2},{4,5},{5,4},{6,7},{7,6},{8,9},{9,8},{10,11... | collective-permute-start | bytes 1572872 | tf_op jit(solution)/shard_map/ppermute | solution.py:539
  60.0 9.2 %collective-permute-start.5 = (f32[1,32,32,128]{3,2,1,0:T(8,128)S(1)}, f32[1,32,32,128]{3,2,1,0:T(8,128)S(1)}, u32[]{:S(2)}, u32[]{:S(2)}) collective-permute-start(f32[1,32,32,128]{3,2,1,0:T(8,128)S(1)} %pack.7.refs_2_), channel_id=1, source_target_pairs={{0,16},{1,9},{2,18},{3,11},{4,20},{5,13},{6,22},{7,15},{8,24},{9,1... | collective-permute-start | bytes 1572872 | tf_op jit(solution)/shard_map/ppermute | solution.py:530
  63.9 38.7 %collective-permute-start.16 = (f32[3,32,32,128]{3,2,1,0:T(8,128)S(1)}, f32[3,32,32,128]{3,2,1,0:T(8,128)S(1)}, u32[]{:S(2)}, u32[]{:S(2)}) collective-permute-start(f32[3,32,32,128]{3,2,1,0:T(8,128)S(1)} %pack.8.refs_6_), channel_id=1, source_target_pairs={{0,16},{1,9},{2,18},{3,11},{4,20},{5,13},{6,22},{7,15},{8,24},{9,1... | collective-permute-start | bytes 4718600 | tf_op jit(solution)/shard_map/ppermute | solution.py:530
  70.3 14.9 %collective-permute-start.10 = (f32[1,32,32,128]{3,2,1,0:T(8,128)S(1)}, f32[1,32,32,128]{3,2,1,0:T(8,128)S(1)}, u32[]{:S(2)}, u32[]{:S(2)}) collective-permute-start(f32[1,32,32,128]{3,2,1,0:T(8,128)S(1)} %mix.7.refs_5_), channel_id=1, source_target_pairs={{0,8},{1,17},{2,10},{3,19},{4,12},{5,21},{6,14},{7,23},{8,0},{9,25... | collective-permute-start | bytes 1572872 | tf_op jit(solution)/shard_map/ppermute | solution.py:530
  72.1 24.9 %collective-permute-start.13 = (f32[2,4,128,128]{3,2,1,0:T(8,128)S(1)}, f32[2,4,128,128]{3,2,1,0:T(8,128)S(1)}, u32[]{:S(2)}, u32[]{:S(2)}) collective-permute-start(f32[2,4,128,128]{3,2,1,0:T(8,128)S(1)} %coefficients.3.refs_2_.refs_3_), channel_id=1, source_target_pairs={{0,4},{1,5},{2,6},{3,7},{4,0},{5,1},{6,2},{7,3},{8,12},{9,13},{10,... | collective-permute-start | bytes 1572872 | tf_op jit(solution)/shard_map/ppermute | solution.py:539
  72.7 27.5 %collective-permute-start.12 = (f32[2,2,8,32,128]{4,3,2,1,0:T(8,128)}, f32[2,2,8,32,128]{4,3,2,1,0:T(8,128)S(1)}, u32[]{:S(2)}, u32[]{:S(2)}) collective-permute-start(f32[2,2,8,32,128]{4,3,2,1,0:T(8,128)} %join.7.refs_4_), channel_id=1, source_target_pairs={{0,2},{1,3},{2,0},{3,1},{4,6},{5,7},{6,4},{7,5},{8,10},{9,11},{10,... | collective-permute-start | bytes 1572872 | tf_op jit(solution)/shard_map/ppermute | solution.py:539
  100.0 13.6 %collective-permute-start.15 = (f32[2,2,8,32,128]{4,3,2,1,0:T(8,128)S(1)}, f32[2,2,8,32,128]{4,3,2,1,0:T(8,128)S(1)}, u32[]{:S(2)}, u32[]{:S(2)}) collective-permute-start(f32[2,2,8,32,128]{4,3,2,1,0:T(8,128)S(1)} %get-tuple-element.38), channel_id=1, source_target_pairs={{0,2},{1,3},{2,0},{3,1},{4,6},{5,7},{6,4},{7,5},{8,10},{9,11},{10,... | collective-permute-start | bytes 1572872 | tf_op jit(solution)/shard_map/ppermute | solution.py:539
  113.6 20.3 %collective-permute-start.18 = (f32[2,2,8,32,128]{4,3,2,1,0:T(8,128)S(1)}, f32[2,2,8,32,128]{4,3,2,1,0:T(8,128)S(1)}, u32[]{:S(2)}, u32[]{:S(2)}) collective-permute-start(f32[2,2,8,32,128]{4,3,2,1,0:T(8,128)S(1)} %join.9.refs_6_), channel_id=1, source_target_pairs={{0,1},{1,0},{2,3},{3,2},{4,5},{5,4},{6,7},{7,6},{8,9},{9,8},{10,11... | collective-permute-start | bytes 1572872 | tf_op jit(solution)/shard_map/ppermute | solution.py:539
  113.7 26.2 %collective-permute-start.14 = (f32[2,4,128,128]{3,2,1,0:T(8,128)S(1)}, f32[2,4,128,128]{3,2,1,0:T(8,128)S(1)}, u32[]{:S(2)}, u32[]{:S(2)}) collective-permute-start(f32[2,4,128,128]{3,2,1,0:T(8,128)S(1)} %coefficients.4.refs_2_.refs_3_), channel_id=1, source_target_pairs={{0,4},{1,5},{2,6},{3,7},{4,0},{5,1},{6,2},{7,3},{8,12},{9,13},{10,... | collective-permute-start | bytes 1572872 | tf_op jit(solution)/shard_map/ppermute | solution.py:539
  114.7 27.8 %collective-permute-start.11 = (f32[2,32,32,128]{3,2,1,0:T(8,128)S(1)}, f32[2,32,32,128]{3,2,1,0:T(8,128)S(1)}, u32[]{:S(2)}, u32[]{:S(2)}) collective-permute-start(f32[2,32,32,128]{3,2,1,0:T(8,128)S(1)} %pack.9.refs_8_), channel_id=1, source_target_pairs={{0,16},{1,9},{2,18},{3,11},{4,20},{5,13},{6,22},{7,15},{8,24},{9,1... | collective-permute-start | bytes 3145736 | tf_op jit(solution)/shard_map/ppermute | solution.py:530
  115.1 17.1 %collective-permute-start.19 = (f32[2,1,8,32,128]{4,3,2,1,0:T(8,128)S(1)}, f32[2,1,8,32,128]{4,3,2,1,0:T(8,128)S(1)}, u32[]{:S(2)}, u32[]{:S(2)}) collective-permute-start(f32[2,1,8,32,128]{4,3,2,1,0:T(8,128)S(1)} %join.8.refs_4_), channel_id=1, source_target_pairs={{0,2},{1,3},{2,0},{3,1},{4,6},{5,7},{6,4},{7,5},{8,10},{9,11},{10,... | collective-permute-start | bytes 786440 | tf_op jit(solution)/shard_map/ppermute | solution.py:539
  116.8 56.5 %collective-permute-start.25 = (f32[3,32,32,128]{3,2,1,0:T(8,128)S(1)}, f32[3,32,32,128]{3,2,1,0:T(8,128)}, u32[]{:S(2)}, u32[]{:S(2)}) collective-permute-start(f32[3,32,32,128]{3,2,1,0:T(8,128)S(1)} %mix.8.refs_2_), channel_id=1, source_target_pairs={{0,8},{1,17},{2,10},{3,19},{4,12},{5,21},{6,14},{7,23},{8,0},{9,25... | collective-permute-start | bytes 4718600 | tf_op jit(solution)/shard_map/ppermute | solution.py:530
  142.4 14.0 %collective-permute-start.22 = (f32[2,2,8,32,128]{4,3,2,1,0:T(8,128)S(1)}, f32[2,2,8,32,128]{4,3,2,1,0:T(8,128)S(1)}, u32[]{:S(2)}, u32[]{:S(2)}) collective-permute-start(f32[2,2,8,32,128]{4,3,2,1,0:T(8,128)S(1)} %get-tuple-element.43), channel_id=1, source_target_pairs={{0,2},{1,3},{2,0},{3,1},{4,6},{5,7},{6,4},{7,5},{8,10},{9,11},{10,... | collective-permute-start | bytes 1572872 | tf_op jit(solution)/shard_map/ppermute | solution.py:539
  156.5 31.0 %collective-permute-start.20 = (f32[2,32,32,128]{3,2,1,0:T(8,128)S(1)}, f32[2,32,32,128]{3,2,1,0:T(8,128)S(1)}, u32[]{:S(2)}, u32[]{:S(2)}) collective-permute-start(f32[2,32,32,128]{3,2,1,0:T(8,128)S(1)} %mix.9.refs_2_), channel_id=1, source_target_pairs={{0,8},{1,17},{2,10},{3,19},{4,12},{5,21},{6,14},{7,23},{8,0},{9,25... | collective-permute-start | bytes 3145736 | tf_op jit(solution)/shard_map/ppermute | solution.py:530
  158.2 13.3 %collective-permute-start.21 = (f32[1,4,128,128]{3,2,1,0:T(8,128)S(1)}, f32[1,4,128,128]{3,2,1,0:T(8,128)S(1)}, u32[]{:S(2)}, u32[]{:S(2)}) collective-permute-start(f32[1,4,128,128]{3,2,1,0:T(8,128)S(1)} %coefficients.5.refs_5_.refs_3_), channel_id=1, source_target_pairs={{0,4},{1,5},{2,6},{3,7},{4,0},{5,1},{6,2},{7,3},{8,12},{9,13},{10,... | collective-permute-start | bytes 786440 | tf_op jit(solution)/shard_map/ppermute | solution.py:539
  173.2 8.3 %collective-permute-start.24 = (f32[2,1,8,32,128]{4,3,2,1,0:T(8,128)S(1)}, f32[2,1,8,32,128]{4,3,2,1,0:T(8,128)S(1)}, u32[]{:S(2)}, u32[]{:S(2)}) collective-permute-start(f32[2,1,8,32,128]{4,3,2,1,0:T(8,128)S(1)} %get-tuple-element.46), channel_id=1, source_target_pairs={{0,2},{1,3},{2,0},{3,1},{4,6},{5,7},{6,4},{7,5},{8,10},{9,11},{10,... | collective-permute-start | bytes 786440 | tf_op jit(solution)/shard_map/ppermute | solution.py:539
  (22 other events, 263.0 us)

commit v4 on v3

--- a/solution.py
+++ b/solution.py
@@ -8,7 +8,7 @@
 from jax.experimental.pallas import tpu as pltpu
 from jax.sharding import PartitionSpec as P
 
-QUAD = 4
+CORES = 2
 NEAR_SIZES = (2, 2, 1)
 FAR_SIZES = (3, 2)
 ORDER = (
@@ -19,30 +19,24 @@
     ("mix", 1),
     ("spread", 0),
     ("pack", 2),
-    ("join", 0),
+    ("coef", 0),
+    ("pack", 3),
+    ("mix", 2),
     ("spread", 1),
-    ("pack", 3),
-    ("coef", 0),
-    ("join", 1),
-    ("mix", 2),
+    ("coef", 1),
+    ("mix", 3),
     ("spread", 2),
     ("pack", 4),
+    ("coef", 2),
+    ("mix", 4),
     ("filter", 0),
-    ("coef", 1),
-    ("join", 2),
-    ("mix", 3),
-    ("back", 0),
-    ("coef", 2),
     ("near", 0),
     ("filter", 1),
-    ("mix", 4),
-    ("back", 1),
+    ("far", 3),
     ("near", 1),
     ("filter", 2),
-    ("far", 3),
-    ("back", 2),
+    ("far", 4),
     ("near", 2),
-    ("far", 4),
 )
 SMEM = pl.BlockSpec(memory_space=pltpu.SMEM)
 ANY = pl.BlockSpec(memory_space=pl.ANY)
@@ -94,7 +88,7 @@
     def __init__(self, ints, reals, slots, near):
         self.ints, self.reals, self.slots, self.near = ints, reals, slots, near
         self.slot, self.place = ints[0], ints[1]
-        self.rank = self.place % QUAD
+        self.rank = self.place % CORES
 
     def weight(self, i, j):
         return self.reals[self.ints[2 + i] - self.ints[2 + j] + self.slots - 1]
@@ -271,8 +265,8 @@
         self.shape, self.table, self.back = shape, table, back
         self.fields, self.block, self.rows, self.cells = shape
         self.pairs = near // 2
-        self.owned = self.pairs // QUAD
-        self.cycles = near // QUAD
+        self.owned = self.pairs // CORES
+        self.cycles = near // CORES
         self.depth = table.shape[2]
 
     def scalars(self, ints, reals):
@@ -283,14 +277,6 @@
 
     def part(self):
         return pl.BlockSpec((1, self.cycles, self.block, self.cells), lambda i, *_: (i, 0, 0, 0))
-
-    def parts(self, count, first=0):
-        shape = (count, 1, self.cycles, self.block, self.cells)
-        return pl.BlockSpec(shape, lambda i, *_: (first, i, 0, 0, 0))
-
-    def quad_shapes(self, fields):
-        one = (fields, self.cycles, self.block, self.cells)
-        return [shaped(*one), shaped(2, *one), shaped(2, *one)]
 
     def mix(self, center, first, lo, hi, index, token):
         count = max(1, self.slots // 2 - 1)
@@ -317,18 +303,16 @@
 
     def spread(self, local, others, lo, hi, token):
         def kernel(ints, reals, local, *refs):
-            others, (mine, core, chip), (flat, stage) = refs[:-5], refs[-5:-2], refs[-2:]
+            others, (mine, core, flat, stage) = refs[:-4], refs[-4:]
             scalars = self.scalars(ints, reals)
             flat[...] = sums(scalars, local, others).reshape(flat.shape)
-            for o in range(QUAD):
+            for o in range(CORES):
                 for j in range(self.owned):
                     for a in range(2):
                         r = o * self.owned + j + a * self.pairs
                         stage[o, 2 * j + a] = flat[pl.ds(r, self.block, stride=self.near), :]
             mine[0] = stage[scalars.rank]
-            core[0, 0] = stage[scalars.rank ^ 1]
-            core[1, 0] = stage[scalars.rank ^ 3]
-            chip[0, 0] = stage[scalars.rank ^ 2]
+            core[0] = stage[1 - scalars.rank]
 
         return call(
             kernel,
@@ -337,33 +321,17 @@
             (hi - lo,),
             [self.ints, self.reals, local] + others,
             [SMEM, SMEM, self.side(lo, 0)] + [self.side(0, 0)] * len(others),
-            [self.part(), self.parts(2), self.parts(1)],
-            self.quad_shapes(hi - lo),
+            [self.part()] * 2,
+            [shaped(hi - lo, self.cycles, self.block, self.cells)] * 2,
             [
                 pltpu.VMEM((self.block * self.near, self.cells), jnp.float32),
-                pltpu.VMEM((QUAD, self.cycles, self.block, self.cells), jnp.float32),
+                pltpu.VMEM((CORES, self.cycles, self.block, self.cells), jnp.float32),
             ],
-        )
-
-    def join(self, held, new, token):
-        def kernel(held, new, out):
-            out[...] = new[...]
-
-        return call(
-            kernel,
-            "join",
-            token,
-            (held.shape[1],),
-            [held, new],
-            [ANY, self.parts(1, 1)],
-            self.parts(1, 1),
-            shaped(*held.shape),
-            alias={0: 0},
         )
 
     def own_rows(self, shape):
         return pl.BlockSpec(
-            (1, self.owned) + shape, lambda i, ints: (ints[1] // QUAD, ints[1] % QUAD, 0, 0)
+            (1, self.owned) + shape, lambda i, ints: (ints[1] // CORES, ints[1] % CORES, 0, 0)
         )
 
     def table_call(self, kernel, name, fields, inputs, in_specs, out_specs, out_shape, scratch, token):
@@ -387,19 +355,19 @@
     def block4(self, *shape):
         return pl.BlockSpec((1,) + shape, lambda i, ints: (i, 0, 0, 0))
 
-    def coefficients(self, mine, core, chip, token):
+    def coefficients(self, mine, core, token):
         fields = mine.shape[0]
 
-        def kernel(ints, reals, table, mine, core, chip, out, column):
+        def kernel(ints, reals, table, mine, core, out, column):
             scalars = self.scalars(ints, reals)
             row = lax.broadcasted_iota(jnp.int32, (self.depth, self.cells), 0)
-            for k, part in enumerate((mine[0], core[0, 0], chip[0, 0], chip[1, 0])):
-                column[:, scalars.rank ^ k] = part
+            column[:, scalars.rank] = mine[0]
+            column[:, 1 - scalars.rank] = core[0]
             for j in range(self.owned):
                 modes = [
                     jnp.dot(
                         table[0, j],
-                        column[2 * j + a].reshape(QUAD * self.block, self.cells),
+                        column[2 * j + a].reshape(CORES * self.block, self.cells),
                         precision=lax.Precision.HIGHEST,
                         preferred_element_type=jnp.float32,
                     )
@@ -412,64 +380,58 @@
             kernel,
             "coefficients",
             fields,
-            [self.reals, self.table, mine, core, chip],
-            [SMEM, self.own_rows(self.table.shape[2:]), self.part(), self.parts(1), self.parts(2)],
+            [self.reals, self.table, mine, core],
+            [SMEM, self.own_rows(self.table.shape[2:]), self.part(), self.part()],
             self.block4(self.owned, self.depth, self.cells),
             shaped(fields, self.owned, self.depth, self.cells),
-            [pltpu.VMEM((self.cycles, QUAD, self.block, self.cells), jnp.float32)],
+            [pltpu.VMEM((self.cycles, CORES, self.block, self.cells), jnp.float32)],
             token,
         )
 
-    def filtered(self, own, other, mine, core, chip, token):
+    def filtered(self, total, mine, core, token):
         fields = mine.shape[0]
 
-        def kernel(ints, reals, back, own, other, mine, core, chip, *refs):
-            (mine_out, core_out, chip_out), waves = refs[:3], refs[3]
+        def kernel(ints, reals, back, total, mine, core, mine_out, core_out, waves):
             scalars = self.scalars(ints, reals)
             row = lax.broadcasted_iota(jnp.int32, (self.depth, self.cells), 0)
-            source = (mine.at[0], core.at[0, 0], chip.at[0, 0], chip.at[1, 0])
-            result = (mine_out.at[0], core_out.at[0, 0], chip_out.at[0, 0], chip_out.at[1, 0])
             for j in range(self.owned):
                 pair = scalars.rank * self.owned + j
-                total = own[0, j] + other[0, j]
                 keep = row < scalars.split(pair)
                 for a in range(2):
-                    waves[2 * j + a] = jnp.dot(
+                    c = 2 * j + a
+                    waves[c] = jnp.dot(
                         back[0, j],
-                        jnp.where(keep if a == 0 else jnp.logical_not(keep), total, 0.0),
+                        jnp.where(keep if a == 0 else jnp.logical_not(keep), total[0, j], 0.0),
                         precision=lax.Precision.HIGHEST,
                         preferred_element_type=jnp.float32,
-                    ).reshape(QUAD, self.block, self.cells)
-                    r = pair + a * self.pairs
-                    for k in range(QUAD):
-                        result[k][2 * j + a] = (
-                            scalars.base(r) * source[k][2 * j + a]
-                            + scalars.scale(r) * waves[2 * j + a, scalars.rank ^ k]
-                        )
-
-        modes = self.block4(self.owned, self.depth, self.cells)
+                    ).reshape(CORES, self.block, self.cells)
+                    base = scalars.base(pair + a * self.pairs)
+                    scale = scalars.scale(pair + a * self.pairs)
+                    mine_out[0, c] = base * mine[0, c] + scale * waves[c, scalars.rank]
+                    core_out[0, c] = base * core[0, c] + scale * waves[c, 1 - scalars.rank]
+
         return self.table_call(
             kernel,
             "filtered",
             fields,
-            [self.reals, self.back, own, other, mine, core, chip],
-            [SMEM, self.own_rows(self.back.shape[2:]), modes, modes]
-            + [self.part(), self.parts(1), self.parts(2)],
-            [self.part(), self.parts(1), self.parts(2)],
-            self.quad_shapes(fields),
-            [pltpu.VMEM((self.cycles, QUAD, self.block, self.cells), jnp.float32)],
+            [self.reals, self.back, total, mine, core],
+            [SMEM, self.own_rows(self.back.shape[2:])]
+            + [self.block4(self.owned, self.depth, self.cells), self.part(), self.part()],
+            [self.part()] * 2,
+            [shaped(*mine.shape)] * 2,
+            [pltpu.VMEM((self.cycles, CORES, self.block, self.cells), jnp.float32)],
             token,
         )
 
-    def place_near(self, mine, core, chip, held, lo, hi, token):
+    def place_near(self, mine, core, held, lo, hi, token):
         carried = [] if held is None else [held]
 
-        def kernel(ints, reals, mine, core, chip, *refs):
+        def kernel(ints, reals, mine, core, *refs):
             out, stage = refs[-2:]
             rank = self.scalars(ints, reals).rank
-            for k, part in enumerate((mine[0], core[0, 0], chip[0, 0], core[1, 0])):
-                stage[rank ^ k] = part
-            for o in range(QUAD):
+            stage[rank] = mine[0]
+            stage[1 - rank] = core[0]
+            for o in range(CORES):
                 for j in range(self.owned):
                     for a in range(2):
                         out[0, :, o * self.owned + j + a * self.pairs, :] = stage[o, 2 * j + a]
@@ -479,12 +441,12 @@
             "place_near",
             token,
             (hi - lo,),
-            [self.ints, self.reals, mine, core, chip] + carried,
-            [SMEM, SMEM, self.part(), self.parts(2), self.parts(1)] + [ANY] * len(carried),
+            [self.ints, self.reals, mine, core] + carried,
+            [SMEM, SMEM, self.part(), self.part()] + [ANY] * len(carried),
             self.side(lo, 0),
             shaped(*self.shape),
-            [pltpu.VMEM((QUAD, self.cycles, self.block, self.cells), jnp.float32)],
-            alias={5: 0} if carried else None,
+            [pltpu.VMEM((CORES, self.cycles, self.block, self.cells), jnp.float32)],
+            alias={4: 0} if carried else None,
         )
 
     def place_far(self, local, others, held, lo, hi, token):
@@ -520,7 +482,8 @@
     fields, block, cycles, cells = center.shape
     near = cycles // 2
     points = block * sectors
-    quads = sectors // QUAD
+    chips = sectors // CORES
+    lines = [[c * CORES + i for c in range(chips)] for i in range(CORES)]
 
     def to_partner(x, pick):
         pairs = []
@@ -535,14 +498,18 @@
     def to_later(x, s):
         return to_partner(x, lambda i, core: later_partner(i, core, slots, s))
 
-    def to_sector(x, k):
-        return lax.ppermute(x, "space", [(i, i ^ k) for i in range(sectors)])
+    def to_core(x):
+        return lax.ppermute(x, "space", [(i, i ^ 1) for i in range(sectors)])
 
     def ring(x, step):
         return lax.ppermute(x, "space", [(i, (i + step) % sectors) for i in range(sectors)])
 
+    def line_order(g):
+        flipped = lines[::-1] if g % 2 else lines
+        return [line[::-1] for line in flipped] if g // 2 % 2 else flipped
+
     table, split, base, scale = mode_layout(points, near)
-    table = table.reshape(table.shape[0], table.shape[1], quads, QUAD * block).transpose(2, 0, 1, 3)
+    table = table.reshape(table.shape[0], table.shape[1], chips, CORES * block).transpose(2, 0, 1, 3)
     here = jnp.stack([lax.axis_index("inst"), lax.axis_index("space")])
     ints = jnp.concatenate([here, inst_map, jnp.asarray(split)])
     reals = jnp.asarray(np.concatenate([spectral_values(slots), base, scale]).astype(np.float32))
@@ -558,7 +525,7 @@
 
     groups = [(lo, hi, 0) for lo, hi in spans(NEAR_SIZES, fields)]
     groups += [(lo, hi, 1) for lo, hi in spans(FAR_SIZES, fields)]
-    first, others, parts, own, done = {}, {}, {}, {}, {}
+    first, others, parts, totals, done = {}, {}, {}, {}, {}
     token, local, held, halos = None, None, None, None
     for step, g in ORDER:
         lo, hi, index = groups[g]
@@ -577,29 +544,16 @@
             token = mixed[0]
             others[g] = [first[g]] + [to_later(x, s + 1) for s, x in enumerate(mixed)]
         elif step == "spread":
-            mine, core, chip = plan.spread(local, others[g], lo, hi, token)
+            mine, core = plan.spread(local, others[g], lo, hi, token)
             token = mine
-            parts[g] = mine, to_sector(core, 1), chip
-        elif step == "join":
-            mine, core, chip = parts[g]
-            token = plan.join(chip, core, token)
-            parts[g] = mine, core, to_sector(token, 2)
+            parts[g] = mine, to_core(core)
         elif step == "coef":
-            part = token = plan.coefficients(*parts[g], token)
-            stride = QUAD
-            while 2 * stride < sectors:
-                part = part + to_sector(part, stride)
-                stride = 2 * stride
-            other = to_sector(part, stride) if stride < sectors else jnp.zeros_like(part)
-            own[g] = part, other
+            token = plan.coefficients(*parts[g], token)
+            totals[g] = lax.psum(token, "space", axis_index_groups=line_order(g))
         elif step == "filter":
-            mine, core, chip = plan.filtered(*own[g], *parts[g], token)
+            mine, core = plan.filtered(totals[g], *parts[g], token)
             token = mine
-            done[g] = mine, core, to_sector(chip, 2)
-        elif step == "back":
-            mine, core, chip = done[g]
-            token = plan.join(core, chip, token)
-            done[g] = mine, to_sector(token, 1), chip
+            done[g] = mine, to_core(core)
         elif step == "near":
             held = token = plan.place_near(*done[g], held, lo, hi, None if token is held else token)
         else:

time: 190 us -> 262 us (1.38)
  waiting for transfers between devices: 96.2 us -> 139 us
  Pallas kernels: 61.7 us -> 75.6 us
  between operations: 0.43 us -> 13.4 us
  local copies, waits for them, and re-layouts: 3.89 us -> 13.4 us
  starting transfers between devices: 27.4 us -> 19.1 us
    psum x0 -> x3, waiting for transfers between devices: none -> 83.2 us  [body(): totals[g] = lax.psum(token, 'space', axis_index_groups=line_order(g))]
    ppermute x15 -> x6, waiting for transfers between devices: 64.5 us -> 2.32 us  [to_core(): return lax.ppermute(x, 'space', [(i, i ^ 1) for i in range(sectors)])]
    ppermute x10, waiting for transfers between devices: 28.1 us -> 52.4 us  [to_partner(): return lax.ppermute(x, ('inst', 'space'), pairs)]
    unnamed x39 -> x61, local copies, waits for them, and re-layouts: 3.89 us -> 13.4 us
    pallas_call x6, Pallas kernels: 13.7 us -> 22.6 us  [table_call(): pl.pallas_call(lambda *refs: kernel(*refs[:count + 1], *refs[count + 1 +...]
    ppermute x15 -> x6, starting transfers between devices: 10.1 us -> 1.59 us  [to_core(): return lax.ppermute(x, 'space', [(i, i ^ 1) for i in range(sectors)])]
    pallas_call x25 -> x19, Pallas kernels: 48 us -> 53 us  [call(): pl.pallas_call(lambda *refs: kernel(*refs[:len(inputs)], *refs[len(inputs...]
    ppermute x2, waiting for transfers between devices: 3.5 us -> 0.77 us  [ring(): lax.ppermute(x, 'space', [(i, (i + step) % sectors) for i in range(sector...]
  transfers between devices with their start and end apart: 27 -> 21, of which waited for: 14 -> 11; matrix products, arithmetic and copies ran while one was open for 0% -> 0% of each run, Pallas kernels for 30% -> 27%
where the time goes in v4:
time: 262 us; the launch traced here: 260 us
  waiting for transfers between devices  139 us (53%)
  Pallas kernels  75.6 us (29%)
  starting transfers between devices  19.1 us (7%)
  local copies, waits for them, and re-layouts  13.4 us (5%)
  between operations  13.4 us (5%)
    psum x3, waiting for transfers between devices, body(): totals[g] = lax.psum(token, 'space', axis_index_groups=line_order(g))  83.2 us
    pallas_call x19, Pallas kernels, call(): pl.pallas_call(lambda *refs: kernel(*refs[:len(inputs)], *refs[len(inputs...  53 us
    ppermute x10, waiting for transfers between devices, to_partner(): return lax.ppermute(x, ('inst', 'space'), pairs)  52.4 us
    pallas_call x6, Pallas kernels, table_call(): pl.pallas_call(lambda *refs: kernel(*refs[:count + 1], *refs[count + 1 +...  22.6 us
    ppermute x10, starting transfers between devices, to_partner(): return lax.ppermute(x, ('inst', 'space'), pairs)  13.9 us
    unnamed x61, local copies, waits for them, and re-layouts  13.4 us
  transfers between devices with their start and end apart: 21, of which 11 were waited for; matrix products, arithmetic and copies ran while one was open for 0% of the time, Pallas kernels for 27%

profile of v4, /device:TPU:0, one launch (start us, length us, event | category | flops | bytes accessed | tf_op | source)
XLA Modules:
  0.0 260.4 jit_solution(13516869213072059957)
XLA Ops:
  7.8 2.3 pack.5
  10.1 3.0 %collective-permute-start.2 = (f32[2,32,32,128]{3,2,1,0:T(8,128)}, f32[2,32,32,128]{3,2,1,0:T(8,128)S(1)}, u32[]{:S(2)}, u32[]{:S(2)}) collective-permute-start(f32[2,32,32,128]{3,2,1,0:T(8,128)} %get-tuple-element.22.refs_1_), channel_id=1, source_target_pairs={{0,16},{1,9},{2,18},{3,11},{4,20},{5,13},{6,22},{7,15},{8,24},{9,1... | collective-permute-start | bytes 3145736 | tf_op jit(solution)/shard_map/ppermute | solution.py:493
  13.1 3.5 %collective-permute-start.1 = (f32[6,1,64,128]{3,2,1,0:T(8,128)}, f32[6,1,64,128]{3,2,1,0:T(8,128)}, u32[]{:S(2)}, u32[]{:S(2)}) collective-permute-start(f32[6,1,64,128]{3,2,1,0:T(8,128)} %get-tuple-element.21), channel_id=1, source_target_pairs={{0,7},{1,0},{2,1},{3,2},{4,3},{5,4},{6,5},{7,6},{8,15},{9,8},{10,9... | collective-permute-start | bytes 589832 | tf_op jit(solution)/shard_map/ppermute | solution.py:505
  20.4 12.3 %local_part.1.refs_4_.refs_2_ = f32[5,32,64,128]{3,2,1,0:T(8,128)} custom-call(f32[5,5]{1,0:T(8,128)S(1)} %copy-done.25, f32[5]{0:T(128)S(1)} %copy-done.26, s32[5,3]{1,0:T(8,128)S(1)} %copy.16.refs_2_, f32[5,32,64,128]{3,2,1,0:T(8,128)} %bitcast.9, f32[5,32,64,128]{3,2,1,0:T(8,128)} %bitcast.10, f32[5,32,64,128]{3,2,1,0:T(8,128)} %bitcast.11, ...), custom_call_target="tpu_custom_call" | custom-call | tf_op jit(solution)/shard_map/local_part/pallas_call | solution.py:126
  37.3 2.5 mix.6.refs_5_
  39.8 9.2 %collective-permute-done.3.refs_4_ = f32[2,32,32,128]{3,2,1,0:T(8,128)S(1)} collective-permute-done((f32[2,32,32,128]{3,2,1,0:T(8,128)S(1)}, f32[2,32,32,128]{3,2,1,0:T(8,128)S(1)}, u32[]{:S(2)}, u32[]{:S(2)}) %collective-permute-start.3) | collective-permute-done | bytes 1048608 | tf_op jit(solution)/shard_map/ppermute | solution.py:493
  54.6 4.4 %coefficients.3.refs_1_ = f32[2,8,128,128]{3,2,1,0:T(8,128)} custom-call(s32[22]{0:T(128)S(1)} %pad_add_fusion.refs_0_, f32[71]{0:T(128)S(1)} %copy-done.24, f32[4,16,128,64]{3,2,1,0:T(8,128)} %constant.18.clone.refs_2_, f32[2,16,32,128]{3,2,1,0:T(8,128)S(1)} %get-tuple-element.23.refs_1_.refs_3_.refs_4_, ...), custom_call_target="tpu_custom_call" | custom-call | tf_op jit(solution)/shard_map/coefficients/pallas_call | solution.py:340
  60.6 2.2 pack.8.refs_4_
  65.0 24.0 %collective-permute-done.5.refs_3_ = f32[1,32,32,128]{3,2,1,0:T(8,128)S(1)} collective-permute-done((f32[1,32,32,128]{3,2,1,0:T(8,128)}, f32[1,32,32,128]{3,2,1,0:T(8,128)S(1)}, u32[]{:S(2)}, u32[]{:S(2)}) %collective-permute-start.5) | collective-permute-done | bytes 524320 | tf_op jit(solution)/shard_map/ppermute | solution.py:493
  91.1 2.9 %spread.4 = (f32[2,16,32,128]{3,2,1,0:T(8,128)S(1)}, f32[2,16,32,128]{3,2,1,0:T(8,128)}) custom-call(s32[22]{0:T(128)S(1)} %pad_add_fusion.refs_0_, f32[71]{0:T(128)S(1)} %copy-done.24, f32[5,32,64,128]{3,2,1,0:T(8,128)} %local_part.1.refs_4_.refs_2_, f32[2,32,32,128]{3,2,1,0:T(8,128)S(1)} %copy-done.13, f32[2,32,32,128]{3,2,1,0:T(8,128)} %collective-permute-done.9.refs_4_, ...), custom_call_target="tpu_custom_call" | custom-call | tf_op jit(solution)/shard_map/spread/pallas_call | solution.py:126
  98.1 4.5 %coefficients.4.refs_4_ = f32[2,8,128,128]{3,2,1,0:T(8,128)} custom-call(s32[22]{0:T(128)S(1)} %pad_add_fusion.refs_0_, f32[71]{0:T(128)S(1)} %copy-done.24, f32[4,16,128,64]{3,2,1,0:T(8,128)} %constant.18.clone.refs_2_, f32[2,16,32,128]{3,2,1,0:T(8,128)S(1)} %copy-done.6, f32[2,16,32,128]{3,2,1,0:T(8,128)} %collective-permute-done.10.refs_4_.refs_5_, ...), custom_call_target="tpu_custom_call" | custom-call | tf_op jit(solution)/shard_map/coefficients/pallas_call | solution.py:340
  102.7 4.1 %mix.8.refs_5_ = f32[3,32,32,128]{3,2,1,0:T(8,128)} custom-call(s32[22]{0:T(128)S(1)} %pad_add_fusion.refs_0_, f32[71]{0:T(128)S(1)} %copy-done.24, f32[5,32,64,128]{3,2,1,0:T(8,128)} %bitcast.17, f32[3,32,32,128]{3,2,1,0:T(8,128)S(1)} %collective-permute-done.8.refs_3_, f32[2,8,128,128]{3,2,1,0:T(8,128)} %coefficients.4.refs_4_), custom_call_target="tpu_custom_call" | custom-call | tf_op jit(solution)/shard_map/mix/pallas_call | solution.py:126
  113.4 3.4 %coefficients.5.refs_4_ = f32[1,8,128,128]{3,2,1,0:T(8,128)} custom-call(s32[22]{0:T(128)S(1)} %pad_add_fusion.refs_0_, f32[71]{0:T(128)S(1)} %copy-done.24, f32[4,16,128,64]{3,2,1,0:T(8,128)} %constant.18.clone.refs_2_, f32[1,16,32,128]{3,2,1,0:T(8,128)S(1)} %get-tuple-element.27.refs_1_.refs_3_.refs_4_, ...), custom_call_target="tpu_custom_call" | custom-call | tf_op jit(solution)/shard_map/coefficients/pallas_call | solution.py:340
  117.5 17.5 %collective-permute-done.12.refs_3_ = f32[2,32,32,128]{3,2,1,0:T(8,128)S(1)} collective-permute-done((f32[2,32,32,128]{3,2,1,0:T(8,128)S(1)}, f32[2,32,32,128]{3,2,1,0:T(8,128)S(1)}, u32[]{:S(2)}, u32[]{:S(2)}) %collective-permute-start.12) | collective-permute-done | bytes 1048608 | tf_op jit(solution)/shard_map/ppermute | solution.py:493
  138.2 9.8 %all-reduce.8.cloned.1.call-done.refs_3_ = f32[2,8,128,128]{3,2,1,0:T(8,128)} async-done(((f32[2,8,128,128]{3,2,1,0:T(8,128)}), f32[2,8,128,128]{3,2,1,0:T(8,128)}) %all-reduce.8.cloned.1.call-update) | async-done | bytes 1048592 | tf_op jit(solution)/shard_map/psum | solution.py:552
  150.3 3.8 %filtered.3 = (f32[2,16,32,128]{3,2,1,0:T(8,128)S(1)}, f32[2,16,32,128]{3,2,1,0:T(8,128)S(1)}) custom-call(s32[22]{0:T(128)S(1)} %pad_add_fusion.refs_0_, f32[71]{0:T(128)S(1)} %copy-done.24, f32[4,16,64,128]{3,2,1,0:T(8,128)} %constant.19.clone.refs_2_, f32[2,8,128,128]{3,2,1,0:T(8,128)S(1)} %copy-done.20, f32[2,16,32,128]{3,2,1,0:T(8,128)S(1)} %copy-done.9, ...), custom_call_target="tpu_custom_call" | custom-call | tf_op jit(solution)/shard_map/filtered/pallas_call | solution.py:340
  156.0 2.4 place_near.3.refs_6_.refs_5_
  158.4 43.3 %all-reduce.6.cloned.1.call-done.refs_3_ = f32[2,8,128,128]{3,2,1,0:T(8,128)} async-done(((f32[2,8,128,128]{3,2,1,0:T(8,128)}), f32[2,8,128,128]{3,2,1,0:T(8,128)}) %all-reduce.6.cloned.1.call-update) | async-done | bytes 1048592 | tf_op jit(solution)/shard_map/psum | solution.py:552
  203.0 4.4 %filtered.4 = (f32[2,16,32,128]{3,2,1,0:T(8,128)S(1)}, f32[2,16,32,128]{3,2,1,0:T(8,128)}) custom-call(s32[22]{0:T(128)S(1)} %pad_add_fusion.refs_0_, f32[71]{0:T(128)S(1)} %copy-done.24, f32[4,16,64,128]{3,2,1,0:T(8,128)S(1)} %copy-done.2, f32[2,8,128,128]{3,2,1,0:T(8,128)S(1)} %copy-done.19, f32[2,16,32,128]{3,2,1,0:T(8,128)S(1)} %copy-done.7, ...), custom_call_target="tpu_custom_call" | custom-call | tf_op jit(solution)/shard_map/filtered/pallas_call | solution.py:340
  208.8 3.8 %place_far.2.refs_4_ = f32[5,32,64,128]{3,2,1,0:T(8,128)} custom-call(s32[22]{0:T(128)S(1)} %pad_add_fusion.refs_0_, f32[71]{0:T(128)S(1)} %copy-done.24, f32[5,32,64,128]{3,2,1,0:T(8,128)} %local_part.1.refs_4_.refs_2_, f32[3,32,32,128]{3,2,1,0:T(8,128)S(1)} %copy-done.4, ...), custom_call_target="tpu_custom_call", output_to_operand_aliasing={{}: (5, {})} | custom-call | tf_op jit(solution)/shard_map/place_far/pallas_call | solution.py:126
  212.7 2.5 place_near.4.refs_6_.refs_5_
  215.1 30.2 %all-reduce.4.cloned.1.call-done.refs_3_ = f32[1,8,128,128]{3,2,1,0:T(8,128)} async-done(((f32[1,8,128,128]{3,2,1,0:T(8,128)}), f32[1,8,128,128]{3,2,1,0:T(8,128)}) %all-reduce.4.cloned.1.call-update) | async-done | bytes 524304 | tf_op jit(solution)/shard_map/psum | solution.py:552
  247.3 2.2 filtered.5
  249.6 2.5 place_far.3.refs_4_
  (108 shorter events, 46.5 us)
Async XLA Ops:
  10.1 22.7 %collective-permute-start.2 = (f32[2,32,32,128]{3,2,1,0:T(8,128)}, f32[2,32,32,128]{3,2,1,0:T(8,128)S(1)}, u32[]{:S(2)}, u32[]{:S(2)}) collective-permute-start(f32[2,32,32,128]{3,2,1,0:T(8,128)} %get-tuple-element.22.refs_1_), channel_id=1, source_target_pairs={{0,16},{1,9},{2,18},{3,11},{4,20},{5,13},{6,22},{7,15},{8,24},{9,1... | collective-permute-start | bytes 3145736 | tf_op jit(solution)/shard_map/ppermute | solution.py:493
  13.1 7.3 %collective-permute-start = (f32[6,1,64,128]{3,2,1,0:T(8,128)}, f32[6,1,64,128]{3,2,1,0:T(8,128)S(1)}, u32[]{:S(2)}, u32[]{:S(2)}) collective-permute-start(f32[6,1,64,128]{3,2,1,0:T(8,128)} %get-tuple-element.20), channel_id=1, source_target_pairs={{0,1},{1,2},{2,3},{3,4},{4,5},{5,6},{6,7},{7,0},{8,9},{9,10},{10,1... | collective-permute-start | bytes 589832 | tf_op jit(solution)/shard_map/ppermute | solution.py:505
  13.1 7.3 %collective-permute-start.1 = (f32[6,1,64,128]{3,2,1,0:T(8,128)}, f32[6,1,64,128]{3,2,1,0:T(8,128)}, u32[]{:S(2)}, u32[]{:S(2)}) collective-permute-start(f32[6,1,64,128]{3,2,1,0:T(8,128)} %get-tuple-element.21), channel_id=1, source_target_pairs={{0,7},{1,0},{2,1},{3,2},{4,3},{5,4},{6,5},{7,6},{8,15},{9,8},{10,9... | collective-permute-start | bytes 589832 | tf_op jit(solution)/shard_map/ppermute | solution.py:505
  18.7 18.6 %collective-permute-start.4 = (f32[2,32,32,128]{3,2,1,0:T(8,128)}, f32[2,32,32,128]{3,2,1,0:T(8,128)S(1)}, u32[]{:S(2)}, u32[]{:S(2)}) collective-permute-start(f32[2,32,32,128]{3,2,1,0:T(8,128)} %pack.6.refs_12_), channel_id=1, source_target_pairs={{0,16},{1,9},{2,18},{3,11},{4,20},{5,13},{6,22},{7,15},{8,24},{9,1... | collective-permute-start | bytes 3145736 | tf_op jit(solution)/shard_map/ppermute | solution.py:493
  34.1 14.9 %collective-permute-start.3 = (f32[2,32,32,128]{3,2,1,0:T(8,128)S(1)}, f32[2,32,32,128]{3,2,1,0:T(8,128)S(1)}, u32[]{:S(2)}, u32[]{:S(2)}) collective-permute-start(f32[2,32,32,128]{3,2,1,0:T(8,128)S(1)} %mix.5.refs_4_), channel_id=1, source_target_pairs={{0,8},{1,17},{2,10},{3,19},{4,12},{5,21},{6,14},{7,23},{8,0},{9,25... | collective-permute-start | bytes 3145736 | tf_op jit(solution)/shard_map/ppermute | solution.py:493
  51.1 3.5 %collective-permute-start.6 = (f32[2,16,32,128]{3,2,1,0:T(8,128)S(1)}, f32[2,16,32,128]{3,2,1,0:T(8,128)S(1)}, u32[]{:S(2)}, u32[]{:S(2)}) collective-permute-start(f32[2,16,32,128]{3,2,1,0:T(8,128)S(1)} %get-tuple-element.24), channel_id=1, source_target_pairs={{0,1},{1,0},{2,3},{3,2},{4,5},{5,4},{6,7},{7,6},{8,9},{9,8},{10,11... | collective-permute-start | bytes 1572872 | tf_op jit(solution)/shard_map/ppermute | solution.py:502
  52.0 39.1 %collective-permute-start.9 = (f32[2,32,32,128]{3,2,1,0:T(8,128)}, f32[2,32,32,128]{3,2,1,0:T(8,128)}, u32[]{:S(2)}, u32[]{:S(2)}) collective-permute-start(f32[2,32,32,128]{3,2,1,0:T(8,128)} %mix.6.refs_5_), channel_id=1, source_target_pairs={{0,8},{1,17},{2,10},{3,19},{4,12},{5,21},{6,14},{7,23},{8,0},{9,25... | collective-permute-start | bytes 3145736 | tf_op jit(solution)/shard_map/ppermute | solution.py:493
  62.9 85.1 %all-reduce.8.cloned.1.call-start = ((), (), s32[]{:S(2)}) async-start(), calls=%async_computation.2 | async-start | bytes 2097152 | tf_op jit(solution)/shard_map/psum | solution.py:552
  62.9 39.8 %collective-permute-start.8 = (f32[3,32,32,128]{3,2,1,0:T(8,128)S(1)}, f32[3,32,32,128]{3,2,1,0:T(8,128)S(1)}, u32[]{:S(2)}, u32[]{:S(2)}) collective-permute-start(f32[3,32,32,128]{3,2,1,0:T(8,128)S(1)} %pack.8.refs_4_), channel_id=1, source_target_pairs={{0,16},{1,9},{2,18},{3,11},{4,20},{5,13},{6,22},{7,15},{8,24},{9,1... | collective-permute-start | bytes 4718600 | tf_op jit(solution)/shard_map/ppermute | solution.py:493
  63.5 25.5 %collective-permute-start.5 = (f32[1,32,32,128]{3,2,1,0:T(8,128)}, f32[1,32,32,128]{3,2,1,0:T(8,128)S(1)}, u32[]{:S(2)}, u32[]{:S(2)}) collective-permute-start(f32[1,32,32,128]{3,2,1,0:T(8,128)} %copy-done.16), channel_id=1, source_target_pairs={{0,16},{1,9},{2,18},{3,11},{4,20},{5,13},{6,22},{7,15},{8,24},{9,1... | collective-permute-start | bytes 1572872 | tf_op jit(solution)/shard_map/ppermute | solution.py:493
  94.8 2.3 collective-permute-start.10
  95.2 11.6 %collective-permute-start.7 = (f32[1,32,32,128]{3,2,1,0:T(8,128)}, f32[1,32,32,128]{3,2,1,0:T(8,128)}, u32[]{:S(2)}, u32[]{:S(2)}) collective-permute-start(f32[1,32,32,128]{3,2,1,0:T(8,128)} %mix.7.refs_5_), channel_id=1, source_target_pairs={{0,8},{1,17},{2,10},{3,19},{4,12},{5,21},{6,14},{7,23},{8,0},{9,25... | collective-permute-start | bytes 1572872 | tf_op jit(solution)/shard_map/ppermute | solution.py:493
  106.7 95.0 %all-reduce.6.cloned.1.call-start = ((), (), s32[]{:S(2)}) async-start(), calls=%async_computation.1 | async-start | bytes 2097152 | tf_op jit(solution)/shard_map/psum | solution.py:552
  109.7 25.3 %collective-permute-start.12 = (f32[2,32,32,128]{3,2,1,0:T(8,128)S(1)}, f32[2,32,32,128]{3,2,1,0:T(8,128)S(1)}, u32[]{:S(2)}, u32[]{:S(2)}) collective-permute-start(f32[2,32,32,128]{3,2,1,0:T(8,128)S(1)} %pack.9.refs_5_), channel_id=1, source_target_pairs={{0,16},{1,9},{2,18},{3,11},{4,20},{5,13},{6,22},{7,15},{8,24},{9,1... | collective-permute-start | bytes 3145736 | tf_op jit(solution)/shard_map/ppermute | solution.py:493
  110.4 97.0 %collective-permute-start.15 = (f32[3,32,32,128]{3,2,1,0:T(8,128)}, f32[3,32,32,128]{3,2,1,0:T(8,128)}, u32[]{:S(2)}, u32[]{:S(2)}) collective-permute-start(f32[3,32,32,128]{3,2,1,0:T(8,128)} %mix.8.refs_5_), channel_id=1, source_target_pairs={{0,8},{1,17},{2,10},{3,19},{4,12},{5,21},{6,14},{7,23},{8,0},{9,25... | collective-permute-start | bytes 4718600 | tf_op jit(solution)/shard_map/ppermute | solution.py:493
  111.8 1.6 collective-permute-start.11
  138.2 63.5 %copy-start.2 = (f32[4,16,64,128]{3,2,1,0:T(8,128)S(1)}, f32[4,16,64,128]{3,2,1,0:T(8,128)}, u32[]{:S(2)}) copy-start(f32[4,16,64,128]{3,2,1,0:T(8,128)} %constant.19.clone.refs_2_) | copy-start | bytes 6291460
  138.2 63.5 %copy-start.7 = (f32[2,16,32,128]{3,2,1,0:T(8,128)S(1)}, f32[2,16,32,128]{3,2,1,0:T(8,128)}, u32[]{:S(2)}) copy-start(f32[2,16,32,128]{3,2,1,0:T(8,128)} %copy-done.5) | copy-start | bytes 1572868
  138.2 107.1 %all-reduce.4.cloned.1.call-start = ((), (), s32[]{:S(2)}) async-start(), calls=%async_computation | async-start | bytes 1048576 | tf_op jit(solution)/shard_map/psum | solution.py:552
  154.0 2.0 collective-permute-start.13
  154.1 95.4 %collective-permute-start.17 = (f32[2,32,32,128]{3,2,1,0:T(8,128)}, f32[2,32,32,128]{3,2,1,0:T(8,128)}, u32[]{:S(2)}, u32[]{:S(2)}) collective-permute-start(f32[2,32,32,128]{3,2,1,0:T(8,128)} %mix.9.refs_6_), channel_id=1, source_target_pairs={{0,8},{1,17},{2,10},{3,19},{4,12},{5,21},{6,14},{7,23},{8,0},{9,25... | collective-permute-start | bytes 3145736 | tf_op jit(solution)/shard_map/ppermute | solution.py:493
  207.3 5.3 %collective-permute-start.14 = (f32[2,16,32,128]{3,2,1,0:T(8,128)}, f32[2,16,32,128]{3,2,1,0:T(8,128)S(1)}, u32[]{:S(2)}, u32[]{:S(2)}) collective-permute-start(f32[2,16,32,128]{3,2,1,0:T(8,128)} %get-tuple-element.32), channel_id=1, source_target_pairs={{0,1},{1,0},{2,3},{3,2},{4,5},{5,4},{6,7},{7,6},{8,9},{9,8},{10,11... | collective-permute-start | bytes 1572872 | tf_op jit(solution)/shard_map/ppermute | solution.py:502
  215.1 34.5 %copy-start.11 = (f32[2,32,32,128]{3,2,1,0:T(8,128)S(1)}, f32[2,32,32,128]{3,2,1,0:T(8,128)}, u32[]{:S(2)}) copy-start(f32[2,32,32,128]{3,2,1,0:T(8,128)} %copy-done.10) | copy-start | bytes 3145732
  249.5 2.6 collective-permute-start.16
  (27 other events, 173.0 us)
Sparse Core Ops, SparseCore 0:
  96.8 51.1 all-reduce.7
  150.5 51.1 all-reduce.5
  207.5 37.7 all-reduce.3

commit v5 on v3

--- a/solution.py
+++ b/solution.py
@@ -44,6 +44,9 @@
     ("near", 2),
     ("far", 4),
 )
+DEPTH = 99
+CROSS = 99
+FREE = ("join", "back", "near")
 SMEM = pl.BlockSpec(memory_space=pltpu.SMEM)
 ANY = pl.BlockSpec(memory_space=pl.ANY)
 COST = pl.CostEstimate(flops=0, bytes_accessed=0, transcendentals=0)
@@ -128,7 +131,7 @@
 
 
 def call(kernel, name, token, grid, inputs, in_specs, out_specs, out_shape, scratch=(), alias=None):
-    extra = [] if token is None else [token]
+    extra = [t for t in token or () if all(t is not x for x in inputs)]
     return pl.pallas_call(
         lambda *refs: kernel(*refs[: len(inputs)], *refs[len(inputs) + len(extra) :]),
         grid=grid,
@@ -367,7 +370,7 @@
         )
 
     def table_call(self, kernel, name, fields, inputs, in_specs, out_specs, out_shape, scratch, token):
-        extra = [] if token is None else [token]
+        extra = [t for t in token or () if all(t is not x for x in inputs)]
         count = len(inputs)
         return pl.pallas_call(
             lambda *refs: kernel(*refs[: count + 1], *refs[count + 1 + len(extra) :]),
@@ -559,53 +562,65 @@
     groups = [(lo, hi, 0) for lo, hi in spans(NEAR_SIZES, fields)]
     groups += [(lo, hi, 1) for lo, hi in spans(FAR_SIZES, fields)]
     first, others, parts, own, done = {}, {}, {}, {}, {}
-    token, local, held, halos = None, None, None, None
+    last, local, held, halos = None, None, None, None
+    sent, crossed = [], []
     for step, g in ORDER:
         lo, hi, index = groups[g]
+        before = last
+        token = [] if last is None or step in FREE else [last]
+        if step in ("pack", "mix"):
+            token += sent[-DEPTH : len(sent) - DEPTH + 1] if len(sent) >= DEPTH else []
+        if step in ("join", "coef", "filter"):
+            token += crossed[-CROSS : len(crossed) - CROSS + 1] if len(crossed) >= CROSS else []
         if step == "pack":
             packed = pack(center, viscosity, lo, hi, index, near, halos is None, token)
-            token = packed[0]
+            last = packed[0]
             first[g] = to_first(packed[0])
+            sent.append(first[g])
             if halos is None:
                 halos = ring(packed[1], 1), ring(packed[2], -1)
         elif step == "local":
-            local = token = local_part(
+            local = last = local_part(
                 center, source[0], viscosity, kappa, coupling, bc_flags, *halos, token
             )
         elif step == "mix":
             mixed = plan.mix(center, first[g], lo, hi, index, token)
-            token = mixed[0]
+            last = mixed[0]
             others[g] = [first[g]] + [to_later(x, s + 1) for s, x in enumerate(mixed)]
+            sent.append(others[g][-1])
         elif step == "spread":
             mine, core, chip = plan.spread(local, others[g], lo, hi, token)
-            token = mine
+            last = mine
             parts[g] = mine, to_sector(core, 1), chip
         elif step == "join":
             mine, core, chip = parts[g]
-            token = plan.join(chip, core, token)
-            parts[g] = mine, core, to_sector(token, 2)
+            last = plan.join(chip, core, token)
+            parts[g] = mine, core, to_sector(last, 2)
+            crossed.append(parts[g][2])
         elif step == "coef":
-            part = token = plan.coefficients(*parts[g], token)
+            part = last = plan.coefficients(*parts[g], token)
             stride = QUAD
             while 2 * stride < sectors:
                 part = part + to_sector(part, stride)
                 stride = 2 * stride
             other = to_sector(part, stride) if stride < sectors else jnp.zeros_like(part)
             own[g] = part, other
+            crossed.append(other)
         elif step == "filter":
             mine, core, chip = plan.filtered(*own[g], *parts[g], token)
-            token = mine
+            last = mine
             done[g] = mine, core, to_sector(chip, 2)
+            crossed.append(done[g][2])
         elif step == "back":
             mine, core, chip = done[g]
-            token = plan.join(core, chip, token)
-            done[g] = mine, to_sector(token, 1), chip
+            last = plan.join(core, chip, token)
+            done[g] = mine, to_sector(last, 1), chip
         elif step == "near":
-            held = token = plan.place_near(*done[g], held, lo, hi, None if token is held else token)
+            held = last = plan.place_near(*done[g], held, lo, hi, token)
         else:
-            held = token = plan.place_far(
-                local, others[g], held, lo, hi, None if token is held else token
-            )
+            held = last = plan.place_far(local, others[g], held, lo, hi, token)
+        if step in FREE:
+            last = before
     return held[None]
 
 

time: 190 us -> 186 us (0.979)
  waiting for transfers between devices: 96.2 us -> 87.3 us
  local copies, waits for them, and re-layouts: 3.89 us -> 7.11 us
  starting transfers between devices: 27.4 us -> 29.9 us
    ppermute x15, waiting for transfers between devices: 64.5 us -> 51.7 us  [to_sector(): return lax.ppermute(x, 'space', [(i, i ^ k) for i in range(sectors)])]
    ppermute x10, waiting for transfers between devices: 28.1 us -> 32.2 us  [to_partner(): return lax.ppermute(x, ('inst', 'space'), pairs)]
    unnamed x39 -> x40, local copies, waits for them, and re-layouts: 3.89 us -> 7.11 us
    ppermute x15, starting transfers between devices: 10.1 us -> 12.8 us  [to_sector(): return lax.ppermute(x, 'space', [(i, i ^ k) for i in range(sectors)])]
  transfers between devices with their start and end apart: 27 -> 27, of which waited for: 14 -> 10; matrix products, arithmetic and copies ran while one was open for 0% -> 3% of each run, Pallas kernels for 30% -> 30%
where the time goes in v5:
time: 186 us
  waiting for transfers between devices  87.3 us (47%)
  Pallas kernels  60.7 us (33%)
  starting transfers between devices  29.9 us (16%)
  local copies, waits for them, and re-layouts  7.11 us (4%)
    ppermute x15, waiting for transfers between devices, to_sector(): return lax.ppermute(x, 'space', [(i, i ^ k) for i in range(sectors)])  51.7 us
    pallas_call x25, Pallas kernels, call(): pl.pallas_call(lambda *refs: kernel(*refs[:len(inputs)], *refs[len(inputs...  47 us
    ppermute x10, waiting for transfers between devices, to_partner(): return lax.ppermute(x, ('inst', 'space'), pairs)  32.2 us
    pallas_call x6, Pallas kernels, table_call(): pl.pallas_call(lambda *refs: kernel(*refs[:count + 1], *refs[count + 1 +...  13.7 us
    ppermute x10, starting transfers between devices, to_partner(): return lax.ppermute(x, ('inst', 'space'), pairs)  13.5 us
    ppermute x15, starting transfers between devices, to_sector(): return lax.ppermute(x, 'space', [(i, i ^ k) for i in range(sectors)])  12.8 us
    unnamed x40, local copies, waits for them, and re-layouts  7.11 us
  transfers between devices with their start and end apart: 27, of which 10 were waited for; matrix products, arithmetic and copies ran while one was open for 3% of the time, Pallas kernels for 30%

profile of v5, /device:TPU:0, one launch (start us, length us, event | category | flops | bytes accessed | tf_op | source)
XLA Modules:
  0.0 185.6 jit_solution(12733316840370770823)
XLA Ops:
  3.6 3.0 %collective-permute-start.2 = (f32[2,32,32,128]{3,2,1,0:T(8,128)}, f32[2,32,32,128]{3,2,1,0:T(8,128)S(1)}, u32[]{:S(2)}, u32[]{:S(2)}) collective-permute-start(f32[2,32,32,128]{3,2,1,0:T(8,128)} %get-tuple-element.28.refs_1_), channel_id=1, source_target_pairs={{0,16},{1,9},{2,18},{3,11},{4,20},{5,13},{6,22},{7,15},{8,24},{9,1... | collective-permute-start | bytes 3145736 | tf_op jit(solution)/shard_map/ppermute | solution.py:533
  8.8 3.5 %collective-permute-start.1 = (f32[6,1,64,128]{3,2,1,0:T(8,128)}, f32[6,1,64,128]{3,2,1,0:T(8,128)}, u32[]{:S(2)}, u32[]{:S(2)}) collective-permute-start(f32[6,1,64,128]{3,2,1,0:T(8,128)} %get-tuple-element.27), channel_id=1, source_target_pairs={{0,7},{1,0},{2,1},{3,2},{4,3},{5,4},{6,5},{7,6},{8,15},{9,8},{10,9... | collective-permute-start | bytes 589832 | tf_op jit(solution)/shard_map/ppermute | solution.py:545
  12.5 3.5 %collective-permute-done.refs_10_ = f32[6,1,64,128]{3,2,1,0:T(8,128)S(1)} collective-permute-done((f32[6,1,64,128]{3,2,1,0:T(8,128)}, f32[6,1,64,128]{3,2,1,0:T(8,128)S(1)}, u32[]{:S(2)}, u32[]{:S(2)}) %collective-permute-start) | collective-permute-done | bytes 196640 | tf_op jit(solution)/shard_map/ppermute | solution.py:545
  16.0 12.3 %local_part.1.refs_4_.refs_2_ = f32[5,32,64,128]{3,2,1,0:T(8,128)} custom-call(f32[5,5]{1,0:T(8,128)S(1)} %copy-done.11, f32[5]{0:T(128)S(1)} %copy-done.12, s32[5,3]{1,0:T(8,128)S(1)} %copy.22.refs_2_, f32[5,32,64,128]{3,2,1,0:T(8,128)} %bitcast.9, f32[5,32,64,128]{3,2,1,0:T(8,128)} %bitcast.10, f32[5,32,64,128]{3,2,1,0:T(8,128)} %bitcast.11, ...), custom_call_target="tpu_custom_call" | custom-call | tf_op jit(solution)/shard_map/local_part/pallas_call | solution.py:135
  34.4 10.2 %collective-permute-done.3.refs_4_ = f32[2,32,32,128]{3,2,1,0:T(8,128)S(1)} collective-permute-done((f32[2,32,32,128]{3,2,1,0:T(8,128)S(1)}, f32[2,32,32,128]{3,2,1,0:T(8,128)S(1)}, u32[]{:S(2)}, u32[]{:S(2)}) %collective-permute-start.3) | collective-permute-done | bytes 1048608 | tf_op jit(solution)/shard_map/ppermute | solution.py:533
  50.7 9.9 %collective-permute-done.8.refs_4_ = f32[2,32,32,128]{3,2,1,0:T(8,128)S(1)} collective-permute-done((f32[2,32,32,128]{3,2,1,0:T(8,128)S(1)}, f32[2,32,32,128]{3,2,1,0:T(8,128)S(1)}, u32[]{:S(2)}, u32[]{:S(2)}) %collective-permute-start.8) | collective-permute-done | bytes 1048608 | tf_op jit(solution)/shard_map/ppermute | solution.py:533
  68.5 2.4 %coefficients.3.refs_4_.refs_3_ = f32[2,4,128,128]{3,2,1,0:T(8,128)S(1)} custom-call(s32[22]{0:T(128)S(1)} %pad_add_fusion.refs_0_, f32[71]{0:T(128)S(1)} %copy-done.10, f32[2,16,128,128]{3,2,1,0:T(8,128)S(1)} %copy-done.3, f32[2,8,32,128]{3,2,1,0:T(8,128)S(1)} %get-tuple-element.29.refs_1_.refs_3_.refs_5_, ...), custom_call_target="tpu_custom_call" | custom-call | tf_op jit(solution)/shard_map/coefficients/pallas_call | solution.py:375
  75.0 12.0 %collective-permute-done.9.refs_4_ = f32[1,32,32,128]{3,2,1,0:T(8,128)S(1)} collective-permute-done((f32[1,32,32,128]{3,2,1,0:T(8,128)S(1)}, f32[1,32,32,128]{3,2,1,0:T(8,128)S(1)}, u32[]{:S(2)}, u32[]{:S(2)}) %collective-permute-start.9) | collective-permute-done | bytes 524320 | tf_op jit(solution)/shard_map/ppermute | solution.py:533
  91.4 8.0 %collective-permute-done.13.refs_4_ = f32[2,4,128,128]{3,2,1,0:T(8,128)S(1)} collective-permute-done((f32[2,4,128,128]{3,2,1,0:T(8,128)S(1)}, f32[2,4,128,128]{3,2,1,0:T(8,128)S(1)}, u32[]{:S(2)}, u32[]{:S(2)}) %collective-permute-start.13) | collective-permute-done | bytes 524320 | tf_op jit(solution)/shard_map/ppermute | solution.py:542
  99.4 3.0 %filtered.3 = (f32[2,8,32,128]{3,2,1,0:T(8,128)S(1)}, f32[2,2,8,32,128]{4,3,2,1,0:T(8,128)S(1)}, f32[2,2,8,32,128]{4,3,2,1,0:T(8,128)S(1)}) custom-call(s32[22]{0:T(128)S(1)} %pad_add_fusion.refs_0_, f32[71]{0:T(128)S(1)} %copy-done.10, f32[2,16,128,128]{3,2,1,0:T(8,128)} %constant.19.clone.refs_2_, f32[2,4,128,128]{3,2,1,0:T(8,128)S(1)} %coefficients.3.refs_4_.refs_3_, ...), custom_call_target="tpu_custom_call" | custom-call | tf_op jit(solution)/shard_map/filtered/pallas_call | solution.py:375
  102.5 2.4 %coefficients.4.refs_4_.refs_3_ = f32[2,4,128,128]{3,2,1,0:T(8,128)S(1)} custom-call(s32[22]{0:T(128)S(1)} %pad_add_fusion.refs_0_, f32[71]{0:T(128)S(1)} %copy-done.10, f32[2,16,128,128]{3,2,1,0:T(8,128)S(1)} %copy-done.3, f32[2,8,32,128]{3,2,1,0:T(8,128)S(1)} %get-tuple-element.32.refs_1_.refs_3_.refs_5_, ...), custom_call_target="tpu_custom_call" | custom-call | tf_op jit(solution)/shard_map/coefficients/pallas_call | solution.py:375
  105.0 2.5 %mix.8.refs_6_ = f32[3,32,32,128]{3,2,1,0:T(8,128)S(1)} custom-call(s32[22]{0:T(128)S(1)} %pad_add_fusion.refs_0_, f32[71]{0:T(128)S(1)} %copy-done.10, f32[5,32,64,128]{3,2,1,0:T(8,128)} %bitcast.17, f32[3,32,32,128]{3,2,1,0:T(8,128)S(1)} %collective-permute-done.17.refs_3_, f32[2,4,128,128]{3,2,1,0:T(8,128)S(1)} %coefficients.4.refs_4_.refs_3_), custom_call_target="tpu_custom_call" | custom-call | tf_op jit(solution)/shard_map/mix/pallas_call | solution.py:135
  108.0 2.7 %collective-permute-start.16 = (f32[2,1,8,32,128]{4,3,2,1,0:T(8,128)S(1)}, f32[2,1,8,32,128]{4,3,2,1,0:T(8,128)S(1)}, u32[]{:S(2)}, u32[]{:S(2)}) collective-permute-start(f32[2,1,8,32,128]{4,3,2,1,0:T(8,128)S(1)} %join.8), channel_id=1, source_target_pairs={{0,2},{1,3},{2,0},{3,1},{4,6},{5,7},{6,4},{7,5},{8,10},{9,11},{10,... | collective-permute-start | bytes 786440 | tf_op jit(solution)/shard_map/ppermute | solution.py:542
  110.8 12.1 %collective-permute-done.16.refs_5_.refs_7_ = f32[2,1,8,32,128]{4,3,2,1,0:T(8,128)S(1)} collective-permute-done((f32[2,1,8,32,128]{4,3,2,1,0:T(8,128)S(1)}, f32[2,1,8,32,128]{4,3,2,1,0:T(8,128)S(1)}, u32[]{:S(2)}, u32[]{:S(2)}) %collective-permute-start.16) | collective-permute-done | bytes 262176 | tf_op jit(solution)/shard_map/ppermute | solution.py:542
  124.6 5.2 %collective-permute-done.14.refs_4_ = f32[2,4,128,128]{3,2,1,0:T(8,128)S(1)} collective-permute-done((f32[2,4,128,128]{3,2,1,0:T(8,128)S(1)}, f32[2,4,128,128]{3,2,1,0:T(8,128)S(1)}, u32[]{:S(2)}, u32[]{:S(2)}) %collective-permute-start.14) | collective-permute-done | bytes 524320 | tf_op jit(solution)/shard_map/ppermute | solution.py:542
  129.9 2.5 %filtered.4 = (f32[2,8,32,128]{3,2,1,0:T(8,128)S(1)}, f32[2,2,8,32,128]{4,3,2,1,0:T(8,128)S(1)}, f32[2,2,8,32,128]{4,3,2,1,0:T(8,128)S(1)}) custom-call(s32[22]{0:T(128)S(1)} %pad_add_fusion.refs_0_, f32[71]{0:T(128)S(1)} %copy-done.10, f32[2,16,128,128]{3,2,1,0:T(8,128)S(1)} %copy-done.2, f32[2,4,128,128]{3,2,1,0:T(8,128)S(1)} %coefficients.4.refs_4_.refs_3_, ...), custom_call_target="tpu_custom_call" | custom-call | tf_op jit(solution)/shard_map/filtered/pallas_call | solution.py:375
  134.5 4.1 %collective-permute-start.19 = (f32[1,4,128,128]{3,2,1,0:T(8,128)S(1)}, f32[1,4,128,128]{3,2,1,0:T(8,128)S(1)}, u32[]{:S(2)}, u32[]{:S(2)}) collective-permute-start(f32[1,4,128,128]{3,2,1,0:T(8,128)S(1)} %coefficients.5.refs_8_.refs_3_), channel_id=1, source_target_pairs={{0,4},{1,5},{2,6},{3,7},{4,0},{5,1},{6,2},{7,3},{8,12},{9,13},{10,... | collective-permute-start | bytes 786440 | tf_op jit(solution)/shard_map/ppermute | solution.py:542
  138.6 7.3 %collective-permute-done.25.refs_1_.refs_4_ = f32[2,2,8,32,128]{4,3,2,1,0:T(8,128)S(1)} collective-permute-done((f32[2,2,8,32,128]{4,3,2,1,0:T(8,128)}, f32[2,2,8,32,128]{4,3,2,1,0:T(8,128)S(1)}, u32[]{:S(2)}, u32[]{:S(2)}) %collective-permute-start.25) | collective-permute-done | bytes 524320 | tf_op jit(solution)/shard_map/ppermute | solution.py:542
  146.0 10.3 %collective-permute-done.23.refs_1_.refs_4_ = f32[2,2,8,32,128]{4,3,2,1,0:T(8,128)S(1)} collective-permute-done((f32[2,2,8,32,128]{4,3,2,1,0:T(8,128)S(1)}, f32[2,2,8,32,128]{4,3,2,1,0:T(8,128)S(1)}, u32[]{:S(2)}, u32[]{:S(2)}) %collective-permute-start.23) | collective-permute-done | bytes 524320 | tf_op jit(solution)/shard_map/ppermute | solution.py:542
  158.2 8.7 %collective-permute-done.20.refs_1_.refs_4_ = f32[2,1,8,32,128]{4,3,2,1,0:T(8,128)S(1)} collective-permute-done((f32[2,1,8,32,128]{4,3,2,1,0:T(8,128)S(1)}, f32[2,1,8,32,128]{4,3,2,1,0:T(8,128)S(1)}, u32[]{:S(2)}, u32[]{:S(2)}) %collective-permute-start.20) | collective-permute-done | bytes 262176 | tf_op jit(solution)/shard_map/ppermute | solution.py:542
  167.0 2.5 %place_near.3.refs_5_ = f32[5,32,64,128]{3,2,1,0:T(8,128)} custom-call(s32[22]{0:T(128)S(1)} %pad_add_fusion.refs_0_, f32[71]{0:T(128)S(1)} %copy-done.10, f32[2,8,32,128]{3,2,1,0:T(8,128)S(1)} %get-tuple-element.36.refs_6_.refs_2_, f32[2,2,8,32,128]{4,3,2,1,0:T(8,128)S(1)} %collective-permute-done.26.refs_3_, ...), custom_call_target="tpu_custom_call" | custom-call | tf_op jit(solution)/shard_map/place_near/pallas_call | solution.py:135
  169.5 2.5 %place_near.4.refs_5_ = f32[5,32,64,128]{3,2,1,0:T(8,128)} custom-call(s32[22]{0:T(128)S(1)} %pad_add_fusion.refs_0_, f32[71]{0:T(128)S(1)} %copy-done.10, f32[2,8,32,128]{3,2,1,0:T(8,128)S(1)} %get-tuple-element.39.refs_4_.refs_2_, f32[2,2,8,32,128]{4,3,2,1,0:T(8,128)S(1)} %collective-permute-done.24.refs_3_, ...), custom_call_target="tpu_custom_call", output_to_operand_aliasing={{}: (5, {})} | custom-call | tf_op jit(solution)/shard_map/place_near/pallas_call | solution.py:135
  172.0 3.9 %place_far.2.refs_6_ = f32[5,32,64,128]{3,2,1,0:T(8,128)} custom-call(s32[22]{0:T(128)S(1)} %pad_add_fusion.refs_0_, f32[71]{0:T(128)S(1)} %copy-done.10, f32[5,32,64,128]{3,2,1,0:T(8,128)} %local_part.1.refs_4_.refs_2_, f32[3,32,32,128]{3,2,1,0:T(8,128)S(1)} %collective-permute-done.17.refs_3_, ...), custom_call_target="tpu_custom_call", output_to_operand_aliasing={{}: (5, {})} | custom-call | tf_op jit(solution)/shard_map/place_far/pallas_call | solution.py:135
  175.9 5.7 %copy.31.refs_5_ = f32[5,32,64,128]{3,2,1,0:T(8,128)} copy(f32[5,32,64,128]{3,2,1,0:T(8,128)} %place_far.2.refs_6_) | data formatting | bytes 10485760
  (103 shorter events, 44.8 us)
Async XLA Ops:
  3.6 24.8 %collective-permute-start.2 = (f32[2,32,32,128]{3,2,1,0:T(8,128)}, f32[2,32,32,128]{3,2,1,0:T(8,128)S(1)}, u32[]{:S(2)}, u32[]{:S(2)}) collective-permute-start(f32[2,32,32,128]{3,2,1,0:T(8,128)} %get-tuple-element.28.refs_1_), channel_id=1, source_target_pairs={{0,16},{1,9},{2,18},{3,11},{4,20},{5,13},{6,22},{7,15},{8,24},{9,1... | collective-permute-start | bytes 3145736 | tf_op jit(solution)/shard_map/ppermute | solution.py:533
  8.7 23.1 %collective-permute-start.4 = (f32[2,32,32,128]{3,2,1,0:T(8,128)}, f32[2,32,32,128]{3,2,1,0:T(8,128)S(1)}, u32[]{:S(2)}, u32[]{:S(2)}) collective-permute-start(f32[2,32,32,128]{3,2,1,0:T(8,128)} %pack.6.refs_12_), channel_id=1, source_target_pairs={{0,16},{1,9},{2,18},{3,11},{4,20},{5,13},{6,22},{7,15},{8,24},{9,1... | collective-permute-start | bytes 3145736 | tf_op jit(solution)/shard_map/ppermute | solution.py:533
  29.7 14.9 %collective-permute-start.3 = (f32[2,32,32,128]{3,2,1,0:T(8,128)S(1)}, f32[2,32,32,128]{3,2,1,0:T(8,128)S(1)}, u32[]{:S(2)}, u32[]{:S(2)}) collective-permute-start(f32[2,32,32,128]{3,2,1,0:T(8,128)S(1)} %mix.5.refs_4_), channel_id=1, source_target_pairs={{0,8},{1,17},{2,10},{3,19},{4,12},{5,21},{6,14},{7,23},{8,0},{9,25... | collective-permute-start | bytes 3145736 | tf_op jit(solution)/shard_map/ppermute | solution.py:533
  33.2 27.4 %collective-permute-start.8 = (f32[2,32,32,128]{3,2,1,0:T(8,128)S(1)}, f32[2,32,32,128]{3,2,1,0:T(8,128)S(1)}, u32[]{:S(2)}, u32[]{:S(2)}) collective-permute-start(f32[2,32,32,128]{3,2,1,0:T(8,128)S(1)} %mix.6.refs_5_), channel_id=1, source_target_pairs={{0,8},{1,17},{2,10},{3,19},{4,12},{5,21},{6,14},{7,23},{8,0},{9,25... | collective-permute-start | bytes 3145736 | tf_op jit(solution)/shard_map/ppermute | solution.py:533
  48.3 22.6 %collective-permute-start.5 = (f32[1,32,32,128]{3,2,1,0:T(8,128)S(1)}, f32[1,32,32,128]{3,2,1,0:T(8,128)S(1)}, u32[]{:S(2)}, u32[]{:S(2)}) collective-permute-start(f32[1,32,32,128]{3,2,1,0:T(8,128)S(1)} %pack.7.refs_5_), channel_id=1, source_target_pairs={{0,16},{1,9},{2,18},{3,11},{4,20},{5,13},{6,22},{7,15},{8,24},{9,1... | collective-permute-start | bytes 1572872 | tf_op jit(solution)/shard_map/ppermute | solution.py:533
  50.1 18.3 %collective-permute-start.7 = (f32[2,2,8,32,128]{4,3,2,1,0:T(8,128)S(1)}, f32[2,2,8,32,128]{4,3,2,1,0:T(8,128)S(1)}, u32[]{:S(2)}, u32[]{:S(2)}) collective-permute-start(f32[2,2,8,32,128]{4,3,2,1,0:T(8,128)S(1)} %join.6), channel_id=1, source_target_pairs={{0,2},{1,3},{2,0},{3,1},{4,6},{5,7},{6,4},{7,5},{8,10},{9,11},{10,... | collective-permute-start | bytes 1572872 | tf_op jit(solution)/shard_map/ppermute | solution.py:542
  65.2 39.8 %collective-permute-start.17 = (f32[3,32,32,128]{3,2,1,0:T(8,128)S(1)}, f32[3,32,32,128]{3,2,1,0:T(8,128)S(1)}, u32[]{:S(2)}, u32[]{:S(2)}) collective-permute-start(f32[3,32,32,128]{3,2,1,0:T(8,128)S(1)} %pack.8.refs_6_), channel_id=1, source_target_pairs={{0,16},{1,9},{2,18},{3,11},{4,20},{5,13},{6,22},{7,15},{8,24},{9,1... | collective-permute-start | bytes 4718600 | tf_op jit(solution)/shard_map/ppermute | solution.py:533
  67.4 7.3 %collective-permute-start.11 = (f32[2,2,8,32,128]{4,3,2,1,0:T(8,128)S(1)}, f32[2,2,8,32,128]{4,3,2,1,0:T(8,128)S(1)}, u32[]{:S(2)}, u32[]{:S(2)}) collective-permute-start(f32[2,2,8,32,128]{4,3,2,1,0:T(8,128)S(1)} %get-tuple-element.34), channel_id=1, source_target_pairs={{0,1},{1,0},{2,3},{3,2},{4,5},{5,4},{6,7},{7,6},{8,9},{9,8},{10,11... | collective-permute-start | bytes 1572872 | tf_op jit(solution)/shard_map/ppermute | solution.py:542
  72.1 14.9 %collective-permute-start.9 = (f32[1,32,32,128]{3,2,1,0:T(8,128)S(1)}, f32[1,32,32,128]{3,2,1,0:T(8,128)S(1)}, u32[]{:S(2)}, u32[]{:S(2)}) collective-permute-start(f32[1,32,32,128]{3,2,1,0:T(8,128)S(1)} %mix.7.refs_5_), channel_id=1, source_target_pairs={{0,8},{1,17},{2,10},{3,19},{4,12},{5,21},{6,14},{7,23},{8,0},{9,25... | collective-permute-start | bytes 1572872 | tf_op jit(solution)/shard_map/ppermute | solution.py:533
  72.6 26.9 %collective-permute-start.13 = (f32[2,4,128,128]{3,2,1,0:T(8,128)S(1)}, f32[2,4,128,128]{3,2,1,0:T(8,128)S(1)}, u32[]{:S(2)}, u32[]{:S(2)}) collective-permute-start(f32[2,4,128,128]{3,2,1,0:T(8,128)S(1)} %coefficients.3.refs_4_.refs_3_), channel_id=1, source_target_pairs={{0,4},{1,5},{2,6},{3,7},{4,0},{5,1},{6,2},{7,3},{8,12},{9,13},{10,... | collective-permute-start | bytes 1572872 | tf_op jit(solution)/shard_map/ppermute | solution.py:542
  74.8 27.6 %collective-permute-start.12 = (f32[2,2,8,32,128]{4,3,2,1,0:T(8,128)S(1)}, f32[2,2,8,32,128]{4,3,2,1,0:T(8,128)S(1)}, u32[]{:S(2)}, u32[]{:S(2)}) collective-permute-start(f32[2,2,8,32,128]{4,3,2,1,0:T(8,128)S(1)} %join.7), channel_id=1, source_target_pairs={{0,2},{1,3},{2,0},{3,1},{4,6},{5,7},{6,4},{7,5},{8,10},{9,11},{10,... | collective-permute-start | bytes 1572872 | tf_op jit(solution)/shard_map/ppermute | solution.py:542
  89.8 42.6 %collective-permute-start.10 = (f32[2,32,32,128]{3,2,1,0:T(8,128)S(1)}, f32[2,32,32,128]{3,2,1,0:T(8,128)S(1)}, u32[]{:S(2)}, u32[]{:S(2)}) collective-permute-start(f32[2,32,32,128]{3,2,1,0:T(8,128)S(1)} %pack.9.refs_8_), channel_id=1, source_target_pairs={{0,16},{1,9},{2,18},{3,11},{4,20},{5,13},{6,22},{7,15},{8,24},{9,1... | collective-permute-start | bytes 3145736 | tf_op jit(solution)/shard_map/ppermute | solution.py:533
  91.4 16.6 %collective-permute-start.15 = (f32[2,1,8,32,128]{4,3,2,1,0:T(8,128)S(1)}, f32[2,1,8,32,128]{4,3,2,1,0:T(8,128)S(1)}, u32[]{:S(2)}, u32[]{:S(2)}) collective-permute-start(f32[2,1,8,32,128]{4,3,2,1,0:T(8,128)S(1)} %get-tuple-element.37), channel_id=1, source_target_pairs={{0,1},{1,0},{2,3},{3,2},{4,5},{5,4},{6,7},{7,6},{8,9},{9,8},{10,11... | collective-permute-start | bytes 786440 | tf_op jit(solution)/shard_map/ppermute | solution.py:542
  104.9 25.0 %collective-permute-start.14 = (f32[2,4,128,128]{3,2,1,0:T(8,128)S(1)}, f32[2,4,128,128]{3,2,1,0:T(8,128)S(1)}, u32[]{:S(2)}, u32[]{:S(2)}) collective-permute-start(f32[2,4,128,128]{3,2,1,0:T(8,128)S(1)} %coefficients.4.refs_4_.refs_3_), channel_id=1, source_target_pairs={{0,4},{1,5},{2,6},{3,7},{4,0},{5,1},{6,2},{7,3},{8,12},{9,13},{10,... | collective-permute-start | bytes 1572872 | tf_op jit(solution)/shard_map/ppermute | solution.py:542
  107.5 64.5 %collective-permute-start.22 = (f32[3,32,32,128]{3,2,1,0:T(8,128)S(1)}, f32[3,32,32,128]{3,2,1,0:T(8,128)}, u32[]{:S(2)}, u32[]{:S(2)}) collective-permute-start(f32[3,32,32,128]{3,2,1,0:T(8,128)S(1)} %mix.8.refs_6_), channel_id=1, source_target_pairs={{0,8},{1,17},{2,10},{3,19},{4,12},{5,21},{6,14},{7,23},{8,0},{9,25... | collective-permute-start | bytes 4718600 | tf_op jit(solution)/shard_map/ppermute | solution.py:533
  108.0 14.9 %collective-permute-start.16 = (f32[2,1,8,32,128]{4,3,2,1,0:T(8,128)S(1)}, f32[2,1,8,32,128]{4,3,2,1,0:T(8,128)S(1)}, u32[]{:S(2)}, u32[]{:S(2)}) collective-permute-start(f32[2,1,8,32,128]{4,3,2,1,0:T(8,128)S(1)} %join.8), channel_id=1, source_target_pairs={{0,2},{1,3},{2,0},{3,1},{4,6},{5,7},{6,4},{7,5},{8,10},{9,11},{10,... | collective-permute-start | bytes 786440 | tf_op jit(solution)/shard_map/ppermute | solution.py:542
  110.7 35.1 %collective-permute-start.25 = (f32[2,2,8,32,128]{4,3,2,1,0:T(8,128)}, f32[2,2,8,32,128]{4,3,2,1,0:T(8,128)S(1)}, u32[]{:S(2)}, u32[]{:S(2)}) collective-permute-start(f32[2,2,8,32,128]{4,3,2,1,0:T(8,128)} %copy-done.13), channel_id=1, source_target_pairs={{0,2},{1,3},{2,0},{3,1},{4,6},{5,7},{6,4},{7,5},{8,10},{9,11},{10,... | collective-permute-start | bytes 1572872 | tf_op jit(solution)/shard_map/ppermute | solution.py:542
  132.4 23.9 %collective-permute-start.23 = (f32[2,2,8,32,128]{4,3,2,1,0:T(8,128)S(1)}, f32[2,2,8,32,128]{4,3,2,1,0:T(8,128)S(1)}, u32[]{:S(2)}, u32[]{:S(2)}) collective-permute-start(f32[2,2,8,32,128]{4,3,2,1,0:T(8,128)S(1)} %get-tuple-element.44), channel_id=1, source_target_pairs={{0,2},{1,3},{2,0},{3,1},{4,6},{5,7},{6,4},{7,5},{8,10},{9,11},{10,... | collective-permute-start | bytes 1572872 | tf_op jit(solution)/shard_map/ppermute | solution.py:542
  133.8 49.6 %collective-permute-start.18 = (f32[2,32,32,128]{3,2,1,0:T(8,128)S(1)}, f32[2,32,32,128]{3,2,1,0:T(8,128)S(1)}, u32[]{:S(2)}, u32[]{:S(2)}) collective-permute-start(f32[2,32,32,128]{3,2,1,0:T(8,128)S(1)} %mix.9.refs_8_), channel_id=1, source_target_pairs={{0,8},{1,17},{2,10},{3,19},{4,12},{5,21},{6,14},{7,23},{8,0},{9,25... | collective-permute-start | bytes 3145736 | tf_op jit(solution)/shard_map/ppermute | solution.py:533
  134.5 21.9 %collective-permute-start.19 = (f32[1,4,128,128]{3,2,1,0:T(8,128)S(1)}, f32[1,4,128,128]{3,2,1,0:T(8,128)S(1)}, u32[]{:S(2)}, u32[]{:S(2)}) collective-permute-start(f32[1,4,128,128]{3,2,1,0:T(8,128)S(1)} %coefficients.5.refs_8_.refs_3_), channel_id=1, source_target_pairs={{0,4},{1,5},{2,6},{3,7},{4,0},{5,1},{6,2},{7,3},{8,12},{9,13},{10,... | collective-permute-start | bytes 786440 | tf_op jit(solution)/shard_map/ppermute | solution.py:542
  145.9 21.1 %collective-permute-start.26 = (f32[2,2,8,32,128]{4,3,2,1,0:T(8,128)S(1)}, f32[2,2,8,32,128]{4,3,2,1,0:T(8,128)S(1)}, u32[]{:S(2)}, u32[]{:S(2)}) collective-permute-start(f32[2,2,8,32,128]{4,3,2,1,0:T(8,128)S(1)} %join.11), channel_id=1, source_target_pairs={{0,1},{1,0},{2,3},{3,2},{4,5},{5,4},{6,7},{7,6},{8,9},{9,8},{10,11... | collective-permute-start | bytes 1572872 | tf_op jit(solution)/shard_map/ppermute | solution.py:542
  156.3 13.2 %collective-permute-start.24 = (f32[2,2,8,32,128]{4,3,2,1,0:T(8,128)S(1)}, f32[2,2,8,32,128]{4,3,2,1,0:T(8,128)S(1)}, u32[]{:S(2)}, u32[]{:S(2)}) collective-permute-start(f32[2,2,8,32,128]{4,3,2,1,0:T(8,128)S(1)} %join.10), channel_id=1, source_target_pairs={{0,1},{1,0},{2,3},{3,2},{4,5},{5,4},{6,7},{7,6},{8,9},{9,8},{10,11... | collective-permute-start | bytes 1572872 | tf_op jit(solution)/shard_map/ppermute | solution.py:542
  158.1 8.8 %collective-permute-start.20 = (f32[2,1,8,32,128]{4,3,2,1,0:T(8,128)S(1)}, f32[2,1,8,32,128]{4,3,2,1,0:T(8,128)S(1)}, u32[]{:S(2)}, u32[]{:S(2)}) collective-permute-start(f32[2,1,8,32,128]{4,3,2,1,0:T(8,128)S(1)} %get-tuple-element.42), channel_id=1, source_target_pairs={{0,2},{1,3},{2,0},{3,1},{4,6},{5,7},{6,4},{7,5},{8,10},{9,11},{10,... | collective-permute-start | bytes 786440 | tf_op jit(solution)/shard_map/ppermute | solution.py:542
  166.9 14.7 %collective-permute-start.21 = (f32[2,1,8,32,128]{4,3,2,1,0:T(8,128)S(1)}, f32[2,1,8,32,128]{4,3,2,1,0:T(8,128)S(1)}, u32[]{:S(2)}, u32[]{:S(2)}) collective-permute-start(f32[2,1,8,32,128]{4,3,2,1,0:T(8,128)S(1)} %join.9), channel_id=1, source_target_pairs={{0,1},{1,0},{2,3},{3,2},{4,5},{5,4},{6,7},{7,6},{8,9},{9,8},{10,11... | collective-permute-start | bytes 786440 | tf_op jit(solution)/shard_map/ppermute | solution.py:542
  (22 other events, 262.2 us)

commit v6 on v3

--- a/solution.py
+++ b/solution.py
@@ -9,41 +9,53 @@
 from jax.sharding import PartitionSpec as P
 
 QUAD = 4
-NEAR_SIZES = (2, 2, 1)
-FAR_SIZES = (3, 2)
+NEAR_SIZES = (1, 2, 1, 1)
+FAR_SIZES = (2, 1, 2)
 ORDER = (
     ("pack", 0),
     ("pack", 1),
+    ("pack", 2),
     ("local", 0),
     ("mix", 0),
     ("mix", 1),
+    ("mix", 2),
+    ("pack", 6),
     ("spread", 0),
-    ("pack", 2),
+    ("pack", 3),
     ("join", 0),
+    ("pack", 4),
     ("spread", 1),
-    ("pack", 3),
     ("coef", 0),
     ("join", 1),
-    ("mix", 2),
+    ("mix", 4),
+    ("mix", 3),
+    ("pack", 5),
     ("spread", 2),
-    ("pack", 4),
     ("filter", 0),
+    ("join", 2),
     ("coef", 1),
-    ("join", 2),
-    ("mix", 3),
+    ("spread", 3),
+    ("mix", 6),
     ("back", 0),
+    ("join", 3),
     ("coef", 2),
+    ("filter", 1),
+    ("mix", 5),
+    ("far", 4),
+    ("coef", 3),
+    ("filter", 2),
     ("near", 0),
-    ("filter", 1),
-    ("mix", 4),
+    ("filter", 3),
+    ("back", 2),
     ("back", 1),
+    ("far", 5),
+    ("near", 2),
+    ("far", 6),
     ("near", 1),
-    ("filter", 2),
-    ("far", 3),
-    ("back", 2),
-    ("near", 2),
-    ("far", 4),
+    ("back", 3),
+    ("near", 3),
 )
+EDGES = tuple(zip(ORDER[:-1], ORDER[1:]))
 SMEM = pl.BlockSpec(memory_space=pltpu.SMEM)
 ANY = pl.BlockSpec(memory_space=pl.ANY)
 COST = pl.CostEstimate(flops=0, bytes_accessed=0, transcendentals=0)
@@ -128,7 +140,7 @@
 
 
 def call(kernel, name, token, grid, inputs, in_specs, out_specs, out_shape, scratch=(), alias=None):
-    extra = [] if token is None else [token]
+    extra = [t for t in token or () if all(t is not x for x in inputs)]
     return pl.pallas_call(
         lambda *refs: kernel(*refs[: len(inputs)], *refs[len(inputs) + len(extra) :]),
         grid=grid,
@@ -194,6 +206,13 @@
     def cell(f, k):
         return pick(adj[f, max(0, min(k, planes - 1))], before[f, 0], after[f, 0], f, k)
 
+    walls = []
+    for f in range(fields):
+        opens = [(1 - flags[f, i]).astype(jnp.float32) for i in range(3)]
+        wall = jnp.where(col == 0, opens[0], 0.0)
+        wall = wall + jnp.where(col == cells - 1, opens[1], 0.0)
+        walls.append(wall + jnp.where(row == rows - 1, opens[2], 0.0))
+
     for k in range(planes):
         m = visc(k)
         up = ring * (m + visc(k + 1))
@@ -205,11 +224,7 @@
         diag = up + down + outer + inner + east + west
         for f in range(fields):
             p = adj[f, k]
-            opens = [(1 - flags[f, i]).astype(jnp.float32) for i in range(3)]
-            wall = jnp.where(col == 0, opens[0], 0.0)
-            wall = wall + jnp.where(col == cells - 1, opens[1], 0.0)
-            wall = wall + jnp.where(row == rows - 1, opens[2], 0.0)
-            flux = (diag + wall * m) * p
+            flux = (diag + walls[f] * m) * p
             flux = flux - up * cell(f, k + 1) - down * cell(f, k - 1)
             flux = flux - outer * pltpu.roll(p, rows - 1, 0) - inner * pltpu.roll(p, 1, 0)
             flux = flux - east * pltpu.roll(p, cells - 1, 1) - west * pltpu.roll(p, 1, 1)
@@ -367,7 +382,7 @@
         )
 
     def table_call(self, kernel, name, fields, inputs, in_specs, out_specs, out_shape, scratch, token):
-        extra = [] if token is None else [token]
+        extra = [t for t in token or () if all(t is not x for x in inputs)]
         count = len(inputs)
         return pl.pallas_call(
             lambda *refs: kernel(*refs[: count + 1], *refs[count + 1 + len(extra) :]),
@@ -559,33 +574,34 @@
     groups = [(lo, hi, 0) for lo, hi in spans(NEAR_SIZES, fields)]
     groups += [(lo, hi, 1) for lo, hi in spans(FAR_SIZES, fields)]
     first, others, parts, own, done = {}, {}, {}, {}, {}
-    token, local, held, halos = None, None, None, None
+    made, local, held, halos = {}, None, None, None
     for step, g in ORDER:
         lo, hi, index = groups[g]
+        token = [made[before] for before, after in EDGES if after == (step, g)]
         if step == "pack":
             packed = pack(center, viscosity, lo, hi, index, near, halos is None, token)
-            token = packed[0]
+            made[step, g] = packed[0]
             first[g] = to_first(packed[0])
             if halos is None:
                 halos = ring(packed[1], 1), ring(packed[2], -1)
         elif step == "local":
-            local = token = local_part(
+            local = made[step, g] = local_part(
                 center, source[0], viscosity, kappa, coupling, bc_flags, *halos, token
             )
         elif step == "mix":
             mixed = plan.mix(center, first[g], lo, hi, index, token)
-            token = mixed[0]
+            made[step, g] = mixed[0]
             others[g] = [first[g]] + [to_later(x, s + 1) for s, x in enumerate(mixed)]
         elif step == "spread":
             mine, core, chip = plan.spread(local, others[g], lo, hi, token)
-            token = mine
+            made[step, g] = mine
             parts[g] = mine, to_sector(core, 1), chip
         elif step == "join":
             mine, core, chip = parts[g]
-            token = plan.join(chip, core, token)
-            parts[g] = mine, core, to_sector(token, 2)
+            made[step, g] = plan.join(chip, core, token)
+            parts[g] = mine, core, to_sector(made[step, g], 2)
         elif step == "coef":
-            part = token = plan.coefficients(*parts[g], token)
+            part = made[step, g] = plan.coefficients(*parts[g], token)
             stride = QUAD
             while 2 * stride < sectors:
                 part = part + to_sector(part, stride)
@@ -594,18 +610,16 @@
             own[g] = part, other
         elif step == "filter":
             mine, core, chip = plan.filtered(*own[g], *parts[g], token)
-            token = mine
+            made[step, g] = mine
             done[g] = mine, core, to_sector(chip, 2)
         elif step == "back":
             mine, core, chip = done[g]
-            token = plan.join(core, chip, token)
-            done[g] = mine, to_sector(token, 1), chip
+            made[step, g] = plan.join(core, chip, token)
+            done[g] = mine, to_sector(made[step, g], 1), chip
         elif step == "near":
-            held = token = plan.place_near(*done[g], held, lo, hi, None if token is held else token)
+            held = made[step, g] = plan.place_near(*done[g], held, lo, hi, token)
         else:
-            held = token = plan.place_far(
-                local, others[g], held, lo, hi, None if token is held else token
-            )
+            held = made[step, g] = plan.place_far(local, others[g], held, lo, hi, token)
     return held[None]
 
 

time: 190 us -> 161 us (0.85)
  waiting for transfers between devices: 96.2 us -> 46.3 us
  starting transfers between devices: 27.4 us -> 37.7 us
  Pallas kernels: 61.7 us -> 70.1 us
    ppermute x15 -> x20, waiting for transfers between devices: 64.5 us -> 26.4 us  [to_sector(): return lax.ppermute(x, 'space', [(i, i ^ k) for i in range(sectors)])]
    ppermute x10 -> x14, waiting for transfers between devices: 28.1 us -> 20 us  [to_partner(): return lax.ppermute(x, ('inst', 'space'), pairs)]
    pallas_call x25 -> x34, Pallas kernels: 48 us -> 54.2 us  [call(): pl.pallas_call(lambda *refs: kernel(*refs[:len(inputs)], *refs[len(inputs...]
    ppermute x10 -> x14, starting transfers between devices: 13.8 us -> 19.7 us  [to_partner(): return lax.ppermute(x, ('inst', 'space'), pairs)]
    ppermute x15 -> x20, starting transfers between devices: 10.1 us -> 14.5 us  [to_sector(): return lax.ppermute(x, 'space', [(i, i ^ k) for i in range(sectors)])]
    ppermute x2, waiting for transfers between devices: 3.5 us -> 0.01 us  [ring(): lax.ppermute(x, 'space', [(i, (i + step) % sectors) for i in range(sector...]
    pallas_call x6 -> x8, Pallas kernels: 13.7 us -> 15.9 us  [table_call(): pl.pallas_call(lambda *refs: kernel(*refs[:count + 1], *refs[count + 1 +...]
    unnamed x39 -> x41, local copies, waits for them, and re-layouts: 3.89 us -> 4.53 us
  transfers between devices with their start and end apart: 27 -> 36, of which waited for: 14 -> 12; matrix products, arithmetic and copies ran while one was open for 0% -> 1% of each run, Pallas kernels for 30% -> 41%
where the time goes in v6:
time: 161 us; the launch traced here: 160 us
  Pallas kernels  70.1 us (44%)
  waiting for transfers between devices  46.3 us (29%)
  starting transfers between devices  37.7 us (23%)
  local copies, waits for them, and re-layouts  4.53 us (3%)
    pallas_call x34, Pallas kernels, call(): pl.pallas_call(lambda *refs: kernel(*refs[:len(inputs)], *refs[len(inputs...  54.2 us
    ppermute x20, waiting for transfers between devices, to_sector(): return lax.ppermute(x, 'space', [(i, i ^ k) for i in range(sectors)])  26.4 us
    ppermute x14, waiting for transfers between devices, to_partner(): return lax.ppermute(x, ('inst', 'space'), pairs)  20 us
    ppermute x14, starting transfers between devices, to_partner(): return lax.ppermute(x, ('inst', 'space'), pairs)  19.7 us
    pallas_call x8, Pallas kernels, table_call(): pl.pallas_call(lambda *refs: kernel(*refs[:count + 1], *refs[count + 1 +...  15.9 us
    ppermute x20, starting transfers between devices, to_sector(): return lax.ppermute(x, 'space', [(i, i ^ k) for i in range(sectors)])  14.5 us
    unnamed x41, local copies, waits for them, and re-layouts  4.53 us
    ppermute x2, starting transfers between devices, ring(): lax.ppermute(x, 'space', [(i, (i + step) % sectors) for i in range(sector...  3.54 us
  transfers between devices with their start and end apart: 36, of which 12 were waited for; matrix products, arithmetic and copies ran while one was open for 1% of the time, Pallas kernels for 41%

profile of v6, /device:TPU:0, one launch (start us, length us, event | category | flops | bytes accessed | tf_op | source)
XLA Modules:
  0.0 159.8 jit_solution(17504428761806881082)
XLA Ops:
  1.2 2.1 %pack.7 = (f32[1,32,32,128]{3,2,1,0:T(8,128)}, f32[6,1,64,128]{3,2,1,0:T(8,128)}, f32[6,1,64,128]{3,2,1,0:T(8,128)}) custom-call(f32[5,32,64,128]{3,2,1,0:T(8,128)} %bitcast.5, f32[5,32,64,128]{3,2,1,0:T(8,128)} %bitcast.6, f32[32,64,128]{2,1,0:T(8,128)S(1)} %copy-done.3, f32[5,32,64,128]{3,2,1,0:T(8,128)} %bitcast.7, f32[32,64,128]{2,1,0:T(8,128)S(1)} %copy-done.3), custom_call_target="tpu_custom_call" | custom-call | tf_op jit(solution)/shard_map/pack/pallas_call | solution.py:144
  4.7 3.0 %collective-permute-start.5 = (f32[2,32,32,128]{3,2,1,0:T(8,128)S(1)}, f32[2,32,32,128]{3,2,1,0:T(8,128)S(1)}, u32[]{:S(2)}, u32[]{:S(2)}) collective-permute-start(f32[2,32,32,128]{3,2,1,0:T(8,128)S(1)} %pack.8.refs_1_), channel_id=1, source_target_pairs={{0,16},{1,9},{2,18},{3,11},{4,20},{5,13},{6,22},{7,15},{8,24},{9,1... | collective-permute-start | bytes 3145736 | tf_op jit(solution)/shard_map/ppermute | solution.py:545
  7.8 3.5 %collective-permute-start.1 = (f32[6,1,64,128]{3,2,1,0:T(8,128)}, f32[6,1,64,128]{3,2,1,0:T(8,128)S(1)}, u32[]{:S(2)}, u32[]{:S(2)}) collective-permute-start(f32[6,1,64,128]{3,2,1,0:T(8,128)} %get-tuple-element.33), channel_id=1, source_target_pairs={{0,7},{1,0},{2,1},{3,2},{4,3},{5,4},{6,5},{7,6},{8,15},{9,8},{10,9... | collective-permute-start | bytes 589832 | tf_op jit(solution)/shard_map/ppermute | solution.py:557
  13.2 1.9 %collective-permute-start.4 = (f32[1,32,32,128]{3,2,1,0:T(8,128)}, f32[1,32,32,128]{3,2,1,0:T(8,128)}, u32[]{:S(2)}, u32[]{:S(2)}) collective-permute-start(f32[1,32,32,128]{3,2,1,0:T(8,128)} %pack.9.refs_12_), channel_id=1, source_target_pairs={{0,16},{1,9},{2,18},{3,11},{4,20},{5,13},{6,22},{7,15},{8,24},{9,1... | collective-permute-start | bytes 1572872 | tf_op jit(solution)/shard_map/ppermute | solution.py:545
  16.7 12.2 %local_part.1.refs_4_.refs_2_ = f32[5,32,64,128]{3,2,1,0:T(8,128)} custom-call(f32[5,5]{1,0:T(8,128)S(1)} %copy-done.14, f32[5]{0:T(128)S(1)} %copy-done.15, s32[5,3]{1,0:T(8,128)S(1)} %copy.26.refs_2_, f32[5,32,64,128]{3,2,1,0:T(8,128)} %bitcast.10, f32[5,32,64,128]{3,2,1,0:T(8,128)} %bitcast.11, f32[5,32,64,128]{3,2,1,0:T(8,128)} %bitcast.12, ...), custom_call_target="tpu_custom_call" | custom-call | tf_op jit(solution)/shard_map/local_part/pallas_call | solution.py:144
  35.1 2.2 %pack.10.refs_5_ = f32[2,32,32,128]{3,2,1,0:T(8,128)} custom-call(f32[5,32,64,128]{3,2,1,0:T(8,128)} %bitcast.16, f32[1,32,32,128]{3,2,1,0:T(8,128)S(1)} %mix.9.refs_1_), custom_call_target="tpu_custom_call" | custom-call | tf_op jit(solution)/shard_map/pack/pallas_call | solution.py:144
  37.3 2.1 %collective-permute-done.3.refs_4_ = f32[1,32,32,128]{3,2,1,0:T(8,128)S(1)} collective-permute-done((f32[1,32,32,128]{3,2,1,0:T(8,128)S(1)}, f32[1,32,32,128]{3,2,1,0:T(8,128)S(1)}, u32[]{:S(2)}, u32[]{:S(2)}) %collective-permute-start.3) | collective-permute-done | bytes 524320 | tf_op jit(solution)/shard_map/ppermute | solution.py:545
  46.7 7.4 %collective-permute-done.9.refs_4_ = f32[2,32,32,128]{3,2,1,0:T(8,128)S(1)} collective-permute-done((f32[2,32,32,128]{3,2,1,0:T(8,128)S(1)}, f32[2,32,32,128]{3,2,1,0:T(8,128)S(1)}, u32[]{:S(2)}, u32[]{:S(2)}) %collective-permute-start.9) | collective-permute-done | bytes 1048608 | tf_op jit(solution)/shard_map/ppermute | solution.py:545
  54.1 2.1 %spread.5 = (f32[2,8,32,128]{3,2,1,0:T(8,128)S(1)}, f32[2,2,8,32,128]{4,3,2,1,0:T(8,128)S(1)}, f32[2,2,8,32,128]{4,3,2,1,0:T(8,128)S(1)}) custom-call(s32[22]{0:T(128)S(1)} %pad_add_fusion.refs_0_, f32[71]{0:T(128)S(1)} %copy-done.13, f32[5,32,64,128]{3,2,1,0:T(8,128)} %local_part.1.refs_4_.refs_2_, f32[2,32,32,128]{3,2,1,0:T(8,128)S(1)} %collective-permute-done.5.refs_3_, ...), custom_call_target="tpu_custom_call" | custom-call | tf_op jit(solution)/shard_map/spread/pallas_call | solution.py:144
  65.7 7.7 %collective-permute-done.6.refs_3_ = f32[1,32,32,128]{3,2,1,0:T(8,128)S(1)} collective-permute-done((f32[1,32,32,128]{3,2,1,0:T(8,128)S(1)}, f32[1,32,32,128]{3,2,1,0:T(8,128)S(1)}, u32[]{:S(2)}, u32[]{:S(2)}) %collective-permute-start.6) | collective-permute-done | bytes 524320 | tf_op jit(solution)/shard_map/ppermute | solution.py:545
  76.4 1.9 %pack.13.refs_5_ = f32[1,32,32,128]{3,2,1,0:T(8,128)} custom-call(f32[5,32,64,128]{3,2,1,0:T(8,128)} %bitcast.20, f32[1,32,32,128]{3,2,1,0:T(8,128)S(1)} %mix.11.refs_1_), custom_call_target="tpu_custom_call" | custom-call | tf_op jit(solution)/shard_map/pack/pallas_call | solution.py:144
  83.0 2.4 %coefficients.5.refs_5_.refs_3_ = f32[2,4,128,128]{3,2,1,0:T(8,128)S(1)} custom-call(s32[22]{0:T(128)S(1)} %pad_add_fusion.refs_0_, f32[71]{0:T(128)S(1)} %copy-done.13, f32[2,16,128,128]{3,2,1,0:T(8,128)S(1)} %copy-done.2, f32[2,8,32,128]{3,2,1,0:T(8,128)S(1)} %get-tuple-element.40.refs_6_.refs_3_.refs_5_, ...), custom_call_target="tpu_custom_call" | custom-call | tf_op jit(solution)/shard_map/coefficients/pallas_call | solution.py:387
  85.5 2.3 %collective-permute-start.23 = (f32[2,4,128,128]{3,2,1,0:T(8,128)S(1)}, f32[2,4,128,128]{3,2,1,0:T(8,128)S(1)}, u32[]{:S(2)}, u32[]{:S(2)}) collective-permute-start(f32[2,4,128,128]{3,2,1,0:T(8,128)S(1)} %coefficients.5.refs_5_.refs_3_), channel_id=1, source_target_pairs={{0,4},{1,5},{2,6},{3,7},{4,0},{5,1},{6,2},{7,3},{8,12},{9,13},{10,... | collective-permute-start | bytes 1572872 | tf_op jit(solution)/shard_map/ppermute | solution.py:554
  87.7 1.9 %collective-permute-done.12.refs_4_ = f32[1,32,32,128]{3,2,1,0:T(8,128)} collective-permute-done((f32[1,32,32,128]{3,2,1,0:T(8,128)S(1)}, f32[1,32,32,128]{3,2,1,0:T(8,128)}, u32[]{:S(2)}, u32[]{:S(2)}) %collective-permute-start.12) | collective-permute-done | bytes 524320 | tf_op jit(solution)/shard_map/ppermute | solution.py:545
  96.8 9.7 %collective-permute-done.24.refs_5_.refs_7_ = f32[2,1,8,32,128]{4,3,2,1,0:T(8,128)S(1)} collective-permute-done((f32[2,1,8,32,128]{4,3,2,1,0:T(8,128)S(1)}, f32[2,1,8,32,128]{4,3,2,1,0:T(8,128)S(1)}, u32[]{:S(2)}, u32[]{:S(2)}) %collective-permute-start.24) | collective-permute-done | bytes 262176 | tf_op jit(solution)/shard_map/ppermute | solution.py:554
  108.2 3.2 %collective-permute-start.27 = (f32[1,4,128,128]{3,2,1,0:T(8,128)S(1)}, f32[1,4,128,128]{3,2,1,0:T(8,128)S(1)}, u32[]{:S(2)}, u32[]{:S(2)}) collective-permute-start(f32[1,4,128,128]{3,2,1,0:T(8,128)S(1)} %coefficients.6.refs_8_.refs_3_), channel_id=1, source_target_pairs={{0,4},{1,5},{2,6},{3,7},{4,0},{5,1},{6,2},{7,3},{8,12},{9,13},{10,... | collective-permute-start | bytes 786440 | tf_op jit(solution)/shard_map/ppermute | solution.py:554
  112.5 3.2 %filtered.5 = (f32[2,8,32,128]{3,2,1,0:T(8,128)S(1)}, f32[2,2,8,32,128]{4,3,2,1,0:T(8,128)S(1)}, f32[2,2,8,32,128]{4,3,2,1,0:T(8,128)}) custom-call(s32[22]{0:T(128)S(1)} %pad_add_fusion.refs_0_, f32[71]{0:T(128)S(1)} %copy-done.13, f32[2,16,128,128]{3,2,1,0:T(8,128)S(1)} %copy-done.1, f32[2,4,128,128]{3,2,1,0:T(8,128)S(1)} %coefficients.5.refs_5_.refs_3_, ...), custom_call_target="tpu_custom_call" | custom-call | tf_op jit(solution)/shard_map/filtered/pallas_call | solution.py:387
  118.5 2.4 %place_far.3.refs_6_.refs_5_ = f32[5,32,64,128]{3,2,1,0:T(8,128)} custom-call(s32[22]{0:T(128)S(1)} %pad_add_fusion.refs_0_, f32[71]{0:T(128)S(1)} %copy-done.13, f32[5,32,64,128]{3,2,1,0:T(8,128)} %local_part.1.refs_4_.refs_2_, f32[2,32,32,128]{3,2,1,0:T(8,128)S(1)} %collective-permute-done.8.refs_3_, f32[2,32,32,128]{3,2,1,0:T(8,128)} %collective-permute-done.21.refs_4_, ...), custom_call_target="tpu_custom_call" | custom-call | tf_op jit(solution)/shard_map/place_far/pallas_call | solution.py:144
  130.0 8.1 %collective-permute-done.25.refs_4_ = f32[1,4,128,128]{3,2,1,0:T(8,128)S(1)} collective-permute-done((f32[1,4,128,128]{3,2,1,0:T(8,128)S(1)}, f32[1,4,128,128]{3,2,1,0:T(8,128)S(1)}, u32[]{:S(2)}, u32[]{:S(2)}) %collective-permute-start.25) | collective-permute-done | bytes 262176 | tf_op jit(solution)/shard_map/ppermute | solution.py:554
  139.8 4.6 %collective-permute-done.30.refs_1_.refs_4_ = f32[2,1,8,32,128]{4,3,2,1,0:T(8,128)S(1)} collective-permute-done((f32[2,1,8,32,128]{4,3,2,1,0:T(8,128)S(1)}, f32[2,1,8,32,128]{4,3,2,1,0:T(8,128)S(1)}, u32[]{:S(2)}, u32[]{:S(2)}) %collective-permute-start.30) | collective-permute-done | bytes 262176 | tf_op jit(solution)/shard_map/ppermute | solution.py:554
  145.1 2.0 %place_far.4.refs_5_ = f32[5,32,64,128]{3,2,1,0:T(8,128)} custom-call(s32[22]{0:T(128)S(1)} %pad_add_fusion.refs_0_, f32[71]{0:T(128)S(1)} %copy-done.13, f32[5,32,64,128]{3,2,1,0:T(8,128)} %local_part.1.refs_4_.refs_2_, f32[1,32,32,128]{3,2,1,0:T(8,128)S(1)} %copy-done.8, ...), custom_call_target="tpu_custom_call", output_to_operand_aliasing={{}: (5, {})} | custom-call | tf_op jit(solution)/shard_map/place_far/pallas_call | solution.py:144
  148.9 2.5 %place_far.5.refs_5_ = f32[5,32,64,128]{3,2,1,0:T(8,128)} custom-call(s32[22]{0:T(128)S(1)} %pad_add_fusion.refs_0_, f32[71]{0:T(128)S(1)} %copy-done.13, f32[5,32,64,128]{3,2,1,0:T(8,128)} %local_part.1.refs_4_.refs_2_, f32[2,32,32,128]{3,2,1,0:T(8,128)S(1)} %collective-permute-done.19.refs_3_, ...), custom_call_target="tpu_custom_call", output_to_operand_aliasing={{}: (5, {})} | custom-call | tf_op jit(solution)/shard_map/place_far/pallas_call | solution.py:144
  151.4 2.5 %place_near.6.refs_2_.refs_5_ = f32[5,32,64,128]{3,2,1,0:T(8,128)} custom-call(s32[22]{0:T(128)S(1)} %pad_add_fusion.refs_0_, f32[71]{0:T(128)S(1)} %copy-done.13, f32[2,8,32,128]{3,2,1,0:T(8,128)S(1)} %get-tuple-element.50.refs_4_.refs_2_, f32[2,2,8,32,128]{4,3,2,1,0:T(8,128)S(1)} %collective-permute-done.31.refs_3_, ...), custom_call_target="tpu_custom_call", output_to_operand_aliasing={{}: (5, {})} | custom-call | tf_op jit(solution)/shard_map/place_near/pallas_call | solution.py:144
  153.8 2.5 %copy-done = f32[5,32,64,128]{3,2,1,0:T(8,128)S(1)} copy-done((f32[5,32,64,128]{3,2,1,0:T(8,128)S(1)}, f32[5,32,64,128]{3,2,1,0:T(8,128)}, u32[]{:S(2)}) %copy-start) | copy-done | bytes 5242904
  (133 shorter events, 65.9 us)
Async XLA Ops:
  4.7 27.0 %collective-permute-start.5 = (f32[2,32,32,128]{3,2,1,0:T(8,128)S(1)}, f32[2,32,32,128]{3,2,1,0:T(8,128)S(1)}, u32[]{:S(2)}, u32[]{:S(2)}) collective-permute-start(f32[2,32,32,128]{3,2,1,0:T(8,128)S(1)} %pack.8.refs_1_), channel_id=1, source_target_pairs={{0,16},{1,9},{2,18},{3,11},{4,20},{5,13},{6,22},{7,15},{8,24},{9,1... | collective-permute-start | bytes 3145736 | tf_op jit(solution)/shard_map/ppermute | solution.py:545
  7.7 21.1 %collective-permute-start.2 = (f32[1,32,32,128]{3,2,1,0:T(8,128)}, f32[1,32,32,128]{3,2,1,0:T(8,128)}, u32[]{:S(2)}, u32[]{:S(2)}) collective-permute-start(f32[1,32,32,128]{3,2,1,0:T(8,128)} %get-tuple-element.34.refs_1_), channel_id=1, source_target_pairs={{0,16},{1,9},{2,18},{3,11},{4,20},{5,13},{6,22},{7,15},{8,24},{9,1... | collective-permute-start | bytes 1572872 | tf_op jit(solution)/shard_map/ppermute | solution.py:545
  13.2 20.4 %collective-permute-start.4 = (f32[1,32,32,128]{3,2,1,0:T(8,128)}, f32[1,32,32,128]{3,2,1,0:T(8,128)}, u32[]{:S(2)}, u32[]{:S(2)}) collective-permute-start(f32[1,32,32,128]{3,2,1,0:T(8,128)} %pack.9.refs_12_), channel_id=1, source_target_pairs={{0,16},{1,9},{2,18},{3,11},{4,20},{5,13},{6,22},{7,15},{8,24},{9,1... | collective-permute-start | bytes 1572872 | tf_op jit(solution)/shard_map/ppermute | solution.py:545
  33.0 21.1 %collective-permute-start.9 = (f32[2,32,32,128]{3,2,1,0:T(8,128)S(1)}, f32[2,32,32,128]{3,2,1,0:T(8,128)S(1)}, u32[]{:S(2)}, u32[]{:S(2)}) collective-permute-start(f32[2,32,32,128]{3,2,1,0:T(8,128)S(1)} %mix.8.refs_4_), channel_id=1, source_target_pairs={{0,8},{1,17},{2,10},{3,19},{4,12},{5,21},{6,14},{7,23},{8,0},{9,25... | collective-permute-start | bytes 3145736 | tf_op jit(solution)/shard_map/ppermute | solution.py:545
  44.1 19.7 %collective-permute-start.8 = (f32[2,32,32,128]{3,2,1,0:T(8,128)S(1)}, f32[2,32,32,128]{3,2,1,0:T(8,128)S(1)}, u32[]{:S(2)}, u32[]{:S(2)}) collective-permute-start(f32[2,32,32,128]{3,2,1,0:T(8,128)S(1)} %pack.12.refs_5_), channel_id=1, source_target_pairs={{0,16},{1,9},{2,18},{3,11},{4,20},{5,13},{6,22},{7,15},{8,24},{9,1... | collective-permute-start | bytes 3145736 | tf_op jit(solution)/shard_map/ppermute | solution.py:545
  45.9 13.8 %collective-permute-start.11 = (f32[2,1,8,32,128]{4,3,2,1,0:T(8,128)S(1)}, f32[2,1,8,32,128]{4,3,2,1,0:T(8,128)S(1)}, u32[]{:S(2)}, u32[]{:S(2)}) collective-permute-start(f32[2,1,8,32,128]{4,3,2,1,0:T(8,128)S(1)} %join.8.refs_1_), channel_id=1, source_target_pairs={{0,2},{1,3},{2,0},{3,1},{4,6},{5,7},{6,4},{7,5},{8,10},{9,11},{10,... | collective-permute-start | bytes 786440 | tf_op jit(solution)/shard_map/ppermute | solution.py:554
  56.4 17.0 %collective-permute-start.6 = (f32[1,32,32,128]{3,2,1,0:T(8,128)S(1)}, f32[1,32,32,128]{3,2,1,0:T(8,128)S(1)}, u32[]{:S(2)}, u32[]{:S(2)}) collective-permute-start(f32[1,32,32,128]{3,2,1,0:T(8,128)S(1)} %pack.11.refs_2_), channel_id=1, source_target_pairs={{0,16},{1,9},{2,18},{3,11},{4,20},{5,13},{6,22},{7,15},{8,24},{9,1... | collective-permute-start | bytes 1572872 | tf_op jit(solution)/shard_map/ppermute | solution.py:545
  58.2 20.1 %collective-permute-start.14 = (f32[1,32,32,128]{3,2,1,0:T(8,128)S(1)}, f32[1,32,32,128]{3,2,1,0:T(8,128)S(1)}, u32[]{:S(2)}, u32[]{:S(2)}) collective-permute-start(f32[1,32,32,128]{3,2,1,0:T(8,128)S(1)} %mix.9.refs_1_), channel_id=1, source_target_pairs={{0,8},{1,17},{2,10},{3,19},{4,12},{5,21},{6,14},{7,23},{8,0},{9,25... | collective-permute-start | bytes 1572872 | tf_op jit(solution)/shard_map/ppermute | solution.py:545
  59.7 33.1 %collective-permute-start.19 = (f32[2,32,32,128]{3,2,1,0:T(8,128)}, f32[2,32,32,128]{3,2,1,0:T(8,128)S(1)}, u32[]{:S(2)}, u32[]{:S(2)}) collective-permute-start(f32[2,32,32,128]{3,2,1,0:T(8,128)} %pack.10.refs_5_), channel_id=1, source_target_pairs={{0,16},{1,9},{2,18},{3,11},{4,20},{5,13},{6,22},{7,15},{8,24},{9,1... | collective-permute-start | bytes 3145736 | tf_op jit(solution)/shard_map/ppermute | solution.py:545
  61.9 18.6 %collective-permute-start.16 = (f32[1,4,128,128]{3,2,1,0:T(8,128)S(1)}, f32[1,4,128,128]{3,2,1,0:T(8,128)S(1)}, u32[]{:S(2)}, u32[]{:S(2)}) collective-permute-start(f32[1,4,128,128]{3,2,1,0:T(8,128)S(1)} %coefficients.4.refs_2_.refs_3_), channel_id=1, source_target_pairs={{0,4},{1,5},{2,6},{3,7},{4,0},{5,1},{6,2},{7,3},{8,12},{9,13},{10,... | collective-permute-start | bytes 786440 | tf_op jit(solution)/shard_map/ppermute | solution.py:554
  63.8 19.2 %collective-permute-start.13 = (f32[2,2,8,32,128]{4,3,2,1,0:T(8,128)S(1)}, f32[2,2,8,32,128]{4,3,2,1,0:T(8,128)S(1)}, u32[]{:S(2)}, u32[]{:S(2)}) collective-permute-start(f32[2,2,8,32,128]{4,3,2,1,0:T(8,128)S(1)} %join.9.refs_4_), channel_id=1, source_target_pairs={{0,2},{1,3},{2,0},{3,1},{4,6},{5,7},{6,4},{7,5},{8,10},{9,11},{10,... | collective-permute-start | bytes 1572872 | tf_op jit(solution)/shard_map/ppermute | solution.py:554
  74.6 15.0 %collective-permute-start.12 = (f32[1,32,32,128]{3,2,1,0:T(8,128)S(1)}, f32[1,32,32,128]{3,2,1,0:T(8,128)}, u32[]{:S(2)}, u32[]{:S(2)}) collective-permute-start(f32[1,32,32,128]{3,2,1,0:T(8,128)S(1)} %mix.11.refs_1_), channel_id=1, source_target_pairs={{0,8},{1,17},{2,10},{3,19},{4,12},{5,21},{6,14},{7,23},{8,0},{9,25... | collective-permute-start | bytes 1572872 | tf_op jit(solution)/shard_map/ppermute | solution.py:545
  78.3 40.1 %collective-permute-start.21 = (f32[2,32,32,128]{3,2,1,0:T(8,128)S(1)}, f32[2,32,32,128]{3,2,1,0:T(8,128)}, u32[]{:S(2)}, u32[]{:S(2)}) collective-permute-start(f32[2,32,32,128]{3,2,1,0:T(8,128)S(1)} %mix.10.refs_4_), channel_id=1, source_target_pairs={{0,8},{1,17},{2,10},{3,19},{4,12},{5,21},{6,14},{7,23},{8,0},{9,25... | collective-permute-start | bytes 3145736 | tf_op jit(solution)/shard_map/ppermute | solution.py:545
  82.4 10.9 %collective-permute-start.18 = (f32[2,1,8,32,128]{4,3,2,1,0:T(8,128)S(1)}, f32[2,1,8,32,128]{4,3,2,1,0:T(8,128)S(1)}, u32[]{:S(2)}, u32[]{:S(2)}) collective-permute-start(f32[2,1,8,32,128]{4,3,2,1,0:T(8,128)S(1)} %get-tuple-element.49), channel_id=1, source_target_pairs={{0,2},{1,3},{2,0},{3,1},{4,6},{5,7},{6,4},{7,5},{8,10},{9,11},{10,... | collective-permute-start | bytes 786440 | tf_op jit(solution)/shard_map/ppermute | solution.py:554
  85.5 27.0 %collective-permute-start.23 = (f32[2,4,128,128]{3,2,1,0:T(8,128)S(1)}, f32[2,4,128,128]{3,2,1,0:T(8,128)S(1)}, u32[]{:S(2)}, u32[]{:S(2)}) collective-permute-start(f32[2,4,128,128]{3,2,1,0:T(8,128)S(1)} %coefficients.5.refs_5_.refs_3_), channel_id=1, source_target_pairs={{0,4},{1,5},{2,6},{3,7},{4,0},{5,1},{6,2},{7,3},{8,12},{9,13},{10,... | collective-permute-start | bytes 1572872 | tf_op jit(solution)/shard_map/ppermute | solution.py:554
  89.6 26.0 %collective-permute-start.22 = (f32[1,32,32,128]{3,2,1,0:T(8,128)}, f32[1,32,32,128]{3,2,1,0:T(8,128)S(1)}, u32[]{:S(2)}, u32[]{:S(2)}) collective-permute-start(f32[1,32,32,128]{3,2,1,0:T(8,128)} %pack.13.refs_5_), channel_id=1, source_target_pairs={{0,16},{1,9},{2,18},{3,11},{4,20},{5,13},{6,22},{7,15},{8,24},{9,1... | collective-permute-start | bytes 1572872 | tf_op jit(solution)/shard_map/ppermute | solution.py:545
  93.3 13.2 %collective-permute-start.24 = (f32[2,1,8,32,128]{4,3,2,1,0:T(8,128)S(1)}, f32[2,1,8,32,128]{4,3,2,1,0:T(8,128)S(1)}, u32[]{:S(2)}, u32[]{:S(2)}) collective-permute-start(f32[2,1,8,32,128]{4,3,2,1,0:T(8,128)S(1)} %join.10.refs_6_), channel_id=1, source_target_pairs={{0,2},{1,3},{2,0},{3,1},{4,6},{5,7},{6,4},{7,5},{8,10},{9,11},{10,... | collective-permute-start | bytes 786440 | tf_op jit(solution)/shard_map/ppermute | solution.py:554
  95.3 25.7 %collective-permute-start.20 = (f32[2,1,8,32,128]{4,3,2,1,0:T(8,128)S(1)}, f32[2,1,8,32,128]{4,3,2,1,0:T(8,128)S(1)}, u32[]{:S(2)}, u32[]{:S(2)}) collective-permute-start(f32[2,1,8,32,128]{4,3,2,1,0:T(8,128)S(1)} %join.12.refs_6_), channel_id=1, source_target_pairs={{0,2},{1,3},{2,0},{3,1},{4,6},{5,7},{6,4},{7,5},{8,10},{9,11},{10,... | collective-permute-start | bytes 786440 | tf_op jit(solution)/shard_map/ppermute | solution.py:554
  108.2 16.2 %collective-permute-start.27 = (f32[1,4,128,128]{3,2,1,0:T(8,128)S(1)}, f32[1,4,128,128]{3,2,1,0:T(8,128)S(1)}, u32[]{:S(2)}, u32[]{:S(2)}) collective-permute-start(f32[1,4,128,128]{3,2,1,0:T(8,128)S(1)} %coefficients.6.refs_8_.refs_3_), channel_id=1, source_target_pairs={{0,4},{1,5},{2,6},{3,7},{4,0},{5,1},{6,2},{7,3},{8,12},{9,13},{10,... | collective-permute-start | bytes 786440 | tf_op jit(solution)/shard_map/ppermute | solution.py:554
  115.6 28.7 %collective-permute-start.29 = (f32[2,2,8,32,128]{4,3,2,1,0:T(8,128)}, f32[2,2,8,32,128]{4,3,2,1,0:T(8,128)S(1)}, u32[]{:S(2)}, u32[]{:S(2)}) collective-permute-start(f32[2,2,8,32,128]{4,3,2,1,0:T(8,128)} %get-tuple-element.56), channel_id=1, source_target_pairs={{0,2},{1,3},{2,0},{3,1},{4,6},{5,7},{6,4},{7,5},{8,10},{9,11},{10,... | collective-permute-start | bytes 1572872 | tf_op jit(solution)/shard_map/ppermute | solution.py:554
  115.6 33.2 %collective-permute-start.32 = (f32[2,32,32,128]{3,2,1,0:T(8,128)S(1)}, f32[2,32,32,128]{3,2,1,0:T(8,128)}, u32[]{:S(2)}, u32[]{:S(2)}) collective-permute-start(f32[2,32,32,128]{3,2,1,0:T(8,128)S(1)} %mix.12.refs_2_), channel_id=1, source_target_pairs={{0,8},{1,17},{2,10},{3,19},{4,12},{5,21},{6,14},{7,23},{8,0},{9,25... | collective-permute-start | bytes 3145736 | tf_op jit(solution)/shard_map/ppermute | solution.py:545
  122.7 15.4 %collective-permute-start.25 = (f32[1,4,128,128]{3,2,1,0:T(8,128)S(1)}, f32[1,4,128,128]{3,2,1,0:T(8,128)S(1)}, u32[]{:S(2)}, u32[]{:S(2)}) collective-permute-start(f32[1,4,128,128]{3,2,1,0:T(8,128)S(1)} %coefficients.7.refs_8_.refs_3_), channel_id=1, source_target_pairs={{0,4},{1,5},{2,6},{3,7},{4,0},{5,1},{6,2},{7,3},{8,12},{9,13},{10,... | collective-permute-start | bytes 786440 | tf_op jit(solution)/shard_map/ppermute | solution.py:554
  126.2 18.2 %collective-permute-start.30 = (f32[2,1,8,32,128]{4,3,2,1,0:T(8,128)S(1)}, f32[2,1,8,32,128]{4,3,2,1,0:T(8,128)S(1)}, u32[]{:S(2)}, u32[]{:S(2)}) collective-permute-start(f32[2,1,8,32,128]{4,3,2,1,0:T(8,128)S(1)} %get-tuple-element.58), channel_id=1, source_target_pairs={{0,2},{1,3},{2,0},{3,1},{4,6},{5,7},{6,4},{7,5},{8,10},{9,11},{10,... | collective-permute-start | bytes 786440 | tf_op jit(solution)/shard_map/ppermute | solution.py:554
  126.5 18.6 %collective-permute-start.34 = (f32[1,32,32,128]{3,2,1,0:T(8,128)S(1)}, f32[1,32,32,128]{3,2,1,0:T(8,128)S(1)}, u32[]{:S(2)}, u32[]{:S(2)}) collective-permute-start(f32[1,32,32,128]{3,2,1,0:T(8,128)S(1)} %mix.13.refs_5_), channel_id=1, source_target_pairs={{0,8},{1,17},{2,10},{3,19},{4,12},{5,21},{6,14},{7,23},{8,0},{9,25... | collective-permute-start | bytes 1572872 | tf_op jit(solution)/shard_map/ppermute | solution.py:545
  (32 other events, 244.8 us)

commit v7 on v6

--- a/solution.py
+++ b/solution.py
@@ -9,54 +9,59 @@
 from jax.sharding import PartitionSpec as P
 
 QUAD = 4
-NEAR_SIZES = (1, 2, 1, 1)
-FAR_SIZES = (2, 1, 2)
+NEAR_SIZES = (1, 1, 2, 1)
+FAR_SIZES = (2, 1, 1, 1)
 ORDER = (
     ("pack", 0),
+    ("pack", 2),
     ("pack", 1),
-    ("pack", 2),
     ("local", 0),
-    ("mix", 0),
+    ("mix", 2),
     ("mix", 1),
-    ("mix", 2),
+    ("pack", 5),
     ("pack", 6),
-    ("spread", 0),
-    ("pack", 3),
-    ("join", 0),
     ("pack", 4),
     ("spread", 1),
+    ("join", 1),
+    ("pack", 3),
+    ("spread", 2),
+    ("coef", 1),
+    ("mix", 0),
+    ("mix", 3),
+    ("join", 2),
+    ("pack", 7),
+    ("spread", 0),
+    ("filter", 1),
+    ("join", 0),
+    ("mix", 6),
+    ("coef", 2),
+    ("spread", 3),
     ("coef", 0),
-    ("join", 1),
+    ("join", 3),
+    ("mix", 7),
+    ("local", 1),
     ("mix", 4),
-    ("mix", 3),
-    ("pack", 5),
-    ("spread", 2),
+    ("filter", 2),
+    ("back", 1),
+    ("mix", 5),
+    ("coef", 3),
     ("filter", 0),
-    ("join", 2),
-    ("coef", 1),
-    ("spread", 3),
-    ("mix", 6),
+    ("near", 1),
+    ("far", 6),
+    ("back", 2),
+    ("far", 7),
+    ("filter", 3),
     ("back", 0),
-    ("join", 3),
-    ("coef", 2),
-    ("filter", 1),
-    ("mix", 5),
+    ("near", 0),
+    ("near", 2),
     ("far", 4),
-    ("coef", 3),
-    ("filter", 2),
-    ("near", 0),
-    ("filter", 3),
-    ("back", 2),
-    ("back", 1),
+    ("back", 3),
     ("far", 5),
-    ("near", 2),
-    ("far", 6),
-    ("near", 1),
-    ("back", 3),
     ("near", 3),
 )
 EDGES = tuple(zip(ORDER[:-1], ORDER[1:]))
 SMEM = pl.BlockSpec(memory_space=pltpu.SMEM)
+STAMP = pl.BlockSpec((8, 128), lambda i: (0, 0))
 ANY = pl.BlockSpec(memory_space=pl.ANY)
 COST = pl.CostEstimate(flops=0, bytes_accessed=0, transcendentals=0)
 PARAMS = pltpu.CompilerParams(vmem_limit_bytes=48 * 1024 * 1024)
@@ -183,7 +188,7 @@
 
 
 def local_kernel(
-    coupling, kappa, flags, adj, before, after, src, mu, mu_before, mu_after, low, high, out
+    far, coupling, kappa, flags, adj, before, after, next_to, src, mu, mu_before, mu_after, mu_next, low, high, out, stamp
 ):
     fields, planes, rows, cells = adj.shape
     step = pl.program_id(0)
@@ -191,7 +196,8 @@
     last = step == pl.num_programs(0) - 1
     row = lax.broadcasted_iota(jnp.int32, (rows, cells), 0)
     col = lax.broadcasted_iota(jnp.int32, (rows, cells), 1)
-    ring = 0.5 / (row.astype(jnp.float32) + 1.0)
+    ring = 0.5 / ((row + rows * far).astype(jnp.float32) + 1.0)
+    stamp[...] = jnp.zeros_like(stamp)
 
     def pick(source, behind, ahead, f, k):
         if k < 0:
@@ -206,19 +212,31 @@
     def cell(f, k):
         return pick(adj[f, max(0, min(k, planes - 1))], before[f, 0], after[f, 0], f, k)
 
+    def outward(x, edge):
+        moved = pltpu.roll(x, rows - 1, 0)
+        return moved if far else jnp.where(row == rows - 1, edge[:1], moved)
+
+    def inward(x, edge):
+        moved = pltpu.roll(x, 1, 0)
+        return jnp.where(row == 0, edge[-1:], moved) if far else moved
+
     walls = []
     for f in range(fields):
         opens = [(1 - flags[f, i]).astype(jnp.float32) for i in range(3)]
         wall = jnp.where(col == 0, opens[0], 0.0)
         wall = wall + jnp.where(col == cells - 1, opens[1], 0.0)
-        walls.append(wall + jnp.where(row == rows - 1, opens[2], 0.0))
+        walls.append(wall + jnp.where(row == rows - 1, opens[2], 0.0) if far else wall)
 
     for k in range(planes):
         m = visc(k)
         up = ring * (m + visc(k + 1))
         down = ring * (m + visc(k - 1))
-        outer = jnp.where(row < rows - 1, 0.5 * (m + pltpu.roll(m, rows - 1, 0)), 0.0)
-        inner = jnp.where(row > 0, 0.5 * (m + pltpu.roll(m, 1, 0)), 0.0)
+        outer = 0.5 * (m + outward(m, mu_next[k]))
+        inner = 0.5 * (m + inward(m, mu_next[k]))
+        if far:
+            outer = jnp.where(row < rows - 1, outer, 0.0)
+        else:
+            inner = jnp.where(row > 0, inner, 0.0)
         east = jnp.where(col < cells - 1, 0.5 * (m + pltpu.roll(m, cells - 1, 1)), 0.0)
         west = jnp.where(col > 0, 0.5 * (m + pltpu.roll(m, 1, 1)), 0.0)
         diag = up + down + outer + inner + east + west
@@ -226,7 +244,7 @@
             p = adj[f, k]
             flux = (diag + walls[f] * m) * p
             flux = flux - up * cell(f, k + 1) - down * cell(f, k - 1)
-            flux = flux - outer * pltpu.roll(p, rows - 1, 0) - inner * pltpu.roll(p, 1, 0)
+            flux = flux - outer * outward(p, next_to[f, k]) - inner * inward(p, next_to[f, k])
             flux = flux - east * pltpu.roll(p, cells - 1, 1) - west * pltpu.roll(p, 1, 1)
             total = src[f, k] + kappa[f] * flux
             for g in range(fields):
@@ -234,26 +252,29 @@
             out[f, k] = total
 
 
-def local_part(center, source, viscosity, kappa, coupling, flags, low, high, token):
+def local_part(far, center, source, viscosity, kappa, coupling, flags, low, high, token):
     fields, block, rows, cells = center.shape
+    half = rows // 2
     planes = min(4, block)
+    edge = half // 8 - 1 if far else half // 8
 
     def whole(width, index):
-        return pl.BlockSpec((fields, width, rows, cells), lambda i: (0, index(i), 0, 0))
+        return pl.BlockSpec((fields, width, half, cells), lambda i: (0, index(i), far, 0))
 
     def plane(width, index):
-        return pl.BlockSpec((width, rows, cells), lambda i: (index(i), 0, 0))
+        return pl.BlockSpec((width, half, cells), lambda i: (index(i), far, 0))
 
     behind = lambda i: jnp.maximum(i * planes - 1, 0)
     ahead = lambda i: jnp.minimum(i * planes + planes, block - 1)
     here = lambda i: i
-    halo = pl.BlockSpec((fields + 1, 1, rows, cells), lambda i: (0, 0, 0, 0))
+    halo = pl.BlockSpec((fields + 1, 1, half, cells), lambda i: (0, 0, far, 0))
     return call(
-        local_kernel,
+        functools.partial(local_kernel, far),
         "local_part",
         token,
         (block // planes,),
-        [coupling, kappa, flags, center, center, center, source, viscosity, viscosity, viscosity, low, high],
+        [coupling, kappa, flags, center, center, center, center, source]
+        + [viscosity, viscosity, viscosity, viscosity, low, high],
         [
             SMEM,
             SMEM,
@@ -261,15 +282,17 @@
             whole(planes, here),
             whole(1, behind),
             whole(1, ahead),
+            pl.BlockSpec((fields, planes, 8, cells), lambda i: (0, i, edge, 0)),
             whole(planes, here),
             plane(planes, here),
             plane(1, behind),
             plane(1, ahead),
+            pl.BlockSpec((planes, 8, cells), lambda i: (i, edge, 0)),
             halo,
             halo,
         ],
-        whole(planes, here),
-        shaped(*center.shape),
+        [pl.BlockSpec((fields, planes, half, cells), lambda i: (0, i, 0, 0)), STAMP],
+        [shaped(fields, block, half, cells), shaped(8, 128)],
     )
 
 
@@ -480,7 +503,8 @@
         carried = [] if held is None else [held]
 
         def kernel(ints, reals, mine, core, chip, *refs):
-            out, stage = refs[-2:]
+            out, stamp, stage = refs[-3:]
+            stamp[...] = jnp.zeros_like(stamp)
             rank = self.scalars(ints, reals).rank
             for k, part in enumerate((mine[0], core[0, 0], chip[0, 0], core[1, 0])):
                 stage[rank ^ k] = part
@@ -496,15 +520,16 @@
             (hi - lo,),
             [self.ints, self.reals, mine, core, chip] + carried,
             [SMEM, SMEM, self.part(), self.parts(2), self.parts(1)] + [ANY] * len(carried),
-            self.side(lo, 0),
-            shaped(*self.shape),
+            [self.side(lo, 0), STAMP],
+            [shaped(*self.shape), shaped(8, 128)],
             [pltpu.VMEM((QUAD, self.cycles, self.block, self.cells), jnp.float32)],
             alias={5: 0} if carried else None,
         )
 
     def place_far(self, local, others, held, lo, hi, token):
         def kernel(ints, reals, local, *refs):
-            others, out = refs[: len(refs) - 1 - len(carried)], refs[-1]
+            others, (out, stamp) = refs[: len(refs) - 2 - len(carried)], refs[-2:]
+            stamp[...] = jnp.zeros_like(stamp)
             out[0] = sums(self.scalars(ints, reals), local, others)
 
         carried = [] if held is None else [held]
@@ -514,11 +539,11 @@
             token,
             (hi - lo,),
             [self.ints, self.reals, local] + others + carried,
-            [SMEM, SMEM, self.side(lo, 1)]
+            [SMEM, SMEM, self.side(lo, 0)]
             + [self.side(0, 0)] * len(others)
             + [ANY] * len(carried),
-            self.side(lo, 1),
-            shaped(*self.shape),
+            [self.side(lo, 1), STAMP],
+            [shaped(*self.shape), shaped(8, 128)],
             alias={3 + len(others): 0} if carried else None,
         )
 
@@ -574,7 +599,7 @@
     groups = [(lo, hi, 0) for lo, hi in spans(NEAR_SIZES, fields)]
     groups += [(lo, hi, 1) for lo, hi in spans(FAR_SIZES, fields)]
     first, others, parts, own, done = {}, {}, {}, {}, {}
-    made, local, held, halos = {}, None, None, None
+    made, local, held, halos = {}, {}, None, None
     for step, g in ORDER:
         lo, hi, index = groups[g]
         token = [made[before] for before, after in EDGES if after == (step, g)]
@@ -585,15 +610,15 @@
             if halos is None:
                 halos = ring(packed[1], 1), ring(packed[2], -1)
         elif step == "local":
-            local = made[step, g] = local_part(
-                center, source[0], viscosity, kappa, coupling, bc_flags, *halos, token
+            local[g], made[step, g] = local_part(
+                g, center, source[0], viscosity, kappa, coupling, bc_flags, *halos, token
             )
         elif step == "mix":
             mixed = plan.mix(center, first[g], lo, hi, index, token)
             made[step, g] = mixed[0]
             others[g] = [first[g]] + [to_later(x, s + 1) for s, x in enumerate(mixed)]
         elif step == "spread":
-            mine, core, chip = plan.spread(local, others[g], lo, hi, token)
+            mine, core, chip = plan.spread(local[0], others[g], lo, hi, token)
             made[step, g] = mine
             parts[g] = mine, to_sector(core, 1), chip
         elif step == "join":
@@ -617,9 +642,9 @@
             made[step, g] = plan.join(core, chip, token)
             done[g] = mine, to_sector(made[step, g], 1), chip
         elif step == "near":
-            held = made[step, g] = plan.place_near(*done[g], held, lo, hi, token)
+            held, made[step, g] = plan.place_near(*done[g], held, lo, hi, token)
         else:
-            held = made[step, g] = plan.place_far(local, others[g], held, lo, hi, token)
+            held, made[step, g] = plan.place_far(local[1], others[g], held, lo, hi, token)
     return held[None]
 
 

time: 161 us -> 178 us (1.11)
  Pallas kernels: 70.1 us -> 81.2 us
  local copies, waits for them, and re-layouts: 4.53 us -> 12.3 us
  waiting for transfers between devices: 46.3 us -> 41.1 us
  starting transfers between devices: 37.7 us -> 41.1 us
    pallas_call x34 -> x38, Pallas kernels: 54.2 us -> 64.2 us  [call(): pl.pallas_call(lambda *refs: kernel(*refs[:len(inputs)], *refs[len(inputs...]
    unnamed x41 -> x101, local copies, waits for them, and re-layouts: 4.53 us -> 12.3 us
    ppermute x14 -> x16, waiting for transfers between devices: 20 us -> 13.9 us  [to_partner(): return lax.ppermute(x, ('inst', 'space'), pairs)]
    ppermute x2, waiting for transfers between devices: 0.01 us -> 2.84 us  [ring(): lax.ppermute(x, 'space', [(i, (i + step) % sectors) for i in range(sector...]
    ppermute x14 -> x16, starting transfers between devices: 19.7 us -> 22.1 us  [to_partner(): return lax.ppermute(x, ('inst', 'space'), pairs)]
    ppermute x20, waiting for transfers between devices: 26.4 us -> 24.4 us  [to_sector(): return lax.ppermute(x, 'space', [(i, i ^ k) for i in range(sectors)])]
  transfers between devices with their start and end apart: 36 -> 38, of which waited for: 12 -> 14; matrix products, arithmetic and copies ran while one was open for 1% -> 0% of each run, Pallas kernels for 41% -> 42%
where the time goes in v7:
time: 178 us; the launch traced here: 177 us
  Pallas kernels  81.2 us (46%)
  starting transfers between devices  41.1 us (23%)
  waiting for transfers between devices  41.1 us (23%)
  local copies, waits for them, and re-layouts  12.3 us (7%)
    pallas_call x38, Pallas kernels, call(): pl.pallas_call(lambda *refs: kernel(*refs[:len(inputs)], *refs[len(inputs...  64.2 us
    ppermute x20, waiting for transfers between devices, to_sector(): return lax.ppermute(x, 'space', [(i, i ^ k) for i in range(sectors)])  24.4 us
    ppermute x16, starting transfers between devices, to_partner(): return lax.ppermute(x, ('inst', 'space'), pairs)  22.1 us
    pallas_call x8, Pallas kernels, table_call(): pl.pallas_call(lambda *refs: kernel(*refs[:count + 1], *refs[count + 1 +...  17 us
    ppermute x20, starting transfers between devices, to_sector(): return lax.ppermute(x, 'space', [(i, i ^ k) for i in range(sectors)])  15.5 us
    ppermute x16, waiting for transfers between devices, to_partner(): return lax.ppermute(x, ('inst', 'space'), pairs)  13.9 us
    unnamed x101, local copies, waits for them, and re-layouts  12.3 us
  transfers between devices with their start and end apart: 38, of which 14 were waited for; matrix products, arithmetic and copies ran while one was open for 0% of the time, Pallas kernels for 42%

profile of v7, /device:TPU:0, one launch (start us, length us, event | category | flops | bytes accessed | tf_op | source)
XLA Modules:
  0.0 177.0 jit_solution(4300801599852460390)
XLA Ops:
  1.2 2.1 %pack.8 = (f32[1,32,32,128]{3,2,1,0:T(8,128)}, f32[6,1,64,128]{3,2,1,0:T(8,128)}, f32[6,1,64,128]{3,2,1,0:T(8,128)}) custom-call(f32[5,32,64,128]{3,2,1,0:T(8,128)} %bitcast.5, f32[5,32,64,128]{3,2,1,0:T(8,128)} %bitcast.6, f32[32,64,128]{2,1,0:T(8,128)S(1)} %copy-done, f32[5,32,64,128]{3,2,1,0:T(8,128)} %bitcast.7, f32[32,64,128]{2,1,0:T(8,128)S(1)} %copy-done), custom_call_target="tpu_custom_call" | custom-call | tf_op jit(solution)/shard_map/pack/pallas_call | solution.py:149
  4.7 3.0 %collective-permute-start.3 = (f32[2,32,32,128]{3,2,1,0:T(8,128)S(1)}, f32[2,32,32,128]{3,2,1,0:T(8,128)S(1)}, u32[]{:S(2)}, u32[]{:S(2)}) collective-permute-start(f32[2,32,32,128]{3,2,1,0:T(8,128)S(1)} %pack.9.refs_1_), channel_id=1, source_target_pairs={{0,16},{1,9},{2,18},{3,11},{4,20},{5,13},{6,22},{7,15},{8,24},{9,1... | collective-permute-start | bytes 3145736 | tf_op jit(solution)/shard_map/ppermute | solution.py:570
  9.6 3.5 %collective-permute-start.1 = (f32[6,1,64,128]{3,2,1,0:T(8,128)}, f32[6,1,64,128]{3,2,1,0:T(8,128)S(1)}, u32[]{:S(2)}, u32[]{:S(2)}) collective-permute-start(f32[6,1,64,128]{3,2,1,0:T(8,128)} %get-tuple-element.52), channel_id=1, source_target_pairs={{0,7},{1,0},{2,1},{3,2},{4,3},{5,4},{6,5},{7,6},{8,15},{9,8},{10,9... | collective-permute-start | bytes 589832 | tf_op jit(solution)/shard_map/ppermute | solution.py:582
  14.0 2.8 %collective-permute-done.refs_12_ = f32[6,1,64,128]{3,2,1,0:T(8,128)S(1)} collective-permute-done((f32[6,1,64,128]{3,2,1,0:T(8,128)}, f32[6,1,64,128]{3,2,1,0:T(8,128)S(1)}, u32[]{:S(2)}, u32[]{:S(2)}) %collective-permute-start) | collective-permute-done | bytes 196640 | tf_op jit(solution)/shard_map/ppermute | solution.py:582
  17.5 7.6 %local_part.2 = (f32[5,32,32,128]{3,2,1,0:T(8,128)S(1)}, f32[8,128]{1,0:T(8,128)S(1)}) custom-call(f32[5,5]{1,0:T(8,128)S(1)} %copy-done.43, f32[5]{0:T(128)S(1)} %copy-done.44, s32[5,3]{1,0:T(8,128)S(1)} %copy.27.refs_2_, f32[5,32,64,128]{3,2,1,0:T(8,128)} %bitcast.10, f32[5,32,64,128]{3,2,1,0:T(8,128)} %bitcast.11, f32[5,32,64,128]{3,2,1,0:T(8,128)} %bitcast.12, ...), custom_call_target="tpu_custom_call" | custom-call | tf_op jit(solution)/shard_map/local_part/pallas_call | solution.py:149
  26.7 2.5 %mix.8.refs_4_ = f32[2,32,32,128]{3,2,1,0:T(8,128)} custom-call(s32[22]{0:T(128)S(1)} %pad_add_fusion.refs_0_, f32[71]{0:T(128)S(1)} %copy-done.40, f32[5,32,64,128]{3,2,1,0:T(8,128)} %bitcast.14, f32[2,32,32,128]{3,2,1,0:T(8,128)S(1)} %collective-permute-done.3.refs_3_, f32[8,128]{1,0:T(8,128)S(1)} %get-tuple-element.55.refs_4_), custom_call_target="tpu_custom_call" | custom-call | tf_op jit(solution)/shard_map/mix/pallas_call | solution.py:149
  30.5 2.1 %collective-permute-start.4 = (f32[1,32,32,128]{3,2,1,0:T(8,128)S(1)}, f32[1,32,32,128]{3,2,1,0:T(8,128)S(1)}, u32[]{:S(2)}, u32[]{:S(2)}) collective-permute-start(f32[1,32,32,128]{3,2,1,0:T(8,128)S(1)} %mix.9.refs_1_), channel_id=1, source_target_pairs={{0,8},{1,17},{2,10},{3,19},{4,12},{5,21},{6,14},{7,23},{8,0},{9,25... | collective-permute-start | bytes 1572872 | tf_op jit(solution)/shard_map/ppermute | solution.py:570
  33.8 2.1 %pack.12.refs_1_ = f32[1,32,32,128]{3,2,1,0:T(8,128)} custom-call(f32[5,32,64,128]{3,2,1,0:T(8,128)} %bitcast.17, f32[1,32,32,128]{3,2,1,0:T(8,128)S(1)} %pack.11.refs_1_), custom_call_target="tpu_custom_call" | custom-call | tf_op jit(solution)/shard_map/pack/pallas_call | solution.py:149
  49.2 5.3 %collective-permute-done.9.refs_4_ = f32[2,32,32,128]{3,2,1,0:T(8,128)} collective-permute-done((f32[2,32,32,128]{3,2,1,0:T(8,128)}, f32[2,32,32,128]{3,2,1,0:T(8,128)}, u32[]{:S(2)}, u32[]{:S(2)}) %collective-permute-start.9) | collective-permute-done | bytes 1048608 | tf_op jit(solution)/shard_map/ppermute | solution.py:570
  54.5 2.9 %spread.5 = (f32[2,8,32,128]{3,2,1,0:T(8,128)S(1)}, f32[2,2,8,32,128]{4,3,2,1,0:T(8,128)S(1)}, f32[2,2,8,32,128]{4,3,2,1,0:T(8,128)}) custom-call(s32[22]{0:T(128)S(1)} %pad_add_fusion.refs_0_, f32[71]{0:T(128)S(1)} %copy-done.40, f32[5,32,32,128]{3,2,1,0:T(8,128)} %copy-done.2, f32[2,32,32,128]{3,2,1,0:T(8,128)S(1)} %copy-done.9, ...), custom_call_target="tpu_custom_call" | custom-call | tf_op jit(solution)/shard_map/spread/pallas_call | solution.py:149
  76.6 1.9 %collective-permute-start.10 = (f32[1,32,32,128]{3,2,1,0:T(8,128)S(1)}, f32[1,32,32,128]{3,2,1,0:T(8,128)}, u32[]{:S(2)}, u32[]{:S(2)}) collective-permute-start(f32[1,32,32,128]{3,2,1,0:T(8,128)S(1)} %mix.11.refs_2_), channel_id=1, source_target_pairs={{0,8},{1,17},{2,10},{3,19},{4,12},{5,21},{6,14},{7,23},{8,0},{9,25... | collective-permute-start | bytes 1572872 | tf_op jit(solution)/shard_map/ppermute | solution.py:570
  80.3 2.4 %filtered.4 = (f32[1,8,32,128]{3,2,1,0:T(8,128)S(1)}, f32[2,1,8,32,128]{4,3,2,1,0:T(8,128)S(1)}, f32[2,1,8,32,128]{4,3,2,1,0:T(8,128)}) custom-call(s32[22]{0:T(128)S(1)} %pad_add_fusion.refs_0_, f32[71]{0:T(128)S(1)} %copy-done.40, f32[2,16,128,128]{3,2,1,0:T(8,128)S(1)} %copy-done.6, f32[1,4,128,128]{3,2,1,0:T(8,128)S(1)} %coefficients.4.refs_4_.refs_3_, ...), custom_call_target="tpu_custom_call" | custom-call | tf_op jit(solution)/shard_map/filtered/pallas_call | solution.py:410
  86.8 2.1 %mix.12.refs_6_ = f32[1,32,32,128]{3,2,1,0:T(8,128)} custom-call(s32[22]{0:T(128)S(1)} %pad_add_fusion.refs_0_, f32[71]{0:T(128)S(1)} %copy-done.40, f32[5,32,64,128]{3,2,1,0:T(8,128)} %bitcast.22, f32[1,32,32,128]{3,2,1,0:T(8,128)} %collective-permute-done.13.refs_3_, f32[2,1,8,32,128]{4,3,2,1,0:T(8,128)} %join.10.refs_4_), custom_call_target="tpu_custom_call" | custom-call | tf_op jit(solution)/shard_map/mix/pallas_call | solution.py:149
  88.9 2.1 %collective-permute-done.12.refs_5_.refs_7_ = f32[2,2,8,32,128]{4,3,2,1,0:T(8,128)S(1)} collective-permute-done((f32[2,2,8,32,128]{4,3,2,1,0:T(8,128)}, f32[2,2,8,32,128]{4,3,2,1,0:T(8,128)S(1)}, u32[]{:S(2)}, u32[]{:S(2)}) %collective-permute-start.12) | collective-permute-done | bytes 524320 | tf_op jit(solution)/shard_map/ppermute | solution.py:579
  91.0 2.4 %coefficients.5.refs_5_.refs_3_ = f32[2,4,128,128]{3,2,1,0:T(8,128)S(1)} custom-call(s32[22]{0:T(128)S(1)} %pad_add_fusion.refs_0_, f32[71]{0:T(128)S(1)} %copy-done.40, f32[2,16,128,128]{3,2,1,0:T(8,128)S(1)} %copy-done.5, f32[2,8,32,128]{3,2,1,0:T(8,128)S(1)} %get-tuple-element.59.refs_6_.refs_3_.refs_5_, ...), custom_call_target="tpu_custom_call" | custom-call | tf_op jit(solution)/shard_map/coefficients/pallas_call | solution.py:410
  99.7 2.4 %collective-permute-start.21 = (f32[2,1,8,32,128]{4,3,2,1,0:T(8,128)}, f32[2,1,8,32,128]{4,3,2,1,0:T(8,128)S(1)}, u32[]{:S(2)}, u32[]{:S(2)}) collective-permute-start(f32[2,1,8,32,128]{4,3,2,1,0:T(8,128)} %get-tuple-element.70), channel_id=1, source_target_pairs={{0,2},{1,3},{2,0},{3,1},{4,6},{5,7},{6,4},{7,5},{8,10},{9,11},{10,... | collective-permute-start | bytes 786440 | tf_op jit(solution)/shard_map/ppermute | solution.py:579
  105.5 18.1 %collective-permute-done.22.refs_4_ = f32[2,4,128,128]{3,2,1,0:T(8,128)S(1)} collective-permute-done((f32[2,4,128,128]{3,2,1,0:T(8,128)S(1)}, f32[2,4,128,128]{3,2,1,0:T(8,128)S(1)}, u32[]{:S(2)}, u32[]{:S(2)}) %collective-permute-start.22) | collective-permute-done | bytes 524320 | tf_op jit(solution)/shard_map/ppermute | solution.py:579
  125.2 7.7 %local_part.3 = (f32[5,32,32,128]{3,2,1,0:T(8,128)S(1)}, f32[8,128]{1,0:T(8,128)S(1)}) custom-call(f32[5,5]{1,0:T(8,128)S(1)} %copy-done.43, f32[5]{0:T(128)S(1)} %copy-done.45, s32[5,3]{1,0:T(8,128)S(1)} %copy.27.refs_2_, f32[5,32,64,128]{3,2,1,0:T(8,128)} %bitcast.24, f32[5,32,64,128]{3,2,1,0:T(8,128)} %bitcast.25, f32[5,32,64,128]{3,2,1,0:T(8,128)} %bitcast.26, ...), custom_call_target="tpu_custom_call" | custom-call | tf_op jit(solution)/shard_map/local_part/pallas_call | solution.py:149
  134.3 3.6 %filtered.5 = (f32[2,8,32,128]{3,2,1,0:T(8,128)S(1)}, f32[2,2,8,32,128]{4,3,2,1,0:T(8,128)S(1)}, f32[2,2,8,32,128]{4,3,2,1,0:T(8,128)}) custom-call(s32[22]{0:T(128)S(1)} %pad_add_fusion.refs_0_, f32[71]{0:T(128)S(1)} %copy-done.40, f32[2,16,128,128]{3,2,1,0:T(8,128)} %constant.19.clone.refs_2_, f32[2,4,128,128]{3,2,1,0:T(8,128)S(1)} %coefficients.5.refs_5_.refs_3_, ...), custom_call_target="tpu_custom_call" | custom-call | tf_op jit(solution)/shard_map/filtered/pallas_call | solution.py:410
  147.3 2.1 %collective-permute-start.25 = (f32[1,4,128,128]{3,2,1,0:T(8,128)S(1)}, f32[1,4,128,128]{3,2,1,0:T(8,128)S(1)}, u32[]{:S(2)}, u32[]{:S(2)}) collective-permute-start(f32[1,4,128,128]{3,2,1,0:T(8,128)S(1)} %coefficients.7.refs_8_.refs_3_), channel_id=1, source_target_pairs={{0,4},{1,5},{2,6},{3,7},{4,0},{5,1},{6,2},{7,3},{8,12},{9,13},{10,... | collective-permute-start | bytes 786440 | tf_op jit(solution)/shard_map/ppermute | solution.py:579
  152.4 2.1 %place_far.4 = (f32[5,32,64,128]{3,2,1,0:T(8,128)}, f32[8,128]{1,0:T(8,128)S(1)}) custom-call(s32[22]{0:T(128)S(1)} %pad_add_fusion.refs_0_, f32[71]{0:T(128)S(1)} %copy-done.40, f32[5,32,32,128]{3,2,1,0:T(8,128)S(1)} %get-tuple-element.73.refs_2_, f32[1,32,32,128]{3,2,1,0:T(8,128)} %collective-permute-done.13.refs_3_, ...), custom_call_target="tpu_custom_call", output_to_operand_aliasing={{0}: (5, {})} | custom-call | tf_op jit(solution)/shard_map/place_far/pallas_call | solution.py:149
  154.8 4.4 %collective-permute-done.26.refs_4_ = f32[1,32,32,128]{3,2,1,0:T(8,128)S(1)} collective-permute-done((f32[1,32,32,128]{3,2,1,0:T(8,128)S(1)}, f32[1,32,32,128]{3,2,1,0:T(8,128)S(1)}, u32[]{:S(2)}, u32[]{:S(2)}) %collective-permute-start.26) | collective-permute-done | bytes 524320 | tf_op jit(solution)/shard_map/ppermute | solution.py:570
  167.7 2.5 %place_near.6 = (f32[5,32,64,128]{3,2,1,0:T(8,128)}, f32[8,128]{1,0:T(8,128)S(1)}) custom-call(s32[22]{0:T(128)S(1)} %pad_add_fusion.refs_0_, f32[71]{0:T(128)S(1)} %copy-done.40, f32[2,8,32,128]{3,2,1,0:T(8,128)S(1)} %get-tuple-element.72.refs_2_, f32[2,2,8,32,128]{4,3,2,1,0:T(8,128)S(1)} %collective-permute-done.33.refs_3_, ...), custom_call_target="tpu_custom_call", output_to_operand_aliasing={{0}: (5, {})} | custom-call | tf_op jit(solution)/shard_map/place_near/pallas_call | solution.py:149
  170.1 2.2 %place_far.6 = (f32[5,32,64,128]{3,2,1,0:T(8,128)}, f32[8,128]{1,0:T(8,128)S(1)}) custom-call(s32[22]{0:T(128)S(1)} %pad_add_fusion.refs_0_, f32[71]{0:T(128)S(1)} %copy-done.40, f32[5,32,32,128]{3,2,1,0:T(8,128)S(1)} %get-tuple-element.73.refs_2_, f32[2,32,32,128]{3,2,1,0:T(8,128)S(1)} %collective-permute-done.23.refs_3_, ...), custom_call_target="tpu_custom_call", output_to_operand_aliasing={{0}: (5, {})} | custom-call | tf_op jit(solution)/shard_map/place_far/pallas_call | solution.py:149
  (201 shorter events, 86.6 us)
Async XLA Ops:
  4.7 22.0 %collective-permute-start.3 = (f32[2,32,32,128]{3,2,1,0:T(8,128)S(1)}, f32[2,32,32,128]{3,2,1,0:T(8,128)S(1)}, u32[]{:S(2)}, u32[]{:S(2)}) collective-permute-start(f32[2,32,32,128]{3,2,1,0:T(8,128)S(1)} %pack.9.refs_1_), channel_id=1, source_target_pairs={{0,16},{1,9},{2,18},{3,11},{4,20},{5,13},{6,22},{7,15},{8,24},{9,1... | collective-permute-start | bytes 3145736 | tf_op jit(solution)/shard_map/ppermute | solution.py:570
  9.6 19.6 %collective-permute-start.2 = (f32[1,32,32,128]{3,2,1,0:T(8,128)}, f32[1,32,32,128]{3,2,1,0:T(8,128)}, u32[]{:S(2)}, u32[]{:S(2)}) collective-permute-start(f32[1,32,32,128]{3,2,1,0:T(8,128)} %pack.10.refs_14_), channel_id=1, source_target_pairs={{0,16},{1,9},{2,18},{3,11},{4,20},{5,13},{6,22},{7,15},{8,24},{9,1... | collective-permute-start | bytes 1572872 | tf_op jit(solution)/shard_map/ppermute | solution.py:570
  32.6 21.9 %collective-permute-start.9 = (f32[2,32,32,128]{3,2,1,0:T(8,128)}, f32[2,32,32,128]{3,2,1,0:T(8,128)}, u32[]{:S(2)}, u32[]{:S(2)}) collective-permute-start(f32[2,32,32,128]{3,2,1,0:T(8,128)} %mix.8.refs_4_), channel_id=1, source_target_pairs={{0,8},{1,17},{2,10},{3,19},{4,12},{5,21},{6,14},{7,23},{8,0},{9,25... | collective-permute-start | bytes 3145736 | tf_op jit(solution)/shard_map/ppermute | solution.py:570
  44.7 16.2 %collective-permute-start.7 = (f32[1,32,32,128]{3,2,1,0:T(8,128)}, f32[1,32,32,128]{3,2,1,0:T(8,128)S(1)}, u32[]{:S(2)}, u32[]{:S(2)}) collective-permute-start(f32[1,32,32,128]{3,2,1,0:T(8,128)} %get-tuple-element.53.refs_1_), channel_id=1, source_target_pairs={{0,16},{1,9},{2,18},{3,11},{4,20},{5,13},{6,22},{7,15},{8,24},{9,1... | collective-permute-start | bytes 1572872 | tf_op jit(solution)/shard_map/ppermute | solution.py:570
  47.9 20.5 %collective-permute-start.6 = (f32[1,32,32,128]{3,2,1,0:T(8,128)}, f32[1,32,32,128]{3,2,1,0:T(8,128)S(1)}, u32[]{:S(2)}, u32[]{:S(2)}) collective-permute-start(f32[1,32,32,128]{3,2,1,0:T(8,128)} %pack.14.refs_5_), channel_id=1, source_target_pairs={{0,16},{1,9},{2,18},{3,11},{4,20},{5,13},{6,22},{7,15},{8,24},{9,1... | collective-permute-start | bytes 1572872 | tf_op jit(solution)/shard_map/ppermute | solution.py:570
  57.3 13.5 %collective-permute-start.11 = (f32[2,2,8,32,128]{4,3,2,1,0:T(8,128)S(1)}, f32[2,2,8,32,128]{4,3,2,1,0:T(8,128)S(1)}, u32[]{:S(2)}, u32[]{:S(2)}) collective-permute-start(f32[2,2,8,32,128]{4,3,2,1,0:T(8,128)S(1)} %get-tuple-element.60), channel_id=1, source_target_pairs={{0,1},{1,0},{2,3},{3,2},{4,5},{5,4},{6,7},{7,6},{8,9},{9,8},{10,11... | collective-permute-start | bytes 1572872 | tf_op jit(solution)/shard_map/ppermute | solution.py:579
  65.7 14.6 %collective-permute-start.16 = (f32[1,4,128,128]{3,2,1,0:T(8,128)S(1)}, f32[1,4,128,128]{3,2,1,0:T(8,128)S(1)}, u32[]{:S(2)}, u32[]{:S(2)}) collective-permute-start(f32[1,4,128,128]{3,2,1,0:T(8,128)S(1)} %coefficients.4.refs_4_.refs_3_), channel_id=1, source_target_pairs={{0,4},{1,5},{2,6},{3,7},{4,0},{5,1},{6,2},{7,3},{8,12},{9,13},{10,... | collective-permute-start | bytes 786440 | tf_op jit(solution)/shard_map/ppermute | solution.py:579
  66.9 18.3 %collective-permute-start.13 = (f32[1,32,32,128]{3,2,1,0:T(8,128)}, f32[1,32,32,128]{3,2,1,0:T(8,128)}, u32[]{:S(2)}, u32[]{:S(2)}) collective-permute-start(f32[1,32,32,128]{3,2,1,0:T(8,128)} %pack.12.refs_1_), channel_id=1, source_target_pairs={{0,16},{1,9},{2,18},{3,11},{4,20},{5,13},{6,22},{7,15},{8,24},{9,1... | collective-permute-start | bytes 1572872 | tf_op jit(solution)/shard_map/ppermute | solution.py:570
  68.4 35.4 %collective-permute-start.23 = (f32[2,32,32,128]{3,2,1,0:T(8,128)S(1)}, f32[2,32,32,128]{3,2,1,0:T(8,128)S(1)}, u32[]{:S(2)}, u32[]{:S(2)}) collective-permute-start(f32[2,32,32,128]{3,2,1,0:T(8,128)S(1)} %pack.13.refs_5_), channel_id=1, source_target_pairs={{0,16},{1,9},{2,18},{3,11},{4,20},{5,13},{6,22},{7,15},{8,24},{9,1... | collective-permute-start | bytes 3145736 | tf_op jit(solution)/shard_map/ppermute | solution.py:570
  71.6 19.4 %collective-permute-start.12 = (f32[2,2,8,32,128]{4,3,2,1,0:T(8,128)}, f32[2,2,8,32,128]{4,3,2,1,0:T(8,128)S(1)}, u32[]{:S(2)}, u32[]{:S(2)}) collective-permute-start(f32[2,2,8,32,128]{4,3,2,1,0:T(8,128)} %join.9.refs_1_), channel_id=1, source_target_pairs={{0,2},{1,3},{2,0},{3,1},{4,6},{5,7},{6,4},{7,5},{8,10},{9,11},{10,... | collective-permute-start | bytes 1572872 | tf_op jit(solution)/shard_map/ppermute | solution.py:579
  76.6 18.3 %collective-permute-start.10 = (f32[1,32,32,128]{3,2,1,0:T(8,128)S(1)}, f32[1,32,32,128]{3,2,1,0:T(8,128)}, u32[]{:S(2)}, u32[]{:S(2)}) collective-permute-start(f32[1,32,32,128]{3,2,1,0:T(8,128)S(1)} %mix.11.refs_2_), channel_id=1, source_target_pairs={{0,8},{1,17},{2,10},{3,19},{4,12},{5,21},{6,14},{7,23},{8,0},{9,25... | collective-permute-start | bytes 1572872 | tf_op jit(solution)/shard_map/ppermute | solution.py:570
  83.5 14.6 %collective-permute-start.18 = (f32[2,1,8,32,128]{4,3,2,1,0:T(8,128)}, f32[2,1,8,32,128]{4,3,2,1,0:T(8,128)S(1)}, u32[]{:S(2)}, u32[]{:S(2)}) collective-permute-start(f32[2,1,8,32,128]{4,3,2,1,0:T(8,128)} %join.10.refs_4_), channel_id=1, source_target_pairs={{0,2},{1,3},{2,0},{3,1},{4,6},{5,7},{6,4},{7,5},{8,10},{9,11},{10,... | collective-permute-start | bytes 786440 | tf_op jit(solution)/shard_map/ppermute | solution.py:579
  85.2 18.8 %collective-permute-start.24 = (f32[1,32,32,128]{3,2,1,0:T(8,128)}, f32[1,32,32,128]{3,2,1,0:T(8,128)S(1)}, u32[]{:S(2)}, u32[]{:S(2)}) collective-permute-start(f32[1,32,32,128]{3,2,1,0:T(8,128)} %pack.15.refs_5_), channel_id=1, source_target_pairs={{0,16},{1,9},{2,18},{3,11},{4,20},{5,13},{6,22},{7,15},{8,24},{9,1... | collective-permute-start | bytes 1572872 | tf_op jit(solution)/shard_map/ppermute | solution.py:570
  93.4 30.2 %collective-permute-start.22 = (f32[2,4,128,128]{3,2,1,0:T(8,128)S(1)}, f32[2,4,128,128]{3,2,1,0:T(8,128)S(1)}, u32[]{:S(2)}, u32[]{:S(2)}) collective-permute-start(f32[2,4,128,128]{3,2,1,0:T(8,128)S(1)} %coefficients.5.refs_5_.refs_3_), channel_id=1, source_target_pairs={{0,4},{1,5},{2,6},{3,7},{4,0},{5,1},{6,2},{7,3},{8,12},{9,13},{10,... | collective-permute-start | bytes 1572872 | tf_op jit(solution)/shard_map/ppermute | solution.py:579
  94.9 43.1 %collective-permute-start.20 = (f32[1,32,32,128]{3,2,1,0:T(8,128)S(1)}, f32[1,32,32,128]{3,2,1,0:T(8,128)S(1)}, u32[]{:S(2)}, u32[]{:S(2)}) collective-permute-start(f32[1,32,32,128]{3,2,1,0:T(8,128)S(1)} %copy-done.11), channel_id=1, source_target_pairs={{0,16},{1,9},{2,18},{3,11},{4,20},{5,13},{6,22},{7,15},{8,24},{9,1... | collective-permute-start | bytes 1572872 | tf_op jit(solution)/shard_map/ppermute | solution.py:570
  99.7 39.1 %collective-permute-start.21 = (f32[2,1,8,32,128]{4,3,2,1,0:T(8,128)}, f32[2,1,8,32,128]{4,3,2,1,0:T(8,128)S(1)}, u32[]{:S(2)}, u32[]{:S(2)}) collective-permute-start(f32[2,1,8,32,128]{4,3,2,1,0:T(8,128)} %get-tuple-element.70), channel_id=1, source_target_pairs={{0,2},{1,3},{2,0},{3,1},{4,6},{5,7},{6,4},{7,5},{8,10},{9,11},{10,... | collective-permute-start | bytes 786440 | tf_op jit(solution)/shard_map/ppermute | solution.py:579
  103.8 35.5 %collective-permute-start.29 = (f32[1,4,128,128]{3,2,1,0:T(8,128)S(1)}, f32[1,4,128,128]{3,2,1,0:T(8,128)S(1)}, u32[]{:S(2)}, u32[]{:S(2)}) collective-permute-start(f32[1,4,128,128]{3,2,1,0:T(8,128)S(1)} %coefficients.6.refs_2_.refs_3_), channel_id=1, source_target_pairs={{0,4},{1,5},{2,6},{3,7},{4,0},{5,1},{6,2},{7,3},{8,12},{9,13},{10,... | collective-permute-start | bytes 786440 | tf_op jit(solution)/shard_map/ppermute | solution.py:579
  104.0 36.0 %collective-permute-start.19 = (f32[2,1,8,32,128]{4,3,2,1,0:T(8,128)S(1)}, f32[2,1,8,32,128]{4,3,2,1,0:T(8,128)S(1)}, u32[]{:S(2)}, u32[]{:S(2)}) collective-permute-start(f32[2,1,8,32,128]{4,3,2,1,0:T(8,128)S(1)} %join.11.refs_4_), channel_id=1, source_target_pairs={{0,2},{1,3},{2,0},{3,1},{4,6},{5,7},{6,4},{7,5},{8,10},{9,11},{10,... | collective-permute-start | bytes 786440 | tf_op jit(solution)/shard_map/ppermute | solution.py:579
  123.6 28.7 %collective-permute-start.27 = (f32[1,32,32,128]{3,2,1,0:T(8,128)}, f32[1,32,32,128]{3,2,1,0:T(8,128)}, u32[]{:S(2)}, u32[]{:S(2)}) collective-permute-start(f32[1,32,32,128]{3,2,1,0:T(8,128)} %mix.12.refs_6_), channel_id=1, source_target_pairs={{0,8},{1,17},{2,10},{3,19},{4,12},{5,21},{6,14},{7,23},{8,0},{9,25... | collective-permute-start | bytes 1572872 | tf_op jit(solution)/shard_map/ppermute | solution.py:570
  138.8 15.7 %collective-permute-start.30 = (f32[2,2,8,32,128]{4,3,2,1,0:T(8,128)}, f32[2,2,8,32,128]{4,3,2,1,0:T(8,128)S(1)}, u32[]{:S(2)}, u32[]{:S(2)}) collective-permute-start(f32[2,2,8,32,128]{4,3,2,1,0:T(8,128)} %get-tuple-element.79), channel_id=1, source_target_pairs={{0,2},{1,3},{2,0},{3,1},{4,6},{5,7},{6,4},{7,5},{8,10},{9,11},{10,... | collective-permute-start | bytes 1572872 | tf_op jit(solution)/shard_map/ppermute | solution.py:579
  138.8 31.3 %collective-permute-start.32 = (f32[2,32,32,128]{3,2,1,0:T(8,128)S(1)}, f32[2,32,32,128]{3,2,1,0:T(8,128)}, u32[]{:S(2)}, u32[]{:S(2)}) collective-permute-start(f32[2,32,32,128]{3,2,1,0:T(8,128)S(1)} %mix.14.refs_8_), channel_id=1, source_target_pairs={{0,8},{1,17},{2,10},{3,19},{4,12},{5,21},{6,14},{7,23},{8,0},{9,25... | collective-permute-start | bytes 3145736 | tf_op jit(solution)/shard_map/ppermute | solution.py:570
  140.0 19.2 %collective-permute-start.26 = (f32[1,32,32,128]{3,2,1,0:T(8,128)S(1)}, f32[1,32,32,128]{3,2,1,0:T(8,128)S(1)}, u32[]{:S(2)}, u32[]{:S(2)}) collective-permute-start(f32[1,32,32,128]{3,2,1,0:T(8,128)S(1)} %mix.13.refs_14_), channel_id=1, source_target_pairs={{0,8},{1,17},{2,10},{3,19},{4,12},{5,21},{6,14},{7,23},{8,0},{9,25... | collective-permute-start | bytes 1572872 | tf_op jit(solution)/shard_map/ppermute | solution.py:570
  147.3 14.4 %collective-permute-start.25 = (f32[1,4,128,128]{3,2,1,0:T(8,128)S(1)}, f32[1,4,128,128]{3,2,1,0:T(8,128)S(1)}, u32[]{:S(2)}, u32[]{:S(2)}) collective-permute-start(f32[1,4,128,128]{3,2,1,0:T(8,128)S(1)} %coefficients.7.refs_8_.refs_3_), channel_id=1, source_target_pairs={{0,4},{1,5},{2,6},{3,7},{4,0},{5,1},{6,2},{7,3},{8,12},{9,13},{10,... | collective-permute-start | bytes 786440 | tf_op jit(solution)/shard_map/ppermute | solution.py:579
  154.7 12.9 %collective-permute-start.33 = (f32[2,2,8,32,128]{4,3,2,1,0:T(8,128)S(1)}, f32[2,2,8,32,128]{4,3,2,1,0:T(8,128)S(1)}, u32[]{:S(2)}, u32[]{:S(2)}) collective-permute-start(f32[2,2,8,32,128]{4,3,2,1,0:T(8,128)S(1)} %join.13.refs_6_), channel_id=1, source_target_pairs={{0,1},{1,0},{2,3},{3,2},{4,5},{5,4},{6,7},{7,6},{8,9},{9,8},{10,11... | collective-permute-start | bytes 1572872 | tf_op jit(solution)/shard_map/ppermute | solution.py:579
  (64 other events, 511.6 us)

commit v8 on v7

--- a/solution.py
+++ b/solution.py
@@ -9,62 +9,51 @@
 from jax.sharding import PartitionSpec as P
 
 QUAD = 4
-NEAR_SIZES = (1, 1, 2, 1)
-FAR_SIZES = (2, 1, 1, 1)
+NEAR_SIZES = (2, 2, 1)
+FAR_SIZES = (1, 2, 2)
 ORDER = (
     ("pack", 0),
+    ("pack", 3),
+    ("pack", 1),
+    ("pack", 4),
+    ("local", 0),
     ("pack", 2),
-    ("pack", 1),
-    ("local", 0),
+    ("mix", 0),
+    ("mix", 1),
+    ("spread", 0),
+    ("join", 0),
+    ("spread", 1),
+    ("pack", 5),
     ("mix", 2),
-    ("mix", 1),
-    ("pack", 5),
-    ("pack", 6),
-    ("pack", 4),
-    ("spread", 1),
+    ("coef", 0),
     ("join", 1),
-    ("pack", 3),
     ("spread", 2),
     ("coef", 1),
-    ("mix", 0),
+    ("mix", 5),
+    ("join", 2),
+    ("filter", 0),
     ("mix", 3),
-    ("join", 2),
-    ("pack", 7),
-    ("spread", 0),
+    ("local", 1),
+    ("coef", 2),
+    ("mix", 4),
     ("filter", 1),
-    ("join", 0),
-    ("mix", 6),
-    ("coef", 2),
-    ("spread", 3),
-    ("coef", 0),
-    ("join", 3),
-    ("mix", 7),
-    ("local", 1),
-    ("mix", 4),
+    ("back", 0),
     ("filter", 2),
+    ("far", 5),
+    ("near", 0),
     ("back", 1),
-    ("mix", 5),
-    ("coef", 3),
-    ("filter", 0),
+    ("far", 3),
+    ("far", 4),
+    ("back", 2),
+    ("near", 2),
     ("near", 1),
-    ("far", 6),
-    ("back", 2),
-    ("far", 7),
-    ("filter", 3),
-    ("back", 0),
-    ("near", 0),
-    ("near", 2),
-    ("far", 4),
-    ("back", 3),
-    ("far", 5),
-    ("near", 3),
 )
 EDGES = tuple(zip(ORDER[:-1], ORDER[1:]))
 SMEM = pl.BlockSpec(memory_space=pltpu.SMEM)
 STAMP = pl.BlockSpec((8, 128), lambda i: (0, 0))
 ANY = pl.BlockSpec(memory_space=pl.ANY)
 COST = pl.CostEstimate(flops=0, bytes_accessed=0, transcendentals=0)
-PARAMS = pltpu.CompilerParams(vmem_limit_bytes=48 * 1024 * 1024)
+PARAMS = pltpu.CompilerParams(vmem_limit_bytes=24 * 1024 * 1024)
 
 
 def spectral_values(slots):

time: 178 us -> 161 us (0.904)
  Pallas kernels: 81.2 us -> 48.7 us
  waiting for transfers between devices: 41.1 us -> 67.7 us
  starting transfers between devices: 41.1 us -> 34 us
  local copies, waits for them, and re-layouts: 12.3 us -> 9.42 us
    pallas_call x38 -> x29, Pallas kernels: 64.2 us -> 35.4 us  [call(): pl.pallas_call(lambda *refs: kernel(*refs[:len(inputs)], *refs[len(inputs...]
    ppermute x16 -> x12, waiting for transfers between devices: 13.9 us -> 27.5 us  [to_partner(): return lax.ppermute(x, ('inst', 'space'), pairs)]
    ppermute x20 -> x15, waiting for transfers between devices: 24.4 us -> 37.5 us  [to_sector(): return lax.ppermute(x, 'space', [(i, i ^ k) for i in range(sectors)])]
    ppermute x16 -> x12, starting transfers between devices: 22.1 us -> 14.6 us  [to_partner(): return lax.ppermute(x, ('inst', 'space'), pairs)]
    pallas_call x8 -> x6, Pallas kernels: 17 us -> 13.2 us  [table_call(): pl.pallas_call(lambda *refs: kernel(*refs[:count + 1], *refs[count + 1 +...]
    unnamed x101 -> x35, local copies, waits for them, and re-layouts: 12.3 us -> 9.42 us
    ppermute x20 -> x15, starting transfers between devices: 15.5 us -> 15.9 us  [to_sector(): return lax.ppermute(x, 'space', [(i, i ^ k) for i in range(sectors)])]
  transfers between devices with their start and end apart: 38 -> 29, of which waited for: 14 -> 12; matrix products, arithmetic and copies ran while one was open for 0% -> 1% of each run, Pallas kernels for 42% -> 28%
where the time goes in v8:
time: 161 us
  waiting for transfers between devices  67.7 us (42%)
  Pallas kernels  48.7 us (30%)
  starting transfers between devices  34 us (21%)
  local copies, waits for them, and re-layouts  9.42 us (6%)
    ppermute x15, waiting for transfers between devices, to_sector(): return lax.ppermute(x, 'space', [(i, i ^ k) for i in range(sectors)])  37.5 us
    pallas_call x29, Pallas kernels, call(): pl.pallas_call(lambda *refs: kernel(*refs[:len(inputs)], *refs[len(inputs...  35.4 us
    ppermute x12, waiting for transfers between devices, to_partner(): return lax.ppermute(x, ('inst', 'space'), pairs)  27.5 us
    ppermute x15, starting transfers between devices, to_sector(): return lax.ppermute(x, 'space', [(i, i ^ k) for i in range(sectors)])  15.9 us
    ppermute x12, starting transfers between devices, to_partner(): return lax.ppermute(x, ('inst', 'space'), pairs)  14.6 us
    pallas_call x6, Pallas kernels, table_call(): pl.pallas_call(lambda *refs: kernel(*refs[:count + 1], *refs[count + 1 +...  13.2 us
    unnamed x35, local copies, waits for them, and re-layouts  9.42 us
    ppermute x2, starting transfers between devices, ring(): lax.ppermute(x, 'space', [(i, (i + step) % sectors) for i in range(sector...  3.59 us
  transfers between devices with their start and end apart: 29, of which 12 were waited for; matrix products, arithmetic and copies ran while one was open for 1% of the time, Pallas kernels for 28%

profile of v8, /device:TPU:0, one launch (start us, length us, event | category | flops | bytes accessed | tf_op | source)
XLA Modules:
  0.0 161.0 jit_solution(17229302188455533681)
XLA Ops:
  0.0 2.5 %copy-done = f32[1,5,32,64,128]{4,3,2,1,0:T(8,128)S(1)} copy-done((f32[1,5,32,64,128]{4,3,2,1,0:T(8,128)S(1)}, f32[1,5,32,64,128]{4,3,2,1,0:T(8,128)}, u32[]{:S(2)}) %copy-start) | copy-done | bytes 5242904
  4.9 3.0 %collective-permute-start.3 = (f32[2,32,32,128]{3,2,1,0:T(8,128)}, f32[2,32,32,128]{3,2,1,0:T(8,128)}, u32[]{:S(2)}, u32[]{:S(2)}) collective-permute-start(f32[2,32,32,128]{3,2,1,0:T(8,128)} %get-tuple-element.43.refs_1_), channel_id=1, source_target_pairs={{0,16},{1,9},{2,18},{3,11},{4,20},{5,13},{6,22},{7,15},{8,24},{9,1... | collective-permute-start | bytes 3145736 | tf_op jit(solution)/shard_map/ppermute | solution.py:559
  9.3 3.5 %collective-permute-start.1 = (f32[6,1,64,128]{3,2,1,0:T(8,128)}, f32[6,1,64,128]{3,2,1,0:T(8,128)S(1)}, u32[]{:S(2)}, u32[]{:S(2)}) collective-permute-start(f32[6,1,64,128]{3,2,1,0:T(8,128)} %get-tuple-element.42), channel_id=1, source_target_pairs={{0,7},{1,0},{2,1},{3,2},{4,3},{5,4},{6,5},{7,6},{8,15},{9,8},{10,9... | collective-permute-start | bytes 589832 | tf_op jit(solution)/shard_map/ppermute | solution.py:571
  13.9 2.6 %collective-permute-done.refs_12_ = f32[6,1,64,128]{3,2,1,0:T(8,128)S(1)} collective-permute-done((f32[6,1,64,128]{3,2,1,0:T(8,128)}, f32[6,1,64,128]{3,2,1,0:T(8,128)S(1)}, u32[]{:S(2)}, u32[]{:S(2)}) %collective-permute-start) | collective-permute-done | bytes 196640 | tf_op jit(solution)/shard_map/ppermute | solution.py:571
  16.5 2.5 %copy-done.1 = f32[1,5,32,64,128]{4,3,2,1,0:T(8,128)S(1)} copy-done((f32[1,5,32,64,128]{4,3,2,1,0:T(8,128)S(1)}, f32[1,5,32,64,128]{4,3,2,1,0:T(8,128)}, u32[]{:S(2)}) %copy-start.1) | copy-done | bytes 5242904
  19.0 2.5 %copy-done.4 = f32[1,5,32,64,128]{4,3,2,1,0:T(8,128)S(1)} copy-done((f32[1,5,32,64,128]{4,3,2,1,0:T(8,128)S(1)}, f32[1,5,32,64,128]{4,3,2,1,0:T(8,128)}, u32[]{:S(2)}) %copy-start.4) | copy-done | bytes 5242904
  21.5 5.6 %local_part.2 = (f32[5,32,32,128]{3,2,1,0:T(8,128)S(1)}, f32[8,128]{1,0:T(8,128)S(1)}) custom-call(f32[5,5]{1,0:T(8,128)S(1)} %copy-done.10, f32[5]{0:T(128)S(1)} %copy-done.11, s32[5,3]{1,0:T(8,128)S(1)} %copy.23.refs_2_, f32[5,32,64,128]{3,2,1,0:T(8,128)S(1)} %bitcast.11, f32[5,32,64,128]{3,2,1,0:T(8,128)S(1)} %bitcast.12, ...), custom_call_target="tpu_custom_call" | custom-call | tf_op jit(solution)/shard_map/local_part/pallas_call | solution.py:138
  35.0 9.0 %collective-permute-done.5.refs_4_ = f32[2,32,32,128]{3,2,1,0:T(8,128)S(1)} collective-permute-done((f32[2,32,32,128]{3,2,1,0:T(8,128)S(1)}, f32[2,32,32,128]{3,2,1,0:T(8,128)S(1)}, u32[]{:S(2)}, u32[]{:S(2)}) %collective-permute-start.5) | collective-permute-done | bytes 1048608 | tf_op jit(solution)/shard_map/ppermute | solution.py:559
  50.2 9.7 %collective-permute-done.4.refs_4_ = f32[2,32,32,128]{3,2,1,0:T(8,128)S(1)} collective-permute-done((f32[2,32,32,128]{3,2,1,0:T(8,128)S(1)}, f32[2,32,32,128]{3,2,1,0:T(8,128)S(1)}, u32[]{:S(2)}, u32[]{:S(2)}) %collective-permute-start.4) | collective-permute-done | bytes 1048608 | tf_op jit(solution)/shard_map/ppermute | solution.py:559
  67.9 2.4 %coefficients.3.refs_2_.refs_3_ = f32[2,4,128,128]{3,2,1,0:T(8,128)S(1)} custom-call(s32[22]{0:T(128)S(1)} %pad_add_fusion.refs_0_, f32[71]{0:T(128)S(1)} %copy-done.9, f32[2,16,128,128]{3,2,1,0:T(8,128)S(1)} %copy-done.6, f32[2,8,32,128]{3,2,1,0:T(8,128)S(1)} %get-tuple-element.48.refs_2_.refs_3_.refs_5_, ...), custom_call_target="tpu_custom_call" | custom-call | tf_op jit(solution)/shard_map/coefficients/pallas_call | solution.py:399
  73.4 7.9 %collective-permute-done.11.refs_4_ = f32[1,32,32,128]{3,2,1,0:T(8,128)S(1)} collective-permute-done((f32[1,32,32,128]{3,2,1,0:T(8,128)S(1)}, f32[1,32,32,128]{3,2,1,0:T(8,128)S(1)}, u32[]{:S(2)}, u32[]{:S(2)}) %collective-permute-start.11) | collective-permute-done | bytes 524320 | tf_op jit(solution)/shard_map/ppermute | solution.py:559
  82.5 11.1 %collective-permute-done.10.refs_5_.refs_7_ = f32[2,2,8,32,128]{4,3,2,1,0:T(8,128)S(1)} collective-permute-done((f32[2,2,8,32,128]{4,3,2,1,0:T(8,128)S(1)}, f32[2,2,8,32,128]{4,3,2,1,0:T(8,128)S(1)}, u32[]{:S(2)}, u32[]{:S(2)}) %collective-permute-start.10) | collective-permute-done | bytes 524320 | tf_op jit(solution)/shard_map/ppermute | solution.py:568
  93.6 2.4 %coefficients.4.refs_4_.refs_3_ = f32[2,4,128,128]{3,2,1,0:T(8,128)S(1)} custom-call(s32[22]{0:T(128)S(1)} %pad_add_fusion.refs_0_, f32[71]{0:T(128)S(1)} %copy-done.9, f32[2,16,128,128]{3,2,1,0:T(8,128)S(1)} %copy-done.6, f32[2,8,32,128]{3,2,1,0:T(8,128)S(1)} %get-tuple-element.49.refs_1_.refs_3_.refs_5_, ...), custom_call_target="tpu_custom_call" | custom-call | tf_op jit(solution)/shard_map/coefficients/pallas_call | solution.py:399
  97.8 2.5 %collective-permute-start.16 = (f32[2,1,8,32,128]{4,3,2,1,0:T(8,128)S(1)}, f32[2,1,8,32,128]{4,3,2,1,0:T(8,128)S(1)}, u32[]{:S(2)}, u32[]{:S(2)}) collective-permute-start(f32[2,1,8,32,128]{4,3,2,1,0:T(8,128)S(1)} %join.8.refs_8_), channel_id=1, source_target_pairs={{0,2},{1,3},{2,0},{3,1},{4,6},{5,7},{6,4},{7,5},{8,10},{9,11},{10,... | collective-permute-start | bytes 786440 | tf_op jit(solution)/shard_map/ppermute | solution.py:568
  100.4 2.5 %filtered.3 = (f32[2,8,32,128]{3,2,1,0:T(8,128)S(1)}, f32[2,2,8,32,128]{4,3,2,1,0:T(8,128)S(1)}, f32[2,2,8,32,128]{4,3,2,1,0:T(8,128)S(1)}) custom-call(s32[22]{0:T(128)S(1)} %pad_add_fusion.refs_0_, f32[71]{0:T(128)S(1)} %copy-done.9, f32[2,16,128,128]{3,2,1,0:T(8,128)S(1)} %copy-done.5, f32[2,4,128,128]{3,2,1,0:T(8,128)S(1)} %coefficients.3.refs_2_.refs_3_, ...), custom_call_target="tpu_custom_call" | custom-call | tf_op jit(solution)/shard_map/filtered/pallas_call | solution.py:399
  103.7 5.6 %local_part.3 = (f32[5,32,32,128]{3,2,1,0:T(8,128)S(1)}, f32[8,128]{1,0:T(8,128)S(1)}) custom-call(f32[5,5]{1,0:T(8,128)S(1)} %copy-done.10, f32[5]{0:T(128)S(1)} %copy-done.11, s32[5,3]{1,0:T(8,128)S(1)} %copy.23.refs_2_, f32[5,32,64,128]{3,2,1,0:T(8,128)S(1)} %bitcast.24, f32[5,32,64,128]{3,2,1,0:T(8,128)S(1)} %bitcast.25, ...), custom_call_target="tpu_custom_call" | custom-call | tf_op jit(solution)/shard_map/local_part/pallas_call | solution.py:138
  109.3 5.5 %collective-permute-done.16.refs_5_.refs_7_ = f32[2,1,8,32,128]{4,3,2,1,0:T(8,128)S(1)} collective-permute-done((f32[2,1,8,32,128]{4,3,2,1,0:T(8,128)S(1)}, f32[2,1,8,32,128]{4,3,2,1,0:T(8,128)S(1)}, u32[]{:S(2)}, u32[]{:S(2)}) %collective-permute-start.16) | collective-permute-done | bytes 262176 | tf_op jit(solution)/shard_map/ppermute | solution.py:568
  117.4 3.1 %collective-permute-start.23 = (f32[1,4,128,128]{3,2,1,0:T(8,128)S(1)}, f32[1,4,128,128]{3,2,1,0:T(8,128)S(1)}, u32[]{:S(2)}, u32[]{:S(2)}) collective-permute-start(f32[1,4,128,128]{3,2,1,0:T(8,128)S(1)} %coefficients.5.refs_4_.refs_3_), channel_id=1, source_target_pairs={{0,4},{1,5},{2,6},{3,7},{4,0},{5,1},{6,2},{7,3},{8,12},{9,13},{10,... | collective-permute-start | bytes 786440 | tf_op jit(solution)/shard_map/ppermute | solution.py:568
  120.5 2.4 %collective-permute-done.12.refs_4_ = f32[2,4,128,128]{3,2,1,0:T(8,128)S(1)} collective-permute-done((f32[2,4,128,128]{3,2,1,0:T(8,128)S(1)}, f32[2,4,128,128]{3,2,1,0:T(8,128)S(1)}, u32[]{:S(2)}, u32[]{:S(2)}) %collective-permute-start.12) | collective-permute-done | bytes 524320 | tf_op jit(solution)/shard_map/ppermute | solution.py:568
  122.9 2.5 %filtered.4 = (f32[2,8,32,128]{3,2,1,0:T(8,128)S(1)}, f32[2,2,8,32,128]{4,3,2,1,0:T(8,128)S(1)}, f32[2,2,8,32,128]{4,3,2,1,0:T(8,128)S(1)}) custom-call(s32[22]{0:T(128)S(1)} %pad_add_fusion.refs_0_, f32[71]{0:T(128)S(1)} %copy-done.9, f32[2,16,128,128]{3,2,1,0:T(8,128)S(1)} %copy-done.5, f32[2,4,128,128]{3,2,1,0:T(8,128)S(1)} %coefficients.4.refs_4_.refs_3_, ...), custom_call_target="tpu_custom_call" | custom-call | tf_op jit(solution)/shard_map/filtered/pallas_call | solution.py:399
  125.4 9.6 %collective-permute-done.20.refs_1_.refs_4_ = f32[2,2,8,32,128]{4,3,2,1,0:T(8,128)S(1)} collective-permute-done((f32[2,2,8,32,128]{4,3,2,1,0:T(8,128)S(1)}, f32[2,2,8,32,128]{4,3,2,1,0:T(8,128)S(1)}, u32[]{:S(2)}, u32[]{:S(2)}) %collective-permute-start.20) | collective-permute-done | bytes 524320 | tf_op jit(solution)/shard_map/ppermute | solution.py:568
  141.9 2.5 %place_near.3 = (f32[5,32,64,128]{3,2,1,0:T(8,128)}, f32[8,128]{1,0:T(8,128)S(1)}) custom-call(s32[22]{0:T(128)S(1)} %pad_add_fusion.refs_0_, f32[71]{0:T(128)S(1)} %copy-done.9, f32[2,8,32,128]{3,2,1,0:T(8,128)S(1)} %get-tuple-element.55.refs_4_.refs_2_, f32[2,2,8,32,128]{4,3,2,1,0:T(8,128)S(1)} %collective-permute-done.21.refs_3_, ...), custom_call_target="tpu_custom_call", output_to_operand_aliasing={{0}: (5, {})} | custom-call | tf_op jit(solution)/shard_map/place_near/pallas_call | solution.py:138
  144.4 5.5 %collective-permute-done.19.refs_1_.refs_4_ = f32[2,2,8,32,128]{4,3,2,1,0:T(8,128)S(1)} collective-permute-done((f32[2,2,8,32,128]{4,3,2,1,0:T(8,128)S(1)}, f32[2,2,8,32,128]{4,3,2,1,0:T(8,128)S(1)}, u32[]{:S(2)}, u32[]{:S(2)}) %collective-permute-start.19) | collective-permute-done | bytes 524320 | tf_op jit(solution)/shard_map/ppermute | solution.py:568
  158.5 2.5 %place_near.5 = (f32[5,32,64,128]{3,2,1,0:T(8,128)}, f32[8,128]{1,0:T(8,128)}) custom-call(s32[22]{0:T(128)S(1)} %pad_add_fusion.refs_0_, f32[71]{0:T(128)S(1)} %copy-done.9, f32[2,8,32,128]{3,2,1,0:T(8,128)S(1)} %get-tuple-element.57.refs_2_, f32[2,2,8,32,128]{4,3,2,1,0:T(8,128)S(1)} %collective-permute-done.24.refs_3_, ...), custom_call_target="tpu_custom_call", output_to_operand_aliasing={{0}: (5, {})} | custom-call | tf_op jit(solution)/shard_map/place_near/pallas_call | solution.py:138
  (107 shorter events, 51.9 us)
Async XLA Ops:
  4.9 22.2 %collective-permute-start.3 = (f32[2,32,32,128]{3,2,1,0:T(8,128)}, f32[2,32,32,128]{3,2,1,0:T(8,128)}, u32[]{:S(2)}, u32[]{:S(2)}) collective-permute-start(f32[2,32,32,128]{3,2,1,0:T(8,128)} %get-tuple-element.43.refs_1_), channel_id=1, source_target_pairs={{0,16},{1,9},{2,18},{3,11},{4,20},{5,13},{6,22},{7,15},{8,24},{9,1... | collective-permute-start | bytes 3145736 | tf_op jit(solution)/shard_map/ppermute | solution.py:559
  9.1 23.0 %collective-permute-start.2 = (f32[2,32,32,128]{3,2,1,0:T(8,128)}, f32[2,32,32,128]{3,2,1,0:T(8,128)S(1)}, u32[]{:S(2)}, u32[]{:S(2)}) collective-permute-start(f32[2,32,32,128]{3,2,1,0:T(8,128)} %pack.8.refs_1_), channel_id=1, source_target_pairs={{0,16},{1,9},{2,18},{3,11},{4,20},{5,13},{6,22},{7,15},{8,24},{9,1... | collective-permute-start | bytes 3145736 | tf_op jit(solution)/shard_map/ppermute | solution.py:559
  9.2 7.3 %collective-permute-start = (f32[6,1,64,128]{3,2,1,0:T(8,128)}, f32[6,1,64,128]{3,2,1,0:T(8,128)S(1)}, u32[]{:S(2)}, u32[]{:S(2)}) collective-permute-start(f32[6,1,64,128]{3,2,1,0:T(8,128)} %get-tuple-element.41), channel_id=1, source_target_pairs={{0,1},{1,2},{2,3},{3,4},{4,5},{5,6},{6,7},{7,0},{8,9},{9,10},{10,1... | collective-permute-start | bytes 589832 | tf_op jit(solution)/shard_map/ppermute | solution.py:571
  29.1 14.9 %collective-permute-start.5 = (f32[2,32,32,128]{3,2,1,0:T(8,128)S(1)}, f32[2,32,32,128]{3,2,1,0:T(8,128)S(1)}, u32[]{:S(2)}, u32[]{:S(2)}) collective-permute-start(f32[2,32,32,128]{3,2,1,0:T(8,128)S(1)} %mix.6.refs_4_), channel_id=1, source_target_pairs={{0,8},{1,17},{2,10},{3,19},{4,12},{5,21},{6,14},{7,23},{8,0},{9,25... | collective-permute-start | bytes 3145736 | tf_op jit(solution)/shard_map/ppermute | solution.py:559
  32.9 26.9 %collective-permute-start.4 = (f32[2,32,32,128]{3,2,1,0:T(8,128)S(1)}, f32[2,32,32,128]{3,2,1,0:T(8,128)S(1)}, u32[]{:S(2)}, u32[]{:S(2)}) collective-permute-start(f32[2,32,32,128]{3,2,1,0:T(8,128)S(1)} %mix.7.refs_5_), channel_id=1, source_target_pairs={{0,8},{1,17},{2,10},{3,19},{4,12},{5,21},{6,14},{7,23},{8,0},{9,25... | collective-permute-start | bytes 3145736 | tf_op jit(solution)/shard_map/ppermute | solution.py:559
  47.8 17.9 %collective-permute-start.9 = (f32[1,32,32,128]{3,2,1,0:T(8,128)S(1)}, f32[1,32,32,128]{3,2,1,0:T(8,128)S(1)}, u32[]{:S(2)}, u32[]{:S(2)}) collective-permute-start(f32[1,32,32,128]{3,2,1,0:T(8,128)S(1)} %pack.10.refs_4_), channel_id=1, source_target_pairs={{0,16},{1,9},{2,18},{3,11},{4,20},{5,13},{6,22},{7,15},{8,24},{9,1... | collective-permute-start | bytes 1572872 | tf_op jit(solution)/shard_map/ppermute | solution.py:559
  49.6 18.3 %collective-permute-start.8 = (f32[2,2,8,32,128]{4,3,2,1,0:T(8,128)S(1)}, f32[2,2,8,32,128]{4,3,2,1,0:T(8,128)S(1)}, u32[]{:S(2)}, u32[]{:S(2)}) collective-permute-start(f32[2,2,8,32,128]{4,3,2,1,0:T(8,128)S(1)} %join.6.refs_5_), channel_id=1, source_target_pairs={{0,2},{1,3},{2,0},{3,1},{4,6},{5,7},{6,4},{7,5},{8,10},{9,11},{10,... | collective-permute-start | bytes 1572872 | tf_op jit(solution)/shard_map/ppermute | solution.py:568
  61.4 8.9 %collective-permute-start.7 = (f32[2,2,8,32,128]{4,3,2,1,0:T(8,128)S(1)}, f32[2,2,8,32,128]{4,3,2,1,0:T(8,128)S(1)}, u32[]{:S(2)}, u32[]{:S(2)}) collective-permute-start(f32[2,2,8,32,128]{4,3,2,1,0:T(8,128)S(1)} %get-tuple-element.50), channel_id=1, source_target_pairs={{0,1},{1,0},{2,3},{3,2},{4,5},{5,4},{6,7},{7,6},{8,9},{9,8},{10,11... | collective-permute-start | bytes 1572872 | tf_op jit(solution)/shard_map/ppermute | solution.py:568
  63.9 32.2 %collective-permute-start.15 = (f32[2,32,32,128]{3,2,1,0:T(8,128)S(1)}, f32[2,32,32,128]{3,2,1,0:T(8,128)S(1)}, u32[]{:S(2)}, u32[]{:S(2)}) collective-permute-start(f32[2,32,32,128]{3,2,1,0:T(8,128)S(1)} %pack.11.refs_4_), channel_id=1, source_target_pairs={{0,16},{1,9},{2,18},{3,11},{4,20},{5,13},{6,22},{7,15},{8,24},{9,1... | collective-permute-start | bytes 3145736 | tf_op jit(solution)/shard_map/ppermute | solution.py:559
  66.3 14.9 %collective-permute-start.11 = (f32[1,32,32,128]{3,2,1,0:T(8,128)S(1)}, f32[1,32,32,128]{3,2,1,0:T(8,128)S(1)}, u32[]{:S(2)}, u32[]{:S(2)}) collective-permute-start(f32[1,32,32,128]{3,2,1,0:T(8,128)S(1)} %mix.8.refs_6_), channel_id=1, source_target_pairs={{0,8},{1,17},{2,10},{3,19},{4,12},{5,21},{6,14},{7,23},{8,0},{9,25... | collective-permute-start | bytes 1572872 | tf_op jit(solution)/shard_map/ppermute | solution.py:559
  70.4 23.2 %collective-permute-start.10 = (f32[2,2,8,32,128]{4,3,2,1,0:T(8,128)S(1)}, f32[2,2,8,32,128]{4,3,2,1,0:T(8,128)S(1)}, u32[]{:S(2)}, u32[]{:S(2)}) collective-permute-start(f32[2,2,8,32,128]{4,3,2,1,0:T(8,128)S(1)} %join.7.refs_5_), channel_id=1, source_target_pairs={{0,2},{1,3},{2,0},{3,1},{4,6},{5,7},{6,4},{7,5},{8,10},{9,11},{10,... | collective-permute-start | bytes 1572872 | tf_op jit(solution)/shard_map/ppermute | solution.py:568
  71.1 45.4 %collective-permute-start.13 = (f32[2,32,32,128]{3,2,1,0:T(8,128)S(1)}, f32[2,32,32,128]{3,2,1,0:T(8,128)S(1)}, u32[]{:S(2)}, u32[]{:S(2)}) collective-permute-start(f32[2,32,32,128]{3,2,1,0:T(8,128)S(1)} %pack.9.refs_14_), channel_id=1, source_target_pairs={{0,16},{1,9},{2,18},{3,11},{4,20},{5,13},{6,22},{7,15},{8,24},{9,1... | collective-permute-start | bytes 3145736 | tf_op jit(solution)/shard_map/ppermute | solution.py:559
  71.6 26.2 %collective-permute-start.18 = (f32[2,4,128,128]{3,2,1,0:T(8,128)S(1)}, f32[2,4,128,128]{3,2,1,0:T(8,128)S(1)}, u32[]{:S(2)}, u32[]{:S(2)}) collective-permute-start(f32[2,4,128,128]{3,2,1,0:T(8,128)S(1)} %coefficients.3.refs_2_.refs_3_), channel_id=1, source_target_pairs={{0,4},{1,5},{2,6},{3,7},{4,0},{5,1},{6,2},{7,3},{8,12},{9,13},{10,... | collective-permute-start | bytes 1572872 | tf_op jit(solution)/shard_map/ppermute | solution.py:568
  81.2 21.7 %collective-permute-start.17 = (f32[1,32,32,128]{3,2,1,0:T(8,128)S(1)}, f32[1,32,32,128]{3,2,1,0:T(8,128)S(1)}, u32[]{:S(2)}, u32[]{:S(2)}) collective-permute-start(f32[1,32,32,128]{3,2,1,0:T(8,128)S(1)} %copy-done.8), channel_id=1, source_target_pairs={{0,16},{1,9},{2,18},{3,11},{4,20},{5,13},{6,22},{7,15},{8,24},{9,1... | collective-permute-start | bytes 1572872 | tf_op jit(solution)/shard_map/ppermute | solution.py:559
  96.0 26.8 %collective-permute-start.12 = (f32[2,4,128,128]{3,2,1,0:T(8,128)S(1)}, f32[2,4,128,128]{3,2,1,0:T(8,128)S(1)}, u32[]{:S(2)}, u32[]{:S(2)}) collective-permute-start(f32[2,4,128,128]{3,2,1,0:T(8,128)S(1)} %coefficients.4.refs_4_.refs_3_), channel_id=1, source_target_pairs={{0,4},{1,5},{2,6},{3,7},{4,0},{5,1},{6,2},{7,3},{8,12},{9,13},{10,... | collective-permute-start | bytes 1572872 | tf_op jit(solution)/shard_map/ppermute | solution.py:568
  97.7 40.6 %collective-permute-start.22 = (f32[2,32,32,128]{3,2,1,0:T(8,128)S(1)}, f32[2,32,32,128]{3,2,1,0:T(8,128)S(1)}, u32[]{:S(2)}, u32[]{:S(2)}) collective-permute-start(f32[2,32,32,128]{3,2,1,0:T(8,128)S(1)} %mix.9.refs_2_), channel_id=1, source_target_pairs={{0,8},{1,17},{2,10},{3,19},{4,12},{5,21},{6,14},{7,23},{8,0},{9,25... | collective-permute-start | bytes 3145736 | tf_op jit(solution)/shard_map/ppermute | solution.py:559
  97.8 17.0 %collective-permute-start.16 = (f32[2,1,8,32,128]{4,3,2,1,0:T(8,128)S(1)}, f32[2,1,8,32,128]{4,3,2,1,0:T(8,128)S(1)}, u32[]{:S(2)}, u32[]{:S(2)}) collective-permute-start(f32[2,1,8,32,128]{4,3,2,1,0:T(8,128)S(1)} %join.8.refs_8_), channel_id=1, source_target_pairs={{0,2},{1,3},{2,0},{3,1},{4,6},{5,7},{6,4},{7,5},{8,10},{9,11},{10,... | collective-permute-start | bytes 786440 | tf_op jit(solution)/shard_map/ppermute | solution.py:568
  102.9 32.0 %collective-permute-start.20 = (f32[2,2,8,32,128]{4,3,2,1,0:T(8,128)S(1)}, f32[2,2,8,32,128]{4,3,2,1,0:T(8,128)S(1)}, u32[]{:S(2)}, u32[]{:S(2)}) collective-permute-start(f32[2,2,8,32,128]{4,3,2,1,0:T(8,128)S(1)} %get-tuple-element.61), channel_id=1, source_target_pairs={{0,2},{1,3},{2,0},{3,1},{4,6},{5,7},{6,4},{7,5},{8,10},{9,11},{10,... | collective-permute-start | bytes 1572872 | tf_op jit(solution)/shard_map/ppermute | solution.py:568
  117.3 34.1 %collective-permute-start.26 = (f32[2,32,32,128]{3,2,1,0:T(8,128)S(1)}, f32[2,32,32,128]{3,2,1,0:T(8,128)S(1)}, u32[]{:S(2)}, u32[]{:S(2)}) collective-permute-start(f32[2,32,32,128]{3,2,1,0:T(8,128)S(1)} %mix.11.refs_8_), channel_id=1, source_target_pairs={{0,8},{1,17},{2,10},{3,19},{4,12},{5,21},{6,14},{7,23},{8,0},{9,25... | collective-permute-start | bytes 3145736 | tf_op jit(solution)/shard_map/ppermute | solution.py:559
  117.4 17.8 %collective-permute-start.23 = (f32[1,4,128,128]{3,2,1,0:T(8,128)S(1)}, f32[1,4,128,128]{3,2,1,0:T(8,128)S(1)}, u32[]{:S(2)}, u32[]{:S(2)}) collective-permute-start(f32[1,4,128,128]{3,2,1,0:T(8,128)S(1)} %coefficients.5.refs_4_.refs_3_), channel_id=1, source_target_pairs={{0,4},{1,5},{2,6},{3,7},{4,0},{5,1},{6,2},{7,3},{8,12},{9,13},{10,... | collective-permute-start | bytes 786440 | tf_op jit(solution)/shard_map/ppermute | solution.py:568
  135.1 14.8 %collective-permute-start.19 = (f32[2,2,8,32,128]{4,3,2,1,0:T(8,128)S(1)}, f32[2,2,8,32,128]{4,3,2,1,0:T(8,128)S(1)}, u32[]{:S(2)}, u32[]{:S(2)}) collective-permute-start(f32[2,2,8,32,128]{4,3,2,1,0:T(8,128)S(1)} %get-tuple-element.59), channel_id=1, source_target_pairs={{0,2},{1,3},{2,0},{3,1},{4,6},{5,7},{6,4},{7,5},{8,10},{9,11},{10,... | collective-permute-start | bytes 1572872 | tf_op jit(solution)/shard_map/ppermute | solution.py:568
  135.2 14.8 %collective-permute-start.27 = (f32[1,32,32,128]{3,2,1,0:T(8,128)S(1)}, f32[1,32,32,128]{3,2,1,0:T(8,128)S(1)}, u32[]{:S(2)}, u32[]{:S(2)}) collective-permute-start(f32[1,32,32,128]{3,2,1,0:T(8,128)S(1)} %mix.10.refs_14_), channel_id=1, source_target_pairs={{0,8},{1,17},{2,10},{3,19},{4,12},{5,21},{6,14},{7,23},{8,0},{9,25... | collective-permute-start | bytes 1572872 | tf_op jit(solution)/shard_map/ppermute | solution.py:559
  138.3 16.8 %collective-permute-start.25 = (f32[2,1,8,32,128]{4,3,2,1,0:T(8,128)S(1)}, f32[2,1,8,32,128]{4,3,2,1,0:T(8,128)S(1)}, u32[]{:S(2)}, u32[]{:S(2)}) collective-permute-start(f32[2,1,8,32,128]{4,3,2,1,0:T(8,128)S(1)} %get-tuple-element.68), channel_id=1, source_target_pairs={{0,2},{1,3},{2,0},{3,1},{4,6},{5,7},{6,4},{7,5},{8,10},{9,11},{10,... | collective-permute-start | bytes 786440 | tf_op jit(solution)/shard_map/ppermute | solution.py:568
  149.9 8.6 %collective-permute-start.24 = (f32[2,2,8,32,128]{4,3,2,1,0:T(8,128)S(1)}, f32[2,2,8,32,128]{4,3,2,1,0:T(8,128)S(1)}, u32[]{:S(2)}, u32[]{:S(2)}) collective-permute-start(f32[2,2,8,32,128]{4,3,2,1,0:T(8,128)S(1)} %join.10.refs_6_), channel_id=1, source_target_pairs={{0,1},{1,0},{2,3},{3,2},{4,5},{5,4},{6,7},{7,6},{8,9},{9,8},{10,11... | collective-permute-start | bytes 1572872 | tf_op jit(solution)/shard_map/ppermute | solution.py:568
  (22 other events, 152.9 us)

commit v9 on v8

--- a/solution.py
+++ b/solution.py
@@ -9,51 +9,60 @@
 from jax.sharding import PartitionSpec as P
 
 QUAD = 4
-NEAR_SIZES = (2, 2, 1)
-FAR_SIZES = (1, 2, 2)
+NEAR_SIZES = (1, 2, 1, 1)
+FAR_SIZES = (2, 2, 1)
 ORDER = (
     ("pack", 0),
+    ("pack", 1),
+    ("mix", 0),
     ("pack", 3),
-    ("pack", 1),
-    ("pack", 4),
     ("local", 0),
-    ("pack", 2),
-    ("mix", 0),
+    ("mix", 3),
     ("mix", 1),
     ("spread", 0),
+    ("pack", 6),
+    ("pack", 4),
     ("join", 0),
+    ("spread", 3),
+    ("pack", 5),
+    ("join", 3),
+    ("pack", 2),
     ("spread", 1),
-    ("pack", 5),
+    ("coef", 3),
     ("mix", 2),
     ("coef", 0),
     ("join", 1),
+    ("filter", 3),
     ("spread", 2),
+    ("mix", 4),
+    ("mix", 6),
     ("coef", 1),
-    ("mix", 5),
     ("join", 2),
     ("filter", 0),
-    ("mix", 3),
+    ("back", 3),
+    ("coef", 2),
+    ("mix", 5),
     ("local", 1),
-    ("coef", 2),
-    ("mix", 4),
+    ("near", 3),
     ("filter", 1),
+    ("far", 6),
+    ("filter", 2),
     ("back", 0),
-    ("filter", 2),
-    ("far", 5),
     ("near", 0),
     ("back", 1),
-    ("far", 3),
     ("far", 4),
     ("back", 2),
+    ("far", 5),
     ("near", 2),
     ("near", 1),
 )
 EDGES = tuple(zip(ORDER[:-1], ORDER[1:]))
+PACK = 60
+LOCAL = 52
 SMEM = pl.BlockSpec(memory_space=pltpu.SMEM)
-STAMP = pl.BlockSpec((8, 128), lambda i: (0, 0))
 ANY = pl.BlockSpec(memory_space=pl.ANY)
 COST = pl.CostEstimate(flops=0, bytes_accessed=0, transcendentals=0)
-PARAMS = pltpu.CompilerParams(vmem_limit_bytes=24 * 1024 * 1024)
+MIB = 1024 * 1024
 
 
 def spectral_values(slots):
@@ -133,17 +142,31 @@
     return (slot // 2 + s) % (slots // 2) * 2 + slot % 2
 
 
-def call(kernel, name, token, grid, inputs, in_specs, out_specs, out_shape, scratch=(), alias=None):
-    extra = [t for t in token or () if all(t is not x for x in inputs)]
+def stamped(kernel, inputs, extra, out_specs, out_shape):
+    out_specs = out_specs if isinstance(out_specs, list) else [out_specs]
+    out_shape = out_shape if isinstance(out_shape, list) else [out_shape]
+    skip, end = inputs + extra, inputs + extra + len(out_shape)
+
+    def body(*refs):
+        refs[end][...] = jnp.zeros_like(refs[end])
+        kernel(*refs[:inputs], *refs[skip:end], *refs[end + 1 :])
+
+    stamp = pl.BlockSpec((8, 128), lambda i, *_: (0, 0))
+    return body, out_specs + [stamp], out_shape + [shaped(8, 128)]
+
+
+def call(kernel, name, token, grid, inputs, in_specs, out_specs, out_shape, scratch=(), alias=None, grant=24):
+    extra = list(token)
+    kernel, out_specs, out_shape = stamped(kernel, len(inputs), len(extra), out_specs, out_shape)
     return pl.pallas_call(
-        lambda *refs: kernel(*refs[: len(inputs)], *refs[len(inputs) + len(extra) :]),
+        kernel,
         grid=grid,
         in_specs=list(in_specs) + [ANY] * len(extra),
         out_specs=out_specs,
         out_shape=out_shape,
         scratch_shapes=list(scratch),
         input_output_aliases=alias or {},
-        compiler_params=PARAMS,
+        compiler_params=pltpu.CompilerParams(vmem_limit_bytes=grant * MIB),
         cost_estimate=COST,
         name=name,
     )(*inputs, *extra)
@@ -153,7 +176,7 @@
     return jax.ShapeDtypeStruct(shape, jnp.float32)
 
 
-def pack(center, viscosity, lo, hi, index, near, edges, token):
+def pack(center, viscosity, lo, hi, index, near, edges, token, early):
     fields, block, rows, cells = center.shape
     inputs, in_specs = [center], [pl.BlockSpec((1, block, near, cells), lambda i: (lo + i, 0, index, 0))]
     shapes = [shaped(hi - lo, block, near, cells)]
@@ -173,11 +196,11 @@
             edge[:fields] = refs[2 * e][...]
             edge[fields] = refs[2 * e + 1][...]
 
-    return call(kernel, "pack", token, (hi - lo,), inputs, in_specs, out_specs, shapes)
+    return call(kernel, "pack", token, (hi - lo,), inputs, in_specs, out_specs, shapes, grant=PACK if early else 24)
 
 
 def local_kernel(
-    far, coupling, kappa, flags, adj, before, after, next_to, src, mu, mu_before, mu_after, mu_next, low, high, out, stamp
+    far, coupling, kappa, flags, adj, before, after, next_to, src, mu, mu_before, mu_after, mu_next, low, high, out
 ):
     fields, planes, rows, cells = adj.shape
     step = pl.program_id(0)
@@ -186,7 +209,6 @@
     row = lax.broadcasted_iota(jnp.int32, (rows, cells), 0)
     col = lax.broadcasted_iota(jnp.int32, (rows, cells), 1)
     ring = 0.5 / ((row + rows * far).astype(jnp.float32) + 1.0)
-    stamp[...] = jnp.zeros_like(stamp)
 
     def pick(source, behind, ahead, f, k):
         if k < 0:
@@ -280,8 +302,9 @@
             halo,
             halo,
         ],
-        [pl.BlockSpec((fields, planes, half, cells), lambda i: (0, i, 0, 0)), STAMP],
-        [shaped(fields, block, half, cells), shaped(8, 128)],
+        pl.BlockSpec((fields, planes, half, cells), lambda i: (0, i, 0, 0)),
+        shaped(fields, block, half, cells),
+        grant=24 if far else LOCAL,
     )
 
 
@@ -394,10 +417,10 @@
         )
 
     def table_call(self, kernel, name, fields, inputs, in_specs, out_specs, out_shape, scratch, token):
-        extra = [t for t in token or () if all(t is not x for x in inputs)]
-        count = len(inputs)
+        extra = list(token)
+        kernel, out_specs, out_shape = stamped(kernel, 1 + len(inputs), len(extra), out_specs, out_shape)
         return pl.pallas_call(
-            lambda *refs: kernel(*refs[: count + 1], *refs[count + 1 + len(extra) :]),
+            kernel,
             grid_spec=pltpu.PrefetchScalarGridSpec(
                 num_scalar_prefetch=1,
                 grid=(fields,),
@@ -406,7 +429,7 @@
                 scratch_shapes=scratch,
             ),
             out_shape=out_shape,
-            compiler_params=PARAMS,
+            compiler_params=pltpu.CompilerParams(vmem_limit_bytes=24 * MIB),
             cost_estimate=COST,
             name=name,
         )(self.ints, *inputs, *extra)
@@ -492,8 +515,7 @@
         carried = [] if held is None else [held]
 
         def kernel(ints, reals, mine, core, chip, *refs):
-            out, stamp, stage = refs[-3:]
-            stamp[...] = jnp.zeros_like(stamp)
+            out, stage = refs[-2:]
             rank = self.scalars(ints, reals).rank
             for k, part in enumerate((mine[0], core[0, 0], chip[0, 0], core[1, 0])):
                 stage[rank ^ k] = part
@@ -509,16 +531,15 @@
             (hi - lo,),
             [self.ints, self.reals, mine, core, chip] + carried,
             [SMEM, SMEM, self.part(), self.parts(2), self.parts(1)] + [ANY] * len(carried),
-            [self.side(lo, 0), STAMP],
-            [shaped(*self.shape), shaped(8, 128)],
+            self.side(lo, 0),
+            shaped(*self.shape),
             [pltpu.VMEM((QUAD, self.cycles, self.block, self.cells), jnp.float32)],
             alias={5: 0} if carried else None,
         )
 
     def place_far(self, local, others, held, lo, hi, token):
         def kernel(ints, reals, local, *refs):
-            others, (out, stamp) = refs[: len(refs) - 2 - len(carried)], refs[-2:]
-            stamp[...] = jnp.zeros_like(stamp)
+            others, out = refs[: len(refs) - 1 - len(carried)], refs[-1]
             out[0] = sums(self.scalars(ints, reals), local, others)
 
         carried = [] if held is None else [held]
@@ -531,8 +552,8 @@
             [SMEM, SMEM, self.side(lo, 0)]
             + [self.side(0, 0)] * len(others)
             + [ANY] * len(carried),
-            [self.side(lo, 1), STAMP],
-            [shaped(*self.shape), shaped(8, 128)],
+            self.side(lo, 1),
+            shaped(*self.shape),
             alias={3 + len(others): 0} if carried else None,
         )
 
@@ -593,29 +614,27 @@
         lo, hi, index = groups[g]
         token = [made[before] for before, after in EDGES if after == (step, g)]
         if step == "pack":
-            packed = pack(center, viscosity, lo, hi, index, near, halos is None, token)
-            made[step, g] = packed[0]
+            early = 0 not in local
+            *packed, stamp = pack(center, viscosity, lo, hi, index, near, halos is None, token, early)
             first[g] = to_first(packed[0])
             if halos is None:
                 halos = ring(packed[1], 1), ring(packed[2], -1)
         elif step == "local":
-            local[g], made[step, g] = local_part(
+            local[g], stamp = local_part(
                 g, center, source[0], viscosity, kappa, coupling, bc_flags, *halos, token
             )
         elif step == "mix":
-            mixed = plan.mix(center, first[g], lo, hi, index, token)
-            made[step, g] = mixed[0]
+            *mixed, stamp = plan.mix(center, first[g], lo, hi, index, token)
             others[g] = [first[g]] + [to_later(x, s + 1) for s, x in enumerate(mixed)]
         elif step == "spread":
-            mine, core, chip = plan.spread(local[0], others[g], lo, hi, token)
-            made[step, g] = mine
+            mine, core, chip, stamp = plan.spread(local[0], others[g], lo, hi, token)
             parts[g] = mine, to_sector(core, 1), chip
         elif step == "join":
             mine, core, chip = parts[g]
-            made[step, g] = plan.join(chip, core, token)
-            parts[g] = mine, core, to_sector(made[step, g], 2)
+            chip, stamp = plan.join(chip, core, token)
+            parts[g] = mine, core, to_sector(chip, 2)
         elif step == "coef":
-            part = made[step, g] = plan.coefficients(*parts[g], token)
+            part, stamp = plan.coefficients(*parts[g], token)
             stride = QUAD
             while 2 * stride < sectors:
                 part = part + to_sector(part, stride)
@@ -623,17 +642,17 @@
             other = to_sector(part, stride) if stride < sectors else jnp.zeros_like(part)
             own[g] = part, other
         elif step == "filter":
-            mine, core, chip = plan.filtered(*own[g], *parts[g], token)
-            made[step, g] = mine
+            mine, core, chip, stamp = plan.filtered(*own[g], *parts[g], token)
             done[g] = mine, core, to_sector(chip, 2)
         elif step == "back":
             mine, core, chip = done[g]
-            made[step, g] = plan.join(core, chip, token)
-            done[g] = mine, to_sector(made[step, g], 1), chip
+            core, stamp = plan.join(core, chip, token)
+            done[g] = mine, to_sector(core, 1), chip
         elif step == "near":
-            held, made[step, g] = plan.place_near(*done[g], held, lo, hi, token)
+            held, stamp = plan.place_near(*done[g], held, lo, hi, token)
         else:
-            held, made[step, g] = plan.place_far(local[1], others[g], held, lo, hi, token)
+            held, stamp = plan.place_far(local[1], others[g], held, lo, hi, token)
+        made[step, g] = stamp
     return held[None]
 
 

time: 161 us -> 174 us (1.081)
  Pallas kernels: 48.7 us -> 61.2 us
  local copies, waits for them, and re-layouts: 9.42 us -> 6.1 us
  waiting for transfers between devices: 67.7 us -> 70.8 us
    ppermute x15 -> x20, waiting for transfers between devices: 37.5 us -> 52.3 us  [to_sector(): return lax.ppermute(x, 'space', [(i, i ^ k) for i in range(sectors)])]
    pallas_call x35 -> x43, Pallas kernels: 48.7 us -> 61.2 us  [the longest x35 45.8 us: call(): pl.pallas_call(kernel, grid=grid, in_specs=list(in_specs) + [ANY] * len(e...]
    ppermute x12 -> x14, waiting for transfers between devices: 27.5 us -> 15.5 us  [to_partner(): return lax.ppermute(x, ('inst', 'space'), pairs)]
    unnamed x35 -> x39, local copies, waits for them, and re-layouts: 9.42 us -> 6.1 us
    ppermute x12 -> x14, starting transfers between devices: 14.6 us -> 15.1 us  [to_partner(): return lax.ppermute(x, ('inst', 'space'), pairs)]
    ppermute x15 -> x20, starting transfers between devices: 15.9 us -> 15.8 us  [to_sector(): return lax.ppermute(x, 'space', [(i, i ^ k) for i in range(sectors)])]
  transfers between devices with their start and end apart: 29 -> 36, of which waited for: 12 -> 16; matrix products, arithmetic and copies ran while one was open for 1% -> 0% of each run, Pallas kernels for 28% -> 33%
where the time goes in v9:
time: 174 us; the launch traced here: 173 us
  waiting for transfers between devices  70.8 us (41%)
  Pallas kernels  61.2 us (35%)
  starting transfers between devices  34.5 us (20%)
  local copies, waits for them, and re-layouts  6.1 us (4%)
    ppermute x20, waiting for transfers between devices, to_sector(): return lax.ppermute(x, 'space', [(i, i ^ k) for i in range(sectors)])  52.3 us
    pallas_call x35, Pallas kernels, call(): pl.pallas_call(kernel, grid=grid, in_specs=list(in_specs) + [ANY] * len(e...  45.8 us
    ppermute x20, starting transfers between devices, to_sector(): return lax.ppermute(x, 'space', [(i, i ^ k) for i in range(sectors)])  15.8 us
    ppermute x14, waiting for transfers between devices, to_partner(): return lax.ppermute(x, ('inst', 'space'), pairs)  15.5 us
    pallas_call x8, Pallas kernels, table_call(): pl.pallas_call(kernel, grid_spec=pltpu.PrefetchScalarGridSpec(num_scalar_...  15.4 us
    ppermute x14, starting transfers between devices, to_partner(): return lax.ppermute(x, ('inst', 'space'), pairs)  15.1 us
    unnamed x39, local copies, waits for them, and re-layouts  6.1 us
    ppermute x2, starting transfers between devices, ring(): lax.ppermute(x, 'space', [(i, (i + step) % sectors) for i in range(sector...  3.54 us
  transfers between devices with their start and end apart: 36, of which 16 were waited for; matrix products, arithmetic and copies ran while one was open for 0% of the time, Pallas kernels for 33%

profile of v9, /device:TPU:0, one launch (start us, length us, event | category | flops | bytes accessed | tf_op | source)
XLA Modules:
  0.0 173.1 jit_solution(9125196336565596715)
XLA Ops:
  0.0 2.1 %pack.7 = (f32[1,32,32,128]{3,2,1,0:T(8,128)}, f32[6,1,64,128]{3,2,1,0:T(8,128)}, f32[6,1,64,128]{3,2,1,0:T(8,128)}, f32[8,128]{1,0:T(8,128)}) custom-call(f32[5,32,64,128]{3,2,1,0:T(8,128)} %bitcast.5, f32[5,32,64,128]{3,2,1,0:T(8,128)} %bitcast.6, f32[32,64,128]{2,1,0:T(8,128)} %refs_11_.3, f32[5,32,64,128]{3,2,1,0:T(8,128)} %bitcast.7, ...), custom_call_target="tpu_custom_call" | custom-call | tf_op jit(solution)/shard_map/pack/pallas_call | solution.py:161
  2.1 3.0 %collective-permute-start.2 = (f32[1,32,32,128]{3,2,1,0:T(8,128)}, f32[1,32,32,128]{3,2,1,0:T(8,128)S(1)}, u32[]{:S(2)}, u32[]{:S(2)}) collective-permute-start(f32[1,32,32,128]{3,2,1,0:T(8,128)} %get-tuple-element.110), channel_id=1, source_target_pairs={{0,16},{1,9},{2,18},{3,11},{4,20},{5,13},{6,22},{7,15},{8,24},{9,1... | collective-permute-start | bytes 1572872 | tf_op jit(solution)/shard_map/ppermute | solution.py:580
  5.1 2.0 %pack.8 = (f32[2,32,32,128]{3,2,1,0:T(8,128)}, f32[8,128]{1,0:T(8,128)}) custom-call(f32[5,32,64,128]{3,2,1,0:T(8,128)} %bitcast.8, f32[8,128]{1,0:T(8,128)} %get-tuple-element.111.refs_1_), custom_call_target="tpu_custom_call" | custom-call | tf_op jit(solution)/shard_map/pack/pallas_call | solution.py:161
  7.3 5.2 %collective-permute-done.2.refs_3_ = f32[1,32,32,128]{3,2,1,0:T(8,128)S(1)} collective-permute-done((f32[1,32,32,128]{3,2,1,0:T(8,128)}, f32[1,32,32,128]{3,2,1,0:T(8,128)S(1)}, u32[]{:S(2)}, u32[]{:S(2)}) %collective-permute-start.2) | collective-permute-done | bytes 524320 | tf_op jit(solution)/shard_map/ppermute | solution.py:580
  12.5 2.7 %copy-done = f32[1,5,32,64,128]{4,3,2,1,0:T(8,128)S(1)} copy-done((f32[1,5,32,64,128]{4,3,2,1,0:T(8,128)S(1)}, f32[1,5,32,64,128]{4,3,2,1,0:T(8,128)}, u32[]{:S(2)}) %copy-start) | copy-done | bytes 5242904
  19.9 2.0 %collective-permute-start.4 = (f32[1,32,32,128]{3,2,1,0:T(8,128)}, f32[1,32,32,128]{3,2,1,0:T(8,128)}, u32[]{:S(2)}, u32[]{:S(2)}) collective-permute-start(f32[1,32,32,128]{3,2,1,0:T(8,128)} %get-tuple-element.117), channel_id=1, source_target_pairs={{0,16},{1,9},{2,18},{3,11},{4,20},{5,13},{6,22},{7,15},{8,24},{9,1... | collective-permute-start | bytes 1572872 | tf_op jit(solution)/shard_map/ppermute | solution.py:580
  23.4 3.5 %collective-permute-start.1 = (f32[6,1,64,128]{3,2,1,0:T(8,128)}, f32[6,1,64,128]{3,2,1,0:T(8,128)S(1)}, u32[]{:S(2)}, u32[]{:S(2)}) collective-permute-start(f32[6,1,64,128]{3,2,1,0:T(8,128)} %get-tuple-element.109), channel_id=1, source_target_pairs={{0,7},{1,0},{2,1},{3,2},{4,3},{5,4},{6,5},{7,6},{8,15},{9,8},{10,9... | collective-permute-start | bytes 589832 | tf_op jit(solution)/shard_map/ppermute | solution.py:592
  27.7 3.0 %collective-permute-done.refs_12_ = f32[6,1,64,128]{3,2,1,0:T(8,128)S(1)} collective-permute-done((f32[6,1,64,128]{3,2,1,0:T(8,128)}, f32[6,1,64,128]{3,2,1,0:T(8,128)S(1)}, u32[]{:S(2)}, u32[]{:S(2)}) %collective-permute-start) | collective-permute-done | bytes 196640 | tf_op jit(solution)/shard_map/ppermute | solution.py:592
  32.0 8.6 %local_part.2 = (f32[5,32,32,128]{3,2,1,0:T(8,128)}, f32[8,128]{1,0:T(8,128)S(1)}) custom-call(f32[5,5]{1,0:T(8,128)S(1)} %copy-done.8, f32[5]{0:T(128)S(1)} %copy-done.12, s32[5,3]{1,0:T(8,128)S(1)} %copy.26.refs_2_, f32[5,32,64,128]{3,2,1,0:T(8,128)} %bitcast.10, f32[5,32,64,128]{3,2,1,0:T(8,128)} %bitcast.11, f32[5,32,64,128]{3,2,1,0:T(8,128)} %bitcast.12, ...), custom_call_target="tpu_custom_call" | custom-call | tf_op jit(solution)/shard_map/local_part/pallas_call | solution.py:161
  58.1 8.4 %collective-permute-done.5.refs_4_ = f32[2,32,32,128]{3,2,1,0:T(8,128)S(1)} collective-permute-done((f32[2,32,32,128]{3,2,1,0:T(8,128)S(1)}, f32[2,32,32,128]{3,2,1,0:T(8,128)S(1)}, u32[]{:S(2)}, u32[]{:S(2)}) %collective-permute-start.5) | collective-permute-done | bytes 1048608 | tf_op jit(solution)/shard_map/ppermute | solution.py:580
  75.2 5.8 %collective-permute-done.11.refs_5_.refs_7_ = f32[2,1,8,32,128]{4,3,2,1,0:T(8,128)S(1)} collective-permute-done((f32[2,1,8,32,128]{4,3,2,1,0:T(8,128)S(1)}, f32[2,1,8,32,128]{4,3,2,1,0:T(8,128)S(1)}, u32[]{:S(2)}, u32[]{:S(2)}) %collective-permute-start.11) | collective-permute-done | bytes 262176 | tf_op jit(solution)/shard_map/ppermute | solution.py:589
  84.8 2.7 %collective-permute-done.18.refs_4_ = f32[1,4,128,128]{3,2,1,0:T(8,128)S(1)} collective-permute-done((f32[1,4,128,128]{3,2,1,0:T(8,128)S(1)}, f32[1,4,128,128]{3,2,1,0:T(8,128)S(1)}, u32[]{:S(2)}, u32[]{:S(2)}) %collective-permute-start.18) | collective-permute-done | bytes 262176 | tf_op jit(solution)/shard_map/ppermute | solution.py:589
  90.4 2.1 %collective-permute-start.21 = (f32[1,4,128,128]{3,2,1,0:T(8,128)S(1)}, f32[1,4,128,128]{3,2,1,0:T(8,128)S(1)}, u32[]{:S(2)}, u32[]{:S(2)}) collective-permute-start(f32[1,4,128,128]{3,2,1,0:T(8,128)S(1)} %get-tuple-element.162.refs_3_), channel_id=1, source_target_pairs={{0,4},{1,5},{2,6},{3,7},{4,0},{5,1},{6,2},{7,3},{8,12},{9,13},{10,... | collective-permute-start | bytes 786440 | tf_op jit(solution)/shard_map/ppermute | solution.py:589
  94.1 13.9 %collective-permute-done.14.refs_5_.refs_7_ = f32[2,2,8,32,128]{4,3,2,1,0:T(8,128)S(1)} collective-permute-done((f32[2,2,8,32,128]{4,3,2,1,0:T(8,128)S(1)}, f32[2,2,8,32,128]{4,3,2,1,0:T(8,128)S(1)}, u32[]{:S(2)}, u32[]{:S(2)}) %collective-permute-start.14) | collective-permute-done | bytes 524320 | tf_op jit(solution)/shard_map/ppermute | solution.py:589
  108.0 2.4 %coefficients.6 = (f32[2,4,128,128]{3,2,1,0:T(8,128)S(1)}, f32[8,128]{1,0:T(8,128)S(1)}) custom-call(s32[22]{0:T(128)S(1)} %pad_add_fusion.refs_0_, f32[71]{0:T(128)S(1)} %copy-done.7, f32[2,16,128,128]{3,2,1,0:T(8,128)S(1)} %copy-done.4, f32[2,8,32,128]{3,2,1,0:T(8,128)S(1)} %get-tuple-element.136.refs_3_.refs_5_, ...), custom_call_target="tpu_custom_call" | custom-call | tf_op jit(solution)/shard_map/coefficients/pallas_call | solution.py:422
  114.8 5.3 %collective-permute-done.20.refs_1_.refs_4_ = f32[2,1,8,32,128]{4,3,2,1,0:T(8,128)S(1)} collective-permute-done((f32[2,1,8,32,128]{4,3,2,1,0:T(8,128)S(1)}, f32[2,1,8,32,128]{4,3,2,1,0:T(8,128)S(1)}, u32[]{:S(2)}, u32[]{:S(2)}) %collective-permute-start.20) | collective-permute-done | bytes 262176 | tf_op jit(solution)/shard_map/ppermute | solution.py:589
  120.2 3.8 %collective-permute-done.25.refs_5_.refs_7_ = f32[2,1,8,32,128]{4,3,2,1,0:T(8,128)S(1)} collective-permute-done((f32[2,1,8,32,128]{4,3,2,1,0:T(8,128)S(1)}, f32[2,1,8,32,128]{4,3,2,1,0:T(8,128)S(1)}, u32[]{:S(2)}, u32[]{:S(2)}) %collective-permute-start.25) | collective-permute-done | bytes 262176 | tf_op jit(solution)/shard_map/ppermute | solution.py:589
  127.7 5.6 %local_part.3 = (f32[5,32,32,128]{3,2,1,0:T(8,128)S(1)}, f32[8,128]{1,0:T(8,128)S(1)}) custom-call(f32[5,5]{1,0:T(8,128)S(1)} %copy-done.8, f32[5]{0:T(128)S(1)} %copy-done.12, s32[5,3]{1,0:T(8,128)S(1)} %copy.26.refs_2_, f32[5,32,64,128]{3,2,1,0:T(8,128)S(1)} %bitcast.27, f32[5,32,64,128]{3,2,1,0:T(8,128)S(1)} %bitcast.28, f32[5,32,64,128]{3,2,1,0:T(8,128)S(1)} %bitcast.29, ...), custom_call_target="tpu_custom_call" | custom-call | tf_op jit(solution)/shard_map/local_part/pallas_call | solution.py:161
  133.4 2.5 %collective-permute-start.27 = (f32[2,1,8,32,128]{4,3,2,1,0:T(8,128)S(1)}, f32[2,1,8,32,128]{4,3,2,1,0:T(8,128)S(1)}, u32[]{:S(2)}, u32[]{:S(2)}) collective-permute-start(f32[2,1,8,32,128]{4,3,2,1,0:T(8,128)S(1)} %get-tuple-element.182), channel_id=1, source_target_pairs={{0,2},{1,3},{2,0},{3,1},{4,6},{5,7},{6,4},{7,5},{8,10},{9,11},{10,... | collective-permute-start | bytes 786440 | tf_op jit(solution)/shard_map/ppermute | solution.py:589
  137.8 4.0 %collective-permute-done.19.refs_4_ = f32[2,4,128,128]{3,2,1,0:T(8,128)S(1)} collective-permute-done((f32[2,4,128,128]{3,2,1,0:T(8,128)S(1)}, f32[2,4,128,128]{3,2,1,0:T(8,128)S(1)}, u32[]{:S(2)}, u32[]{:S(2)}) %collective-permute-start.19) | collective-permute-done | bytes 524320 | tf_op jit(solution)/shard_map/ppermute | solution.py:589
  142.4 2.7 %filtered.6 = (f32[2,8,32,128]{3,2,1,0:T(8,128)S(1)}, f32[2,2,8,32,128]{4,3,2,1,0:T(8,128)S(1)}, f32[2,2,8,32,128]{4,3,2,1,0:T(8,128)S(1)}, f32[8,128]{1,0:T(8,128)S(1)}) custom-call(s32[22]{0:T(128)S(1)} %pad_add_fusion.refs_0_, f32[71]{0:T(128)S(1)} %copy-done.7, f32[2,16,128,128]{3,2,1,0:T(8,128)S(1)} %copy-done.3, ...), custom_call_target="tpu_custom_call" | custom-call | tf_op jit(solution)/shard_map/filtered/pallas_call | solution.py:422
  153.7 7.8 %collective-permute-done.26.refs_1_.refs_4_ = f32[2,2,8,32,128]{4,3,2,1,0:T(8,128)S(1)} collective-permute-done((f32[2,2,8,32,128]{4,3,2,1,0:T(8,128)S(1)}, f32[2,2,8,32,128]{4,3,2,1,0:T(8,128)S(1)}, u32[]{:S(2)}, u32[]{:S(2)}) %collective-permute-start.26) | collective-permute-done | bytes 524320 | tf_op jit(solution)/shard_map/ppermute | solution.py:589
  163.3 3.7 %collective-permute-done.32.refs_1_.refs_4_ = f32[2,1,8,32,128]{4,3,2,1,0:T(8,128)S(1)} collective-permute-done((f32[2,1,8,32,128]{4,3,2,1,0:T(8,128)S(1)}, f32[2,1,8,32,128]{4,3,2,1,0:T(8,128)S(1)}, u32[]{:S(2)}, u32[]{:S(2)}) %collective-permute-start.32) | collective-permute-done | bytes 262176 | tf_op jit(solution)/shard_map/ppermute | solution.py:589
  170.6 2.5 %place_near.7 = (f32[5,32,64,128]{3,2,1,0:T(8,128)}, f32[8,128]{1,0:T(8,128)}) custom-call(s32[22]{0:T(128)S(1)} %pad_add_fusion.refs_0_, f32[71]{0:T(128)S(1)} %copy-done.7, f32[2,8,32,128]{3,2,1,0:T(8,128)S(1)} %get-tuple-element.177.refs_2_, f32[2,2,8,32,128]{4,3,2,1,0:T(8,128)S(1)} %collective-permute-done.31.refs_3_, ...), custom_call_target="tpu_custom_call", output_to_operand_aliasing={{0}: (5, {})} | custom-call | tf_op jit(solution)/shard_map/place_near/pallas_call | solution.py:161
  (133 shorter events, 67.2 us)
Async XLA Ops:
  7.2 35.4 %collective-permute-start.3 = (f32[2,32,32,128]{3,2,1,0:T(8,128)}, f32[2,32,32,128]{3,2,1,0:T(8,128)S(1)}, u32[]{:S(2)}, u32[]{:S(2)}) collective-permute-start(f32[2,32,32,128]{3,2,1,0:T(8,128)} %get-tuple-element.116), channel_id=1, source_target_pairs={{0,16},{1,9},{2,18},{3,11},{4,20},{5,13},{6,22},{7,15},{8,24},{9,1... | collective-permute-start | bytes 3145736 | tf_op jit(solution)/shard_map/ppermute | solution.py:580
  19.9 20.7 %collective-permute-start.4 = (f32[1,32,32,128]{3,2,1,0:T(8,128)}, f32[1,32,32,128]{3,2,1,0:T(8,128)}, u32[]{:S(2)}, u32[]{:S(2)}) collective-permute-start(f32[1,32,32,128]{3,2,1,0:T(8,128)} %get-tuple-element.117), channel_id=1, source_target_pairs={{0,16},{1,9},{2,18},{3,11},{4,20},{5,13},{6,22},{7,15},{8,24},{9,1... | collective-permute-start | bytes 1572872 | tf_op jit(solution)/shard_map/ppermute | solution.py:580
  21.9 23.0 %collective-permute-start.7 = (f32[1,32,32,128]{3,2,1,0:T(8,128)}, f32[1,32,32,128]{3,2,1,0:T(8,128)}, u32[]{:S(2)}, u32[]{:S(2)}) collective-permute-start(f32[1,32,32,128]{3,2,1,0:T(8,128)} %get-tuple-element.122), channel_id=1, source_target_pairs={{0,8},{1,17},{2,10},{3,19},{4,12},{5,21},{6,14},{7,23},{8,0},{9,25... | collective-permute-start | bytes 1572872 | tf_op jit(solution)/shard_map/ppermute | solution.py:580
  43.3 23.1 %collective-permute-start.5 = (f32[2,32,32,128]{3,2,1,0:T(8,128)S(1)}, f32[2,32,32,128]{3,2,1,0:T(8,128)S(1)}, u32[]{:S(2)}, u32[]{:S(2)}) collective-permute-start(f32[2,32,32,128]{3,2,1,0:T(8,128)S(1)} %get-tuple-element.120), channel_id=1, source_target_pairs={{0,8},{1,17},{2,10},{3,19},{4,12},{5,21},{6,14},{7,23},{8,0},{9,25... | collective-permute-start | bytes 3145736 | tf_op jit(solution)/shard_map/ppermute | solution.py:580
  55.3 18.6 %collective-permute-start.12 = (f32[1,32,32,128]{3,2,1,0:T(8,128)S(1)}, f32[1,32,32,128]{3,2,1,0:T(8,128)S(1)}, u32[]{:S(2)}, u32[]{:S(2)}) collective-permute-start(f32[1,32,32,128]{3,2,1,0:T(8,128)S(1)} %get-tuple-element.141), channel_id=1, source_target_pairs={{0,16},{1,9},{2,18},{3,11},{4,20},{5,13},{6,22},{7,15},{8,24},{9,1... | collective-permute-start | bytes 1572872 | tf_op jit(solution)/shard_map/ppermute | solution.py:580
  55.9 34.5 %collective-permute-start.16 = (f32[2,32,32,128]{3,2,1,0:T(8,128)S(1)}, f32[2,32,32,128]{3,2,1,0:T(8,128)S(1)}, u32[]{:S(2)}, u32[]{:S(2)}) collective-permute-start(f32[2,32,32,128]{3,2,1,0:T(8,128)S(1)} %get-tuple-element.150), channel_id=1, source_target_pairs={{0,16},{1,9},{2,18},{3,11},{4,20},{5,13},{6,22},{7,15},{8,24},{9,1... | collective-permute-start | bytes 3145736 | tf_op jit(solution)/shard_map/ppermute | solution.py:580
  57.4 13.4 %collective-permute-start.13 = (f32[2,1,8,32,128]{4,3,2,1,0:T(8,128)S(1)}, f32[2,1,8,32,128]{4,3,2,1,0:T(8,128)S(1)}, u32[]{:S(2)}, u32[]{:S(2)}) collective-permute-start(f32[2,1,8,32,128]{4,3,2,1,0:T(8,128)S(1)} %get-tuple-element.143), channel_id=1, source_target_pairs={{0,2},{1,3},{2,0},{3,1},{4,6},{5,7},{6,4},{7,5},{8,10},{9,11},{10,... | collective-permute-start | bytes 786440 | tf_op jit(solution)/shard_map/ppermute | solution.py:589
  68.0 15.2 %collective-permute-start.10 = (f32[2,2,8,32,128]{4,3,2,1,0:T(8,128)S(1)}, f32[2,2,8,32,128]{4,3,2,1,0:T(8,128)S(1)}, u32[]{:S(2)}, u32[]{:S(2)}) collective-permute-start(f32[2,2,8,32,128]{4,3,2,1,0:T(8,128)S(1)} %get-tuple-element.137), channel_id=1, source_target_pairs={{0,1},{1,0},{2,3},{3,2},{4,5},{5,4},{6,7},{7,6},{8,9},{9,8},{10,11... | collective-permute-start | bytes 1572872 | tf_op jit(solution)/shard_map/ppermute | solution.py:589
  72.5 15.0 %collective-permute-start.18 = (f32[1,4,128,128]{3,2,1,0:T(8,128)S(1)}, f32[1,4,128,128]{3,2,1,0:T(8,128)S(1)}, u32[]{:S(2)}, u32[]{:S(2)}) collective-permute-start(f32[1,4,128,128]{3,2,1,0:T(8,128)S(1)} %get-tuple-element.152.refs_3_), channel_id=1, source_target_pairs={{0,4},{1,5},{2,6},{3,7},{4,0},{5,1},{6,2},{7,3},{8,12},{9,13},{10,... | collective-permute-start | bytes 786440 | tf_op jit(solution)/shard_map/ppermute | solution.py:589
  74.6 14.7 %collective-permute-start.17 = (f32[1,32,32,128]{3,2,1,0:T(8,128)S(1)}, f32[1,32,32,128]{3,2,1,0:T(8,128)S(1)}, u32[]{:S(2)}, u32[]{:S(2)}) collective-permute-start(f32[1,32,32,128]{3,2,1,0:T(8,128)S(1)} %get-tuple-element.151), channel_id=1, source_target_pairs={{0,8},{1,17},{2,10},{3,19},{4,12},{5,21},{6,14},{7,23},{8,0},{9,25... | collective-permute-start | bytes 1572872 | tf_op jit(solution)/shard_map/ppermute | solution.py:580
  83.2 43.1 %collective-permute-start.24 = (f32[2,32,32,128]{3,2,1,0:T(8,128)S(1)}, f32[2,32,32,128]{3,2,1,0:T(8,128)S(1)}, u32[]{:S(2)}, u32[]{:S(2)}) collective-permute-start(f32[2,32,32,128]{3,2,1,0:T(8,128)S(1)} %get-tuple-element.169), channel_id=1, source_target_pairs={{0,16},{1,9},{2,18},{3,11},{4,20},{5,13},{6,22},{7,15},{8,24},{9,1... | collective-permute-start | bytes 3145736 | tf_op jit(solution)/shard_map/ppermute | solution.py:580
  87.5 20.5 %collective-permute-start.14 = (f32[2,2,8,32,128]{4,3,2,1,0:T(8,128)S(1)}, f32[2,2,8,32,128]{4,3,2,1,0:T(8,128)S(1)}, u32[]{:S(2)}, u32[]{:S(2)}) collective-permute-start(f32[2,2,8,32,128]{4,3,2,1,0:T(8,128)S(1)} %get-tuple-element.148), channel_id=1, source_target_pairs={{0,2},{1,3},{2,0},{3,1},{4,6},{5,7},{6,4},{7,5},{8,10},{9,11},{10,... | collective-permute-start | bytes 1572872 | tf_op jit(solution)/shard_map/ppermute | solution.py:589
  90.3 20.1 %collective-permute-start.22 = (f32[2,1,8,32,128]{4,3,2,1,0:T(8,128)S(1)}, f32[2,1,8,32,128]{4,3,2,1,0:T(8,128)S(1)}, u32[]{:S(2)}, u32[]{:S(2)}) collective-permute-start(f32[2,1,8,32,128]{4,3,2,1,0:T(8,128)S(1)} %get-tuple-element.164), channel_id=1, source_target_pairs={{0,1},{1,0},{2,3},{3,2},{4,5},{5,4},{6,7},{7,6},{8,9},{9,8},{10,11... | collective-permute-start | bytes 786440 | tf_op jit(solution)/shard_map/ppermute | solution.py:589
  90.4 22.2 %collective-permute-start.21 = (f32[1,4,128,128]{3,2,1,0:T(8,128)S(1)}, f32[1,4,128,128]{3,2,1,0:T(8,128)S(1)}, u32[]{:S(2)}, u32[]{:S(2)}) collective-permute-start(f32[1,4,128,128]{3,2,1,0:T(8,128)S(1)} %get-tuple-element.162.refs_3_), channel_id=1, source_target_pairs={{0,4},{1,5},{2,6},{3,7},{4,0},{5,1},{6,2},{7,3},{8,12},{9,13},{10,... | collective-permute-start | bytes 786440 | tf_op jit(solution)/shard_map/ppermute | solution.py:589
  93.3 26.8 %collective-permute-start.20 = (f32[2,1,8,32,128]{4,3,2,1,0:T(8,128)S(1)}, f32[2,1,8,32,128]{4,3,2,1,0:T(8,128)S(1)}, u32[]{:S(2)}, u32[]{:S(2)}) collective-permute-start(f32[2,1,8,32,128]{4,3,2,1,0:T(8,128)S(1)} %get-tuple-element.161), channel_id=1, source_target_pairs={{0,2},{1,3},{2,0},{3,1},{4,6},{5,7},{6,4},{7,5},{8,10},{9,11},{10,... | collective-permute-start | bytes 786440 | tf_op jit(solution)/shard_map/ppermute | solution.py:589
  110.4 13.6 %collective-permute-start.25 = (f32[2,1,8,32,128]{4,3,2,1,0:T(8,128)S(1)}, f32[2,1,8,32,128]{4,3,2,1,0:T(8,128)S(1)}, u32[]{:S(2)}, u32[]{:S(2)}) collective-permute-start(f32[2,1,8,32,128]{4,3,2,1,0:T(8,128)S(1)} %get-tuple-element.171), channel_id=1, source_target_pairs={{0,2},{1,3},{2,0},{3,1},{4,6},{5,7},{6,4},{7,5},{8,10},{9,11},{10,... | collective-permute-start | bytes 786440 | tf_op jit(solution)/shard_map/ppermute | solution.py:589
  110.5 31.3 %collective-permute-start.19 = (f32[2,4,128,128]{3,2,1,0:T(8,128)S(1)}, f32[2,4,128,128]{3,2,1,0:T(8,128)S(1)}, u32[]{:S(2)}, u32[]{:S(2)}) collective-permute-start(f32[2,4,128,128]{3,2,1,0:T(8,128)S(1)} %get-tuple-element.158.refs_3_), channel_id=1, source_target_pairs={{0,4},{1,5},{2,6},{3,7},{4,0},{5,1},{6,2},{7,3},{8,12},{9,13},{10,... | collective-permute-start | bytes 1572872 | tf_op jit(solution)/shard_map/ppermute | solution.py:589
  112.5 32.5 %collective-permute-start.29 = (f32[1,32,32,128]{3,2,1,0:T(8,128)S(1)}, f32[1,32,32,128]{3,2,1,0:T(8,128)S(1)}, u32[]{:S(2)}, u32[]{:S(2)}) collective-permute-start(f32[1,32,32,128]{3,2,1,0:T(8,128)S(1)} %get-tuple-element.185), channel_id=1, source_target_pairs={{0,8},{1,17},{2,10},{3,19},{4,12},{5,21},{6,14},{7,23},{8,0},{9,25... | collective-permute-start | bytes 1572872 | tf_op jit(solution)/shard_map/ppermute | solution.py:580
  124.1 37.6 %collective-permute-start.33 = (f32[2,32,32,128]{3,2,1,0:T(8,128)S(1)}, f32[2,32,32,128]{3,2,1,0:T(8,128)S(1)}, u32[]{:S(2)}, u32[]{:S(2)}) collective-permute-start(f32[2,32,32,128]{3,2,1,0:T(8,128)S(1)} %get-tuple-element.198), channel_id=1, source_target_pairs={{0,8},{1,17},{2,10},{3,19},{4,12},{5,21},{6,14},{7,23},{8,0},{9,25... | collective-permute-start | bytes 3145736 | tf_op jit(solution)/shard_map/ppermute | solution.py:580
  126.3 20.3 %collective-permute-start.28 = (f32[1,4,128,128]{3,2,1,0:T(8,128)S(1)}, f32[1,4,128,128]{3,2,1,0:T(8,128)S(1)}, u32[]{:S(2)}, u32[]{:S(2)}) collective-permute-start(f32[1,4,128,128]{3,2,1,0:T(8,128)S(1)} %get-tuple-element.183.refs_3_), channel_id=1, source_target_pairs={{0,4},{1,5},{2,6},{3,7},{4,0},{5,1},{6,2},{7,3},{8,12},{9,13},{10,... | collective-permute-start | bytes 786440 | tf_op jit(solution)/shard_map/ppermute | solution.py:589
  133.4 16.9 %collective-permute-start.27 = (f32[2,1,8,32,128]{4,3,2,1,0:T(8,128)S(1)}, f32[2,1,8,32,128]{4,3,2,1,0:T(8,128)S(1)}, u32[]{:S(2)}, u32[]{:S(2)}) collective-permute-start(f32[2,1,8,32,128]{4,3,2,1,0:T(8,128)S(1)} %get-tuple-element.182), channel_id=1, source_target_pairs={{0,2},{1,3},{2,0},{3,1},{4,6},{5,7},{6,4},{7,5},{8,10},{9,11},{10,... | collective-permute-start | bytes 786440 | tf_op jit(solution)/shard_map/ppermute | solution.py:589
  141.8 25.3 %collective-permute-start.35 = (f32[2,32,32,128]{3,2,1,0:T(8,128)S(1)}, f32[2,32,32,128]{3,2,1,0:T(8,128)S(1)}, u32[]{:S(2)}, u32[]{:S(2)}) collective-permute-start(f32[2,32,32,128]{3,2,1,0:T(8,128)S(1)} %get-tuple-element.203), channel_id=1, source_target_pairs={{0,8},{1,17},{2,10},{3,19},{4,12},{5,21},{6,14},{7,23},{8,0},{9,25... | collective-permute-start | bytes 3145736 | tf_op jit(solution)/shard_map/ppermute | solution.py:580
  145.1 16.4 %collective-permute-start.26 = (f32[2,2,8,32,128]{4,3,2,1,0:T(8,128)S(1)}, f32[2,2,8,32,128]{4,3,2,1,0:T(8,128)S(1)}, u32[]{:S(2)}, u32[]{:S(2)}) collective-permute-start(f32[2,2,8,32,128]{4,3,2,1,0:T(8,128)S(1)} %get-tuple-element.179), channel_id=1, source_target_pairs={{0,2},{1,3},{2,0},{3,1},{4,6},{5,7},{6,4},{7,5},{8,10},{9,11},{10,... | collective-permute-start | bytes 1572872 | tf_op jit(solution)/shard_map/ppermute | solution.py:589
  150.3 16.7 %collective-permute-start.32 = (f32[2,1,8,32,128]{4,3,2,1,0:T(8,128)S(1)}, f32[2,1,8,32,128]{4,3,2,1,0:T(8,128)S(1)}, u32[]{:S(2)}, u32[]{:S(2)}) collective-permute-start(f32[2,1,8,32,128]{4,3,2,1,0:T(8,128)S(1)} %get-tuple-element.197), channel_id=1, source_target_pairs={{0,2},{1,3},{2,0},{3,1},{4,6},{5,7},{6,4},{7,5},{8,10},{9,11},{10,... | collective-permute-start | bytes 786440 | tf_op jit(solution)/shard_map/ppermute | solution.py:589
  (31 other events, 237.0 us)

commit v10 on v9

--- a/solution.py
+++ b/solution.py
@@ -9,50 +9,42 @@
 from jax.sharding import PartitionSpec as P
 
 QUAD = 4
-NEAR_SIZES = (1, 2, 1, 1)
-FAR_SIZES = (2, 2, 1)
+NEAR_SIZES = (2, 2, 1)
+FAR_SIZES = (1, 2, 2)
 ORDER = (
     ("pack", 0),
+    ("pack", 3),
     ("pack", 1),
+    ("pack", 4),
+    ("local", 0),
+    ("pack", 2),
     ("mix", 0),
-    ("pack", 3),
-    ("local", 0),
-    ("mix", 3),
     ("mix", 1),
     ("spread", 0),
-    ("pack", 6),
-    ("pack", 4),
     ("join", 0),
-    ("spread", 3),
+    ("spread", 1),
     ("pack", 5),
-    ("join", 3),
-    ("pack", 2),
-    ("spread", 1),
-    ("coef", 3),
     ("mix", 2),
     ("coef", 0),
     ("join", 1),
-    ("filter", 3),
     ("spread", 2),
-    ("mix", 4),
-    ("mix", 6),
     ("coef", 1),
+    ("mix", 5),
     ("join", 2),
     ("filter", 0),
-    ("back", 3),
+    ("mix", 3),
+    ("local", 1),
     ("coef", 2),
-    ("mix", 5),
-    ("local", 1),
-    ("near", 3),
+    ("mix", 4),
     ("filter", 1),
-    ("far", 6),
+    ("back", 0),
     ("filter", 2),
-    ("back", 0),
+    ("far", 5),
     ("near", 0),
     ("back", 1),
+    ("far", 3),
     ("far", 4),
     ("back", 2),
-    ("far", 5),
     ("near", 2),
     ("near", 1),
 )

time: 174 us -> 160 us (0.920)
  local copies, waits for them, and re-layouts: 6.1 us -> 1.43 us
  Pallas kernels: 61.2 us -> 57.8 us
  starting transfers between devices: 34.5 us -> 31.7 us
  waiting for transfers between devices: 70.8 us -> 68.4 us
    ppermute x20 -> x15, waiting for transfers between devices: 52.3 us -> 38.8 us  [to_sector(): return lax.ppermute(x, 'space', [(i, i ^ k) for i in range(sectors)])]
    ppermute x14 -> x12, waiting for transfers between devices: 15.5 us -> 28.4 us  [to_partner(): return lax.ppermute(x, ('inst', 'space'), pairs)]
    unnamed x39, local copies, waits for them, and re-layouts: 6.1 us -> 1.43 us
    ppermute x14 -> x12, starting transfers between devices: 15.1 us -> 12.7 us  [to_partner(): return lax.ppermute(x, ('inst', 'space'), pairs)]
    pallas_call x8 -> x6, Pallas kernels: 15.4 us -> 13.3 us  [table_call(): pl.pallas_call(kernel, grid_spec=pltpu.PrefetchScalarGridSpec(num_scalar_...]
    ppermute x2, waiting for transfers between devices: 2.95 us -> 1.15 us  [ring(): lax.ppermute(x, 'space', [(i, (i + step) % sectors) for i in range(sector...]
    pallas_call x35 -> x29, Pallas kernels: 45.8 us -> 44.6 us  [call(): pl.pallas_call(kernel, grid=grid, in_specs=list(in_specs) + [ANY] * len(e...]
    ppermute x20 -> x15, starting transfers between devices: 15.8 us -> 15.5 us  [to_sector(): return lax.ppermute(x, 'space', [(i, i ^ k) for i in range(sectors)])]
  transfers between devices with their start and end apart: 36 -> 29, of which waited for: 16 -> 11; matrix products, arithmetic and copies ran while one was open for 0% -> 0% of each run, Pallas kernels for 33% -> 33%
where the time goes in v10:
time: 160 us
  waiting for transfers between devices  68.4 us (43%)
  Pallas kernels  57.8 us (36%)
  starting transfers between devices  31.7 us (20%)
    pallas_call x29, Pallas kernels, call(): pl.pallas_call(kernel, grid=grid, in_specs=list(in_specs) + [ANY] * len(e...  44.6 us
    ppermute x15, waiting for transfers between devices, to_sector(): return lax.ppermute(x, 'space', [(i, i ^ k) for i in range(sectors)])  38.8 us
    ppermute x12, waiting for transfers between devices, to_partner(): return lax.ppermute(x, ('inst', 'space'), pairs)  28.4 us
    ppermute x15, starting transfers between devices, to_sector(): return lax.ppermute(x, 'space', [(i, i ^ k) for i in range(sectors)])  15.5 us
    pallas_call x6, Pallas kernels, table_call(): pl.pallas_call(kernel, grid_spec=pltpu.PrefetchScalarGridSpec(num_scalar_...  13.3 us
    ppermute x12, starting transfers between devices, to_partner(): return lax.ppermute(x, ('inst', 'space'), pairs)  12.7 us
    ppermute x2, starting transfers between devices, ring(): lax.ppermute(x, 'space', [(i, (i + step) % sectors) for i in range(sector...  3.53 us
  transfers between devices with their start and end apart: 29, of which 11 were waited for; matrix products, arithmetic and copies ran while one was open for 0% of the time, Pallas kernels for 33%

profile of v10, /device:TPU:0, one launch (start us, length us, event | category | flops | bytes accessed | tf_op | source)
XLA Modules:
  0.0 159.9 jit_solution(13613650762613108213)
XLA Ops:
  0.0 2.3 %pack.6 = (f32[2,32,32,128]{3,2,1,0:T(8,128)}, f32[6,1,64,128]{3,2,1,0:T(8,128)}, f32[6,1,64,128]{3,2,1,0:T(8,128)}, f32[8,128]{1,0:T(8,128)}) custom-call(f32[5,32,64,128]{3,2,1,0:T(8,128)} %bitcast.5, f32[5,32,64,128]{3,2,1,0:T(8,128)} %bitcast.6, f32[32,64,128]{2,1,0:T(8,128)} %refs_11_.3, f32[5,32,64,128]{3,2,1,0:T(8,128)} %bitcast.7, ...), custom_call_target="tpu_custom_call" | custom-call | tf_op jit(solution)/shard_map/pack/pallas_call | solution.py:153
  2.3 3.0 %collective-permute-start.3 = (f32[2,32,32,128]{3,2,1,0:T(8,128)}, f32[2,32,32,128]{3,2,1,0:T(8,128)}, u32[]{:S(2)}, u32[]{:S(2)}) collective-permute-start(f32[2,32,32,128]{3,2,1,0:T(8,128)} %get-tuple-element.96), channel_id=1, source_target_pairs={{0,16},{1,9},{2,18},{3,11},{4,20},{5,13},{6,22},{7,15},{8,24},{9,1... | collective-permute-start | bytes 3145736 | tf_op jit(solution)/shard_map/ppermute | solution.py:572
  7.3 2.2 %pack.8 = (f32[2,32,32,128]{3,2,1,0:T(8,128)}, f32[8,128]{1,0:T(8,128)}) custom-call(f32[5,32,64,128]{3,2,1,0:T(8,128)} %bitcast.9, f32[8,128]{1,0:T(8,128)} %get-tuple-element.91.refs_1_), custom_call_target="tpu_custom_call" | custom-call | tf_op jit(solution)/shard_map/pack/pallas_call | solution.py:153
  9.6 3.5 %collective-permute-start.1 = (f32[6,1,64,128]{3,2,1,0:T(8,128)S(1)}, f32[6,1,64,128]{3,2,1,0:T(8,128)S(1)}, u32[]{:S(2)}, u32[]{:S(2)}) collective-permute-start(f32[6,1,64,128]{3,2,1,0:T(8,128)S(1)} %copy-done.13), channel_id=1, source_target_pairs={{0,7},{1,0},{2,1},{3,2},{4,3},{5,4},{6,5},{7,6},{8,15},{9,8},{10,9... | collective-permute-start | bytes 589832 | tf_op jit(solution)/shard_map/ppermute | solution.py:584
  13.2 2.1 %pack.9 = (f32[2,32,32,128]{3,2,1,0:T(8,128)}, f32[8,128]{1,0:T(8,128)}) custom-call(f32[5,32,64,128]{3,2,1,0:T(8,128)} %bitcast.10, f32[8,128]{1,0:T(8,128)} %get-tuple-element.92.refs_1_), custom_call_target="tpu_custom_call" | custom-call | tf_op jit(solution)/shard_map/pack/pallas_call | solution.py:153
  17.3 8.6 %local_part.2 = (f32[5,32,32,128]{3,2,1,0:T(8,128)}, f32[8,128]{1,0:T(8,128)S(1)}) custom-call(f32[5,5]{1,0:T(8,128)S(1)} %copy-done.5, f32[5]{0:T(128)S(1)} %copy-done.7, s32[5,3]{1,0:T(8,128)S(1)} %copy.23.refs_2_, f32[5,32,64,128]{3,2,1,0:T(8,128)} %bitcast.11, f32[5,32,64,128]{3,2,1,0:T(8,128)} %bitcast.12, f32[5,32,64,128]{3,2,1,0:T(8,128)} %bitcast.13, ...), custom_call_target="tpu_custom_call" | custom-call | tf_op jit(solution)/shard_map/local_part/pallas_call | solution.py:153
  32.4 10.5 %collective-permute-done.5.refs_4_ = f32[2,32,32,128]{3,2,1,0:T(8,128)S(1)} collective-permute-done((f32[2,32,32,128]{3,2,1,0:T(8,128)S(1)}, f32[2,32,32,128]{3,2,1,0:T(8,128)S(1)}, u32[]{:S(2)}, u32[]{:S(2)}) %collective-permute-start.5) | collective-permute-done | bytes 1048608 | tf_op jit(solution)/shard_map/ppermute | solution.py:572
  42.9 2.1 %spread.3 = (f32[2,8,32,128]{3,2,1,0:T(8,128)S(1)}, f32[2,2,8,32,128]{4,3,2,1,0:T(8,128)S(1)}, f32[2,2,8,32,128]{4,3,2,1,0:T(8,128)S(1)}, f32[8,128]{1,0:T(8,128)S(1)}) custom-call(s32[22]{0:T(128)S(1)} %pad_add_fusion.refs_0_, f32[71]{0:T(128)S(1)} %copy-done.4, f32[5,32,32,128]{3,2,1,0:T(8,128)S(1)} %copy-done.1, ...), custom_call_target="tpu_custom_call" | custom-call | tf_op jit(solution)/shard_map/spread/pallas_call | solution.py:153
  49.0 10.0 %collective-permute-done.4.refs_4_ = f32[2,32,32,128]{3,2,1,0:T(8,128)S(1)} collective-permute-done((f32[2,32,32,128]{3,2,1,0:T(8,128)S(1)}, f32[2,32,32,128]{3,2,1,0:T(8,128)S(1)}, u32[]{:S(2)}, u32[]{:S(2)}) %collective-permute-start.4) | collective-permute-done | bytes 1048608 | tf_op jit(solution)/shard_map/ppermute | solution.py:572
  66.8 2.4 %coefficients.3 = (f32[2,4,128,128]{3,2,1,0:T(8,128)S(1)}, f32[8,128]{1,0:T(8,128)S(1)}) custom-call(s32[22]{0:T(128)S(1)} %pad_add_fusion.refs_0_, f32[71]{0:T(128)S(1)} %copy-done.4, f32[2,16,128,128]{3,2,1,0:T(8,128)S(1)} %copy-done.3, f32[2,8,32,128]{3,2,1,0:T(8,128)S(1)} %get-tuple-element.110.refs_3_.refs_5_, ...), custom_call_target="tpu_custom_call" | custom-call | tf_op jit(solution)/shard_map/coefficients/pallas_call | solution.py:414
  72.2 8.0 %collective-permute-done.11.refs_4_ = f32[1,32,32,128]{3,2,1,0:T(8,128)S(1)} collective-permute-done((f32[1,32,32,128]{3,2,1,0:T(8,128)S(1)}, f32[1,32,32,128]{3,2,1,0:T(8,128)S(1)}, u32[]{:S(2)}, u32[]{:S(2)}) %collective-permute-start.11) | collective-permute-done | bytes 524320 | tf_op jit(solution)/shard_map/ppermute | solution.py:572
  81.5 11.0 %collective-permute-done.10.refs_5_.refs_7_ = f32[2,2,8,32,128]{4,3,2,1,0:T(8,128)S(1)} collective-permute-done((f32[2,2,8,32,128]{4,3,2,1,0:T(8,128)S(1)}, f32[2,2,8,32,128]{4,3,2,1,0:T(8,128)S(1)}, u32[]{:S(2)}, u32[]{:S(2)}) %collective-permute-start.10) | collective-permute-done | bytes 524320 | tf_op jit(solution)/shard_map/ppermute | solution.py:581
  92.5 2.4 %coefficients.4 = (f32[2,4,128,128]{3,2,1,0:T(8,128)S(1)}, f32[8,128]{1,0:T(8,128)S(1)}) custom-call(s32[22]{0:T(128)S(1)} %pad_add_fusion.refs_0_, f32[71]{0:T(128)S(1)} %copy-done.4, f32[2,16,128,128]{3,2,1,0:T(8,128)S(1)} %copy-done.3, f32[2,8,32,128]{3,2,1,0:T(8,128)S(1)} %get-tuple-element.107.refs_3_.refs_5_, ...), custom_call_target="tpu_custom_call" | custom-call | tf_op jit(solution)/shard_map/coefficients/pallas_call | solution.py:414
  96.6 2.5 %collective-permute-start.16 = (f32[2,1,8,32,128]{4,3,2,1,0:T(8,128)S(1)}, f32[2,1,8,32,128]{4,3,2,1,0:T(8,128)S(1)}, u32[]{:S(2)}, u32[]{:S(2)}) collective-permute-start(f32[2,1,8,32,128]{4,3,2,1,0:T(8,128)S(1)} %get-tuple-element.129), channel_id=1, source_target_pairs={{0,2},{1,3},{2,0},{3,1},{4,6},{5,7},{6,4},{7,5},{8,10},{9,11},{10,... | collective-permute-start | bytes 786440 | tf_op jit(solution)/shard_map/ppermute | solution.py:581
  99.2 2.5 %filtered.3 = (f32[2,8,32,128]{3,2,1,0:T(8,128)S(1)}, f32[2,2,8,32,128]{4,3,2,1,0:T(8,128)S(1)}, f32[2,2,8,32,128]{4,3,2,1,0:T(8,128)S(1)}, f32[8,128]{1,0:T(8,128)S(1)}) custom-call(s32[22]{0:T(128)S(1)} %pad_add_fusion.refs_0_, f32[71]{0:T(128)S(1)} %copy-done.4, f32[2,16,128,128]{3,2,1,0:T(8,128)S(1)} %copy-done.2, ...), custom_call_target="tpu_custom_call" | custom-call | tf_op jit(solution)/shard_map/filtered/pallas_call | solution.py:414
  102.5 5.6 %local_part.3 = (f32[5,32,32,128]{3,2,1,0:T(8,128)S(1)}, f32[8,128]{1,0:T(8,128)S(1)}) custom-call(f32[5,5]{1,0:T(8,128)S(1)} %copy-done.5, f32[5]{0:T(128)S(1)} %copy-done.7, s32[5,3]{1,0:T(8,128)S(1)} %copy.23.refs_2_, f32[5,32,64,128]{3,2,1,0:T(8,128)S(1)} %bitcast.24, f32[5,32,64,128]{3,2,1,0:T(8,128)S(1)} %bitcast.25, f32[5,32,64,128]{3,2,1,0:T(8,128)S(1)} %bitcast.26, ...), custom_call_target="tpu_custom_call" | custom-call | tf_op jit(solution)/shard_map/local_part/pallas_call | solution.py:153
  108.2 5.4 %collective-permute-done.16.refs_5_.refs_7_ = f32[2,1,8,32,128]{4,3,2,1,0:T(8,128)S(1)} collective-permute-done((f32[2,1,8,32,128]{4,3,2,1,0:T(8,128)S(1)}, f32[2,1,8,32,128]{4,3,2,1,0:T(8,128)S(1)}, u32[]{:S(2)}, u32[]{:S(2)}) %collective-permute-start.16) | collective-permute-done | bytes 262176 | tf_op jit(solution)/shard_map/ppermute | solution.py:581
  116.3 3.1 %collective-permute-start.23 = (f32[1,4,128,128]{3,2,1,0:T(8,128)S(1)}, f32[1,4,128,128]{3,2,1,0:T(8,128)S(1)}, u32[]{:S(2)}, u32[]{:S(2)}) collective-permute-start(f32[1,4,128,128]{3,2,1,0:T(8,128)S(1)} %get-tuple-element.148.refs_3_), channel_id=1, source_target_pairs={{0,4},{1,5},{2,6},{3,7},{4,0},{5,1},{6,2},{7,3},{8,12},{9,13},{10,... | collective-permute-start | bytes 786440 | tf_op jit(solution)/shard_map/ppermute | solution.py:581
  119.4 2.2 %collective-permute-done.12.refs_4_ = f32[2,4,128,128]{3,2,1,0:T(8,128)S(1)} collective-permute-done((f32[2,4,128,128]{3,2,1,0:T(8,128)S(1)}, f32[2,4,128,128]{3,2,1,0:T(8,128)S(1)}, u32[]{:S(2)}, u32[]{:S(2)}) %collective-permute-start.12) | collective-permute-done | bytes 524320 | tf_op jit(solution)/shard_map/ppermute | solution.py:581
  121.6 2.5 %filtered.4 = (f32[2,8,32,128]{3,2,1,0:T(8,128)S(1)}, f32[2,2,8,32,128]{4,3,2,1,0:T(8,128)S(1)}, f32[2,2,8,32,128]{4,3,2,1,0:T(8,128)S(1)}, f32[8,128]{1,0:T(8,128)S(1)}) custom-call(s32[22]{0:T(128)S(1)} %pad_add_fusion.refs_0_, f32[71]{0:T(128)S(1)} %copy-done.4, f32[2,16,128,128]{3,2,1,0:T(8,128)S(1)} %copy-done.2, ...), custom_call_target="tpu_custom_call" | custom-call | tf_op jit(solution)/shard_map/filtered/pallas_call | solution.py:414
  124.1 9.7 %collective-permute-done.20.refs_1_.refs_4_ = f32[2,2,8,32,128]{4,3,2,1,0:T(8,128)S(1)} collective-permute-done((f32[2,2,8,32,128]{4,3,2,1,0:T(8,128)S(1)}, f32[2,2,8,32,128]{4,3,2,1,0:T(8,128)S(1)}, u32[]{:S(2)}, u32[]{:S(2)}) %collective-permute-start.20) | collective-permute-done | bytes 524320 | tf_op jit(solution)/shard_map/ppermute | solution.py:581
  139.5 2.5 %place_near.3 = (f32[5,32,64,128]{3,2,1,0:T(8,128)}, f32[8,128]{1,0:T(8,128)S(1)}) custom-call(s32[22]{0:T(128)S(1)} %pad_add_fusion.refs_0_, f32[71]{0:T(128)S(1)} %copy-done.4, f32[2,8,32,128]{3,2,1,0:T(8,128)S(1)} %get-tuple-element.141.refs_2_, f32[2,2,8,32,128]{4,3,2,1,0:T(8,128)S(1)} %collective-permute-done.21.refs_3_, ...), custom_call_target="tpu_custom_call", output_to_operand_aliasing={{0}: (5, {})} | custom-call | tf_op jit(solution)/shard_map/place_near/pallas_call | solution.py:153
  142.0 6.8 %collective-permute-done.19.refs_1_.refs_4_ = f32[2,2,8,32,128]{4,3,2,1,0:T(8,128)S(1)} collective-permute-done((f32[2,2,8,32,128]{4,3,2,1,0:T(8,128)S(1)}, f32[2,2,8,32,128]{4,3,2,1,0:T(8,128)S(1)}, u32[]{:S(2)}, u32[]{:S(2)}) %collective-permute-start.19) | collective-permute-done | bytes 524320 | tf_op jit(solution)/shard_map/ppermute | solution.py:581
  157.4 2.5 %place_near.5 = (f32[5,32,64,128]{3,2,1,0:T(8,128)}, f32[8,128]{1,0:T(8,128)}) custom-call(s32[22]{0:T(128)S(1)} %pad_add_fusion.refs_0_, f32[71]{0:T(128)S(1)} %copy-done.4, f32[2,8,32,128]{3,2,1,0:T(8,128)S(1)} %get-tuple-element.138.refs_2_, f32[2,2,8,32,128]{4,3,2,1,0:T(8,128)S(1)} %collective-permute-done.24.refs_3_, ...), custom_call_target="tpu_custom_call", output_to_operand_aliasing={{0}: (5, {})} | custom-call | tf_op jit(solution)/shard_map/place_near/pallas_call | solution.py:153
  (111 shorter events, 45.9 us)
Async XLA Ops:
  2.3 23.6 %collective-permute-start.3 = (f32[2,32,32,128]{3,2,1,0:T(8,128)}, f32[2,32,32,128]{3,2,1,0:T(8,128)}, u32[]{:S(2)}, u32[]{:S(2)}) collective-permute-start(f32[2,32,32,128]{3,2,1,0:T(8,128)} %get-tuple-element.96), channel_id=1, source_target_pairs={{0,16},{1,9},{2,18},{3,11},{4,20},{5,13},{6,22},{7,15},{8,24},{9,1... | collective-permute-start | bytes 3145736 | tf_op jit(solution)/shard_map/ppermute | solution.py:572
  9.5 20.6 %collective-permute-start.2 = (f32[2,32,32,128]{3,2,1,0:T(8,128)}, f32[2,32,32,128]{3,2,1,0:T(8,128)S(1)}, u32[]{:S(2)}, u32[]{:S(2)}) collective-permute-start(f32[2,32,32,128]{3,2,1,0:T(8,128)} %get-tuple-element.95), channel_id=1, source_target_pairs={{0,16},{1,9},{2,18},{3,11},{4,20},{5,13},{6,22},{7,15},{8,24},{9,1... | collective-permute-start | bytes 3145736 | tf_op jit(solution)/shard_map/ppermute | solution.py:572
  9.5 7.0 %collective-permute-start = (f32[6,1,64,128]{3,2,1,0:T(8,128)S(1)}, f32[6,1,64,128]{3,2,1,0:T(8,128)S(1)}, u32[]{:S(2)}, u32[]{:S(2)}) collective-permute-start(f32[6,1,64,128]{3,2,1,0:T(8,128)S(1)} %copy-done.14), channel_id=1, source_target_pairs={{0,1},{1,2},{2,3},{3,4},{4,5},{5,6},{6,7},{7,0},{8,9},{9,10},{10,1... | collective-permute-start | bytes 589832 | tf_op jit(solution)/shard_map/ppermute | solution.py:584
  28.0 14.9 %collective-permute-start.5 = (f32[2,32,32,128]{3,2,1,0:T(8,128)S(1)}, f32[2,32,32,128]{3,2,1,0:T(8,128)S(1)}, u32[]{:S(2)}, u32[]{:S(2)}) collective-permute-start(f32[2,32,32,128]{3,2,1,0:T(8,128)S(1)} %get-tuple-element.101), channel_id=1, source_target_pairs={{0,8},{1,17},{2,10},{3,19},{4,12},{5,21},{6,14},{7,23},{8,0},{9,25... | collective-permute-start | bytes 3145736 | tf_op jit(solution)/shard_map/ppermute | solution.py:572
  30.9 28.1 %collective-permute-start.4 = (f32[2,32,32,128]{3,2,1,0:T(8,128)S(1)}, f32[2,32,32,128]{3,2,1,0:T(8,128)S(1)}, u32[]{:S(2)}, u32[]{:S(2)}) collective-permute-start(f32[2,32,32,128]{3,2,1,0:T(8,128)S(1)} %get-tuple-element.100), channel_id=1, source_target_pairs={{0,8},{1,17},{2,10},{3,19},{4,12},{5,21},{6,14},{7,23},{8,0},{9,25... | collective-permute-start | bytes 3145736 | tf_op jit(solution)/shard_map/ppermute | solution.py:572
  46.5 18.1 %collective-permute-start.9 = (f32[1,32,32,128]{3,2,1,0:T(8,128)S(1)}, f32[1,32,32,128]{3,2,1,0:T(8,128)S(1)}, u32[]{:S(2)}, u32[]{:S(2)}) collective-permute-start(f32[1,32,32,128]{3,2,1,0:T(8,128)S(1)} %get-tuple-element.112), channel_id=1, source_target_pairs={{0,16},{1,9},{2,18},{3,11},{4,20},{5,13},{6,22},{7,15},{8,24},{9,1... | collective-permute-start | bytes 1572872 | tf_op jit(solution)/shard_map/ppermute | solution.py:572
  48.3 18.5 %collective-permute-start.8 = (f32[2,2,8,32,128]{4,3,2,1,0:T(8,128)S(1)}, f32[2,2,8,32,128]{4,3,2,1,0:T(8,128)S(1)}, u32[]{:S(2)}, u32[]{:S(2)}) collective-permute-start(f32[2,2,8,32,128]{4,3,2,1,0:T(8,128)S(1)} %get-tuple-element.111), channel_id=1, source_target_pairs={{0,2},{1,3},{2,0},{3,1},{4,6},{5,7},{6,4},{7,5},{8,10},{9,11},{10,... | collective-permute-start | bytes 1572872 | tf_op jit(solution)/shard_map/ppermute | solution.py:581
  60.6 8.7 %collective-permute-start.7 = (f32[2,2,8,32,128]{4,3,2,1,0:T(8,128)S(1)}, f32[2,2,8,32,128]{4,3,2,1,0:T(8,128)S(1)}, u32[]{:S(2)}, u32[]{:S(2)}) collective-permute-start(f32[2,2,8,32,128]{4,3,2,1,0:T(8,128)S(1)} %get-tuple-element.108), channel_id=1, source_target_pairs={{0,1},{1,0},{2,3},{3,2},{4,5},{5,4},{6,7},{7,6},{8,9},{9,8},{10,11... | collective-permute-start | bytes 1572872 | tf_op jit(solution)/shard_map/ppermute | solution.py:581
  62.8 32.2 %collective-permute-start.15 = (f32[2,32,32,128]{3,2,1,0:T(8,128)S(1)}, f32[2,32,32,128]{3,2,1,0:T(8,128)S(1)}, u32[]{:S(2)}, u32[]{:S(2)}) collective-permute-start(f32[2,32,32,128]{3,2,1,0:T(8,128)S(1)} %get-tuple-element.126), channel_id=1, source_target_pairs={{0,16},{1,9},{2,18},{3,11},{4,20},{5,13},{6,22},{7,15},{8,24},{9,1... | collective-permute-start | bytes 3145736 | tf_op jit(solution)/shard_map/ppermute | solution.py:572
  65.2 14.9 %collective-permute-start.11 = (f32[1,32,32,128]{3,2,1,0:T(8,128)S(1)}, f32[1,32,32,128]{3,2,1,0:T(8,128)S(1)}, u32[]{:S(2)}, u32[]{:S(2)}) collective-permute-start(f32[1,32,32,128]{3,2,1,0:T(8,128)S(1)} %get-tuple-element.118), channel_id=1, source_target_pairs={{0,8},{1,17},{2,10},{3,19},{4,12},{5,21},{6,14},{7,23},{8,0},{9,25... | collective-permute-start | bytes 1572872 | tf_op jit(solution)/shard_map/ppermute | solution.py:572
  69.3 23.2 %collective-permute-start.10 = (f32[2,2,8,32,128]{4,3,2,1,0:T(8,128)S(1)}, f32[2,2,8,32,128]{4,3,2,1,0:T(8,128)S(1)}, u32[]{:S(2)}, u32[]{:S(2)}) collective-permute-start(f32[2,2,8,32,128]{4,3,2,1,0:T(8,128)S(1)} %get-tuple-element.117), channel_id=1, source_target_pairs={{0,2},{1,3},{2,0},{3,1},{4,6},{5,7},{6,4},{7,5},{8,10},{9,11},{10,... | collective-permute-start | bytes 1572872 | tf_op jit(solution)/shard_map/ppermute | solution.py:581
  70.1 45.3 %collective-permute-start.13 = (f32[2,32,32,128]{3,2,1,0:T(8,128)S(1)}, f32[2,32,32,128]{3,2,1,0:T(8,128)S(1)}, u32[]{:S(2)}, u32[]{:S(2)}) collective-permute-start(f32[2,32,32,128]{3,2,1,0:T(8,128)S(1)} %copy-done.11), channel_id=1, source_target_pairs={{0,16},{1,9},{2,18},{3,11},{4,20},{5,13},{6,22},{7,15},{8,24},{9,1... | collective-permute-start | bytes 3145736 | tf_op jit(solution)/shard_map/ppermute | solution.py:572
  70.6 28.6 %collective-permute-start.18 = (f32[2,4,128,128]{3,2,1,0:T(8,128)S(1)}, f32[2,4,128,128]{3,2,1,0:T(8,128)S(1)}, u32[]{:S(2)}, u32[]{:S(2)}) collective-permute-start(f32[2,4,128,128]{3,2,1,0:T(8,128)S(1)} %get-tuple-element.131.refs_3_), channel_id=1, source_target_pairs={{0,4},{1,5},{2,6},{3,7},{4,0},{5,1},{6,2},{7,3},{8,12},{9,13},{10,... | collective-permute-start | bytes 1572872 | tf_op jit(solution)/shard_map/ppermute | solution.py:581
  80.2 21.5 %collective-permute-start.17 = (f32[1,32,32,128]{3,2,1,0:T(8,128)S(1)}, f32[1,32,32,128]{3,2,1,0:T(8,128)S(1)}, u32[]{:S(2)}, u32[]{:S(2)}) collective-permute-start(f32[1,32,32,128]{3,2,1,0:T(8,128)S(1)} %copy-done.12), channel_id=1, source_target_pairs={{0,16},{1,9},{2,18},{3,11},{4,20},{5,13},{6,22},{7,15},{8,24},{9,1... | collective-permute-start | bytes 1572872 | tf_op jit(solution)/shard_map/ppermute | solution.py:572
  95.0 26.6 %collective-permute-start.12 = (f32[2,4,128,128]{3,2,1,0:T(8,128)S(1)}, f32[2,4,128,128]{3,2,1,0:T(8,128)S(1)}, u32[]{:S(2)}, u32[]{:S(2)}) collective-permute-start(f32[2,4,128,128]{3,2,1,0:T(8,128)S(1)} %get-tuple-element.121.refs_3_), channel_id=1, source_target_pairs={{0,4},{1,5},{2,6},{3,7},{4,0},{5,1},{6,2},{7,3},{8,12},{9,13},{10,... | collective-permute-start | bytes 1572872 | tf_op jit(solution)/shard_map/ppermute | solution.py:581
  96.6 17.0 %collective-permute-start.16 = (f32[2,1,8,32,128]{4,3,2,1,0:T(8,128)S(1)}, f32[2,1,8,32,128]{4,3,2,1,0:T(8,128)S(1)}, u32[]{:S(2)}, u32[]{:S(2)}) collective-permute-start(f32[2,1,8,32,128]{4,3,2,1,0:T(8,128)S(1)} %get-tuple-element.129), channel_id=1, source_target_pairs={{0,2},{1,3},{2,0},{3,1},{4,6},{5,7},{6,4},{7,5},{8,10},{9,11},{10,... | collective-permute-start | bytes 786440 | tf_op jit(solution)/shard_map/ppermute | solution.py:581
  99.2 36.7 %collective-permute-start.22 = (f32[2,32,32,128]{3,2,1,0:T(8,128)S(1)}, f32[2,32,32,128]{3,2,1,0:T(8,128)S(1)}, u32[]{:S(2)}, u32[]{:S(2)}) collective-permute-start(f32[2,32,32,128]{3,2,1,0:T(8,128)S(1)} %get-tuple-element.147), channel_id=1, source_target_pairs={{0,8},{1,17},{2,10},{3,19},{4,12},{5,21},{6,14},{7,23},{8,0},{9,25... | collective-permute-start | bytes 3145736 | tf_op jit(solution)/shard_map/ppermute | solution.py:572
  101.7 32.1 %collective-permute-start.20 = (f32[2,2,8,32,128]{4,3,2,1,0:T(8,128)S(1)}, f32[2,2,8,32,128]{4,3,2,1,0:T(8,128)S(1)}, u32[]{:S(2)}, u32[]{:S(2)}) collective-permute-start(f32[2,2,8,32,128]{4,3,2,1,0:T(8,128)S(1)} %get-tuple-element.143), channel_id=1, source_target_pairs={{0,2},{1,3},{2,0},{3,1},{4,6},{5,7},{6,4},{7,5},{8,10},{9,11},{10,... | collective-permute-start | bytes 1572872 | tf_op jit(solution)/shard_map/ppermute | solution.py:581
  116.2 34.1 %collective-permute-start.26 = (f32[2,32,32,128]{3,2,1,0:T(8,128)S(1)}, f32[2,32,32,128]{3,2,1,0:T(8,128)S(1)}, u32[]{:S(2)}, u32[]{:S(2)}) collective-permute-start(f32[2,32,32,128]{3,2,1,0:T(8,128)S(1)} %get-tuple-element.158), channel_id=1, source_target_pairs={{0,8},{1,17},{2,10},{3,19},{4,12},{5,21},{6,14},{7,23},{8,0},{9,25... | collective-permute-start | bytes 3145736 | tf_op jit(solution)/shard_map/ppermute | solution.py:572
  116.3 17.8 %collective-permute-start.23 = (f32[1,4,128,128]{3,2,1,0:T(8,128)S(1)}, f32[1,4,128,128]{3,2,1,0:T(8,128)S(1)}, u32[]{:S(2)}, u32[]{:S(2)}) collective-permute-start(f32[1,4,128,128]{3,2,1,0:T(8,128)S(1)} %get-tuple-element.148.refs_3_), channel_id=1, source_target_pairs={{0,4},{1,5},{2,6},{3,7},{4,0},{5,1},{6,2},{7,3},{8,12},{9,13},{10,... | collective-permute-start | bytes 786440 | tf_op jit(solution)/shard_map/ppermute | solution.py:581
  134.0 14.8 %collective-permute-start.19 = (f32[2,2,8,32,128]{4,3,2,1,0:T(8,128)S(1)}, f32[2,2,8,32,128]{4,3,2,1,0:T(8,128)S(1)}, u32[]{:S(2)}, u32[]{:S(2)}) collective-permute-start(f32[2,2,8,32,128]{4,3,2,1,0:T(8,128)S(1)} %get-tuple-element.140), channel_id=1, source_target_pairs={{0,2},{1,3},{2,0},{3,1},{4,6},{5,7},{6,4},{7,5},{8,10},{9,11},{10,... | collective-permute-start | bytes 1572872 | tf_op jit(solution)/shard_map/ppermute | solution.py:581
  134.1 14.8 %collective-permute-start.27 = (f32[1,32,32,128]{3,2,1,0:T(8,128)S(1)}, f32[1,32,32,128]{3,2,1,0:T(8,128)S(1)}, u32[]{:S(2)}, u32[]{:S(2)}) collective-permute-start(f32[1,32,32,128]{3,2,1,0:T(8,128)S(1)} %get-tuple-element.159), channel_id=1, source_target_pairs={{0,8},{1,17},{2,10},{3,19},{4,12},{5,21},{6,14},{7,23},{8,0},{9,25... | collective-permute-start | bytes 1572872 | tf_op jit(solution)/shard_map/ppermute | solution.py:572
  135.9 18.0 %collective-permute-start.25 = (f32[2,1,8,32,128]{4,3,2,1,0:T(8,128)S(1)}, f32[2,1,8,32,128]{4,3,2,1,0:T(8,128)S(1)}, u32[]{:S(2)}, u32[]{:S(2)}) collective-permute-start(f32[2,1,8,32,128]{4,3,2,1,0:T(8,128)S(1)} %get-tuple-element.157), channel_id=1, source_target_pairs={{0,2},{1,3},{2,0},{3,1},{4,6},{5,7},{6,4},{7,5},{8,10},{9,11},{10,... | collective-permute-start | bytes 786440 | tf_op jit(solution)/shard_map/ppermute | solution.py:581
  148.8 8.6 %collective-permute-start.24 = (f32[2,2,8,32,128]{4,3,2,1,0:T(8,128)S(1)}, f32[2,2,8,32,128]{4,3,2,1,0:T(8,128)S(1)}, u32[]{:S(2)}, u32[]{:S(2)}) collective-permute-start(f32[2,2,8,32,128]{4,3,2,1,0:T(8,128)S(1)} %get-tuple-element.154), channel_id=1, source_target_pairs={{0,1},{1,0},{2,3},{3,2},{4,5},{5,4},{6,7},{7,6},{8,9},{9,8},{10,11... | collective-permute-start | bytes 1572872 | tf_op jit(solution)/shard_map/ppermute | solution.py:581
  (24 other events, 177.2 us)

commit v11 on v10

--- a/solution.py
+++ b/solution.py
@@ -10,41 +10,41 @@
 
 QUAD = 4
 NEAR_SIZES = (2, 2, 1)
-FAR_SIZES = (1, 2, 2)
+FAR_SIZES = (2, 2, 1)
 ORDER = (
     ("pack", 0),
-    ("pack", 3),
     ("pack", 1),
     ("pack", 4),
     ("local", 0),
+    ("mix", 0),
+    ("local", 1),
+    ("mix", 1),
     ("pack", 2),
-    ("mix", 0),
-    ("mix", 1),
+    ("pack", 3),
     ("spread", 0),
     ("join", 0),
     ("spread", 1),
-    ("pack", 5),
     ("mix", 2),
     ("coef", 0),
     ("join", 1),
     ("spread", 2),
+    ("join", 2),
+    ("pack", 5),
+    ("mix", 4),
     ("coef", 1),
-    ("mix", 5),
-    ("join", 2),
     ("filter", 0),
     ("mix", 3),
-    ("local", 1),
     ("coef", 2),
-    ("mix", 4),
+    ("mix", 5),
     ("filter", 1),
+    ("filter", 2),
     ("back", 0),
-    ("filter", 2),
+    ("far", 4),
+    ("back", 1),
+    ("near", 0),
+    ("far", 3),
+    ("back", 2),
     ("far", 5),
-    ("near", 0),
-    ("back", 1),
-    ("far", 3),
-    ("far", 4),
-    ("back", 2),
     ("near", 2),
     ("near", 1),
 )
@@ -192,7 +192,7 @@
 
 
 def local_kernel(
-    far, coupling, kappa, flags, adj, before, after, next_to, src, mu, mu_before, mu_after, mu_next, low, high, out
+    far, coupling, kappa, flags, adj, before, after, next_to, src, mu, mu_before, mu_after, mu_next, out
 ):
     fields, planes, rows, cells = adj.shape
     step = pl.program_id(0)
@@ -202,18 +202,11 @@
     col = lax.broadcasted_iota(jnp.int32, (rows, cells), 1)
     ring = 0.5 / ((row + rows * far).astype(jnp.float32) + 1.0)
 
-    def pick(source, behind, ahead, f, k):
-        if k < 0:
-            return jnp.where(first, low[f, 0], behind)
-        if k >= planes:
-            return jnp.where(last, high[f, 0], ahead)
-        return source
-
     def visc(k):
-        return pick(mu[max(0, min(k, planes - 1))], mu_before[0], mu_after[0], fields, k)
+        return mu_before[0] if k < 0 else mu_after[0] if k >= planes else mu[k]
 
     def cell(f, k):
-        return pick(adj[f, max(0, min(k, planes - 1))], before[f, 0], after[f, 0], f, k)
+        return before[f, 0] if k < 0 else after[f, 0] if k >= planes else adj[f, k]
 
     def outward(x, edge):
         moved = pltpu.roll(x, rows - 1, 0)
@@ -234,6 +227,10 @@
         m = visc(k)
         up = ring * (m + visc(k + 1))
         down = ring * (m + visc(k - 1))
+        if k == planes - 1:
+            up = jnp.where(last, 0.0, up)
+        if k == 0:
+            down = jnp.where(first, 0.0, down)
         outer = 0.5 * (m + outward(m, mu_next[k]))
         inner = 0.5 * (m + inward(m, mu_next[k]))
         if far:
@@ -255,7 +252,7 @@
             out[f, k] = total
 
 
-def local_part(far, center, source, viscosity, kappa, coupling, flags, low, high, token):
+def local_part(far, center, source, viscosity, kappa, coupling, flags, token):
     fields, block, rows, cells = center.shape
     half = rows // 2
     planes = min(4, block)
@@ -270,14 +267,13 @@
     behind = lambda i: jnp.maximum(i * planes - 1, 0)
     ahead = lambda i: jnp.minimum(i * planes + planes, block - 1)
     here = lambda i: i
-    halo = pl.BlockSpec((fields + 1, 1, half, cells), lambda i: (0, 0, far, 0))
     return call(
         functools.partial(local_kernel, far),
         "local_part",
         token,
         (block // planes,),
         [coupling, kappa, flags, center, center, center, center, source]
-        + [viscosity, viscosity, viscosity, viscosity, low, high],
+        + [viscosity] * 4,
         [
             SMEM,
             SMEM,
@@ -291,8 +287,6 @@
             plane(1, behind),
             plane(1, ahead),
             pl.BlockSpec((planes, 8, cells), lambda i: (i, edge, 0)),
-            halo,
-            halo,
         ],
         pl.BlockSpec((fields, planes, half, cells), lambda i: (0, i, 0, 0)),
         shaped(fields, block, half, cells),
@@ -323,6 +317,25 @@
     def side(self, first, index):
         return pl.BlockSpec((1, self.block, self.near, self.cells), lambda i: (first + i, 0, index, 0))
 
+    def faces(self, lo, side):
+        shape = (1, 1, self.near, self.cells)
+        at = lambda f, k: pl.BlockSpec(shape, lambda i: (f(i), k, side, 0))
+        field = lambda i: lo + i
+        inputs, specs = [self.kappa], [SMEM]
+        for k, halo in zip((0, self.block - 1), self.halos):
+            inputs += [self.center, halo, self.viscosity[None], halo]
+            specs += [at(field, k), at(field, 0), at(lambda i: 0, k), at(lambda i: self.fields, 0)]
+        return inputs, specs
+
+    def face_terms(self, refs, lo, side):
+        kappa, rest = refs[0], refs[1:9]
+        row = lax.broadcasted_iota(jnp.int32, (self.near, self.cells), 0) + side * self.near
+        ring = 0.5 * kappa[lo + pl.program_id(0)] / (row.astype(jnp.float32) + 1.0)
+        here, there, mu, mu_there = rest[:4]
+        low = ring * (mu[0, 0] + mu_there[0, 0]) * (here[0, 0] - there[0, 0])
+        here, there, mu, mu_there = rest[4:]
+        return low, ring * (mu[0, 0] + mu_there[0, 0]) * (here[0, 0] - there[0, 0])
+
     def part(self):
         return pl.BlockSpec((1, self.cycles, self.block, self.cells), lambda i, *_: (i, 0, 0, 0))
 
@@ -358,10 +371,15 @@
         )
 
     def spread(self, local, others, lo, hi, token):
+        faces, face_specs = self.faces(lo, 0)
+
         def kernel(ints, reals, local, *refs):
-            others, (mine, core, chip), (flat, stage) = refs[:-5], refs[-5:-2], refs[-2:]
+            others, (mine, core, chip), (flat, stage) = refs[9:-5], refs[-5:-2], refs[-2:]
             scalars = self.scalars(ints, reals)
             flat[...] = sums(scalars, local, others).reshape(flat.shape)
+            low, high = self.face_terms(refs, lo, 0)
+            flat[: self.near] += low
+            flat[-self.near :] += high
             for o in range(QUAD):
                 for j in range(self.owned):
                     for a in range(2):
@@ -377,8 +395,8 @@
             "spread",
             token,
             (hi - lo,),
-            [self.ints, self.reals, local] + others,
-            [SMEM, SMEM, self.side(lo, 0)] + [self.side(0, 0)] * len(others),
+            [self.ints, self.reals, local] + faces + others,
+            [SMEM, SMEM, self.side(lo, 0)] + face_specs + [self.side(0, 0)] * len(others),
             [self.part(), self.parts(2), self.parts(1)],
             self.quad_shapes(hi - lo),
             [
@@ -530,23 +548,29 @@
         )
 
     def place_far(self, local, others, held, lo, hi, token):
+        carried = [] if held is None else [held]
+        faces, face_specs = self.faces(lo, 1)
+
         def kernel(ints, reals, local, *refs):
-            others, out = refs[: len(refs) - 1 - len(carried)], refs[-1]
+            others, out = refs[9 : len(refs) - 1 - len(carried)], refs[-1]
             out[0] = sums(self.scalars(ints, reals), local, others)
-
-        carried = [] if held is None else [held]
+            low, high = self.face_terms(refs, lo, 1)
+            out[0, 0] += low
+            out[0, self.block - 1] += high
+
         return call(
             kernel,
             "place_far",
             token,
             (hi - lo,),
-            [self.ints, self.reals, local] + others + carried,
+            [self.ints, self.reals, local] + faces + others + carried,
             [SMEM, SMEM, self.side(lo, 0)]
+            + face_specs
             + [self.side(0, 0)] * len(others)
             + [ANY] * len(carried),
             self.side(lo, 1),
             shaped(*self.shape),
-            alias={3 + len(others): 0} if carried else None,
+            alias={3 + len(faces) + len(others): 0} if carried else None,
         )
 
 
@@ -611,9 +635,10 @@
             first[g] = to_first(packed[0])
             if halos is None:
                 halos = ring(packed[1], 1), ring(packed[2], -1)
+                plan.halos, plan.center, plan.viscosity, plan.kappa = halos, center, viscosity, kappa
         elif step == "local":
             local[g], stamp = local_part(
-                g, center, source[0], viscosity, kappa, coupling, bc_flags, *halos, token
+                g, center, source[0], viscosity, kappa, coupling, bc_flags, token
             )
         elif step == "mix":
             *mixed, stamp = plan.mix(center, first[g], lo, hi, index, token)

time: 160 us -> 155 us (0.969)
  waiting for transfers between devices: 68.4 us -> 64.7 us
  starting transfers between devices: 31.7 us -> 29.4 us
  local copies, waits for them, and re-layouts: 1.43 us -> 3.33 us
    ppermute x12, waiting for transfers between devices: 28.4 us -> 14.4 us  [to_partner(): return lax.ppermute(x, ('inst', 'space'), pairs)]
    ppermute x15, waiting for transfers between devices: 38.8 us -> 47 us  [to_sector(): return lax.ppermute(x, 'space', [(i, i ^ k) for i in range(sectors)])]
    ppermute x15, starting transfers between devices: 15.5 us -> 10.5 us  [to_sector(): return lax.ppermute(x, 'space', [(i, i ^ k) for i in range(sectors)])]
    ppermute x12, starting transfers between devices: 12.7 us -> 15.3 us  [to_partner(): return lax.ppermute(x, ('inst', 'space'), pairs)]
    ppermute x2, waiting for transfers between devices: 1.15 us -> 3.25 us  [ring(): lax.ppermute(x, 'space', [(i, (i + step) % sectors) for i in range(sector...]
    unnamed x39 -> x35, local copies, waits for them, and re-layouts: 1.43 us -> 3.33 us
    pallas_call x29, Pallas kernels: 44.6 us -> 42.9 us  [call(): pl.pallas_call(kernel, grid=grid, in_specs=list(in_specs) + [ANY] * len(e...]
  transfers between devices with their start and end apart: 29 -> 29, of which waited for: 11 -> 10; matrix products, arithmetic and copies ran while one was open for 0% -> 0% of each run, Pallas kernels for 33% -> 33%
where the time goes in v11:
time: 155 us; the launch traced here: 154 us
  waiting for transfers between devices  64.7 us (42%)
  Pallas kernels  56.2 us (36%)
  starting transfers between devices  29.4 us (19%)
  local copies, waits for them, and re-layouts  3.33 us (2%)
    ppermute x15, waiting for transfers between devices, to_sector(): return lax.ppermute(x, 'space', [(i, i ^ k) for i in range(sectors)])  47 us
    pallas_call x29, Pallas kernels, call(): pl.pallas_call(kernel, grid=grid, in_specs=list(in_specs) + [ANY] * len(e...  42.9 us
    ppermute x12, starting transfers between devices, to_partner(): return lax.ppermute(x, ('inst', 'space'), pairs)  15.3 us
    ppermute x12, waiting for transfers between devices, to_partner(): return lax.ppermute(x, ('inst', 'space'), pairs)  14.4 us
    pallas_call x6, Pallas kernels, table_call(): pl.pallas_call(kernel, grid_spec=pltpu.PrefetchScalarGridSpec(num_scalar_...  13.3 us
    ppermute x15, starting transfers between devices, to_sector(): return lax.ppermute(x, 'space', [(i, i ^ k) for i in range(sectors)])  10.5 us
    ppermute x2, starting transfers between devices, ring(): lax.ppermute(x, 'space', [(i, (i + step) % sectors) for i in range(sector...  3.54 us
    unnamed x35, local copies, waits for them, and re-layouts  3.33 us
  transfers between devices with their start and end apart: 29, of which 10 were waited for; matrix products, arithmetic and copies ran while one was open for 0% of the time, Pallas kernels for 33%

profile of v11, /device:TPU:0, one launch (start us, length us, event | category | flops | bytes accessed | tf_op | source)
XLA Modules:
  0.0 154.1 jit_solution(946267128330366304)
XLA Ops:
  0.0 2.3 %pack.6 = (f32[2,32,32,128]{3,2,1,0:T(8,128)}, f32[6,1,64,128]{3,2,1,0:T(8,128)}, f32[6,1,64,128]{3,2,1,0:T(8,128)}, f32[8,128]{1,0:T(8,128)}) custom-call(f32[5,32,64,128]{3,2,1,0:T(8,128)} %bitcast.6, f32[5,32,64,128]{3,2,1,0:T(8,128)} %bitcast.7, f32[32,64,128]{2,1,0:T(8,128)} %refs_11_.3, f32[5,32,64,128]{3,2,1,0:T(8,128)} %bitcast.8, ...), custom_call_target="tpu_custom_call" | custom-call | tf_op jit(solution)/shard_map/pack/pallas_call | solution.py:153
  2.4 3.0 %collective-permute-start.3 = (f32[2,32,32,128]{3,2,1,0:T(8,128)}, f32[2,32,32,128]{3,2,1,0:T(8,128)}, u32[]{:S(2)}, u32[]{:S(2)}) collective-permute-start(f32[2,32,32,128]{3,2,1,0:T(8,128)} %get-tuple-element.95), channel_id=1, source_target_pairs={{0,16},{1,9},{2,18},{3,11},{4,20},{5,13},{6,22},{7,15},{8,24},{9,1... | collective-permute-start | bytes 3145736 | tf_op jit(solution)/shard_map/ppermute | solution.py:596
  10.6 8.6 %local_part.2 = (f32[5,32,32,128]{3,2,1,0:T(8,128)}, f32[8,128]{1,0:T(8,128)S(1)}) custom-call(f32[5,5]{1,0:T(8,128)S(1)} %copy-done.7, f32[5]{0:T(128)S(1)} %copy-done.6, s32[5,3]{1,0:T(8,128)S(1)} %copy.23.refs_2_, f32[5,32,64,128]{3,2,1,0:T(8,128)} %bitcast.11, f32[5,32,64,128]{3,2,1,0:T(8,128)} %bitcast.12, f32[5,32,64,128]{3,2,1,0:T(8,128)} %bitcast.13, ...), custom_call_target="tpu_custom_call" | custom-call | tf_op jit(solution)/shard_map/local_part/pallas_call | solution.py:153
  22.7 2.5 %copy-done.2 = f32[1,5,32,64,128]{4,3,2,1,0:T(8,128)S(1)} copy-done((f32[1,5,32,64,128]{4,3,2,1,0:T(8,128)S(1)}, f32[1,5,32,64,128]{4,3,2,1,0:T(8,128)}, u32[]{:S(2)}) %copy-start.2) | copy-done | bytes 5242904
  25.2 5.4 %local_part.3 = (f32[5,32,32,128]{3,2,1,0:T(8,128)S(1)}, f32[8,128]{1,0:T(8,128)S(1)}) custom-call(f32[5,5]{1,0:T(8,128)S(1)} %copy-done.7, f32[5]{0:T(128)S(1)} %copy-done.6, s32[5,3]{1,0:T(8,128)S(1)} %copy.23.refs_2_, f32[5,32,64,128]{3,2,1,0:T(8,128)S(1)} %bitcast.18, f32[5,32,64,128]{3,2,1,0:T(8,128)S(1)} %bitcast.19, f32[5,32,64,128]{3,2,1,0:T(8,128)S(1)} %bitcast.20, ...), custom_call_target="tpu_custom_call" | custom-call | tf_op jit(solution)/shard_map/local_part/pallas_call | solution.py:153
  30.6 5.7 %collective-permute-done.2.refs_3_.refs_12_ = f32[2,32,32,128]{3,2,1,0:T(8,128)S(1)} collective-permute-done((f32[2,32,32,128]{3,2,1,0:T(8,128)}, f32[2,32,32,128]{3,2,1,0:T(8,128)S(1)}, u32[]{:S(2)}, u32[]{:S(2)}) %collective-permute-start.2) | collective-permute-done | bytes 1048608 | tf_op jit(solution)/shard_map/ppermute | solution.py:596
  37.1 2.3 %collective-permute-start.4 = (f32[2,32,32,128]{3,2,1,0:T(8,128)S(1)}, f32[2,32,32,128]{3,2,1,0:T(8,128)S(1)}, u32[]{:S(2)}, u32[]{:S(2)}) collective-permute-start(f32[2,32,32,128]{3,2,1,0:T(8,128)S(1)} %get-tuple-element.99), channel_id=1, source_target_pairs={{0,8},{1,17},{2,10},{3,19},{4,12},{5,21},{6,14},{7,23},{8,0},{9,25... | collective-permute-start | bytes 3145736 | tf_op jit(solution)/shard_map/ppermute | solution.py:596
  39.5 3.5 %collective-permute-start.1 = (f32[6,1,64,128]{3,2,1,0:T(8,128)S(1)}, f32[6,1,64,128]{3,2,1,0:T(8,128)S(1)}, u32[]{:S(2)}, u32[]{:S(2)}) collective-permute-start(f32[6,1,64,128]{3,2,1,0:T(8,128)S(1)} %copy-done.13), channel_id=1, source_target_pairs={{0,7},{1,0},{2,1},{3,2},{4,3},{5,4},{6,5},{7,6},{8,15},{9,8},{10,9... | collective-permute-start | bytes 589832 | tf_op jit(solution)/shard_map/ppermute | solution.py:608
  43.3 3.2 %collective-permute-done.refs_5_.refs_7_ = f32[6,1,64,128]{3,2,1,0:T(8,128)S(1)} collective-permute-done((f32[6,1,64,128]{3,2,1,0:T(8,128)S(1)}, f32[6,1,64,128]{3,2,1,0:T(8,128)S(1)}, u32[]{:S(2)}, u32[]{:S(2)}) %collective-permute-start) | collective-permute-done | bytes 196640 | tf_op jit(solution)/shard_map/ppermute | solution.py:608
  46.5 2.2 %spread.3 = (f32[2,8,32,128]{3,2,1,0:T(8,128)S(1)}, f32[2,2,8,32,128]{4,3,2,1,0:T(8,128)S(1)}, f32[2,2,8,32,128]{4,3,2,1,0:T(8,128)S(1)}, f32[8,128]{1,0:T(8,128)S(1)}) custom-call(s32[22]{0:T(128)S(1)} %pad_add_fusion.refs_0_, f32[71]{0:T(128)S(1)} %copy-done.5, f32[5,32,32,128]{3,2,1,0:T(8,128)S(1)} %copy-done.1, f32[5]{0:T(128)S(1)} %copy-done.6, ...), custom_call_target="tpu_custom_call" | custom-call | tf_op jit(solution)/shard_map/spread/pallas_call | solution.py:153
  55.4 4.7 %collective-permute-done.9.refs_3_.refs_12_ = f32[1,32,32,128]{3,2,1,0:T(8,128)S(1)} collective-permute-done((f32[1,32,32,128]{3,2,1,0:T(8,128)S(1)}, f32[1,32,32,128]{3,2,1,0:T(8,128)S(1)}, u32[]{:S(2)}, u32[]{:S(2)}) %collective-permute-start.9) | collective-permute-done | bytes 524320 | tf_op jit(solution)/shard_map/ppermute | solution.py:596
  62.8 3.9 %collective-permute-done.8.refs_5_.refs_7_ = f32[2,2,8,32,128]{4,3,2,1,0:T(8,128)S(1)} collective-permute-done((f32[2,2,8,32,128]{4,3,2,1,0:T(8,128)S(1)}, f32[2,2,8,32,128]{4,3,2,1,0:T(8,128)S(1)}, u32[]{:S(2)}, u32[]{:S(2)}) %collective-permute-start.8) | collective-permute-done | bytes 524320 | tf_op jit(solution)/shard_map/ppermute | solution.py:605
  66.8 2.4 %coefficients.3 = (f32[2,4,128,128]{3,2,1,0:T(8,128)S(1)}, f32[8,128]{1,0:T(8,128)S(1)}) custom-call(s32[22]{0:T(128)S(1)} %pad_add_fusion.refs_0_, f32[71]{0:T(128)S(1)} %copy-done.5, f32[2,16,128,128]{3,2,1,0:T(8,128)S(1)} %copy-done.4, f32[2,8,32,128]{3,2,1,0:T(8,128)S(1)} %get-tuple-element.111.refs_3_.refs_5_, ...), custom_call_target="tpu_custom_call" | custom-call | tf_op jit(solution)/shard_map/coefficients/pallas_call | solution.py:432
  71.6 4.0 %collective-permute-done.12.refs_13_ = f32[1,32,32,128]{3,2,1,0:T(8,128)S(1)} collective-permute-done((f32[1,32,32,128]{3,2,1,0:T(8,128)S(1)}, f32[1,32,32,128]{3,2,1,0:T(8,128)S(1)}, u32[]{:S(2)}, u32[]{:S(2)}) %collective-permute-start.12) | collective-permute-done | bytes 524320 | tf_op jit(solution)/shard_map/ppermute | solution.py:596
  81.4 13.4 %collective-permute-done.10.refs_5_.refs_7_ = f32[2,2,8,32,128]{4,3,2,1,0:T(8,128)S(1)} collective-permute-done((f32[2,2,8,32,128]{4,3,2,1,0:T(8,128)S(1)}, f32[2,2,8,32,128]{4,3,2,1,0:T(8,128)S(1)}, u32[]{:S(2)}, u32[]{:S(2)}) %collective-permute-start.10) | collective-permute-done | bytes 524320 | tf_op jit(solution)/shard_map/ppermute | solution.py:605
  94.8 2.4 %coefficients.4 = (f32[2,4,128,128]{3,2,1,0:T(8,128)S(1)}, f32[8,128]{1,0:T(8,128)S(1)}) custom-call(s32[22]{0:T(128)S(1)} %pad_add_fusion.refs_0_, f32[71]{0:T(128)S(1)} %copy-done.5, f32[2,16,128,128]{3,2,1,0:T(8,128)S(1)} %copy-done.4, f32[2,8,32,128]{3,2,1,0:T(8,128)S(1)} %get-tuple-element.108.refs_3_.refs_5_, ...), custom_call_target="tpu_custom_call" | custom-call | tf_op jit(solution)/shard_map/coefficients/pallas_call | solution.py:432
  97.7 2.5 %filtered.3 = (f32[2,8,32,128]{3,2,1,0:T(8,128)S(1)}, f32[2,2,8,32,128]{4,3,2,1,0:T(8,128)S(1)}, f32[2,2,8,32,128]{4,3,2,1,0:T(8,128)S(1)}, f32[8,128]{1,0:T(8,128)S(1)}) custom-call(s32[22]{0:T(128)S(1)} %pad_add_fusion.refs_0_, f32[71]{0:T(128)S(1)} %copy-done.5, f32[2,16,128,128]{3,2,1,0:T(8,128)S(1)} %copy-done.3, ...), custom_call_target="tpu_custom_call" | custom-call | tf_op jit(solution)/shard_map/filtered/pallas_call | solution.py:432
  100.2 2.5 %collective-permute-start.21 = (f32[2,2,8,32,128]{4,3,2,1,0:T(8,128)S(1)}, f32[2,2,8,32,128]{4,3,2,1,0:T(8,128)S(1)}, u32[]{:S(2)}, u32[]{:S(2)}) collective-permute-start(f32[2,2,8,32,128]{4,3,2,1,0:T(8,128)S(1)} %get-tuple-element.144), channel_id=1, source_target_pairs={{0,2},{1,3},{2,0},{3,1},{4,6},{5,7},{6,4},{7,5},{8,10},{9,11},{10,... | collective-permute-start | bytes 1572872 | tf_op jit(solution)/shard_map/ppermute | solution.py:605
  108.2 17.7 %collective-permute-done.14.refs_4_ = f32[2,4,128,128]{3,2,1,0:T(8,128)S(1)} collective-permute-done((f32[2,4,128,128]{3,2,1,0:T(8,128)S(1)}, f32[2,4,128,128]{3,2,1,0:T(8,128)S(1)}, u32[]{:S(2)}, u32[]{:S(2)}) %collective-permute-start.14) | collective-permute-done | bytes 524320 | tf_op jit(solution)/shard_map/ppermute | solution.py:605
  125.9 2.5 %filtered.4 = (f32[2,8,32,128]{3,2,1,0:T(8,128)S(1)}, f32[2,2,8,32,128]{4,3,2,1,0:T(8,128)S(1)}, f32[2,2,8,32,128]{4,3,2,1,0:T(8,128)S(1)}, f32[8,128]{1,0:T(8,128)S(1)}) custom-call(s32[22]{0:T(128)S(1)} %pad_add_fusion.refs_0_, f32[71]{0:T(128)S(1)} %copy-done.5, f32[2,16,128,128]{3,2,1,0:T(8,128)S(1)} %copy-done.3, ...), custom_call_target="tpu_custom_call" | custom-call | tf_op jit(solution)/shard_map/filtered/pallas_call | solution.py:432
  128.5 3.6 %collective-permute-done.22.refs_4_ = f32[1,4,128,128]{3,2,1,0:T(8,128)S(1)} collective-permute-done((f32[1,4,128,128]{3,2,1,0:T(8,128)S(1)}, f32[1,4,128,128]{3,2,1,0:T(8,128)S(1)}, u32[]{:S(2)}, u32[]{:S(2)}) %collective-permute-start.22) | collective-permute-done | bytes 262176 | tf_op jit(solution)/shard_map/ppermute | solution.py:605
  136.6 6.8 %collective-permute-done.19.refs_1_.refs_4_ = f32[2,2,8,32,128]{4,3,2,1,0:T(8,128)S(1)} collective-permute-done((f32[2,2,8,32,128]{4,3,2,1,0:T(8,128)S(1)}, f32[2,2,8,32,128]{4,3,2,1,0:T(8,128)S(1)}, u32[]{:S(2)}, u32[]{:S(2)}) %collective-permute-start.19) | collective-permute-done | bytes 524320 | tf_op jit(solution)/shard_map/ppermute | solution.py:605
  143.5 2.5 %place_near.3 = (f32[5,32,64,128]{3,2,1,0:T(8,128)}, f32[8,128]{1,0:T(8,128)S(1)}) custom-call(s32[22]{0:T(128)S(1)} %pad_add_fusion.refs_0_, f32[71]{0:T(128)S(1)} %copy-done.5, f32[2,8,32,128]{3,2,1,0:T(8,128)S(1)} %get-tuple-element.155.refs_2_, f32[2,2,8,32,128]{4,3,2,1,0:T(8,128)S(1)} %collective-permute-done.26.refs_3_, ...), custom_call_target="tpu_custom_call", output_to_operand_aliasing={{0}: (5, {})} | custom-call | tf_op jit(solution)/shard_map/place_near/pallas_call | solution.py:153
  151.6 2.5 %place_near.5 = (f32[5,32,64,128]{3,2,1,0:T(8,128)}, f32[8,128]{1,0:T(8,128)}) custom-call(s32[22]{0:T(128)S(1)} %pad_add_fusion.refs_0_, f32[71]{0:T(128)S(1)} %copy-done.5, f32[2,8,32,128]{3,2,1,0:T(8,128)S(1)} %get-tuple-element.138.refs_2_, f32[2,2,8,32,128]{4,3,2,1,0:T(8,128)S(1)} %collective-permute-done.23.refs_3_, ...), custom_call_target="tpu_custom_call", output_to_operand_aliasing={{0}: (5, {})} | custom-call | tf_op jit(solution)/shard_map/place_near/pallas_call | solution.py:153
  (106 shorter events, 43.2 us)
Async XLA Ops:
  2.4 16.9 %collective-permute-start.3 = (f32[2,32,32,128]{3,2,1,0:T(8,128)}, f32[2,32,32,128]{3,2,1,0:T(8,128)}, u32[]{:S(2)}, u32[]{:S(2)}) collective-permute-start(f32[2,32,32,128]{3,2,1,0:T(8,128)} %get-tuple-element.95), channel_id=1, source_target_pairs={{0,16},{1,9},{2,18},{3,11},{4,20},{5,13},{6,22},{7,15},{8,24},{9,1... | collective-permute-start | bytes 3145736 | tf_op jit(solution)/shard_map/ppermute | solution.py:596
  7.6 28.8 %collective-permute-start.2 = (f32[2,32,32,128]{3,2,1,0:T(8,128)}, f32[2,32,32,128]{3,2,1,0:T(8,128)S(1)}, u32[]{:S(2)}, u32[]{:S(2)}) collective-permute-start(f32[2,32,32,128]{3,2,1,0:T(8,128)} %get-tuple-element.94), channel_id=1, source_target_pairs={{0,16},{1,9},{2,18},{3,11},{4,20},{5,13},{6,22},{7,15},{8,24},{9,1... | collective-permute-start | bytes 3145736 | tf_op jit(solution)/shard_map/ppermute | solution.py:596
  20.7 25.9 %collective-permute-start.5 = (f32[2,32,32,128]{3,2,1,0:T(8,128)S(1)}, f32[2,32,32,128]{3,2,1,0:T(8,128)S(1)}, u32[]{:S(2)}, u32[]{:S(2)}) collective-permute-start(f32[2,32,32,128]{3,2,1,0:T(8,128)S(1)} %get-tuple-element.100), channel_id=1, source_target_pairs={{0,8},{1,17},{2,10},{3,19},{4,12},{5,21},{6,14},{7,23},{8,0},{9,25... | collective-permute-start | bytes 3145736 | tf_op jit(solution)/shard_map/ppermute | solution.py:596
  37.1 16.5 %collective-permute-start.4 = (f32[2,32,32,128]{3,2,1,0:T(8,128)S(1)}, f32[2,32,32,128]{3,2,1,0:T(8,128)S(1)}, u32[]{:S(2)}, u32[]{:S(2)}) collective-permute-start(f32[2,32,32,128]{3,2,1,0:T(8,128)S(1)} %get-tuple-element.99), channel_id=1, source_target_pairs={{0,8},{1,17},{2,10},{3,19},{4,12},{5,21},{6,14},{7,23},{8,0},{9,25... | collective-permute-start | bytes 3145736 | tf_op jit(solution)/shard_map/ppermute | solution.py:596
  50.9 9.2 %collective-permute-start.9 = (f32[1,32,32,128]{3,2,1,0:T(8,128)S(1)}, f32[1,32,32,128]{3,2,1,0:T(8,128)S(1)}, u32[]{:S(2)}, u32[]{:S(2)}) collective-permute-start(f32[1,32,32,128]{3,2,1,0:T(8,128)S(1)} %get-tuple-element.113), channel_id=1, source_target_pairs={{0,16},{1,9},{2,18},{3,11},{4,20},{5,13},{6,22},{7,15},{8,24},{9,1... | collective-permute-start | bytes 1572872 | tf_op jit(solution)/shard_map/ppermute | solution.py:596
  52.4 27.5 %collective-permute-start.11 = (f32[2,32,32,128]{3,2,1,0:T(8,128)S(1)}, f32[2,32,32,128]{3,2,1,0:T(8,128)S(1)}, u32[]{:S(2)}, u32[]{:S(2)}) collective-permute-start(f32[2,32,32,128]{3,2,1,0:T(8,128)S(1)} %copy-done.12), channel_id=1, source_target_pairs={{0,16},{1,9},{2,18},{3,11},{4,20},{5,13},{6,22},{7,15},{8,24},{9,1... | collective-permute-start | bytes 3145736 | tf_op jit(solution)/shard_map/ppermute | solution.py:596
  53.0 13.8 %collective-permute-start.8 = (f32[2,2,8,32,128]{4,3,2,1,0:T(8,128)S(1)}, f32[2,2,8,32,128]{4,3,2,1,0:T(8,128)S(1)}, u32[]{:S(2)}, u32[]{:S(2)}) collective-permute-start(f32[2,2,8,32,128]{4,3,2,1,0:T(8,128)S(1)} %get-tuple-element.112), channel_id=1, source_target_pairs={{0,2},{1,3},{2,0},{3,1},{4,6},{5,7},{6,4},{7,5},{8,10},{9,11},{10,... | collective-permute-start | bytes 1572872 | tf_op jit(solution)/shard_map/ppermute | solution.py:605
  55.3 13.9 %collective-permute-start.7 = (f32[2,2,8,32,128]{4,3,2,1,0:T(8,128)S(1)}, f32[2,2,8,32,128]{4,3,2,1,0:T(8,128)S(1)}, u32[]{:S(2)}, u32[]{:S(2)}) collective-permute-start(f32[2,2,8,32,128]{4,3,2,1,0:T(8,128)S(1)} %get-tuple-element.109), channel_id=1, source_target_pairs={{0,1},{1,0},{2,3},{3,2},{4,5},{5,4},{6,7},{7,6},{8,9},{9,8},{10,11... | collective-permute-start | bytes 1572872 | tf_op jit(solution)/shard_map/ppermute | solution.py:605
  60.7 14.9 %collective-permute-start.12 = (f32[1,32,32,128]{3,2,1,0:T(8,128)S(1)}, f32[1,32,32,128]{3,2,1,0:T(8,128)S(1)}, u32[]{:S(2)}, u32[]{:S(2)}) collective-permute-start(f32[1,32,32,128]{3,2,1,0:T(8,128)S(1)} %get-tuple-element.119), channel_id=1, source_target_pairs={{0,8},{1,17},{2,10},{3,19},{4,12},{5,21},{6,14},{7,23},{8,0},{9,25... | collective-permute-start | bytes 1572872 | tf_op jit(solution)/shard_map/ppermute | solution.py:596
  60.9 39.3 %collective-permute-start.17 = (f32[2,32,32,128]{3,2,1,0:T(8,128)S(1)}, f32[2,32,32,128]{3,2,1,0:T(8,128)S(1)}, u32[]{:S(2)}, u32[]{:S(2)}) collective-permute-start(f32[2,32,32,128]{3,2,1,0:T(8,128)S(1)} %get-tuple-element.131), channel_id=1, source_target_pairs={{0,16},{1,9},{2,18},{3,11},{4,20},{5,13},{6,22},{7,15},{8,24},{9,1... | collective-permute-start | bytes 3145736 | tf_op jit(solution)/shard_map/ppermute | solution.py:596
  69.3 25.5 %collective-permute-start.10 = (f32[2,2,8,32,128]{4,3,2,1,0:T(8,128)S(1)}, f32[2,2,8,32,128]{4,3,2,1,0:T(8,128)S(1)}, u32[]{:S(2)}, u32[]{:S(2)}) collective-permute-start(f32[2,2,8,32,128]{4,3,2,1,0:T(8,128)S(1)} %get-tuple-element.117), channel_id=1, source_target_pairs={{0,2},{1,3},{2,0},{3,1},{4,6},{5,7},{6,4},{7,5},{8,10},{9,11},{10,... | collective-permute-start | bytes 1572872 | tf_op jit(solution)/shard_map/ppermute | solution.py:605
  69.9 27.4 %collective-permute-start.18 = (f32[2,4,128,128]{3,2,1,0:T(8,128)S(1)}, f32[2,4,128,128]{3,2,1,0:T(8,128)S(1)}, u32[]{:S(2)}, u32[]{:S(2)}) collective-permute-start(f32[2,4,128,128]{3,2,1,0:T(8,128)S(1)} %get-tuple-element.132.refs_3_), channel_id=1, source_target_pairs={{0,4},{1,5},{2,6},{3,7},{4,0},{5,1},{6,2},{7,3},{8,12},{9,13},{10,... | collective-permute-start | bytes 1572872 | tf_op jit(solution)/shard_map/ppermute | solution.py:605
  78.4 28.2 %collective-permute-start.15 = (f32[1,32,32,128]{3,2,1,0:T(8,128)S(1)}, f32[1,32,32,128]{3,2,1,0:T(8,128)S(1)}, u32[]{:S(2)}, u32[]{:S(2)}) collective-permute-start(f32[1,32,32,128]{3,2,1,0:T(8,128)S(1)} %get-tuple-element.128), channel_id=1, source_target_pairs={{0,16},{1,9},{2,18},{3,11},{4,20},{5,13},{6,22},{7,15},{8,24},{9,1... | collective-permute-start | bytes 1572872 | tf_op jit(solution)/shard_map/ppermute | solution.py:596
  80.0 23.6 %collective-permute-start.16 = (f32[2,1,8,32,128]{4,3,2,1,0:T(8,128)S(1)}, f32[2,1,8,32,128]{4,3,2,1,0:T(8,128)S(1)}, u32[]{:S(2)}, u32[]{:S(2)}) collective-permute-start(f32[2,1,8,32,128]{4,3,2,1,0:T(8,128)S(1)} %get-tuple-element.130), channel_id=1, source_target_pairs={{0,2},{1,3},{2,0},{3,1},{4,6},{5,7},{6,4},{7,5},{8,10},{9,11},{10,... | collective-permute-start | bytes 786440 | tf_op jit(solution)/shard_map/ppermute | solution.py:605
  94.8 39.3 %collective-permute-start.20 = (f32[2,32,32,128]{3,2,1,0:T(8,128)S(1)}, f32[2,32,32,128]{3,2,1,0:T(8,128)S(1)}, u32[]{:S(2)}, u32[]{:S(2)}) collective-permute-start(f32[2,32,32,128]{3,2,1,0:T(8,128)S(1)} %get-tuple-element.142), channel_id=1, source_target_pairs={{0,8},{1,17},{2,10},{3,19},{4,12},{5,21},{6,14},{7,23},{8,0},{9,25... | collective-permute-start | bytes 3145736 | tf_op jit(solution)/shard_map/ppermute | solution.py:596
  97.3 28.6 %collective-permute-start.14 = (f32[2,4,128,128]{3,2,1,0:T(8,128)S(1)}, f32[2,4,128,128]{3,2,1,0:T(8,128)S(1)}, u32[]{:S(2)}, u32[]{:S(2)}) collective-permute-start(f32[2,4,128,128]{3,2,1,0:T(8,128)S(1)} %get-tuple-element.127.refs_3_), channel_id=1, source_target_pairs={{0,4},{1,5},{2,6},{3,7},{4,0},{5,1},{6,2},{7,3},{8,12},{9,13},{10,... | collective-permute-start | bytes 1572872 | tf_op jit(solution)/shard_map/ppermute | solution.py:605
  100.2 33.7 %collective-permute-start.21 = (f32[2,2,8,32,128]{4,3,2,1,0:T(8,128)S(1)}, f32[2,2,8,32,128]{4,3,2,1,0:T(8,128)S(1)}, u32[]{:S(2)}, u32[]{:S(2)}) collective-permute-start(f32[2,2,8,32,128]{4,3,2,1,0:T(8,128)S(1)} %get-tuple-element.144), channel_id=1, source_target_pairs={{0,2},{1,3},{2,0},{3,1},{4,6},{5,7},{6,4},{7,5},{8,10},{9,11},{10,... | collective-permute-start | bytes 1572872 | tf_op jit(solution)/shard_map/ppermute | solution.py:605
  103.6 42.4 %collective-permute-start.25 = (f32[2,32,32,128]{3,2,1,0:T(8,128)S(1)}, f32[2,32,32,128]{3,2,1,0:T(8,128)S(1)}, u32[]{:S(2)}, u32[]{:S(2)}) collective-permute-start(f32[2,32,32,128]{3,2,1,0:T(8,128)S(1)} %get-tuple-element.154), channel_id=1, source_target_pairs={{0,8},{1,17},{2,10},{3,19},{4,12},{5,21},{6,14},{7,23},{8,0},{9,25... | collective-permute-start | bytes 3145736 | tf_op jit(solution)/shard_map/ppermute | solution.py:596
  106.6 25.5 %collective-permute-start.22 = (f32[1,4,128,128]{3,2,1,0:T(8,128)S(1)}, f32[1,4,128,128]{3,2,1,0:T(8,128)S(1)}, u32[]{:S(2)}, u32[]{:S(2)}) collective-permute-start(f32[1,4,128,128]{3,2,1,0:T(8,128)S(1)} %get-tuple-element.145.refs_3_), channel_id=1, source_target_pairs={{0,4},{1,5},{2,6},{3,7},{4,0},{5,1},{6,2},{7,3},{8,12},{9,13},{10,... | collective-permute-start | bytes 786440 | tf_op jit(solution)/shard_map/ppermute | solution.py:605
  128.4 15.0 %collective-permute-start.19 = (f32[2,2,8,32,128]{4,3,2,1,0:T(8,128)S(1)}, f32[2,2,8,32,128]{4,3,2,1,0:T(8,128)S(1)}, u32[]{:S(2)}, u32[]{:S(2)}) collective-permute-start(f32[2,2,8,32,128]{4,3,2,1,0:T(8,128)S(1)} %get-tuple-element.140), channel_id=1, source_target_pairs={{0,2},{1,3},{2,0},{3,1},{4,6},{5,7},{6,4},{7,5},{8,10},{9,11},{10,... | collective-permute-start | bytes 1572872 | tf_op jit(solution)/shard_map/ppermute | solution.py:605
  133.9 9.6 %collective-permute-start.26 = (f32[2,2,8,32,128]{4,3,2,1,0:T(8,128)S(1)}, f32[2,2,8,32,128]{4,3,2,1,0:T(8,128)S(1)}, u32[]{:S(2)}, u32[]{:S(2)}) collective-permute-start(f32[2,2,8,32,128]{4,3,2,1,0:T(8,128)S(1)} %get-tuple-element.156), channel_id=1, source_target_pairs={{0,1},{1,0},{2,3},{3,2},{4,5},{5,4},{6,7},{7,6},{8,9},{9,8},{10,11... | collective-permute-start | bytes 1572872 | tf_op jit(solution)/shard_map/ppermute | solution.py:605
  134.0 13.7 %collective-permute-start.24 = (f32[2,1,8,32,128]{4,3,2,1,0:T(8,128)S(1)}, f32[2,1,8,32,128]{4,3,2,1,0:T(8,128)S(1)}, u32[]{:S(2)}, u32[]{:S(2)}) collective-permute-start(f32[2,1,8,32,128]{4,3,2,1,0:T(8,128)S(1)} %get-tuple-element.153), channel_id=1, source_target_pairs={{0,2},{1,3},{2,0},{3,1},{4,6},{5,7},{6,4},{7,5},{8,10},{9,11},{10,... | collective-permute-start | bytes 786440 | tf_op jit(solution)/shard_map/ppermute | solution.py:605
  134.1 14.1 %collective-permute-start.28 = (f32[1,32,32,128]{3,2,1,0:T(8,128)S(1)}, f32[1,32,32,128]{3,2,1,0:T(8,128)S(1)}, u32[]{:S(2)}, u32[]{:S(2)}) collective-permute-start(f32[1,32,32,128]{3,2,1,0:T(8,128)S(1)} %get-tuple-element.163), channel_id=1, source_target_pairs={{0,8},{1,17},{2,10},{3,19},{4,12},{5,21},{6,14},{7,23},{8,0},{9,25... | collective-permute-start | bytes 1572872 | tf_op jit(solution)/shard_map/ppermute | solution.py:596
  143.5 8.2 %collective-permute-start.23 = (f32[2,2,8,32,128]{4,3,2,1,0:T(8,128)S(1)}, f32[2,2,8,32,128]{4,3,2,1,0:T(8,128)S(1)}, u32[]{:S(2)}, u32[]{:S(2)}) collective-permute-start(f32[2,2,8,32,128]{4,3,2,1,0:T(8,128)S(1)} %get-tuple-element.150), channel_id=1, source_target_pairs={{0,1},{1,0},{2,3},{3,2},{4,5},{5,4},{6,7},{7,6},{8,9},{9,8},{10,11... | collective-permute-start | bytes 1572872 | tf_op jit(solution)/shard_map/ppermute | solution.py:605
  (22 other events, 147.9 us)

commit v12 on v11

--- a/solution.py
+++ b/solution.py
@@ -13,14 +13,14 @@
 FAR_SIZES = (2, 2, 1)
 ORDER = (
     ("pack", 0),
+    ("pack", 3),
+    ("pack", 2),
     ("pack", 1),
+    ("local", 1),
+    ("mix", 0),
+    ("local", 0),
+    ("mix", 1),
     ("pack", 4),
-    ("local", 0),
-    ("mix", 0),
-    ("local", 1),
-    ("mix", 1),
-    ("pack", 2),
-    ("pack", 3),
     ("spread", 0),
     ("join", 0),
     ("spread", 1),
@@ -28,8 +28,8 @@
     ("coef", 0),
     ("join", 1),
     ("spread", 2),
+    ("pack", 5),
     ("join", 2),
-    ("pack", 5),
     ("mix", 4),
     ("coef", 1),
     ("filter", 0),

time: 155 us -> 150 us (0.968)
  waiting for transfers between devices: 64.7 us -> 53.1 us
  starting transfers between devices: 29.4 us -> 32.8 us
  local copies, waits for them, and re-layouts: 3.33 us -> 6.35 us
    ppermute x15, waiting for transfers between devices: 47 us -> 40.2 us  [to_sector(): return lax.ppermute(x, 'space', [(i, i ^ k) for i in range(sectors)])]
    ppermute x12, waiting for transfers between devices: 14.4 us -> 9.6 us  [to_partner(): return lax.ppermute(x, ('inst', 'space'), pairs)]
    unnamed x35 -> x43, local copies, waits for them, and re-layouts: 3.33 us -> 6.35 us
    ppermute x15, starting transfers between devices: 10.5 us -> 12.5 us  [to_sector(): return lax.ppermute(x, 'space', [(i, i ^ k) for i in range(sectors)])]
  transfers between devices with their start and end apart: 29 -> 29, of which waited for: 10 -> 10; matrix products, arithmetic and copies ran while one was open for 0% -> 0% of each run, Pallas kernels for 33% -> 35%
where the time goes in v12:
time: 150 us; the launch traced here: 149 us
  Pallas kernels  56.6 us (38%)
  waiting for transfers between devices  53.1 us (35%)
  starting transfers between devices  32.8 us (22%)
  local copies, waits for them, and re-layouts  6.35 us (4%)
    pallas_call x29, Pallas kernels, call(): pl.pallas_call(kernel, grid=grid, in_specs=list(in_specs) + [ANY] * len(e...  43.4 us
    ppermute x15, waiting for transfers between devices, to_sector(): return lax.ppermute(x, 'space', [(i, i ^ k) for i in range(sectors)])  40.2 us
    ppermute x12, starting transfers between devices, to_partner(): return lax.ppermute(x, ('inst', 'space'), pairs)  16.8 us
    pallas_call x6, Pallas kernels, table_call(): pl.pallas_call(kernel, grid_spec=pltpu.PrefetchScalarGridSpec(num_scalar_...  13.2 us
    ppermute x15, starting transfers between devices, to_sector(): return lax.ppermute(x, 'space', [(i, i ^ k) for i in range(sectors)])  12.5 us
    ppermute x12, waiting for transfers between devices, to_partner(): return lax.ppermute(x, ('inst', 'space'), pairs)  9.6 us
    unnamed x43, local copies, waits for them, and re-layouts  6.35 us
    ppermute x2, starting transfers between devices, ring(): lax.ppermute(x, 'space', [(i, (i + step) % sectors) for i in range(sector...  3.54 us
  transfers between devices with their start and end apart: 29, of which 10 were waited for; matrix products, arithmetic and copies ran while one was open for 0% of the time, Pallas kernels for 35%

profile of v12, /device:TPU:0, one launch (start us, length us, event | category | flops | bytes accessed | tf_op | source)
XLA Modules:
  0.0 149.4 jit_solution(10000779055420395335)
XLA Ops:
  0.0 2.3 %pack.6 = (f32[2,32,32,128]{3,2,1,0:T(8,128)}, f32[6,1,64,128]{3,2,1,0:T(8,128)}, f32[6,1,64,128]{3,2,1,0:T(8,128)}, f32[8,128]{1,0:T(8,128)}) custom-call(f32[5,32,64,128]{3,2,1,0:T(8,128)} %bitcast.6, f32[5,32,64,128]{3,2,1,0:T(8,128)} %bitcast.7, f32[32,64,128]{2,1,0:T(8,128)} %refs_11_.3, f32[5,32,64,128]{3,2,1,0:T(8,128)} %bitcast.8, ...), custom_call_target="tpu_custom_call" | custom-call | tf_op jit(solution)/shard_map/pack/pallas_call | solution.py:153
  2.3 3.0 %collective-permute-start = (f32[2,32,32,128]{3,2,1,0:T(8,128)}, f32[2,32,32,128]{3,2,1,0:T(8,128)S(1)}, u32[]{:S(2)}, u32[]{:S(2)}) collective-permute-start(f32[2,32,32,128]{3,2,1,0:T(8,128)} %get-tuple-element.88), channel_id=1, source_target_pairs={{0,16},{1,9},{2,18},{3,11},{4,20},{5,13},{6,22},{7,15},{8,24},{9,1... | collective-permute-start | bytes 3145736 | tf_op jit(solution)/shard_map/ppermute | solution.py:596
  11.6 2.5 %copy-done = f32[1,5,32,64,128]{4,3,2,1,0:T(8,128)S(1)} copy-done((f32[1,5,32,64,128]{4,3,2,1,0:T(8,128)S(1)}, f32[1,5,32,64,128]{4,3,2,1,0:T(8,128)}, u32[]{:S(2)}) %copy-start) | copy-done | bytes 5242904
  14.1 2.5 %copy-done.5 = f32[1,5,32,64,128]{4,3,2,1,0:T(8,128)S(1)} copy-done((f32[1,5,32,64,128]{4,3,2,1,0:T(8,128)S(1)}, f32[1,5,32,64,128]{4,3,2,1,0:T(8,128)}, u32[]{:S(2)}) %copy-start.5) | copy-done | bytes 5242904
  17.3 5.4 %local_part.2 = (f32[5,32,32,128]{3,2,1,0:T(8,128)S(1)}, f32[8,128]{1,0:T(8,128)S(1)}) custom-call(f32[5,5]{1,0:T(8,128)S(1)} %copy-done.10, f32[5]{0:T(128)S(1)} %copy-done.9, s32[5,3]{1,0:T(8,128)S(1)} %copy.24.refs_2_, f32[5,32,64,128]{3,2,1,0:T(8,128)S(1)} %bitcast.16, f32[5,32,64,128]{3,2,1,0:T(8,128)S(1)} %bitcast.17, f32[5,32,64,128]{3,2,1,0:T(8,128)S(1)} %bitcast.18, ...), custom_call_target="tpu_custom_call" | custom-call | tf_op jit(solution)/shard_map/local_part/pallas_call | solution.py:153
  26.2 8.5 %local_part.3 = (f32[5,32,32,128]{3,2,1,0:T(8,128)}, f32[8,128]{1,0:T(8,128)S(1)}) custom-call(f32[5,5]{1,0:T(8,128)S(1)} %copy-done.10, f32[5]{0:T(128)S(1)} %copy-done.9, s32[5,3]{1,0:T(8,128)S(1)} %copy.24.refs_2_, f32[5,32,64,128]{3,2,1,0:T(8,128)} %bitcast.12, f32[5,32,64,128]{3,2,1,0:T(8,128)} %bitcast.13, f32[5,32,64,128]{3,2,1,0:T(8,128)} %bitcast.14, ...), custom_call_target="tpu_custom_call" | custom-call | tf_op jit(solution)/shard_map/local_part/pallas_call | solution.py:153
  36.3 3.5 %collective-permute-start.2 = (f32[6,1,64,128]{3,2,1,0:T(8,128)S(1)}, f32[6,1,64,128]{3,2,1,0:T(8,128)S(1)}, u32[]{:S(2)}, u32[]{:S(2)}) collective-permute-start(f32[6,1,64,128]{3,2,1,0:T(8,128)S(1)} %copy-done.17), channel_id=1, source_target_pairs={{0,7},{1,0},{2,1},{3,2},{4,3},{5,4},{6,5},{7,6},{8,15},{9,8},{10,9... | collective-permute-start | bytes 589832 | tf_op jit(solution)/shard_map/ppermute | solution.py:608
  40.1 3.3 %collective-permute-done.1.refs_5_.refs_7_ = f32[6,1,64,128]{3,2,1,0:T(8,128)S(1)} collective-permute-done((f32[6,1,64,128]{3,2,1,0:T(8,128)S(1)}, f32[6,1,64,128]{3,2,1,0:T(8,128)S(1)}, u32[]{:S(2)}, u32[]{:S(2)}) %collective-permute-start.1) | collective-permute-done | bytes 196640 | tf_op jit(solution)/shard_map/ppermute | solution.py:608
  45.0 2.1 %collective-permute-start.6 = (f32[2,2,8,32,128]{4,3,2,1,0:T(8,128)S(1)}, f32[2,2,8,32,128]{4,3,2,1,0:T(8,128)S(1)}, u32[]{:S(2)}, u32[]{:S(2)}) collective-permute-start(f32[2,2,8,32,128]{4,3,2,1,0:T(8,128)S(1)} %get-tuple-element.105), channel_id=1, source_target_pairs={{0,1},{1,0},{2,3},{3,2},{4,5},{5,4},{6,7},{7,6},{8,9},{9,8},{10,11... | collective-permute-start | bytes 1572872 | tf_op jit(solution)/shard_map/ppermute | solution.py:605
  49.9 2.6 %collective-permute-done.4.refs_13_ = f32[2,32,32,128]{3,2,1,0:T(8,128)S(1)} collective-permute-done((f32[2,32,32,128]{3,2,1,0:T(8,128)S(1)}, f32[2,32,32,128]{3,2,1,0:T(8,128)S(1)}, u32[]{:S(2)}, u32[]{:S(2)}) %collective-permute-start.4) | collective-permute-done | bytes 1048608 | tf_op jit(solution)/shard_map/ppermute | solution.py:596
  55.2 2.4 %collective-permute-done.9.refs_3_.refs_12_ = f32[1,32,32,128]{3,2,1,0:T(8,128)S(1)} collective-permute-done((f32[1,32,32,128]{3,2,1,0:T(8,128)S(1)}, f32[1,32,32,128]{3,2,1,0:T(8,128)S(1)}, u32[]{:S(2)}, u32[]{:S(2)}) %collective-permute-start.9) | collective-permute-done | bytes 524320 | tf_op jit(solution)/shard_map/ppermute | solution.py:596
  63.0 2.4 %coefficients.3 = (f32[2,4,128,128]{3,2,1,0:T(8,128)S(1)}, f32[8,128]{1,0:T(8,128)S(1)}) custom-call(s32[22]{0:T(128)S(1)} %pad_add_fusion.refs_0_, f32[71]{0:T(128)S(1)} %copy-done.8, f32[2,16,128,128]{3,2,1,0:T(8,128)S(1)} %copy-done.7, f32[2,8,32,128]{3,2,1,0:T(8,128)S(1)} %get-tuple-element.111.refs_3_.refs_5_, ...), custom_call_target="tpu_custom_call" | custom-call | tf_op jit(solution)/shard_map/coefficients/pallas_call | solution.py:432
  66.1 2.5 %collective-permute-start.18 = (f32[2,4,128,128]{3,2,1,0:T(8,128)S(1)}, f32[2,4,128,128]{3,2,1,0:T(8,128)S(1)}, u32[]{:S(2)}, u32[]{:S(2)}) collective-permute-start(f32[2,4,128,128]{3,2,1,0:T(8,128)S(1)} %get-tuple-element.132.refs_3_), channel_id=1, source_target_pairs={{0,4},{1,5},{2,6},{3,7},{4,0},{5,1},{6,2},{7,3},{8,12},{9,13},{10,... | collective-permute-start | bytes 1572872 | tf_op jit(solution)/shard_map/ppermute | solution.py:605
  68.7 4.5 %collective-permute-done.12.refs_13_ = f32[1,32,32,128]{3,2,1,0:T(8,128)S(1)} collective-permute-done((f32[1,32,32,128]{3,2,1,0:T(8,128)S(1)}, f32[1,32,32,128]{3,2,1,0:T(8,128)S(1)}, u32[]{:S(2)}, u32[]{:S(2)}) %collective-permute-start.12) | collective-permute-done | bytes 524320 | tf_op jit(solution)/shard_map/ppermute | solution.py:596
  80.5 10.9 %collective-permute-done.10.refs_5_.refs_7_ = f32[2,2,8,32,128]{4,3,2,1,0:T(8,128)S(1)} collective-permute-done((f32[2,2,8,32,128]{4,3,2,1,0:T(8,128)S(1)}, f32[2,2,8,32,128]{4,3,2,1,0:T(8,128)S(1)}, u32[]{:S(2)}, u32[]{:S(2)}) %collective-permute-start.10) | collective-permute-done | bytes 524320 | tf_op jit(solution)/shard_map/ppermute | solution.py:605
  92.3 2.4 %coefficients.4 = (f32[2,4,128,128]{3,2,1,0:T(8,128)S(1)}, f32[8,128]{1,0:T(8,128)S(1)}) custom-call(s32[22]{0:T(128)S(1)} %pad_add_fusion.refs_0_, f32[71]{0:T(128)S(1)} %copy-done.8, f32[2,16,128,128]{3,2,1,0:T(8,128)S(1)} %copy-done.7, f32[2,8,32,128]{3,2,1,0:T(8,128)S(1)} %get-tuple-element.108.refs_3_.refs_5_, ...), custom_call_target="tpu_custom_call" | custom-call | tf_op jit(solution)/shard_map/coefficients/pallas_call | solution.py:432
  95.0 2.5 %filtered.3 = (f32[2,8,32,128]{3,2,1,0:T(8,128)S(1)}, f32[2,2,8,32,128]{4,3,2,1,0:T(8,128)S(1)}, f32[2,2,8,32,128]{4,3,2,1,0:T(8,128)S(1)}, f32[8,128]{1,0:T(8,128)S(1)}) custom-call(s32[22]{0:T(128)S(1)} %pad_add_fusion.refs_0_, f32[71]{0:T(128)S(1)} %copy-done.8, f32[2,16,128,128]{3,2,1,0:T(8,128)S(1)} %copy-done.6, ...), custom_call_target="tpu_custom_call" | custom-call | tf_op jit(solution)/shard_map/filtered/pallas_call | solution.py:432
  97.5 2.5 %collective-permute-start.21 = (f32[2,2,8,32,128]{4,3,2,1,0:T(8,128)S(1)}, f32[2,2,8,32,128]{4,3,2,1,0:T(8,128)S(1)}, u32[]{:S(2)}, u32[]{:S(2)}) collective-permute-start(f32[2,2,8,32,128]{4,3,2,1,0:T(8,128)S(1)} %get-tuple-element.144), channel_id=1, source_target_pairs={{0,2},{1,3},{2,0},{3,1},{4,6},{5,7},{6,4},{7,5},{8,10},{9,11},{10,... | collective-permute-start | bytes 1572872 | tf_op jit(solution)/shard_map/ppermute | solution.py:605
  105.1 18.5 %collective-permute-done.14.refs_4_ = f32[2,4,128,128]{3,2,1,0:T(8,128)S(1)} collective-permute-done((f32[2,4,128,128]{3,2,1,0:T(8,128)S(1)}, f32[2,4,128,128]{3,2,1,0:T(8,128)S(1)}, u32[]{:S(2)}, u32[]{:S(2)}) %collective-permute-start.14) | collective-permute-done | bytes 524320 | tf_op jit(solution)/shard_map/ppermute | solution.py:605
  123.6 2.5 %filtered.4 = (f32[2,8,32,128]{3,2,1,0:T(8,128)S(1)}, f32[2,2,8,32,128]{4,3,2,1,0:T(8,128)S(1)}, f32[2,2,8,32,128]{4,3,2,1,0:T(8,128)S(1)}, f32[8,128]{1,0:T(8,128)S(1)}) custom-call(s32[22]{0:T(128)S(1)} %pad_add_fusion.refs_0_, f32[71]{0:T(128)S(1)} %copy-done.8, f32[2,16,128,128]{3,2,1,0:T(8,128)S(1)} %copy-done.6, ...), custom_call_target="tpu_custom_call" | custom-call | tf_op jit(solution)/shard_map/filtered/pallas_call | solution.py:432
  126.1 3.0 %collective-permute-done.22.refs_4_ = f32[1,4,128,128]{3,2,1,0:T(8,128)S(1)} collective-permute-done((f32[1,4,128,128]{3,2,1,0:T(8,128)S(1)}, f32[1,4,128,128]{3,2,1,0:T(8,128)S(1)}, u32[]{:S(2)}, u32[]{:S(2)}) %collective-permute-start.22) | collective-permute-done | bytes 262176 | tf_op jit(solution)/shard_map/ppermute | solution.py:605
  133.5 5.3 %collective-permute-done.19.refs_1_.refs_4_ = f32[2,2,8,32,128]{4,3,2,1,0:T(8,128)S(1)} collective-permute-done((f32[2,2,8,32,128]{4,3,2,1,0:T(8,128)S(1)}, f32[2,2,8,32,128]{4,3,2,1,0:T(8,128)S(1)}, u32[]{:S(2)}, u32[]{:S(2)}) %collective-permute-start.19) | collective-permute-done | bytes 524320 | tf_op jit(solution)/shard_map/ppermute | solution.py:605
  138.9 2.5 %place_near.3 = (f32[5,32,64,128]{3,2,1,0:T(8,128)}, f32[8,128]{1,0:T(8,128)S(1)}) custom-call(s32[22]{0:T(128)S(1)} %pad_add_fusion.refs_0_, f32[71]{0:T(128)S(1)} %copy-done.8, f32[2,8,32,128]{3,2,1,0:T(8,128)S(1)} %get-tuple-element.155.refs_2_, f32[2,2,8,32,128]{4,3,2,1,0:T(8,128)S(1)} %collective-permute-done.26.refs_3_, ...), custom_call_target="tpu_custom_call", output_to_operand_aliasing={{0}: (5, {})} | custom-call | tf_op jit(solution)/shard_map/place_near/pallas_call | solution.py:153
  147.0 2.5 %place_near.5 = (f32[5,32,64,128]{3,2,1,0:T(8,128)}, f32[8,128]{1,0:T(8,128)}) custom-call(s32[22]{0:T(128)S(1)} %pad_add_fusion.refs_0_, f32[71]{0:T(128)S(1)} %copy-done.8, f32[2,8,32,128]{3,2,1,0:T(8,128)S(1)} %get-tuple-element.138.refs_2_, f32[2,2,8,32,128]{4,3,2,1,0:T(8,128)S(1)} %collective-permute-done.23.refs_3_, ...), custom_call_target="tpu_custom_call", output_to_operand_aliasing={{0}: (5, {})} | custom-call | tf_op jit(solution)/shard_map/place_near/pallas_call | solution.py:153
  (114 shorter events, 48.7 us)
Async XLA Ops:
  2.3 20.5 %collective-permute-start = (f32[2,32,32,128]{3,2,1,0:T(8,128)}, f32[2,32,32,128]{3,2,1,0:T(8,128)S(1)}, u32[]{:S(2)}, u32[]{:S(2)}) collective-permute-start(f32[2,32,32,128]{3,2,1,0:T(8,128)} %get-tuple-element.88), channel_id=1, source_target_pairs={{0,16},{1,9},{2,18},{3,11},{4,20},{5,13},{6,22},{7,15},{8,24},{9,1... | collective-permute-start | bytes 3145736 | tf_op jit(solution)/shard_map/ppermute | solution.py:596
  11.5 23.2 %collective-permute-start.3 = (f32[2,32,32,128]{3,2,1,0:T(8,128)}, f32[2,32,32,128]{3,2,1,0:T(8,128)S(1)}, u32[]{:S(2)}, u32[]{:S(2)}) collective-permute-start(f32[2,32,32,128]{3,2,1,0:T(8,128)} %get-tuple-element.98), channel_id=1, source_target_pairs={{0,16},{1,9},{2,18},{3,11},{4,20},{5,13},{6,22},{7,15},{8,24},{9,1... | collective-permute-start | bytes 3145736 | tf_op jit(solution)/shard_map/ppermute | solution.py:596
  24.2 19.2 %collective-permute-start.5 = (f32[2,32,32,128]{3,2,1,0:T(8,128)S(1)}, f32[2,32,32,128]{3,2,1,0:T(8,128)S(1)}, u32[]{:S(2)}, u32[]{:S(2)}) collective-permute-start(f32[2,32,32,128]{3,2,1,0:T(8,128)S(1)} %get-tuple-element.101), channel_id=1, source_target_pairs={{0,8},{1,17},{2,10},{3,19},{4,12},{5,21},{6,14},{7,23},{8,0},{9,25... | collective-permute-start | bytes 3145736 | tf_op jit(solution)/shard_map/ppermute | solution.py:596
  35.5 16.9 %collective-permute-start.4 = (f32[2,32,32,128]{3,2,1,0:T(8,128)S(1)}, f32[2,32,32,128]{3,2,1,0:T(8,128)S(1)}, u32[]{:S(2)}, u32[]{:S(2)}) collective-permute-start(f32[2,32,32,128]{3,2,1,0:T(8,128)S(1)} %get-tuple-element.100), channel_id=1, source_target_pairs={{0,8},{1,17},{2,10},{3,19},{4,12},{5,21},{6,14},{7,23},{8,0},{9,25... | collective-permute-start | bytes 3145736 | tf_op jit(solution)/shard_map/ppermute | solution.py:596
  47.2 10.5 %collective-permute-start.9 = (f32[1,32,32,128]{3,2,1,0:T(8,128)S(1)}, f32[1,32,32,128]{3,2,1,0:T(8,128)S(1)}, u32[]{:S(2)}, u32[]{:S(2)}) collective-permute-start(f32[1,32,32,128]{3,2,1,0:T(8,128)S(1)} %copy-done.16), channel_id=1, source_target_pairs={{0,16},{1,9},{2,18},{3,11},{4,20},{5,13},{6,22},{7,15},{8,24},{9,1... | collective-permute-start | bytes 1572872 | tf_op jit(solution)/shard_map/ppermute | solution.py:596
  48.6 29.3 %collective-permute-start.11 = (f32[2,32,32,128]{3,2,1,0:T(8,128)S(1)}, f32[2,32,32,128]{3,2,1,0:T(8,128)S(1)}, u32[]{:S(2)}, u32[]{:S(2)}) collective-permute-start(f32[2,32,32,128]{3,2,1,0:T(8,128)S(1)} %get-tuple-element.118), channel_id=1, source_target_pairs={{0,16},{1,9},{2,18},{3,11},{4,20},{5,13},{6,22},{7,15},{8,24},{9,1... | collective-permute-start | bytes 3145736 | tf_op jit(solution)/shard_map/ppermute | solution.py:596
  49.2 13.8 %collective-permute-start.8 = (f32[2,2,8,32,128]{4,3,2,1,0:T(8,128)S(1)}, f32[2,2,8,32,128]{4,3,2,1,0:T(8,128)S(1)}, u32[]{:S(2)}, u32[]{:S(2)}) collective-permute-start(f32[2,2,8,32,128]{4,3,2,1,0:T(8,128)S(1)} %get-tuple-element.112), channel_id=1, source_target_pairs={{0,2},{1,3},{2,0},{3,1},{4,6},{5,7},{6,4},{7,5},{8,10},{9,11},{10,... | collective-permute-start | bytes 1572872 | tf_op jit(solution)/shard_map/ppermute | solution.py:605
  54.1 11.3 %collective-permute-start.7 = (f32[2,2,8,32,128]{4,3,2,1,0:T(8,128)S(1)}, f32[2,2,8,32,128]{4,3,2,1,0:T(8,128)S(1)}, u32[]{:S(2)}, u32[]{:S(2)}) collective-permute-start(f32[2,2,8,32,128]{4,3,2,1,0:T(8,128)S(1)} %get-tuple-element.109), channel_id=1, source_target_pairs={{0,1},{1,0},{2,3},{3,2},{4,5},{5,4},{6,7},{7,6},{8,9},{9,8},{10,11... | collective-permute-start | bytes 1572872 | tf_op jit(solution)/shard_map/ppermute | solution.py:605
  58.3 14.9 %collective-permute-start.12 = (f32[1,32,32,128]{3,2,1,0:T(8,128)S(1)}, f32[1,32,32,128]{3,2,1,0:T(8,128)S(1)}, u32[]{:S(2)}, u32[]{:S(2)}) collective-permute-start(f32[1,32,32,128]{3,2,1,0:T(8,128)S(1)} %get-tuple-element.119), channel_id=1, source_target_pairs={{0,8},{1,17},{2,10},{3,19},{4,12},{5,21},{6,14},{7,23},{8,0},{9,25... | collective-permute-start | bytes 1572872 | tf_op jit(solution)/shard_map/ppermute | solution.py:596
  60.4 37.1 %collective-permute-start.17 = (f32[2,32,32,128]{3,2,1,0:T(8,128)S(1)}, f32[2,32,32,128]{3,2,1,0:T(8,128)S(1)}, u32[]{:S(2)}, u32[]{:S(2)}) collective-permute-start(f32[2,32,32,128]{3,2,1,0:T(8,128)S(1)} %copy-done.15), channel_id=1, source_target_pairs={{0,16},{1,9},{2,18},{3,11},{4,20},{5,13},{6,22},{7,15},{8,24},{9,1... | collective-permute-start | bytes 3145736 | tf_op jit(solution)/shard_map/ppermute | solution.py:596
  65.5 25.8 %collective-permute-start.10 = (f32[2,2,8,32,128]{4,3,2,1,0:T(8,128)S(1)}, f32[2,2,8,32,128]{4,3,2,1,0:T(8,128)S(1)}, u32[]{:S(2)}, u32[]{:S(2)}) collective-permute-start(f32[2,2,8,32,128]{4,3,2,1,0:T(8,128)S(1)} %get-tuple-element.117), channel_id=1, source_target_pairs={{0,2},{1,3},{2,0},{3,1},{4,6},{5,7},{6,4},{7,5},{8,10},{9,11},{10,... | collective-permute-start | bytes 1572872 | tf_op jit(solution)/shard_map/ppermute | solution.py:605
  66.1 28.6 %collective-permute-start.18 = (f32[2,4,128,128]{3,2,1,0:T(8,128)S(1)}, f32[2,4,128,128]{3,2,1,0:T(8,128)S(1)}, u32[]{:S(2)}, u32[]{:S(2)}) collective-permute-start(f32[2,4,128,128]{3,2,1,0:T(8,128)S(1)} %get-tuple-element.132.refs_3_), channel_id=1, source_target_pairs={{0,4},{1,5},{2,6},{3,7},{4,0},{5,1},{6,2},{7,3},{8,12},{9,13},{10,... | collective-permute-start | bytes 1572872 | tf_op jit(solution)/shard_map/ppermute | solution.py:605
  75.9 28.5 %collective-permute-start.15 = (f32[1,32,32,128]{3,2,1,0:T(8,128)S(1)}, f32[1,32,32,128]{3,2,1,0:T(8,128)S(1)}, u32[]{:S(2)}, u32[]{:S(2)}) collective-permute-start(f32[1,32,32,128]{3,2,1,0:T(8,128)S(1)} %get-tuple-element.128), channel_id=1, source_target_pairs={{0,16},{1,9},{2,18},{3,11},{4,20},{5,13},{6,22},{7,15},{8,24},{9,1... | collective-permute-start | bytes 1572872 | tf_op jit(solution)/shard_map/ppermute | solution.py:596
  77.9 23.0 %collective-permute-start.16 = (f32[2,1,8,32,128]{4,3,2,1,0:T(8,128)S(1)}, f32[2,1,8,32,128]{4,3,2,1,0:T(8,128)S(1)}, u32[]{:S(2)}, u32[]{:S(2)}) collective-permute-start(f32[2,1,8,32,128]{4,3,2,1,0:T(8,128)S(1)} %get-tuple-element.130), channel_id=1, source_target_pairs={{0,2},{1,3},{2,0},{3,1},{4,6},{5,7},{6,4},{7,5},{8,10},{9,11},{10,... | collective-permute-start | bytes 786440 | tf_op jit(solution)/shard_map/ppermute | solution.py:605
  91.4 39.7 %collective-permute-start.20 = (f32[2,32,32,128]{3,2,1,0:T(8,128)S(1)}, f32[2,32,32,128]{3,2,1,0:T(8,128)S(1)}, u32[]{:S(2)}, u32[]{:S(2)}) collective-permute-start(f32[2,32,32,128]{3,2,1,0:T(8,128)S(1)} %get-tuple-element.142), channel_id=1, source_target_pairs={{0,8},{1,17},{2,10},{3,19},{4,12},{5,21},{6,14},{7,23},{8,0},{9,25... | collective-permute-start | bytes 3145736 | tf_op jit(solution)/shard_map/ppermute | solution.py:596
  94.8 28.8 %collective-permute-start.14 = (f32[2,4,128,128]{3,2,1,0:T(8,128)S(1)}, f32[2,4,128,128]{3,2,1,0:T(8,128)S(1)}, u32[]{:S(2)}, u32[]{:S(2)}) collective-permute-start(f32[2,4,128,128]{3,2,1,0:T(8,128)S(1)} %get-tuple-element.127.refs_3_), channel_id=1, source_target_pairs={{0,4},{1,5},{2,6},{3,7},{4,0},{5,1},{6,2},{7,3},{8,12},{9,13},{10,... | collective-permute-start | bytes 1572872 | tf_op jit(solution)/shard_map/ppermute | solution.py:605
  97.5 33.3 %collective-permute-start.21 = (f32[2,2,8,32,128]{4,3,2,1,0:T(8,128)S(1)}, f32[2,2,8,32,128]{4,3,2,1,0:T(8,128)S(1)}, u32[]{:S(2)}, u32[]{:S(2)}) collective-permute-start(f32[2,2,8,32,128]{4,3,2,1,0:T(8,128)S(1)} %get-tuple-element.144), channel_id=1, source_target_pairs={{0,2},{1,3},{2,0},{3,1},{4,6},{5,7},{6,4},{7,5},{8,10},{9,11},{10,... | collective-permute-start | bytes 1572872 | tf_op jit(solution)/shard_map/ppermute | solution.py:605
  101.0 40.4 %collective-permute-start.25 = (f32[2,32,32,128]{3,2,1,0:T(8,128)S(1)}, f32[2,32,32,128]{3,2,1,0:T(8,128)S(1)}, u32[]{:S(2)}, u32[]{:S(2)}) collective-permute-start(f32[2,32,32,128]{3,2,1,0:T(8,128)S(1)} %get-tuple-element.154), channel_id=1, source_target_pairs={{0,8},{1,17},{2,10},{3,19},{4,12},{5,21},{6,14},{7,23},{8,0},{9,25... | collective-permute-start | bytes 3145736 | tf_op jit(solution)/shard_map/ppermute | solution.py:596
  104.4 24.7 %collective-permute-start.22 = (f32[1,4,128,128]{3,2,1,0:T(8,128)S(1)}, f32[1,4,128,128]{3,2,1,0:T(8,128)S(1)}, u32[]{:S(2)}, u32[]{:S(2)}) collective-permute-start(f32[1,4,128,128]{3,2,1,0:T(8,128)S(1)} %get-tuple-element.145.refs_3_), channel_id=1, source_target_pairs={{0,4},{1,5},{2,6},{3,7},{4,0},{5,1},{6,2},{7,3},{8,12},{9,13},{10,... | collective-permute-start | bytes 786440 | tf_op jit(solution)/shard_map/ppermute | solution.py:605
  126.1 12.7 %collective-permute-start.19 = (f32[2,2,8,32,128]{4,3,2,1,0:T(8,128)S(1)}, f32[2,2,8,32,128]{4,3,2,1,0:T(8,128)S(1)}, u32[]{:S(2)}, u32[]{:S(2)}) collective-permute-start(f32[2,2,8,32,128]{4,3,2,1,0:T(8,128)S(1)} %get-tuple-element.140), channel_id=1, source_target_pairs={{0,2},{1,3},{2,0},{3,1},{4,6},{5,7},{6,4},{7,5},{8,10},{9,11},{10,... | collective-permute-start | bytes 1572872 | tf_op jit(solution)/shard_map/ppermute | solution.py:605
  130.9 8.0 %collective-permute-start.26 = (f32[2,2,8,32,128]{4,3,2,1,0:T(8,128)S(1)}, f32[2,2,8,32,128]{4,3,2,1,0:T(8,128)S(1)}, u32[]{:S(2)}, u32[]{:S(2)}) collective-permute-start(f32[2,2,8,32,128]{4,3,2,1,0:T(8,128)S(1)} %get-tuple-element.156), channel_id=1, source_target_pairs={{0,1},{1,0},{2,3},{3,2},{4,5},{5,4},{6,7},{7,6},{8,9},{9,8},{10,11... | collective-permute-start | bytes 1572872 | tf_op jit(solution)/shard_map/ppermute | solution.py:605
  131.0 12.1 %collective-permute-start.24 = (f32[2,1,8,32,128]{4,3,2,1,0:T(8,128)S(1)}, f32[2,1,8,32,128]{4,3,2,1,0:T(8,128)S(1)}, u32[]{:S(2)}, u32[]{:S(2)}) collective-permute-start(f32[2,1,8,32,128]{4,3,2,1,0:T(8,128)S(1)} %get-tuple-element.153), channel_id=1, source_target_pairs={{0,2},{1,3},{2,0},{3,1},{4,6},{5,7},{6,4},{7,5},{8,10},{9,11},{10,... | collective-permute-start | bytes 786440 | tf_op jit(solution)/shard_map/ppermute | solution.py:605
  131.1 12.5 %collective-permute-start.28 = (f32[1,32,32,128]{3,2,1,0:T(8,128)S(1)}, f32[1,32,32,128]{3,2,1,0:T(8,128)S(1)}, u32[]{:S(2)}, u32[]{:S(2)}) collective-permute-start(f32[1,32,32,128]{3,2,1,0:T(8,128)S(1)} %get-tuple-element.163), channel_id=1, source_target_pairs={{0,8},{1,17},{2,10},{3,19},{4,12},{5,21},{6,14},{7,23},{8,0},{9,25... | collective-permute-start | bytes 1572872 | tf_op jit(solution)/shard_map/ppermute | solution.py:596
  138.8 8.2 %collective-permute-start.23 = (f32[2,2,8,32,128]{4,3,2,1,0:T(8,128)S(1)}, f32[2,2,8,32,128]{4,3,2,1,0:T(8,128)S(1)}, u32[]{:S(2)}, u32[]{:S(2)}) collective-permute-start(f32[2,2,8,32,128]{4,3,2,1,0:T(8,128)S(1)} %get-tuple-element.150), channel_id=1, source_target_pairs={{0,1},{1,0},{2,3},{3,2},{4,5},{5,4},{6,7},{7,6},{8,9},{9,8},{10,11... | collective-permute-start | bytes 1572872 | tf_op jit(solution)/shard_map/ppermute | solution.py:605
  (26 other events, 160.8 us)

commit v13 on v12

--- a/solution.py
+++ b/solution.py
@@ -50,7 +50,7 @@
 )
 EDGES = tuple(zip(ORDER[:-1], ORDER[1:]))
 PACK = 60
-LOCAL = 52
+LOCAL = 24
 SMEM = pl.BlockSpec(memory_space=pltpu.SMEM)
 ANY = pl.BlockSpec(memory_space=pl.ANY)
 COST = pl.CostEstimate(flops=0, bytes_accessed=0, transcendentals=0)
@@ -630,8 +630,7 @@
         lo, hi, index = groups[g]
         token = [made[before] for before, after in EDGES if after == (step, g)]
         if step == "pack":
-            early = 0 not in local
-            *packed, stamp = pack(center, viscosity, lo, hi, index, near, halos is None, token, early)
+            *packed, stamp = pack(center, viscosity, lo, hi, index, near, halos is None, token, halos is None)
             first[g] = to_first(packed[0])
             if halos is None:
                 halos = ring(packed[1], 1), ring(packed[2], -1)

time: 150 us -> 152 us (1.013)
  Pallas kernels: 56.6 us -> 48.7 us
  local copies, waits for them, and re-layouts: 6.35 us -> 12.3 us
  waiting for transfers between devices: 53.1 us -> 58.4 us
    pallas_call x29, Pallas kernels: 43.4 us -> 35.4 us  [call(): pl.pallas_call(kernel, grid=grid, in_specs=list(in_specs) + [ANY] * len(e...]
    unnamed x43 -> x45, local copies, waits for them, and re-layouts: 6.35 us -> 12.3 us
    ppermute x15, waiting for transfers between devices: 40.2 us -> 44.8 us  [to_sector(): return lax.ppermute(x, 'space', [(i, i ^ k) for i in range(sectors)])]
  transfers between devices with their start and end apart: 29 -> 29, of which waited for: 10 -> 11; matrix products, arithmetic and copies ran while one was open for 0% -> 0% of each run, Pallas kernels for 35% -> 29%
where the time goes in v13:
time: 152 us
  waiting for transfers between devices  58.4 us (38%)
  Pallas kernels  48.7 us (32%)
  starting transfers between devices  31.8 us (21%)
  local copies, waits for them, and re-layouts  12.3 us (8%)
    ppermute x15, waiting for transfers between devices, to_sector(): return lax.ppermute(x, 'space', [(i, i ^ k) for i in range(sectors)])  44.8 us
    pallas_call x29, Pallas kernels, call(): pl.pallas_call(kernel, grid=grid, in_specs=list(in_specs) + [ANY] * len(e...  35.4 us
    ppermute x12, starting transfers between devices, to_partner(): return lax.ppermute(x, ('inst', 'space'), pairs)  17 us
    pallas_call x6, Pallas kernels, table_call(): pl.pallas_call(kernel, grid_spec=pltpu.PrefetchScalarGridSpec(num_scalar_...  13.3 us
    unnamed x45, local copies, waits for them, and re-layouts  12.3 us
    ppermute x15, starting transfers between devices, to_sector(): return lax.ppermute(x, 'space', [(i, i ^ k) for i in range(sectors)])  11.3 us
    ppermute x12, waiting for transfers between devices, to_partner(): return lax.ppermute(x, ('inst', 'space'), pairs)  10.4 us
    ppermute x2, starting transfers between devices, ring(): lax.ppermute(x, 'space', [(i, (i + step) % sectors) for i in range(sector...  3.54 us
  transfers between devices with their start and end apart: 29, of which 11 were waited for; matrix products, arithmetic and copies ran while one was open for 0% of the time, Pallas kernels for 29%

profile of v13, /device:TPU:0, one launch (start us, length us, event | category | flops | bytes accessed | tf_op | source)
XLA Modules:
  0.0 151.8 jit_solution(10626134693865230973)
XLA Ops:
  0.0 2.3 %pack.6 = (f32[2,32,32,128]{3,2,1,0:T(8,128)}, f32[6,1,64,128]{3,2,1,0:T(8,128)}, f32[6,1,64,128]{3,2,1,0:T(8,128)}, f32[8,128]{1,0:T(8,128)}) custom-call(f32[5,32,64,128]{3,2,1,0:T(8,128)} %bitcast.6, f32[5,32,64,128]{3,2,1,0:T(8,128)} %bitcast.7, f32[32,64,128]{2,1,0:T(8,128)} %refs_11_.3, f32[5,32,64,128]{3,2,1,0:T(8,128)} %bitcast.8, ...), custom_call_target="tpu_custom_call" | custom-call | tf_op jit(solution)/shard_map/pack/pallas_call | solution.py:153
  2.3 3.0 %collective-permute-start = (f32[2,32,32,128]{3,2,1,0:T(8,128)}, f32[2,32,32,128]{3,2,1,0:T(8,128)S(1)}, u32[]{:S(2)}, u32[]{:S(2)}) collective-permute-start(f32[2,32,32,128]{3,2,1,0:T(8,128)} %get-tuple-element.88), channel_id=1, source_target_pairs={{0,16},{1,9},{2,18},{3,11},{4,20},{5,13},{6,22},{7,15},{8,24},{9,1... | collective-permute-start | bytes 3145736 | tf_op jit(solution)/shard_map/ppermute | solution.py:596
  5.4 2.5 %copy-done = f32[1,5,32,64,128]{4,3,2,1,0:T(8,128)S(1)} copy-done((f32[1,5,32,64,128]{4,3,2,1,0:T(8,128)S(1)}, f32[1,5,32,64,128]{4,3,2,1,0:T(8,128)}, u32[]{:S(2)}) %copy-start) | copy-done | bytes 5242904
  11.5 2.5 %copy-done.1 = f32[1,5,32,64,128]{4,3,2,1,0:T(8,128)S(1)} copy-done((f32[1,5,32,64,128]{4,3,2,1,0:T(8,128)S(1)}, f32[1,5,32,64,128]{4,3,2,1,0:T(8,128)}, u32[]{:S(2)}) %copy-start.1) | copy-done | bytes 5242904
  14.0 2.5 %copy-done.3 = f32[1,5,32,64,128]{4,3,2,1,0:T(8,128)S(1)} copy-done((f32[1,5,32,64,128]{4,3,2,1,0:T(8,128)S(1)}, f32[1,5,32,64,128]{4,3,2,1,0:T(8,128)}, u32[]{:S(2)}) %copy-start.3) | copy-done | bytes 5242904
  16.5 5.4 %local_part.2 = (f32[5,32,32,128]{3,2,1,0:T(8,128)S(1)}, f32[8,128]{1,0:T(8,128)S(1)}) custom-call(f32[5,5]{1,0:T(8,128)S(1)} %copy-done.9, f32[5]{0:T(128)S(1)} %copy-done.8, s32[5,3]{1,0:T(8,128)S(1)} %copy.24.refs_2_, f32[5,32,64,128]{3,2,1,0:T(8,128)S(1)} %bitcast.12, f32[5,32,64,128]{3,2,1,0:T(8,128)S(1)} %bitcast.13, f32[5,32,64,128]{3,2,1,0:T(8,128)S(1)} %bitcast.14, ...), custom_call_target="tpu_custom_call" | custom-call | tf_op jit(solution)/shard_map/local_part/pallas_call | solution.py:153
  24.4 2.5 %copy-done.4 = f32[1,5,32,64,128]{4,3,2,1,0:T(8,128)S(1)} copy-done((f32[1,5,32,64,128]{4,3,2,1,0:T(8,128)S(1)}, f32[1,5,32,64,128]{4,3,2,1,0:T(8,128)}, u32[]{:S(2)}) %copy-start.4) | copy-done | bytes 5242904
  26.9 5.4 %local_part.3 = (f32[5,32,32,128]{3,2,1,0:T(8,128)S(1)}, f32[8,128]{1,0:T(8,128)S(1)}) custom-call(f32[5,5]{1,0:T(8,128)S(1)} %copy-done.9, f32[5]{0:T(128)S(1)} %copy-done.8, s32[5,3]{1,0:T(8,128)S(1)} %copy.24.refs_2_, f32[5,32,64,128]{3,2,1,0:T(8,128)S(1)} %bitcast.17, f32[5,32,64,128]{3,2,1,0:T(8,128)S(1)} %bitcast.18, f32[5,32,64,128]{3,2,1,0:T(8,128)S(1)} %bitcast.19, ...), custom_call_target="tpu_custom_call" | custom-call | tf_op jit(solution)/shard_map/local_part/pallas_call | solution.py:153
  35.0 2.7 %collective-permute-start.4 = (f32[2,32,32,128]{3,2,1,0:T(8,128)S(1)}, f32[2,32,32,128]{3,2,1,0:T(8,128)S(1)}, u32[]{:S(2)}, u32[]{:S(2)}) collective-permute-start(f32[2,32,32,128]{3,2,1,0:T(8,128)S(1)} %get-tuple-element.100), channel_id=1, source_target_pairs={{0,8},{1,17},{2,10},{3,19},{4,12},{5,21},{6,14},{7,23},{8,0},{9,25... | collective-permute-start | bytes 3145736 | tf_op jit(solution)/shard_map/ppermute | solution.py:596
  37.7 3.5 %collective-permute-start.2 = (f32[6,1,64,128]{3,2,1,0:T(8,128)S(1)}, f32[6,1,64,128]{3,2,1,0:T(8,128)S(1)}, u32[]{:S(2)}, u32[]{:S(2)}) collective-permute-start(f32[6,1,64,128]{3,2,1,0:T(8,128)S(1)} %copy-done.18), channel_id=1, source_target_pairs={{0,7},{1,0},{2,1},{3,2},{4,3},{5,4},{6,5},{7,6},{8,15},{9,8},{10,9... | collective-permute-start | bytes 589832 | tf_op jit(solution)/shard_map/ppermute | solution.py:608
  41.5 3.3 %collective-permute-done.1.refs_5_.refs_7_ = f32[6,1,64,128]{3,2,1,0:T(8,128)S(1)} collective-permute-done((f32[6,1,64,128]{3,2,1,0:T(8,128)S(1)}, f32[6,1,64,128]{3,2,1,0:T(8,128)S(1)}, u32[]{:S(2)}, u32[]{:S(2)}) %collective-permute-start.1) | collective-permute-done | bytes 196640 | tf_op jit(solution)/shard_map/ppermute | solution.py:608
  53.8 4.0 %collective-permute-done.9.refs_3_.refs_12_ = f32[1,32,32,128]{3,2,1,0:T(8,128)S(1)} collective-permute-done((f32[1,32,32,128]{3,2,1,0:T(8,128)S(1)}, f32[1,32,32,128]{3,2,1,0:T(8,128)S(1)}, u32[]{:S(2)}, u32[]{:S(2)}) %collective-permute-start.9) | collective-permute-done | bytes 524320 | tf_op jit(solution)/shard_map/ppermute | solution.py:596
  61.9 2.6 %collective-permute-done.8.refs_5_.refs_7_ = f32[2,2,8,32,128]{4,3,2,1,0:T(8,128)S(1)} collective-permute-done((f32[2,2,8,32,128]{4,3,2,1,0:T(8,128)S(1)}, f32[2,2,8,32,128]{4,3,2,1,0:T(8,128)S(1)}, u32[]{:S(2)}, u32[]{:S(2)}) %collective-permute-start.8) | collective-permute-done | bytes 524320 | tf_op jit(solution)/shard_map/ppermute | solution.py:605
  64.4 2.4 %coefficients.3 = (f32[2,4,128,128]{3,2,1,0:T(8,128)S(1)}, f32[8,128]{1,0:T(8,128)S(1)}) custom-call(s32[22]{0:T(128)S(1)} %pad_add_fusion.refs_0_, f32[71]{0:T(128)S(1)} %copy-done.7, f32[2,16,128,128]{3,2,1,0:T(8,128)S(1)} %copy-done.6, f32[2,8,32,128]{3,2,1,0:T(8,128)S(1)} %get-tuple-element.111.refs_3_.refs_5_, ...), custom_call_target="tpu_custom_call" | custom-call | tf_op jit(solution)/shard_map/coefficients/pallas_call | solution.py:432
  69.3 4.0 %collective-permute-done.12.refs_13_ = f32[1,32,32,128]{3,2,1,0:T(8,128)S(1)} collective-permute-done((f32[1,32,32,128]{3,2,1,0:T(8,128)S(1)}, f32[1,32,32,128]{3,2,1,0:T(8,128)S(1)}, u32[]{:S(2)}, u32[]{:S(2)}) %collective-permute-start.12) | collective-permute-done | bytes 524320 | tf_op jit(solution)/shard_map/ppermute | solution.py:596
  80.3 12.1 %collective-permute-done.10.refs_5_.refs_7_ = f32[2,2,8,32,128]{4,3,2,1,0:T(8,128)S(1)} collective-permute-done((f32[2,2,8,32,128]{4,3,2,1,0:T(8,128)S(1)}, f32[2,2,8,32,128]{4,3,2,1,0:T(8,128)S(1)}, u32[]{:S(2)}, u32[]{:S(2)}) %collective-permute-start.10) | collective-permute-done | bytes 524320 | tf_op jit(solution)/shard_map/ppermute | solution.py:605
  92.5 2.4 %coefficients.4 = (f32[2,4,128,128]{3,2,1,0:T(8,128)S(1)}, f32[8,128]{1,0:T(8,128)S(1)}) custom-call(s32[22]{0:T(128)S(1)} %pad_add_fusion.refs_0_, f32[71]{0:T(128)S(1)} %copy-done.7, f32[2,16,128,128]{3,2,1,0:T(8,128)S(1)} %copy-done.6, f32[2,8,32,128]{3,2,1,0:T(8,128)S(1)} %get-tuple-element.108.refs_3_.refs_5_, ...), custom_call_target="tpu_custom_call" | custom-call | tf_op jit(solution)/shard_map/coefficients/pallas_call | solution.py:432
  95.0 2.5 %filtered.3 = (f32[2,8,32,128]{3,2,1,0:T(8,128)S(1)}, f32[2,2,8,32,128]{4,3,2,1,0:T(8,128)S(1)}, f32[2,2,8,32,128]{4,3,2,1,0:T(8,128)S(1)}, f32[8,128]{1,0:T(8,128)S(1)}) custom-call(s32[22]{0:T(128)S(1)} %pad_add_fusion.refs_0_, f32[71]{0:T(128)S(1)} %copy-done.7, f32[2,16,128,128]{3,2,1,0:T(8,128)S(1)} %copy-done.5, ...), custom_call_target="tpu_custom_call" | custom-call | tf_op jit(solution)/shard_map/filtered/pallas_call | solution.py:432
  105.8 17.7 %collective-permute-done.14.refs_4_ = f32[2,4,128,128]{3,2,1,0:T(8,128)S(1)} collective-permute-done((f32[2,4,128,128]{3,2,1,0:T(8,128)S(1)}, f32[2,4,128,128]{3,2,1,0:T(8,128)S(1)}, u32[]{:S(2)}, u32[]{:S(2)}) %collective-permute-start.14) | collective-permute-done | bytes 524320 | tf_op jit(solution)/shard_map/ppermute | solution.py:605
  123.6 2.5 %filtered.4 = (f32[2,8,32,128]{3,2,1,0:T(8,128)S(1)}, f32[2,2,8,32,128]{4,3,2,1,0:T(8,128)S(1)}, f32[2,2,8,32,128]{4,3,2,1,0:T(8,128)S(1)}, f32[8,128]{1,0:T(8,128)S(1)}) custom-call(s32[22]{0:T(128)S(1)} %pad_add_fusion.refs_0_, f32[71]{0:T(128)S(1)} %copy-done.7, f32[2,16,128,128]{3,2,1,0:T(8,128)S(1)} %copy-done.5, ...), custom_call_target="tpu_custom_call" | custom-call | tf_op jit(solution)/shard_map/filtered/pallas_call | solution.py:432
  126.2 3.6 %collective-permute-done.22.refs_4_ = f32[1,4,128,128]{3,2,1,0:T(8,128)S(1)} collective-permute-done((f32[1,4,128,128]{3,2,1,0:T(8,128)S(1)}, f32[1,4,128,128]{3,2,1,0:T(8,128)S(1)}, u32[]{:S(2)}, u32[]{:S(2)}) %collective-permute-start.22) | collective-permute-done | bytes 262176 | tf_op jit(solution)/shard_map/ppermute | solution.py:605
  133.8 7.3 %collective-permute-done.19.refs_1_.refs_4_ = f32[2,2,8,32,128]{4,3,2,1,0:T(8,128)S(1)} collective-permute-done((f32[2,2,8,32,128]{4,3,2,1,0:T(8,128)S(1)}, f32[2,2,8,32,128]{4,3,2,1,0:T(8,128)S(1)}, u32[]{:S(2)}, u32[]{:S(2)}) %collective-permute-start.19) | collective-permute-done | bytes 524320 | tf_op jit(solution)/shard_map/ppermute | solution.py:605
  141.2 2.5 %place_near.3 = (f32[5,32,64,128]{3,2,1,0:T(8,128)}, f32[8,128]{1,0:T(8,128)S(1)}) custom-call(s32[22]{0:T(128)S(1)} %pad_add_fusion.refs_0_, f32[71]{0:T(128)S(1)} %copy-done.7, f32[2,8,32,128]{3,2,1,0:T(8,128)S(1)} %get-tuple-element.155.refs_2_, f32[2,2,8,32,128]{4,3,2,1,0:T(8,128)S(1)} %collective-permute-done.26.refs_3_, ...), custom_call_target="tpu_custom_call", output_to_operand_aliasing={{0}: (5, {})} | custom-call | tf_op jit(solution)/shard_map/place_near/pallas_call | solution.py:153
  149.3 2.5 %place_near.5 = (f32[5,32,64,128]{3,2,1,0:T(8,128)}, f32[8,128]{1,0:T(8,128)}) custom-call(s32[22]{0:T(128)S(1)} %pad_add_fusion.refs_0_, f32[71]{0:T(128)S(1)} %copy-done.7, f32[2,8,32,128]{3,2,1,0:T(8,128)S(1)} %get-tuple-element.138.refs_2_, f32[2,2,8,32,128]{4,3,2,1,0:T(8,128)S(1)} %collective-permute-done.23.refs_3_, ...), custom_call_target="tpu_custom_call", output_to_operand_aliasing={{0}: (5, {})} | custom-call | tf_op jit(solution)/shard_map/place_near/pallas_call | solution.py:153
  (116 shorter events, 49.7 us)
Async XLA Ops:
  2.3 19.7 %collective-permute-start = (f32[2,32,32,128]{3,2,1,0:T(8,128)}, f32[2,32,32,128]{3,2,1,0:T(8,128)S(1)}, u32[]{:S(2)}, u32[]{:S(2)}) collective-permute-start(f32[2,32,32,128]{3,2,1,0:T(8,128)} %get-tuple-element.88), channel_id=1, source_target_pairs={{0,16},{1,9},{2,18},{3,11},{4,20},{5,13},{6,22},{7,15},{8,24},{9,1... | collective-permute-start | bytes 3145736 | tf_op jit(solution)/shard_map/ppermute | solution.py:596
  10.9 23.4 %collective-permute-start.3 = (f32[2,32,32,128]{3,2,1,0:T(8,128)}, f32[2,32,32,128]{3,2,1,0:T(8,128)S(1)}, u32[]{:S(2)}, u32[]{:S(2)}) collective-permute-start(f32[2,32,32,128]{3,2,1,0:T(8,128)} %get-tuple-element.98), channel_id=1, source_target_pairs={{0,16},{1,9},{2,18},{3,11},{4,20},{5,13},{6,22},{7,15},{8,24},{9,1... | collective-permute-start | bytes 3145736 | tf_op jit(solution)/shard_map/ppermute | solution.py:596
  22.8 21.9 %collective-permute-start.5 = (f32[2,32,32,128]{3,2,1,0:T(8,128)S(1)}, f32[2,32,32,128]{3,2,1,0:T(8,128)S(1)}, u32[]{:S(2)}, u32[]{:S(2)}) collective-permute-start(f32[2,32,32,128]{3,2,1,0:T(8,128)S(1)} %get-tuple-element.101), channel_id=1, source_target_pairs={{0,8},{1,17},{2,10},{3,19},{4,12},{5,21},{6,14},{7,23},{8,0},{9,25... | collective-permute-start | bytes 3145736 | tf_op jit(solution)/shard_map/ppermute | solution.py:596
  35.0 16.7 %collective-permute-start.4 = (f32[2,32,32,128]{3,2,1,0:T(8,128)S(1)}, f32[2,32,32,128]{3,2,1,0:T(8,128)S(1)}, u32[]{:S(2)}, u32[]{:S(2)}) collective-permute-start(f32[2,32,32,128]{3,2,1,0:T(8,128)S(1)} %get-tuple-element.100), channel_id=1, source_target_pairs={{0,8},{1,17},{2,10},{3,19},{4,12},{5,21},{6,14},{7,23},{8,0},{9,25... | collective-permute-start | bytes 3145736 | tf_op jit(solution)/shard_map/ppermute | solution.py:596
  48.6 9.2 %collective-permute-start.9 = (f32[1,32,32,128]{3,2,1,0:T(8,128)S(1)}, f32[1,32,32,128]{3,2,1,0:T(8,128)S(1)}, u32[]{:S(2)}, u32[]{:S(2)}) collective-permute-start(f32[1,32,32,128]{3,2,1,0:T(8,128)S(1)} %copy-done.14), channel_id=1, source_target_pairs={{0,16},{1,9},{2,18},{3,11},{4,20},{5,13},{6,22},{7,15},{8,24},{9,1... | collective-permute-start | bytes 1572872 | tf_op jit(solution)/shard_map/ppermute | solution.py:596
  50.1 27.8 %collective-permute-start.11 = (f32[2,32,32,128]{3,2,1,0:T(8,128)S(1)}, f32[2,32,32,128]{3,2,1,0:T(8,128)S(1)}, u32[]{:S(2)}, u32[]{:S(2)}) collective-permute-start(f32[2,32,32,128]{3,2,1,0:T(8,128)S(1)} %get-tuple-element.118), channel_id=1, source_target_pairs={{0,16},{1,9},{2,18},{3,11},{4,20},{5,13},{6,22},{7,15},{8,24},{9,1... | collective-permute-start | bytes 3145736 | tf_op jit(solution)/shard_map/ppermute | solution.py:596
  50.7 13.8 %collective-permute-start.8 = (f32[2,2,8,32,128]{4,3,2,1,0:T(8,128)S(1)}, f32[2,2,8,32,128]{4,3,2,1,0:T(8,128)S(1)}, u32[]{:S(2)}, u32[]{:S(2)}) collective-permute-start(f32[2,2,8,32,128]{4,3,2,1,0:T(8,128)S(1)} %get-tuple-element.112), channel_id=1, source_target_pairs={{0,2},{1,3},{2,0},{3,1},{4,6},{5,7},{6,4},{7,5},{8,10},{9,11},{10,... | collective-permute-start | bytes 1572872 | tf_op jit(solution)/shard_map/ppermute | solution.py:605
  53.4 13.5 %collective-permute-start.7 = (f32[2,2,8,32,128]{4,3,2,1,0:T(8,128)S(1)}, f32[2,2,8,32,128]{4,3,2,1,0:T(8,128)S(1)}, u32[]{:S(2)}, u32[]{:S(2)}) collective-permute-start(f32[2,2,8,32,128]{4,3,2,1,0:T(8,128)S(1)} %get-tuple-element.109), channel_id=1, source_target_pairs={{0,1},{1,0},{2,3},{3,2},{4,5},{5,4},{6,7},{7,6},{8,9},{9,8},{10,11... | collective-permute-start | bytes 1572872 | tf_op jit(solution)/shard_map/ppermute | solution.py:605
  58.4 14.9 %collective-permute-start.12 = (f32[1,32,32,128]{3,2,1,0:T(8,128)S(1)}, f32[1,32,32,128]{3,2,1,0:T(8,128)S(1)}, u32[]{:S(2)}, u32[]{:S(2)}) collective-permute-start(f32[1,32,32,128]{3,2,1,0:T(8,128)S(1)} %get-tuple-element.119), channel_id=1, source_target_pairs={{0,8},{1,17},{2,10},{3,19},{4,12},{5,21},{6,14},{7,23},{8,0},{9,25... | collective-permute-start | bytes 1572872 | tf_op jit(solution)/shard_map/ppermute | solution.py:596
  60.3 37.2 %collective-permute-start.17 = (f32[2,32,32,128]{3,2,1,0:T(8,128)S(1)}, f32[2,32,32,128]{3,2,1,0:T(8,128)S(1)}, u32[]{:S(2)}, u32[]{:S(2)}) collective-permute-start(f32[2,32,32,128]{3,2,1,0:T(8,128)S(1)} %copy-done.12), channel_id=1, source_target_pairs={{0,16},{1,9},{2,18},{3,11},{4,20},{5,13},{6,22},{7,15},{8,24},{9,1... | collective-permute-start | bytes 3145736 | tf_op jit(solution)/shard_map/ppermute | solution.py:596
  66.9 25.5 %collective-permute-start.10 = (f32[2,2,8,32,128]{4,3,2,1,0:T(8,128)S(1)}, f32[2,2,8,32,128]{4,3,2,1,0:T(8,128)S(1)}, u32[]{:S(2)}, u32[]{:S(2)}) collective-permute-start(f32[2,2,8,32,128]{4,3,2,1,0:T(8,128)S(1)} %get-tuple-element.117), channel_id=1, source_target_pairs={{0,2},{1,3},{2,0},{3,1},{4,6},{5,7},{6,4},{7,5},{8,10},{9,11},{10,... | collective-permute-start | bytes 1572872 | tf_op jit(solution)/shard_map/ppermute | solution.py:605
  67.6 27.4 %collective-permute-start.18 = (f32[2,4,128,128]{3,2,1,0:T(8,128)S(1)}, f32[2,4,128,128]{3,2,1,0:T(8,128)S(1)}, u32[]{:S(2)}, u32[]{:S(2)}) collective-permute-start(f32[2,4,128,128]{3,2,1,0:T(8,128)S(1)} %get-tuple-element.132.refs_3_), channel_id=1, source_target_pairs={{0,4},{1,5},{2,6},{3,7},{4,0},{5,1},{6,2},{7,3},{8,12},{9,13},{10,... | collective-permute-start | bytes 1572872 | tf_op jit(solution)/shard_map/ppermute | solution.py:605
  76.0 28.3 %collective-permute-start.15 = (f32[1,32,32,128]{3,2,1,0:T(8,128)S(1)}, f32[1,32,32,128]{3,2,1,0:T(8,128)S(1)}, u32[]{:S(2)}, u32[]{:S(2)}) collective-permute-start(f32[1,32,32,128]{3,2,1,0:T(8,128)S(1)} %get-tuple-element.128), channel_id=1, source_target_pairs={{0,16},{1,9},{2,18},{3,11},{4,20},{5,13},{6,22},{7,15},{8,24},{9,1... | collective-permute-start | bytes 1572872 | tf_op jit(solution)/shard_map/ppermute | solution.py:596
  77.9 22.8 %collective-permute-start.16 = (f32[2,1,8,32,128]{4,3,2,1,0:T(8,128)S(1)}, f32[2,1,8,32,128]{4,3,2,1,0:T(8,128)S(1)}, u32[]{:S(2)}, u32[]{:S(2)}) collective-permute-start(f32[2,1,8,32,128]{4,3,2,1,0:T(8,128)S(1)} %get-tuple-element.130), channel_id=1, source_target_pairs={{0,2},{1,3},{2,0},{3,1},{4,6},{5,7},{6,4},{7,5},{8,10},{9,11},{10,... | collective-permute-start | bytes 786440 | tf_op jit(solution)/shard_map/ppermute | solution.py:605
  92.4 39.3 %collective-permute-start.20 = (f32[2,32,32,128]{3,2,1,0:T(8,128)S(1)}, f32[2,32,32,128]{3,2,1,0:T(8,128)S(1)}, u32[]{:S(2)}, u32[]{:S(2)}) collective-permute-start(f32[2,32,32,128]{3,2,1,0:T(8,128)S(1)} %get-tuple-element.142), channel_id=1, source_target_pairs={{0,8},{1,17},{2,10},{3,19},{4,12},{5,21},{6,14},{7,23},{8,0},{9,25... | collective-permute-start | bytes 3145736 | tf_op jit(solution)/shard_map/ppermute | solution.py:596
  94.9 28.7 %collective-permute-start.14 = (f32[2,4,128,128]{3,2,1,0:T(8,128)S(1)}, f32[2,4,128,128]{3,2,1,0:T(8,128)S(1)}, u32[]{:S(2)}, u32[]{:S(2)}) collective-permute-start(f32[2,4,128,128]{3,2,1,0:T(8,128)S(1)} %get-tuple-element.127.refs_3_), channel_id=1, source_target_pairs={{0,4},{1,5},{2,6},{3,7},{4,0},{5,1},{6,2},{7,3},{8,12},{9,13},{10,... | collective-permute-start | bytes 1572872 | tf_op jit(solution)/shard_map/ppermute | solution.py:605
  97.6 34.0 %collective-permute-start.21 = (f32[2,2,8,32,128]{4,3,2,1,0:T(8,128)S(1)}, f32[2,2,8,32,128]{4,3,2,1,0:T(8,128)S(1)}, u32[]{:S(2)}, u32[]{:S(2)}) collective-permute-start(f32[2,2,8,32,128]{4,3,2,1,0:T(8,128)S(1)} %get-tuple-element.144), channel_id=1, source_target_pairs={{0,2},{1,3},{2,0},{3,1},{4,6},{5,7},{6,4},{7,5},{8,10},{9,11},{10,... | collective-permute-start | bytes 1572872 | tf_op jit(solution)/shard_map/ppermute | solution.py:605
  100.7 43.0 %collective-permute-start.25 = (f32[2,32,32,128]{3,2,1,0:T(8,128)S(1)}, f32[2,32,32,128]{3,2,1,0:T(8,128)S(1)}, u32[]{:S(2)}, u32[]{:S(2)}) collective-permute-start(f32[2,32,32,128]{3,2,1,0:T(8,128)S(1)} %get-tuple-element.154), channel_id=1, source_target_pairs={{0,8},{1,17},{2,10},{3,19},{4,12},{5,21},{6,14},{7,23},{8,0},{9,25... | collective-permute-start | bytes 3145736 | tf_op jit(solution)/shard_map/ppermute | solution.py:596
  104.3 25.5 %collective-permute-start.22 = (f32[1,4,128,128]{3,2,1,0:T(8,128)S(1)}, f32[1,4,128,128]{3,2,1,0:T(8,128)S(1)}, u32[]{:S(2)}, u32[]{:S(2)}) collective-permute-start(f32[1,4,128,128]{3,2,1,0:T(8,128)S(1)} %get-tuple-element.145.refs_3_), channel_id=1, source_target_pairs={{0,4},{1,5},{2,6},{3,7},{4,0},{5,1},{6,2},{7,3},{8,12},{9,13},{10,... | collective-permute-start | bytes 786440 | tf_op jit(solution)/shard_map/ppermute | solution.py:605
  126.1 15.0 %collective-permute-start.19 = (f32[2,2,8,32,128]{4,3,2,1,0:T(8,128)S(1)}, f32[2,2,8,32,128]{4,3,2,1,0:T(8,128)S(1)}, u32[]{:S(2)}, u32[]{:S(2)}) collective-permute-start(f32[2,2,8,32,128]{4,3,2,1,0:T(8,128)S(1)} %get-tuple-element.140), channel_id=1, source_target_pairs={{0,2},{1,3},{2,0},{3,1},{4,6},{5,7},{6,4},{7,5},{8,10},{9,11},{10,... | collective-permute-start | bytes 1572872 | tf_op jit(solution)/shard_map/ppermute | solution.py:605
  131.6 9.6 %collective-permute-start.26 = (f32[2,2,8,32,128]{4,3,2,1,0:T(8,128)S(1)}, f32[2,2,8,32,128]{4,3,2,1,0:T(8,128)S(1)}, u32[]{:S(2)}, u32[]{:S(2)}) collective-permute-start(f32[2,2,8,32,128]{4,3,2,1,0:T(8,128)S(1)} %get-tuple-element.156), channel_id=1, source_target_pairs={{0,1},{1,0},{2,3},{3,2},{4,5},{5,4},{6,7},{7,6},{8,9},{9,8},{10,11... | collective-permute-start | bytes 1572872 | tf_op jit(solution)/shard_map/ppermute | solution.py:605
  131.7 13.7 %collective-permute-start.24 = (f32[2,1,8,32,128]{4,3,2,1,0:T(8,128)S(1)}, f32[2,1,8,32,128]{4,3,2,1,0:T(8,128)S(1)}, u32[]{:S(2)}, u32[]{:S(2)}) collective-permute-start(f32[2,1,8,32,128]{4,3,2,1,0:T(8,128)S(1)} %get-tuple-element.153), channel_id=1, source_target_pairs={{0,2},{1,3},{2,0},{3,1},{4,6},{5,7},{6,4},{7,5},{8,10},{9,11},{10,... | collective-permute-start | bytes 786440 | tf_op jit(solution)/shard_map/ppermute | solution.py:605
  131.8 14.1 %collective-permute-start.28 = (f32[1,32,32,128]{3,2,1,0:T(8,128)S(1)}, f32[1,32,32,128]{3,2,1,0:T(8,128)S(1)}, u32[]{:S(2)}, u32[]{:S(2)}) collective-permute-start(f32[1,32,32,128]{3,2,1,0:T(8,128)S(1)} %get-tuple-element.163), channel_id=1, source_target_pairs={{0,8},{1,17},{2,10},{3,19},{4,12},{5,21},{6,14},{7,23},{8,0},{9,25... | collective-permute-start | bytes 1572872 | tf_op jit(solution)/shard_map/ppermute | solution.py:596
  141.1 8.2 %collective-permute-start.23 = (f32[2,2,8,32,128]{4,3,2,1,0:T(8,128)S(1)}, f32[2,2,8,32,128]{4,3,2,1,0:T(8,128)S(1)}, u32[]{:S(2)}, u32[]{:S(2)}) collective-permute-start(f32[2,2,8,32,128]{4,3,2,1,0:T(8,128)S(1)} %get-tuple-element.150), channel_id=1, source_target_pairs={{0,1},{1,0},{2,3},{3,2},{4,5},{5,4},{6,7},{7,6},{8,9},{9,8},{10,11... | collective-permute-start | bytes 1572872 | tf_op jit(solution)/shard_map/ppermute | solution.py:605
  (27 other events, 128.3 us)

commit v14 on v12

--- a/solution.py
+++ b/solution.py
@@ -255,7 +255,7 @@
 def local_part(far, center, source, viscosity, kappa, coupling, flags, token):
     fields, block, rows, cells = center.shape
     half = rows // 2
-    planes = min(4, block)
+    planes = min(8, block)
     edge = half // 8 - 1 if far else half // 8
 
     def whole(width, index):
@@ -290,7 +290,7 @@
         ],
         pl.BlockSpec((fields, planes, half, cells), lambda i: (0, i, 0, 0)),
         shaped(fields, block, half, cells),
-        grant=24 if far else LOCAL,
+        grant=LOCAL,
     )
 
 

time: 150 us -> 153 us (1.020)
  waiting for transfers between devices: 53.1 us -> 59.8 us
  local copies, waits for them, and re-layouts: 6.35 us -> 3.07 us
  starting transfers between devices: 32.8 us -> 31 us
    ppermute x15, waiting for transfers between devices: 40.2 us -> 45.4 us  [to_sector(): return lax.ppermute(x, 'space', [(i, i ^ k) for i in range(sectors)])]
    unnamed x43 -> x47, local copies, waits for them, and re-layouts: 6.35 us -> 3.07 us
where the time goes in v14:
time: 153 us; the launch traced here: 152 us
  waiting for transfers between devices  59.8 us (39%)
  Pallas kernels  58.1 us (38%)
  starting transfers between devices  31 us (20%)
  local copies, waits for them, and re-layouts  3.07 us (2%)
    ppermute x15, waiting for transfers between devices, to_sector(): return lax.ppermute(x, 'space', [(i, i ^ k) for i in range(sectors)])  45.4 us
    pallas_call x29, Pallas kernels, call(): pl.pallas_call(kernel, grid=grid, in_specs=list(in_specs) + [ANY] * len(e...  44.8 us
    ppermute x12, starting transfers between devices, to_partner(): return lax.ppermute(x, ('inst', 'space'), pairs)  16 us
    pallas_call x6, Pallas kernels, table_call(): pl.pallas_call(kernel, grid_spec=pltpu.PrefetchScalarGridSpec(num_scalar_...  13.3 us
    ppermute x15, starting transfers between devices, to_sector(): return lax.ppermute(x, 'space', [(i, i ^ k) for i in range(sectors)])  11.4 us
    ppermute x12, waiting for transfers between devices, to_partner(): return lax.ppermute(x, ('inst', 'space'), pairs)  11.1 us
    ppermute x2, starting transfers between devices, ring(): lax.ppermute(x, 'space', [(i, (i + step) % sectors) for i in range(sector...  3.54 us
    ppermute x2, waiting for transfers between devices, ring(): lax.ppermute(x, 'space', [(i, (i + step) % sectors) for i in range(sector...  3.3 us
  transfers between devices with their start and end apart: 29, of which 10 were waited for; matrix products, arithmetic and copies ran while one was open for 0% of the time, Pallas kernels for 35%

profile of v14, /device:TPU:0, one launch (start us, length us, event | category | flops | bytes accessed | tf_op | source)
XLA Modules:
  0.0 152.4 jit_solution(6979602866451804877)
XLA Ops:
  0.0 2.3 %pack.6 = (f32[2,32,32,128]{3,2,1,0:T(8,128)}, f32[6,1,64,128]{3,2,1,0:T(8,128)}, f32[6,1,64,128]{3,2,1,0:T(8,128)}, f32[8,128]{1,0:T(8,128)}) custom-call(f32[5,32,64,128]{3,2,1,0:T(8,128)} %bitcast.6, f32[5,32,64,128]{3,2,1,0:T(8,128)} %bitcast.7, f32[32,64,128]{2,1,0:T(8,128)} %refs_11_.3, f32[5,32,64,128]{3,2,1,0:T(8,128)} %bitcast.8, ...), custom_call_target="tpu_custom_call" | custom-call | tf_op jit(solution)/shard_map/pack/pallas_call | solution.py:153
  2.3 3.0 %collective-permute-start = (f32[2,32,32,128]{3,2,1,0:T(8,128)}, f32[2,32,32,128]{3,2,1,0:T(8,128)S(1)}, u32[]{:S(2)}, u32[]{:S(2)}) collective-permute-start(f32[2,32,32,128]{3,2,1,0:T(8,128)} %get-tuple-element.88), channel_id=1, source_target_pairs={{0,16},{1,9},{2,18},{3,11},{4,20},{5,13},{6,22},{7,15},{8,24},{9,1... | collective-permute-start | bytes 3145736 | tf_op jit(solution)/shard_map/ppermute | solution.py:596
  9.5 2.2 %pack.9 = (f32[2,32,32,128]{3,2,1,0:T(8,128)}, f32[8,128]{1,0:T(8,128)}) custom-call(f32[5,32,64,128]{3,2,1,0:T(8,128)} %bitcast.11, f32[8,128]{1,0:T(8,128)} %get-tuple-element.91.refs_1_), custom_call_target="tpu_custom_call" | custom-call | tf_op jit(solution)/shard_map/pack/pallas_call | solution.py:153
  12.5 7.0 %local_part.2 = (f32[5,32,32,128]{3,2,1,0:T(8,128)}, f32[8,128]{1,0:T(8,128)S(1)}) custom-call(f32[5,5]{1,0:T(8,128)S(1)} %copy-done.10, f32[5]{0:T(128)S(1)} %copy-done.9, s32[5,3]{1,0:T(8,128)S(1)} %copy.24.refs_2_, f32[5,32,64,128]{3,2,1,0:T(8,128)} %bitcast.12, f32[5,32,64,128]{3,2,1,0:T(8,128)} %bitcast.13, f32[5,32,64,128]{3,2,1,0:T(8,128)} %bitcast.14, ...), custom_call_target="tpu_custom_call" | custom-call | tf_op jit(solution)/shard_map/local_part/pallas_call | solution.py:153
  24.6 7.0 %local_part.3 = (f32[5,32,32,128]{3,2,1,0:T(8,128)}, f32[8,128]{1,0:T(8,128)S(1)}) custom-call(f32[5,5]{1,0:T(8,128)S(1)} %copy-done.10, f32[5]{0:T(128)S(1)} %copy-done.9, s32[5,3]{1,0:T(8,128)S(1)} %copy.24.refs_2_, f32[5,32,64,128]{3,2,1,0:T(8,128)} %bitcast.16, f32[5,32,64,128]{3,2,1,0:T(8,128)} %bitcast.17, f32[5,32,64,128]{3,2,1,0:T(8,128)} %bitcast.18, ...), custom_call_target="tpu_custom_call" | custom-call | tf_op jit(solution)/shard_map/local_part/pallas_call | solution.py:153
  31.6 2.8 %collective-permute-done.3.refs_3_.refs_12_ = f32[2,32,32,128]{3,2,1,0:T(8,128)} collective-permute-done((f32[2,32,32,128]{3,2,1,0:T(8,128)}, f32[2,32,32,128]{3,2,1,0:T(8,128)}, u32[]{:S(2)}, u32[]{:S(2)}) %collective-permute-start.3) | collective-permute-done | bytes 1048608 | tf_op jit(solution)/shard_map/ppermute | solution.py:596
  36.0 2.3 %collective-permute-start.4 = (f32[2,32,32,128]{3,2,1,0:T(8,128)S(1)}, f32[2,32,32,128]{3,2,1,0:T(8,128)S(1)}, u32[]{:S(2)}, u32[]{:S(2)}) collective-permute-start(f32[2,32,32,128]{3,2,1,0:T(8,128)S(1)} %get-tuple-element.100), channel_id=1, source_target_pairs={{0,8},{1,17},{2,10},{3,19},{4,12},{5,21},{6,14},{7,23},{8,0},{9,25... | collective-permute-start | bytes 3145736 | tf_op jit(solution)/shard_map/ppermute | solution.py:596
  38.3 3.5 %collective-permute-start.2 = (f32[6,1,64,128]{3,2,1,0:T(8,128)S(1)}, f32[6,1,64,128]{3,2,1,0:T(8,128)S(1)}, u32[]{:S(2)}, u32[]{:S(2)}) collective-permute-start(f32[6,1,64,128]{3,2,1,0:T(8,128)S(1)} %copy-done.17), channel_id=1, source_target_pairs={{0,7},{1,0},{2,1},{3,2},{4,3},{5,4},{6,5},{7,6},{8,15},{9,8},{10,9... | collective-permute-start | bytes 589832 | tf_op jit(solution)/shard_map/ppermute | solution.py:608
  42.1 3.3 %collective-permute-done.1.refs_5_.refs_7_ = f32[6,1,64,128]{3,2,1,0:T(8,128)S(1)} collective-permute-done((f32[6,1,64,128]{3,2,1,0:T(8,128)S(1)}, f32[6,1,64,128]{3,2,1,0:T(8,128)S(1)}, u32[]{:S(2)}, u32[]{:S(2)}) %collective-permute-start.1) | collective-permute-done | bytes 196640 | tf_op jit(solution)/shard_map/ppermute | solution.py:608
  51.9 2.1 %spread.4 = (f32[2,8,32,128]{3,2,1,0:T(8,128)S(1)}, f32[2,2,8,32,128]{4,3,2,1,0:T(8,128)S(1)}, f32[2,2,8,32,128]{4,3,2,1,0:T(8,128)S(1)}, f32[8,128]{1,0:T(8,128)S(1)}) custom-call(s32[22]{0:T(128)S(1)} %pad_add_fusion.refs_0_, f32[71]{0:T(128)S(1)} %copy-done.8, f32[5,32,32,128]{3,2,1,0:T(8,128)S(1)} %copy-done.1, f32[5]{0:T(128)S(1)} %copy-done.9, ...), custom_call_target="tpu_custom_call" | custom-call | tf_op jit(solution)/shard_map/spread/pallas_call | solution.py:153
  54.2 4.2 %collective-permute-done.9.refs_3_.refs_12_ = f32[1,32,32,128]{3,2,1,0:T(8,128)S(1)} collective-permute-done((f32[1,32,32,128]{3,2,1,0:T(8,128)S(1)}, f32[1,32,32,128]{3,2,1,0:T(8,128)S(1)}, u32[]{:S(2)}, u32[]{:S(2)}) %collective-permute-start.9) | collective-permute-done | bytes 524320 | tf_op jit(solution)/shard_map/ppermute | solution.py:596
  61.9 3.2 %collective-permute-done.8.refs_5_.refs_7_ = f32[2,2,8,32,128]{4,3,2,1,0:T(8,128)S(1)} collective-permute-done((f32[2,2,8,32,128]{4,3,2,1,0:T(8,128)S(1)}, f32[2,2,8,32,128]{4,3,2,1,0:T(8,128)S(1)}, u32[]{:S(2)}, u32[]{:S(2)}) %collective-permute-start.8) | collective-permute-done | bytes 524320 | tf_op jit(solution)/shard_map/ppermute | solution.py:605
  65.0 2.4 %coefficients.3 = (f32[2,4,128,128]{3,2,1,0:T(8,128)S(1)}, f32[8,128]{1,0:T(8,128)S(1)}) custom-call(s32[22]{0:T(128)S(1)} %pad_add_fusion.refs_0_, f32[71]{0:T(128)S(1)} %copy-done.8, f32[2,16,128,128]{3,2,1,0:T(8,128)S(1)} %copy-done.4, f32[2,8,32,128]{3,2,1,0:T(8,128)S(1)} %get-tuple-element.111.refs_3_.refs_5_, ...), custom_call_target="tpu_custom_call" | custom-call | tf_op jit(solution)/shard_map/coefficients/pallas_call | solution.py:432
  69.9 4.0 %collective-permute-done.12.refs_13_ = f32[1,32,32,128]{3,2,1,0:T(8,128)S(1)} collective-permute-done((f32[1,32,32,128]{3,2,1,0:T(8,128)S(1)}, f32[1,32,32,128]{3,2,1,0:T(8,128)S(1)}, u32[]{:S(2)}, u32[]{:S(2)}) %collective-permute-start.12) | collective-permute-done | bytes 524320 | tf_op jit(solution)/shard_map/ppermute | solution.py:596
  80.4 12.6 %collective-permute-done.10.refs_5_.refs_7_ = f32[2,2,8,32,128]{4,3,2,1,0:T(8,128)S(1)} collective-permute-done((f32[2,2,8,32,128]{4,3,2,1,0:T(8,128)S(1)}, f32[2,2,8,32,128]{4,3,2,1,0:T(8,128)S(1)}, u32[]{:S(2)}, u32[]{:S(2)}) %collective-permute-start.10) | collective-permute-done | bytes 524320 | tf_op jit(solution)/shard_map/ppermute | solution.py:605
  93.1 2.4 %coefficients.4 = (f32[2,4,128,128]{3,2,1,0:T(8,128)S(1)}, f32[8,128]{1,0:T(8,128)S(1)}) custom-call(s32[22]{0:T(128)S(1)} %pad_add_fusion.refs_0_, f32[71]{0:T(128)S(1)} %copy-done.8, f32[2,16,128,128]{3,2,1,0:T(8,128)S(1)} %copy-done.4, f32[2,8,32,128]{3,2,1,0:T(8,128)S(1)} %get-tuple-element.108.refs_3_.refs_5_, ...), custom_call_target="tpu_custom_call" | custom-call | tf_op jit(solution)/shard_map/coefficients/pallas_call | solution.py:432
  95.9 2.5 %filtered.3 = (f32[2,8,32,128]{3,2,1,0:T(8,128)S(1)}, f32[2,2,8,32,128]{4,3,2,1,0:T(8,128)S(1)}, f32[2,2,8,32,128]{4,3,2,1,0:T(8,128)S(1)}, f32[8,128]{1,0:T(8,128)S(1)}) custom-call(s32[22]{0:T(128)S(1)} %pad_add_fusion.refs_0_, f32[71]{0:T(128)S(1)} %copy-done.8, f32[2,16,128,128]{3,2,1,0:T(8,128)S(1)} %copy-done.3, ...), custom_call_target="tpu_custom_call" | custom-call | tf_op jit(solution)/shard_map/filtered/pallas_call | solution.py:432
  98.5 2.6 %collective-permute-start.21 = (f32[2,2,8,32,128]{4,3,2,1,0:T(8,128)S(1)}, f32[2,2,8,32,128]{4,3,2,1,0:T(8,128)S(1)}, u32[]{:S(2)}, u32[]{:S(2)}) collective-permute-start(f32[2,2,8,32,128]{4,3,2,1,0:T(8,128)S(1)} %get-tuple-element.144), channel_id=1, source_target_pairs={{0,2},{1,3},{2,0},{3,1},{4,6},{5,7},{6,4},{7,5},{8,10},{9,11},{10,... | collective-permute-start | bytes 1572872 | tf_op jit(solution)/shard_map/ppermute | solution.py:605
  106.5 17.7 %collective-permute-done.14.refs_4_ = f32[2,4,128,128]{3,2,1,0:T(8,128)S(1)} collective-permute-done((f32[2,4,128,128]{3,2,1,0:T(8,128)S(1)}, f32[2,4,128,128]{3,2,1,0:T(8,128)S(1)}, u32[]{:S(2)}, u32[]{:S(2)}) %collective-permute-start.14) | collective-permute-done | bytes 524320 | tf_op jit(solution)/shard_map/ppermute | solution.py:605
  124.2 2.5 %filtered.4 = (f32[2,8,32,128]{3,2,1,0:T(8,128)S(1)}, f32[2,2,8,32,128]{4,3,2,1,0:T(8,128)S(1)}, f32[2,2,8,32,128]{4,3,2,1,0:T(8,128)S(1)}, f32[8,128]{1,0:T(8,128)S(1)}) custom-call(s32[22]{0:T(128)S(1)} %pad_add_fusion.refs_0_, f32[71]{0:T(128)S(1)} %copy-done.8, f32[2,16,128,128]{3,2,1,0:T(8,128)S(1)} %copy-done.3, ...), custom_call_target="tpu_custom_call" | custom-call | tf_op jit(solution)/shard_map/filtered/pallas_call | solution.py:432
  126.8 3.6 %collective-permute-done.22.refs_4_ = f32[1,4,128,128]{3,2,1,0:T(8,128)S(1)} collective-permute-done((f32[1,4,128,128]{3,2,1,0:T(8,128)S(1)}, f32[1,4,128,128]{3,2,1,0:T(8,128)S(1)}, u32[]{:S(2)}, u32[]{:S(2)}) %collective-permute-start.22) | collective-permute-done | bytes 262176 | tf_op jit(solution)/shard_map/ppermute | solution.py:605
  134.9 6.8 %collective-permute-done.19.refs_1_.refs_4_ = f32[2,2,8,32,128]{4,3,2,1,0:T(8,128)S(1)} collective-permute-done((f32[2,2,8,32,128]{4,3,2,1,0:T(8,128)S(1)}, f32[2,2,8,32,128]{4,3,2,1,0:T(8,128)S(1)}, u32[]{:S(2)}, u32[]{:S(2)}) %collective-permute-start.19) | collective-permute-done | bytes 524320 | tf_op jit(solution)/shard_map/ppermute | solution.py:605
  141.9 2.5 %place_near.3 = (f32[5,32,64,128]{3,2,1,0:T(8,128)}, f32[8,128]{1,0:T(8,128)S(1)}) custom-call(s32[22]{0:T(128)S(1)} %pad_add_fusion.refs_0_, f32[71]{0:T(128)S(1)} %copy-done.8, f32[2,8,32,128]{3,2,1,0:T(8,128)S(1)} %get-tuple-element.155.refs_2_, f32[2,2,8,32,128]{4,3,2,1,0:T(8,128)S(1)} %collective-permute-done.26.refs_3_, ...), custom_call_target="tpu_custom_call", output_to_operand_aliasing={{0}: (5, {})} | custom-call | tf_op jit(solution)/shard_map/place_near/pallas_call | solution.py:153
  149.9 2.5 %place_near.5 = (f32[5,32,64,128]{3,2,1,0:T(8,128)}, f32[8,128]{1,0:T(8,128)}) custom-call(s32[22]{0:T(128)S(1)} %pad_add_fusion.refs_0_, f32[71]{0:T(128)S(1)} %copy-done.8, f32[2,8,32,128]{3,2,1,0:T(8,128)S(1)} %get-tuple-element.138.refs_2_, f32[2,2,8,32,128]{4,3,2,1,0:T(8,128)S(1)} %collective-permute-done.23.refs_3_, ...), custom_call_target="tpu_custom_call", output_to_operand_aliasing={{0}: (5, {})} | custom-call | tf_op jit(solution)/shard_map/place_near/pallas_call | solution.py:153
  (119 shorter events, 46.8 us)
Async XLA Ops:
  2.3 17.2 %collective-permute-start = (f32[2,32,32,128]{3,2,1,0:T(8,128)}, f32[2,32,32,128]{3,2,1,0:T(8,128)S(1)}, u32[]{:S(2)}, u32[]{:S(2)}) collective-permute-start(f32[2,32,32,128]{3,2,1,0:T(8,128)} %get-tuple-element.88), channel_id=1, source_target_pairs={{0,16},{1,9},{2,18},{3,11},{4,20},{5,13},{6,22},{7,15},{8,24},{9,1... | collective-permute-start | bytes 3145736 | tf_op jit(solution)/shard_map/ppermute | solution.py:596
  11.7 22.8 %collective-permute-start.3 = (f32[2,32,32,128]{3,2,1,0:T(8,128)}, f32[2,32,32,128]{3,2,1,0:T(8,128)}, u32[]{:S(2)}, u32[]{:S(2)}) collective-permute-start(f32[2,32,32,128]{3,2,1,0:T(8,128)} %get-tuple-element.98), channel_id=1, source_target_pairs={{0,16},{1,9},{2,18},{3,11},{4,20},{5,13},{6,22},{7,15},{8,24},{9,1... | collective-permute-start | bytes 3145736 | tf_op jit(solution)/shard_map/ppermute | solution.py:596
  22.6 22.8 %collective-permute-start.5 = (f32[2,32,32,128]{3,2,1,0:T(8,128)S(1)}, f32[2,32,32,128]{3,2,1,0:T(8,128)S(1)}, u32[]{:S(2)}, u32[]{:S(2)}) collective-permute-start(f32[2,32,32,128]{3,2,1,0:T(8,128)S(1)} %get-tuple-element.101), channel_id=1, source_target_pairs={{0,8},{1,17},{2,10},{3,19},{4,12},{5,21},{6,14},{7,23},{8,0},{9,25... | collective-permute-start | bytes 3145736 | tf_op jit(solution)/shard_map/ppermute | solution.py:596
  36.0 15.9 %collective-permute-start.4 = (f32[2,32,32,128]{3,2,1,0:T(8,128)S(1)}, f32[2,32,32,128]{3,2,1,0:T(8,128)S(1)}, u32[]{:S(2)}, u32[]{:S(2)}) collective-permute-start(f32[2,32,32,128]{3,2,1,0:T(8,128)S(1)} %get-tuple-element.100), channel_id=1, source_target_pairs={{0,8},{1,17},{2,10},{3,19},{4,12},{5,21},{6,14},{7,23},{8,0},{9,25... | collective-permute-start | bytes 3145736 | tf_op jit(solution)/shard_map/ppermute | solution.py:596
  49.2 9.2 %collective-permute-start.9 = (f32[1,32,32,128]{3,2,1,0:T(8,128)S(1)}, f32[1,32,32,128]{3,2,1,0:T(8,128)S(1)}, u32[]{:S(2)}, u32[]{:S(2)}) collective-permute-start(f32[1,32,32,128]{3,2,1,0:T(8,128)S(1)} %copy-done.16), channel_id=1, source_target_pairs={{0,16},{1,9},{2,18},{3,11},{4,20},{5,13},{6,22},{7,15},{8,24},{9,1... | collective-permute-start | bytes 1572872 | tf_op jit(solution)/shard_map/ppermute | solution.py:596
  50.7 27.4 %collective-permute-start.11 = (f32[2,32,32,128]{3,2,1,0:T(8,128)S(1)}, f32[2,32,32,128]{3,2,1,0:T(8,128)S(1)}, u32[]{:S(2)}, u32[]{:S(2)}) collective-permute-start(f32[2,32,32,128]{3,2,1,0:T(8,128)S(1)} %get-tuple-element.118), channel_id=1, source_target_pairs={{0,16},{1,9},{2,18},{3,11},{4,20},{5,13},{6,22},{7,15},{8,24},{9,1... | collective-permute-start | bytes 3145736 | tf_op jit(solution)/shard_map/ppermute | solution.py:596
  51.3 13.8 %collective-permute-start.8 = (f32[2,2,8,32,128]{4,3,2,1,0:T(8,128)S(1)}, f32[2,2,8,32,128]{4,3,2,1,0:T(8,128)S(1)}, u32[]{:S(2)}, u32[]{:S(2)}) collective-permute-start(f32[2,2,8,32,128]{4,3,2,1,0:T(8,128)S(1)} %get-tuple-element.112), channel_id=1, source_target_pairs={{0,2},{1,3},{2,0},{3,1},{4,6},{5,7},{6,4},{7,5},{8,10},{9,11},{10,... | collective-permute-start | bytes 1572872 | tf_op jit(solution)/shard_map/ppermute | solution.py:605
  54.1 13.4 %collective-permute-start.7 = (f32[2,2,8,32,128]{4,3,2,1,0:T(8,128)S(1)}, f32[2,2,8,32,128]{4,3,2,1,0:T(8,128)S(1)}, u32[]{:S(2)}, u32[]{:S(2)}) collective-permute-start(f32[2,2,8,32,128]{4,3,2,1,0:T(8,128)S(1)} %get-tuple-element.109), channel_id=1, source_target_pairs={{0,1},{1,0},{2,3},{3,2},{4,5},{5,4},{6,7},{7,6},{8,9},{9,8},{10,11... | collective-permute-start | bytes 1572872 | tf_op jit(solution)/shard_map/ppermute | solution.py:605
  59.0 14.9 %collective-permute-start.12 = (f32[1,32,32,128]{3,2,1,0:T(8,128)S(1)}, f32[1,32,32,128]{3,2,1,0:T(8,128)S(1)}, u32[]{:S(2)}, u32[]{:S(2)}) collective-permute-start(f32[1,32,32,128]{3,2,1,0:T(8,128)S(1)} %get-tuple-element.119), channel_id=1, source_target_pairs={{0,8},{1,17},{2,10},{3,19},{4,12},{5,21},{6,14},{7,23},{8,0},{9,25... | collective-permute-start | bytes 1572872 | tf_op jit(solution)/shard_map/ppermute | solution.py:596
  60.4 38.1 %collective-permute-start.17 = (f32[2,32,32,128]{3,2,1,0:T(8,128)S(1)}, f32[2,32,32,128]{3,2,1,0:T(8,128)S(1)}, u32[]{:S(2)}, u32[]{:S(2)}) collective-permute-start(f32[2,32,32,128]{3,2,1,0:T(8,128)S(1)} %copy-done.15), channel_id=1, source_target_pairs={{0,16},{1,9},{2,18},{3,11},{4,20},{5,13},{6,22},{7,15},{8,24},{9,1... | collective-permute-start | bytes 3145736 | tf_op jit(solution)/shard_map/ppermute | solution.py:596
  67.6 25.5 %collective-permute-start.10 = (f32[2,2,8,32,128]{4,3,2,1,0:T(8,128)S(1)}, f32[2,2,8,32,128]{4,3,2,1,0:T(8,128)S(1)}, u32[]{:S(2)}, u32[]{:S(2)}) collective-permute-start(f32[2,2,8,32,128]{4,3,2,1,0:T(8,128)S(1)} %get-tuple-element.117), channel_id=1, source_target_pairs={{0,2},{1,3},{2,0},{3,1},{4,6},{5,7},{6,4},{7,5},{8,10},{9,11},{10,... | collective-permute-start | bytes 1572872 | tf_op jit(solution)/shard_map/ppermute | solution.py:605
  68.2 27.4 %collective-permute-start.18 = (f32[2,4,128,128]{3,2,1,0:T(8,128)S(1)}, f32[2,4,128,128]{3,2,1,0:T(8,128)S(1)}, u32[]{:S(2)}, u32[]{:S(2)}) collective-permute-start(f32[2,4,128,128]{3,2,1,0:T(8,128)S(1)} %get-tuple-element.132.refs_3_), channel_id=1, source_target_pairs={{0,4},{1,5},{2,6},{3,7},{4,0},{5,1},{6,2},{7,3},{8,12},{9,13},{10,... | collective-permute-start | bytes 1572872 | tf_op jit(solution)/shard_map/ppermute | solution.py:605
  76.6 28.3 %collective-permute-start.15 = (f32[1,32,32,128]{3,2,1,0:T(8,128)S(1)}, f32[1,32,32,128]{3,2,1,0:T(8,128)S(1)}, u32[]{:S(2)}, u32[]{:S(2)}) collective-permute-start(f32[1,32,32,128]{3,2,1,0:T(8,128)S(1)} %get-tuple-element.128), channel_id=1, source_target_pairs={{0,16},{1,9},{2,18},{3,11},{4,20},{5,13},{6,22},{7,15},{8,24},{9,1... | collective-permute-start | bytes 1572872 | tf_op jit(solution)/shard_map/ppermute | solution.py:596
  78.1 23.8 %collective-permute-start.16 = (f32[2,1,8,32,128]{4,3,2,1,0:T(8,128)S(1)}, f32[2,1,8,32,128]{4,3,2,1,0:T(8,128)S(1)}, u32[]{:S(2)}, u32[]{:S(2)}) collective-permute-start(f32[2,1,8,32,128]{4,3,2,1,0:T(8,128)S(1)} %get-tuple-element.130), channel_id=1, source_target_pairs={{0,2},{1,3},{2,0},{3,1},{4,6},{5,7},{6,4},{7,5},{8,10},{9,11},{10,... | collective-permute-start | bytes 786440 | tf_op jit(solution)/shard_map/ppermute | solution.py:605
  93.1 39.3 %collective-permute-start.20 = (f32[2,32,32,128]{3,2,1,0:T(8,128)S(1)}, f32[2,32,32,128]{3,2,1,0:T(8,128)S(1)}, u32[]{:S(2)}, u32[]{:S(2)}) collective-permute-start(f32[2,32,32,128]{3,2,1,0:T(8,128)S(1)} %get-tuple-element.142), channel_id=1, source_target_pairs={{0,8},{1,17},{2,10},{3,19},{4,12},{5,21},{6,14},{7,23},{8,0},{9,25... | collective-permute-start | bytes 3145736 | tf_op jit(solution)/shard_map/ppermute | solution.py:596
  95.6 28.7 %collective-permute-start.14 = (f32[2,4,128,128]{3,2,1,0:T(8,128)S(1)}, f32[2,4,128,128]{3,2,1,0:T(8,128)S(1)}, u32[]{:S(2)}, u32[]{:S(2)}) collective-permute-start(f32[2,4,128,128]{3,2,1,0:T(8,128)S(1)} %get-tuple-element.127.refs_3_), channel_id=1, source_target_pairs={{0,4},{1,5},{2,6},{3,7},{4,0},{5,1},{6,2},{7,3},{8,12},{9,13},{10,... | collective-permute-start | bytes 1572872 | tf_op jit(solution)/shard_map/ppermute | solution.py:605
  98.5 33.7 %collective-permute-start.21 = (f32[2,2,8,32,128]{4,3,2,1,0:T(8,128)S(1)}, f32[2,2,8,32,128]{4,3,2,1,0:T(8,128)S(1)}, u32[]{:S(2)}, u32[]{:S(2)}) collective-permute-start(f32[2,2,8,32,128]{4,3,2,1,0:T(8,128)S(1)} %get-tuple-element.144), channel_id=1, source_target_pairs={{0,2},{1,3},{2,0},{3,1},{4,6},{5,7},{6,4},{7,5},{8,10},{9,11},{10,... | collective-permute-start | bytes 1572872 | tf_op jit(solution)/shard_map/ppermute | solution.py:605
  101.9 42.4 %collective-permute-start.25 = (f32[2,32,32,128]{3,2,1,0:T(8,128)S(1)}, f32[2,32,32,128]{3,2,1,0:T(8,128)S(1)}, u32[]{:S(2)}, u32[]{:S(2)}) collective-permute-start(f32[2,32,32,128]{3,2,1,0:T(8,128)S(1)} %get-tuple-element.154), channel_id=1, source_target_pairs={{0,8},{1,17},{2,10},{3,19},{4,12},{5,21},{6,14},{7,23},{8,0},{9,25... | collective-permute-start | bytes 3145736 | tf_op jit(solution)/shard_map/ppermute | solution.py:596
  104.9 25.5 %collective-permute-start.22 = (f32[1,4,128,128]{3,2,1,0:T(8,128)S(1)}, f32[1,4,128,128]{3,2,1,0:T(8,128)S(1)}, u32[]{:S(2)}, u32[]{:S(2)}) collective-permute-start(f32[1,4,128,128]{3,2,1,0:T(8,128)S(1)} %get-tuple-element.145.refs_3_), channel_id=1, source_target_pairs={{0,4},{1,5},{2,6},{3,7},{4,0},{5,1},{6,2},{7,3},{8,12},{9,13},{10,... | collective-permute-start | bytes 786440 | tf_op jit(solution)/shard_map/ppermute | solution.py:605
  126.7 15.0 %collective-permute-start.19 = (f32[2,2,8,32,128]{4,3,2,1,0:T(8,128)S(1)}, f32[2,2,8,32,128]{4,3,2,1,0:T(8,128)S(1)}, u32[]{:S(2)}, u32[]{:S(2)}) collective-permute-start(f32[2,2,8,32,128]{4,3,2,1,0:T(8,128)S(1)} %get-tuple-element.140), channel_id=1, source_target_pairs={{0,2},{1,3},{2,0},{3,1},{4,6},{5,7},{6,4},{7,5},{8,10},{9,11},{10,... | collective-permute-start | bytes 1572872 | tf_op jit(solution)/shard_map/ppermute | solution.py:605
  132.2 9.6 %collective-permute-start.26 = (f32[2,2,8,32,128]{4,3,2,1,0:T(8,128)S(1)}, f32[2,2,8,32,128]{4,3,2,1,0:T(8,128)S(1)}, u32[]{:S(2)}, u32[]{:S(2)}) collective-permute-start(f32[2,2,8,32,128]{4,3,2,1,0:T(8,128)S(1)} %get-tuple-element.156), channel_id=1, source_target_pairs={{0,1},{1,0},{2,3},{3,2},{4,5},{5,4},{6,7},{7,6},{8,9},{9,8},{10,11... | collective-permute-start | bytes 1572872 | tf_op jit(solution)/shard_map/ppermute | solution.py:605
  132.3 13.7 %collective-permute-start.24 = (f32[2,1,8,32,128]{4,3,2,1,0:T(8,128)S(1)}, f32[2,1,8,32,128]{4,3,2,1,0:T(8,128)S(1)}, u32[]{:S(2)}, u32[]{:S(2)}) collective-permute-start(f32[2,1,8,32,128]{4,3,2,1,0:T(8,128)S(1)} %get-tuple-element.153), channel_id=1, source_target_pairs={{0,2},{1,3},{2,0},{3,1},{4,6},{5,7},{6,4},{7,5},{8,10},{9,11},{10,... | collective-permute-start | bytes 786440 | tf_op jit(solution)/shard_map/ppermute | solution.py:605
  132.4 14.2 %collective-permute-start.28 = (f32[1,32,32,128]{3,2,1,0:T(8,128)S(1)}, f32[1,32,32,128]{3,2,1,0:T(8,128)S(1)}, u32[]{:S(2)}, u32[]{:S(2)}) collective-permute-start(f32[1,32,32,128]{3,2,1,0:T(8,128)S(1)} %get-tuple-element.163), channel_id=1, source_target_pairs={{0,8},{1,17},{2,10},{3,19},{4,12},{5,21},{6,14},{7,23},{8,0},{9,25... | collective-permute-start | bytes 1572872 | tf_op jit(solution)/shard_map/ppermute | solution.py:596
  141.8 8.2 %collective-permute-start.23 = (f32[2,2,8,32,128]{4,3,2,1,0:T(8,128)S(1)}, f32[2,2,8,32,128]{4,3,2,1,0:T(8,128)S(1)}, u32[]{:S(2)}, u32[]{:S(2)}) collective-permute-start(f32[2,2,8,32,128]{4,3,2,1,0:T(8,128)S(1)} %get-tuple-element.150), channel_id=1, source_target_pairs={{0,1},{1,0},{2,3},{3,2},{4,5},{5,4},{6,7},{7,6},{8,9},{9,8},{10,11... | collective-permute-start | bytes 1572872 | tf_op jit(solution)/shard_map/ppermute | solution.py:605
  (28 other events, 209.8 us)

commit v15 on v11

--- a/solution.py
+++ b/solution.py
@@ -9,44 +9,44 @@
 from jax.sharding import PartitionSpec as P
 
 QUAD = 4
-NEAR_SIZES = (2, 2, 1)
+NEAR_SIZES = (2, 1, 2)
 FAR_SIZES = (2, 2, 1)
 ORDER = (
     ("pack", 0),
+    ("pack", 2),
+    ("local", 0),
     ("pack", 1),
     ("pack", 4),
-    ("local", 0),
+    ("pack", 3),
     ("mix", 0),
-    ("local", 1),
-    ("mix", 1),
-    ("pack", 2),
-    ("pack", 3),
+    ("pack", 5),
+    ("mix", 2),
     ("spread", 0),
     ("join", 0),
+    ("spread", 2),
+    ("mix", 1),
+    ("coef", 0),
+    ("join", 2),
     ("spread", 1),
-    ("mix", 2),
-    ("coef", 0),
     ("join", 1),
-    ("spread", 2),
-    ("join", 2),
-    ("pack", 5),
+    ("local", 1),
     ("mix", 4),
-    ("coef", 1),
+    ("coef", 2),
     ("filter", 0),
     ("mix", 3),
-    ("coef", 2),
+    ("coef", 1),
     ("mix", 5),
+    ("filter", 2),
     ("filter", 1),
-    ("filter", 2),
     ("back", 0),
     ("far", 4),
-    ("back", 1),
+    ("back", 2),
     ("near", 0),
     ("far", 3),
-    ("back", 2),
+    ("back", 1),
     ("far", 5),
+    ("near", 1),
     ("near", 2),
-    ("near", 1),
 )
 EDGES = tuple(zip(ORDER[:-1], ORDER[1:]))
 PACK = 60

time: 155 us -> 155 us (level)
  waiting for transfers between devices: 64.7 us -> 70 us
  local copies, waits for them, and re-layouts: 3.33 us -> 1.05 us
  Pallas kernels: 56.2 us -> 54.2 us
    ppermute x12, waiting for transfers between devices: 14.4 us -> 24.9 us  [to_partner(): return lax.ppermute(x, ('inst', 'space'), pairs)]
    ppermute x15, waiting for transfers between devices: 47 us -> 41.6 us  [to_sector(): return lax.ppermute(x, 'space', [(i, i ^ k) for i in range(sectors)])]
    unnamed x35, local copies, waits for them, and re-layouts: 3.33 us -> 1.05 us
    pallas_call x29, Pallas kernels: 42.9 us -> 40.9 us  [call(): pl.pallas_call(kernel, grid=grid, in_specs=list(in_specs) + [ANY] * len(e...]
  transfers between devices with their start and end apart: 29 -> 29, of which waited for: 10 -> 11; matrix products, arithmetic and copies ran while one was open for 0% -> 0% of each run, Pallas kernels for 33% -> 32%
where the time goes in v15:
time: 155 us
  waiting for transfers between devices  70 us (45%)
  Pallas kernels  54.2 us (35%)
  starting transfers between devices  29.4 us (19%)
    ppermute x15, waiting for transfers between devices, to_sector(): return lax.ppermute(x, 'space', [(i, i ^ k) for i in range(sectors)])  41.6 us
    pallas_call x29, Pallas kernels, call(): pl.pallas_call(kernel, grid=grid, in_specs=list(in_specs) + [ANY] * len(e...  40.9 us
    ppermute x12, waiting for transfers between devices, to_partner(): return lax.ppermute(x, ('inst', 'space'), pairs)  24.9 us
    ppermute x12, starting transfers between devices, to_partner(): return lax.ppermute(x, ('inst', 'space'), pairs)  15.3 us
    pallas_call x6, Pallas kernels, table_call(): pl.pallas_call(kernel, grid_spec=pltpu.PrefetchScalarGridSpec(num_scalar_...  13.3 us
    ppermute x15, starting transfers between devices, to_sector(): return lax.ppermute(x, 'space', [(i, i ^ k) for i in range(sectors)])  10.6 us
    ppermute x2, starting transfers between devices, ring(): lax.ppermute(x, 'space', [(i, (i + step) % sectors) for i in range(sector...  3.54 us
    ppermute x2, waiting for transfers between devices, ring(): lax.ppermute(x, 'space', [(i, (i + step) % sectors) for i in range(sector...  3.51 us
  transfers between devices with their start and end apart: 29, of which 11 were waited for; matrix products, arithmetic and copies ran while one was open for 0% of the time, Pallas kernels for 32%

profile of v15, /device:TPU:0, one launch (start us, length us, event | category | flops | bytes accessed | tf_op | source)
XLA Modules:
  0.0 155.1 jit_solution(10521816272903253562)
XLA Ops:
  0.0 2.3 %pack.6 = (f32[2,32,32,128]{3,2,1,0:T(8,128)}, f32[6,1,64,128]{3,2,1,0:T(8,128)}, f32[6,1,64,128]{3,2,1,0:T(8,128)}, f32[8,128]{1,0:T(8,128)}) custom-call(f32[5,32,64,128]{3,2,1,0:T(8,128)} %bitcast.6, f32[5,32,64,128]{3,2,1,0:T(8,128)} %bitcast.7, f32[32,64,128]{2,1,0:T(8,128)} %refs_11_.3, f32[5,32,64,128]{3,2,1,0:T(8,128)} %bitcast.8, ...), custom_call_target="tpu_custom_call" | custom-call | tf_op jit(solution)/shard_map/pack/pallas_call | solution.py:153
  2.4 3.0 %collective-permute-start.3 = (f32[2,32,32,128]{3,2,1,0:T(8,128)}, f32[2,32,32,128]{3,2,1,0:T(8,128)}, u32[]{:S(2)}, u32[]{:S(2)}) collective-permute-start(f32[2,32,32,128]{3,2,1,0:T(8,128)} %get-tuple-element.94), channel_id=1, source_target_pairs={{0,16},{1,9},{2,18},{3,11},{4,20},{5,13},{6,22},{7,15},{8,24},{9,1... | collective-permute-start | bytes 3145736 | tf_op jit(solution)/shard_map/ppermute | solution.py:596
  5.4 2.2 %pack.7 = (f32[2,32,32,128]{3,2,1,0:T(8,128)}, f32[8,128]{1,0:T(8,128)}) custom-call(f32[5,32,64,128]{3,2,1,0:T(8,128)} %bitcast.9, f32[8,128]{1,0:T(8,128)} %get-tuple-element.88.refs_1_), custom_call_target="tpu_custom_call" | custom-call | tf_op jit(solution)/shard_map/pack/pallas_call | solution.py:153
  8.4 8.6 %local_part.2 = (f32[5,32,32,128]{3,2,1,0:T(8,128)}, f32[8,128]{1,0:T(8,128)S(1)}) custom-call(f32[5,5]{1,0:T(8,128)S(1)} %copy-done.6, f32[5]{0:T(128)S(1)} %copy-done.5, s32[5,3]{1,0:T(8,128)S(1)} %copy.23.refs_2_, f32[5,32,64,128]{3,2,1,0:T(8,128)} %bitcast.10, f32[5,32,64,128]{3,2,1,0:T(8,128)} %bitcast.11, f32[5,32,64,128]{3,2,1,0:T(8,128)} %bitcast.12, ...), custom_call_target="tpu_custom_call" | custom-call | tf_op jit(solution)/shard_map/local_part/pallas_call | solution.py:153
  22.0 15.4 %collective-permute-done.2.refs_3_.refs_12_ = f32[2,32,32,128]{3,2,1,0:T(8,128)S(1)} collective-permute-done((f32[2,32,32,128]{3,2,1,0:T(8,128)}, f32[2,32,32,128]{3,2,1,0:T(8,128)S(1)}, u32[]{:S(2)}, u32[]{:S(2)}) %collective-permute-start.2) | collective-permute-done | bytes 1048608 | tf_op jit(solution)/shard_map/ppermute | solution.py:596
  38.2 2.3 %collective-permute-start.4 = (f32[2,32,32,128]{3,2,1,0:T(8,128)S(1)}, f32[2,32,32,128]{3,2,1,0:T(8,128)S(1)}, u32[]{:S(2)}, u32[]{:S(2)}) collective-permute-start(f32[2,32,32,128]{3,2,1,0:T(8,128)S(1)} %get-tuple-element.101), channel_id=1, source_target_pairs={{0,8},{1,17},{2,10},{3,19},{4,12},{5,21},{6,14},{7,23},{8,0},{9,25... | collective-permute-start | bytes 3145736 | tf_op jit(solution)/shard_map/ppermute | solution.py:596
  40.5 3.5 %collective-permute-start.1 = (f32[6,1,64,128]{3,2,1,0:T(8,128)S(1)}, f32[6,1,64,128]{3,2,1,0:T(8,128)S(1)}, u32[]{:S(2)}, u32[]{:S(2)}) collective-permute-start(f32[6,1,64,128]{3,2,1,0:T(8,128)S(1)} %copy-done.11), channel_id=1, source_target_pairs={{0,7},{1,0},{2,1},{3,2},{4,3},{5,4},{6,5},{7,6},{8,15},{9,8},{10,9... | collective-permute-start | bytes 589832 | tf_op jit(solution)/shard_map/ppermute | solution.py:608
  44.1 3.5 %collective-permute-done.refs_5_.refs_7_ = f32[6,1,64,128]{3,2,1,0:T(8,128)S(1)} collective-permute-done((f32[6,1,64,128]{3,2,1,0:T(8,128)S(1)}, f32[6,1,64,128]{3,2,1,0:T(8,128)S(1)}, u32[]{:S(2)}, u32[]{:S(2)}) %collective-permute-start) | collective-permute-done | bytes 196640 | tf_op jit(solution)/shard_map/ppermute | solution.py:608
  47.6 2.2 %spread.3 = (f32[2,8,32,128]{3,2,1,0:T(8,128)S(1)}, f32[2,2,8,32,128]{4,3,2,1,0:T(8,128)S(1)}, f32[2,2,8,32,128]{4,3,2,1,0:T(8,128)S(1)}, f32[8,128]{1,0:T(8,128)S(1)}) custom-call(s32[22]{0:T(128)S(1)} %pad_add_fusion.refs_0_, f32[71]{0:T(128)S(1)} %copy-done.4, f32[5,32,32,128]{3,2,1,0:T(8,128)S(1)} %copy-done.1, f32[5]{0:T(128)S(1)} %copy-done.5, ...), custom_call_target="tpu_custom_call" | custom-call | tf_op jit(solution)/shard_map/spread/pallas_call | solution.py:153
  56.4 4.7 %collective-permute-done.9.refs_3_.refs_12_ = f32[1,32,32,128]{3,2,1,0:T(8,128)S(1)} collective-permute-done((f32[1,32,32,128]{3,2,1,0:T(8,128)S(1)}, f32[1,32,32,128]{3,2,1,0:T(8,128)S(1)}, u32[]{:S(2)}, u32[]{:S(2)}) %collective-permute-start.9) | collective-permute-done | bytes 524320 | tf_op jit(solution)/shard_map/ppermute | solution.py:596
  63.8 3.9 %collective-permute-done.8.refs_5_.refs_7_ = f32[2,2,8,32,128]{4,3,2,1,0:T(8,128)S(1)} collective-permute-done((f32[2,2,8,32,128]{4,3,2,1,0:T(8,128)S(1)}, f32[2,2,8,32,128]{4,3,2,1,0:T(8,128)S(1)}, u32[]{:S(2)}, u32[]{:S(2)}) %collective-permute-start.8) | collective-permute-done | bytes 524320 | tf_op jit(solution)/shard_map/ppermute | solution.py:605
  67.7 2.4 %coefficients.3 = (f32[2,4,128,128]{3,2,1,0:T(8,128)S(1)}, f32[8,128]{1,0:T(8,128)S(1)}) custom-call(s32[22]{0:T(128)S(1)} %pad_add_fusion.refs_0_, f32[71]{0:T(128)S(1)} %copy-done.4, f32[2,16,128,128]{3,2,1,0:T(8,128)S(1)} %copy-done.3, f32[2,8,32,128]{3,2,1,0:T(8,128)S(1)} %get-tuple-element.111.refs_3_.refs_5_, ...), custom_call_target="tpu_custom_call" | custom-call | tf_op jit(solution)/shard_map/coefficients/pallas_call | solution.py:432
  72.6 4.0 %collective-permute-done.12.refs_13_ = f32[1,32,32,128]{3,2,1,0:T(8,128)S(1)} collective-permute-done((f32[1,32,32,128]{3,2,1,0:T(8,128)S(1)}, f32[1,32,32,128]{3,2,1,0:T(8,128)S(1)}, u32[]{:S(2)}, u32[]{:S(2)}) %collective-permute-start.12) | collective-permute-done | bytes 524320 | tf_op jit(solution)/shard_map/ppermute | solution.py:596
  80.8 5.5 %local_part.3 = (f32[5,32,32,128]{3,2,1,0:T(8,128)S(1)}, f32[8,128]{1,0:T(8,128)S(1)}) custom-call(f32[5,5]{1,0:T(8,128)S(1)} %copy-done.6, f32[5]{0:T(128)S(1)} %copy-done.5, s32[5,3]{1,0:T(8,128)S(1)} %copy.23.refs_2_, f32[5,32,64,128]{3,2,1,0:T(8,128)S(1)} %bitcast.29, f32[5,32,64,128]{3,2,1,0:T(8,128)S(1)} %bitcast.30, f32[5,32,64,128]{3,2,1,0:T(8,128)S(1)} %bitcast.31, ...), custom_call_target="tpu_custom_call" | custom-call | tf_op jit(solution)/shard_map/local_part/pallas_call | solution.py:153
  87.8 7.9 %collective-permute-done.10.refs_5_.refs_7_ = f32[2,2,8,32,128]{4,3,2,1,0:T(8,128)S(1)} collective-permute-done((f32[2,2,8,32,128]{4,3,2,1,0:T(8,128)S(1)}, f32[2,2,8,32,128]{4,3,2,1,0:T(8,128)S(1)}, u32[]{:S(2)}, u32[]{:S(2)}) %collective-permute-start.10) | collective-permute-done | bytes 524320 | tf_op jit(solution)/shard_map/ppermute | solution.py:605
  95.8 2.4 %coefficients.4 = (f32[2,4,128,128]{3,2,1,0:T(8,128)S(1)}, f32[8,128]{1,0:T(8,128)S(1)}) custom-call(s32[22]{0:T(128)S(1)} %pad_add_fusion.refs_0_, f32[71]{0:T(128)S(1)} %copy-done.4, f32[2,16,128,128]{3,2,1,0:T(8,128)S(1)} %copy-done.3, f32[2,8,32,128]{3,2,1,0:T(8,128)S(1)} %get-tuple-element.108.refs_3_.refs_5_, ...), custom_call_target="tpu_custom_call" | custom-call | tf_op jit(solution)/shard_map/coefficients/pallas_call | solution.py:432
  98.7 2.5 %filtered.3 = (f32[2,8,32,128]{3,2,1,0:T(8,128)S(1)}, f32[2,2,8,32,128]{4,3,2,1,0:T(8,128)S(1)}, f32[2,2,8,32,128]{4,3,2,1,0:T(8,128)S(1)}, f32[8,128]{1,0:T(8,128)S(1)}) custom-call(s32[22]{0:T(128)S(1)} %pad_add_fusion.refs_0_, f32[71]{0:T(128)S(1)} %copy-done.4, f32[2,16,128,128]{3,2,1,0:T(8,128)S(1)} %copy-done.2, ...), custom_call_target="tpu_custom_call" | custom-call | tf_op jit(solution)/shard_map/filtered/pallas_call | solution.py:432
  101.2 2.6 %collective-permute-start.21 = (f32[2,2,8,32,128]{4,3,2,1,0:T(8,128)S(1)}, f32[2,2,8,32,128]{4,3,2,1,0:T(8,128)S(1)}, u32[]{:S(2)}, u32[]{:S(2)}) collective-permute-start(f32[2,2,8,32,128]{4,3,2,1,0:T(8,128)S(1)} %get-tuple-element.144), channel_id=1, source_target_pairs={{0,2},{1,3},{2,0},{3,1},{4,6},{5,7},{6,4},{7,5},{8,10},{9,11},{10,... | collective-permute-start | bytes 1572872 | tf_op jit(solution)/shard_map/ppermute | solution.py:605
  109.2 17.7 %collective-permute-done.14.refs_4_ = f32[2,4,128,128]{3,2,1,0:T(8,128)S(1)} collective-permute-done((f32[2,4,128,128]{3,2,1,0:T(8,128)S(1)}, f32[2,4,128,128]{3,2,1,0:T(8,128)S(1)}, u32[]{:S(2)}, u32[]{:S(2)}) %collective-permute-start.14) | collective-permute-done | bytes 524320 | tf_op jit(solution)/shard_map/ppermute | solution.py:605
  126.9 2.5 %filtered.4 = (f32[2,8,32,128]{3,2,1,0:T(8,128)S(1)}, f32[2,2,8,32,128]{4,3,2,1,0:T(8,128)S(1)}, f32[2,2,8,32,128]{4,3,2,1,0:T(8,128)S(1)}, f32[8,128]{1,0:T(8,128)S(1)}) custom-call(s32[22]{0:T(128)S(1)} %pad_add_fusion.refs_0_, f32[71]{0:T(128)S(1)} %copy-done.4, f32[2,16,128,128]{3,2,1,0:T(8,128)S(1)} %copy-done.2, ...), custom_call_target="tpu_custom_call" | custom-call | tf_op jit(solution)/shard_map/filtered/pallas_call | solution.py:432
  129.5 3.6 %collective-permute-done.22.refs_4_ = f32[1,4,128,128]{3,2,1,0:T(8,128)S(1)} collective-permute-done((f32[1,4,128,128]{3,2,1,0:T(8,128)S(1)}, f32[1,4,128,128]{3,2,1,0:T(8,128)S(1)}, u32[]{:S(2)}, u32[]{:S(2)}) %collective-permute-start.22) | collective-permute-done | bytes 262176 | tf_op jit(solution)/shard_map/ppermute | solution.py:605
  137.6 6.8 %collective-permute-done.19.refs_1_.refs_4_ = f32[2,2,8,32,128]{4,3,2,1,0:T(8,128)S(1)} collective-permute-done((f32[2,2,8,32,128]{4,3,2,1,0:T(8,128)S(1)}, f32[2,2,8,32,128]{4,3,2,1,0:T(8,128)S(1)}, u32[]{:S(2)}, u32[]{:S(2)}) %collective-permute-start.19) | collective-permute-done | bytes 524320 | tf_op jit(solution)/shard_map/ppermute | solution.py:605
  144.6 2.5 %place_near.3 = (f32[5,32,64,128]{3,2,1,0:T(8,128)}, f32[8,128]{1,0:T(8,128)S(1)}) custom-call(s32[22]{0:T(128)S(1)} %pad_add_fusion.refs_0_, f32[71]{0:T(128)S(1)} %copy-done.4, f32[2,8,32,128]{3,2,1,0:T(8,128)S(1)} %get-tuple-element.155.refs_2_, f32[2,2,8,32,128]{4,3,2,1,0:T(8,128)S(1)} %collective-permute-done.26.refs_3_, ...), custom_call_target="tpu_custom_call", output_to_operand_aliasing={{0}: (5, {})} | custom-call | tf_op jit(solution)/shard_map/place_near/pallas_call | solution.py:153
  152.7 2.5 %place_near.5 = (f32[5,32,64,128]{3,2,1,0:T(8,128)}, f32[8,128]{1,0:T(8,128)}) custom-call(s32[22]{0:T(128)S(1)} %pad_add_fusion.refs_0_, f32[71]{0:T(128)S(1)} %copy-done.4, f32[2,8,32,128]{3,2,1,0:T(8,128)S(1)} %get-tuple-element.138.refs_2_, f32[2,2,8,32,128]{4,3,2,1,0:T(8,128)S(1)} %collective-permute-done.23.refs_3_, ...), custom_call_target="tpu_custom_call", output_to_operand_aliasing={{0}: (5, {})} | custom-call | tf_op jit(solution)/shard_map/place_near/pallas_call | solution.py:153
  (107 shorter events, 40.0 us)
Async XLA Ops:
  2.4 16.1 %collective-permute-start.3 = (f32[2,32,32,128]{3,2,1,0:T(8,128)}, f32[2,32,32,128]{3,2,1,0:T(8,128)}, u32[]{:S(2)}, u32[]{:S(2)}) collective-permute-start(f32[2,32,32,128]{3,2,1,0:T(8,128)} %get-tuple-element.94), channel_id=1, source_target_pairs={{0,16},{1,9},{2,18},{3,11},{4,20},{5,13},{6,22},{7,15},{8,24},{9,1... | collective-permute-start | bytes 3145736 | tf_op jit(solution)/shard_map/ppermute | solution.py:596
  7.6 29.8 %collective-permute-start.2 = (f32[2,32,32,128]{3,2,1,0:T(8,128)}, f32[2,32,32,128]{3,2,1,0:T(8,128)S(1)}, u32[]{:S(2)}, u32[]{:S(2)}) collective-permute-start(f32[2,32,32,128]{3,2,1,0:T(8,128)} %get-tuple-element.93), channel_id=1, source_target_pairs={{0,16},{1,9},{2,18},{3,11},{4,20},{5,13},{6,22},{7,15},{8,24},{9,1... | collective-permute-start | bytes 3145736 | tf_op jit(solution)/shard_map/ppermute | solution.py:596
  19.9 27.7 %collective-permute-start.5 = (f32[2,32,32,128]{3,2,1,0:T(8,128)S(1)}, f32[2,32,32,128]{3,2,1,0:T(8,128)S(1)}, u32[]{:S(2)}, u32[]{:S(2)}) collective-permute-start(f32[2,32,32,128]{3,2,1,0:T(8,128)S(1)} %get-tuple-element.102), channel_id=1, source_target_pairs={{0,8},{1,17},{2,10},{3,19},{4,12},{5,21},{6,14},{7,23},{8,0},{9,25... | collective-permute-start | bytes 3145736 | tf_op jit(solution)/shard_map/ppermute | solution.py:596
  38.2 16.4 %collective-permute-start.4 = (f32[2,32,32,128]{3,2,1,0:T(8,128)S(1)}, f32[2,32,32,128]{3,2,1,0:T(8,128)S(1)}, u32[]{:S(2)}, u32[]{:S(2)}) collective-permute-start(f32[2,32,32,128]{3,2,1,0:T(8,128)S(1)} %get-tuple-element.101), channel_id=1, source_target_pairs={{0,8},{1,17},{2,10},{3,19},{4,12},{5,21},{6,14},{7,23},{8,0},{9,25... | collective-permute-start | bytes 3145736 | tf_op jit(solution)/shard_map/ppermute | solution.py:596
  51.9 9.2 %collective-permute-start.9 = (f32[1,32,32,128]{3,2,1,0:T(8,128)S(1)}, f32[1,32,32,128]{3,2,1,0:T(8,128)S(1)}, u32[]{:S(2)}, u32[]{:S(2)}) collective-permute-start(f32[1,32,32,128]{3,2,1,0:T(8,128)S(1)} %get-tuple-element.113), channel_id=1, source_target_pairs={{0,16},{1,9},{2,18},{3,11},{4,20},{5,13},{6,22},{7,15},{8,24},{9,1... | collective-permute-start | bytes 1572872 | tf_op jit(solution)/shard_map/ppermute | solution.py:596
  53.4 32.9 %collective-permute-start.11 = (f32[2,32,32,128]{3,2,1,0:T(8,128)S(1)}, f32[2,32,32,128]{3,2,1,0:T(8,128)S(1)}, u32[]{:S(2)}, u32[]{:S(2)}) collective-permute-start(f32[2,32,32,128]{3,2,1,0:T(8,128)S(1)} %get-tuple-element.118), channel_id=1, source_target_pairs={{0,16},{1,9},{2,18},{3,11},{4,20},{5,13},{6,22},{7,15},{8,24},{9,1... | collective-permute-start | bytes 3145736 | tf_op jit(solution)/shard_map/ppermute | solution.py:596
  54.0 13.8 %collective-permute-start.8 = (f32[2,2,8,32,128]{4,3,2,1,0:T(8,128)S(1)}, f32[2,2,8,32,128]{4,3,2,1,0:T(8,128)S(1)}, u32[]{:S(2)}, u32[]{:S(2)}) collective-permute-start(f32[2,2,8,32,128]{4,3,2,1,0:T(8,128)S(1)} %get-tuple-element.112), channel_id=1, source_target_pairs={{0,2},{1,3},{2,0},{3,1},{4,6},{5,7},{6,4},{7,5},{8,10},{9,11},{10,... | collective-permute-start | bytes 1572872 | tf_op jit(solution)/shard_map/ppermute | solution.py:605
  56.3 13.9 %collective-permute-start.7 = (f32[2,2,8,32,128]{4,3,2,1,0:T(8,128)S(1)}, f32[2,2,8,32,128]{4,3,2,1,0:T(8,128)S(1)}, u32[]{:S(2)}, u32[]{:S(2)}) collective-permute-start(f32[2,2,8,32,128]{4,3,2,1,0:T(8,128)S(1)} %get-tuple-element.109), channel_id=1, source_target_pairs={{0,1},{1,0},{2,3},{3,2},{4,5},{5,4},{6,7},{7,6},{8,9},{9,8},{10,11... | collective-permute-start | bytes 1572872 | tf_op jit(solution)/shard_map/ppermute | solution.py:605
  61.7 14.9 %collective-permute-start.12 = (f32[1,32,32,128]{3,2,1,0:T(8,128)S(1)}, f32[1,32,32,128]{3,2,1,0:T(8,128)S(1)}, u32[]{:S(2)}, u32[]{:S(2)}) collective-permute-start(f32[1,32,32,128]{3,2,1,0:T(8,128)S(1)} %get-tuple-element.119), channel_id=1, source_target_pairs={{0,8},{1,17},{2,10},{3,19},{4,12},{5,21},{6,14},{7,23},{8,0},{9,25... | collective-permute-start | bytes 1572872 | tf_op jit(solution)/shard_map/ppermute | solution.py:596
  61.8 39.3 %collective-permute-start.17 = (f32[2,32,32,128]{3,2,1,0:T(8,128)S(1)}, f32[2,32,32,128]{3,2,1,0:T(8,128)S(1)}, u32[]{:S(2)}, u32[]{:S(2)}) collective-permute-start(f32[2,32,32,128]{3,2,1,0:T(8,128)S(1)} %get-tuple-element.131), channel_id=1, source_target_pairs={{0,16},{1,9},{2,18},{3,11},{4,20},{5,13},{6,22},{7,15},{8,24},{9,1... | collective-permute-start | bytes 3145736 | tf_op jit(solution)/shard_map/ppermute | solution.py:596
  70.3 25.5 %collective-permute-start.10 = (f32[2,2,8,32,128]{4,3,2,1,0:T(8,128)S(1)}, f32[2,2,8,32,128]{4,3,2,1,0:T(8,128)S(1)}, u32[]{:S(2)}, u32[]{:S(2)}) collective-permute-start(f32[2,2,8,32,128]{4,3,2,1,0:T(8,128)S(1)} %get-tuple-element.117), channel_id=1, source_target_pairs={{0,2},{1,3},{2,0},{3,1},{4,6},{5,7},{6,4},{7,5},{8,10},{9,11},{10,... | collective-permute-start | bytes 1572872 | tf_op jit(solution)/shard_map/ppermute | solution.py:605
  70.9 27.4 %collective-permute-start.18 = (f32[2,4,128,128]{3,2,1,0:T(8,128)S(1)}, f32[2,4,128,128]{3,2,1,0:T(8,128)S(1)}, u32[]{:S(2)}, u32[]{:S(2)}) collective-permute-start(f32[2,4,128,128]{3,2,1,0:T(8,128)S(1)} %get-tuple-element.132.refs_3_), channel_id=1, source_target_pairs={{0,4},{1,5},{2,6},{3,7},{4,0},{5,1},{6,2},{7,3},{8,12},{9,13},{10,... | collective-permute-start | bytes 1572872 | tf_op jit(solution)/shard_map/ppermute | solution.py:605
  79.3 28.3 %collective-permute-start.15 = (f32[1,32,32,128]{3,2,1,0:T(8,128)S(1)}, f32[1,32,32,128]{3,2,1,0:T(8,128)S(1)}, u32[]{:S(2)}, u32[]{:S(2)}) collective-permute-start(f32[1,32,32,128]{3,2,1,0:T(8,128)S(1)} %get-tuple-element.128), channel_id=1, source_target_pairs={{0,16},{1,9},{2,18},{3,11},{4,20},{5,13},{6,22},{7,15},{8,24},{9,1... | collective-permute-start | bytes 1572872 | tf_op jit(solution)/shard_map/ppermute | solution.py:596
  86.3 18.3 %collective-permute-start.16 = (f32[2,1,8,32,128]{4,3,2,1,0:T(8,128)S(1)}, f32[2,1,8,32,128]{4,3,2,1,0:T(8,128)S(1)}, u32[]{:S(2)}, u32[]{:S(2)}) collective-permute-start(f32[2,1,8,32,128]{4,3,2,1,0:T(8,128)S(1)} %get-tuple-element.130), channel_id=1, source_target_pairs={{0,2},{1,3},{2,0},{3,1},{4,6},{5,7},{6,4},{7,5},{8,10},{9,11},{10,... | collective-permute-start | bytes 786440 | tf_op jit(solution)/shard_map/ppermute | solution.py:605
  95.8 39.4 %collective-permute-start.20 = (f32[2,32,32,128]{3,2,1,0:T(8,128)S(1)}, f32[2,32,32,128]{3,2,1,0:T(8,128)S(1)}, u32[]{:S(2)}, u32[]{:S(2)}) collective-permute-start(f32[2,32,32,128]{3,2,1,0:T(8,128)S(1)} %get-tuple-element.142), channel_id=1, source_target_pairs={{0,8},{1,17},{2,10},{3,19},{4,12},{5,21},{6,14},{7,23},{8,0},{9,25... | collective-permute-start | bytes 3145736 | tf_op jit(solution)/shard_map/ppermute | solution.py:596
  98.3 28.6 %collective-permute-start.14 = (f32[2,4,128,128]{3,2,1,0:T(8,128)S(1)}, f32[2,4,128,128]{3,2,1,0:T(8,128)S(1)}, u32[]{:S(2)}, u32[]{:S(2)}) collective-permute-start(f32[2,4,128,128]{3,2,1,0:T(8,128)S(1)} %get-tuple-element.127.refs_3_), channel_id=1, source_target_pairs={{0,4},{1,5},{2,6},{3,7},{4,0},{5,1},{6,2},{7,3},{8,12},{9,13},{10,... | collective-permute-start | bytes 1572872 | tf_op jit(solution)/shard_map/ppermute | solution.py:605
  101.2 33.7 %collective-permute-start.21 = (f32[2,2,8,32,128]{4,3,2,1,0:T(8,128)S(1)}, f32[2,2,8,32,128]{4,3,2,1,0:T(8,128)S(1)}, u32[]{:S(2)}, u32[]{:S(2)}) collective-permute-start(f32[2,2,8,32,128]{4,3,2,1,0:T(8,128)S(1)} %get-tuple-element.144), channel_id=1, source_target_pairs={{0,2},{1,3},{2,0},{3,1},{4,6},{5,7},{6,4},{7,5},{8,10},{9,11},{10,... | collective-permute-start | bytes 1572872 | tf_op jit(solution)/shard_map/ppermute | solution.py:605
  104.6 42.4 %collective-permute-start.25 = (f32[2,32,32,128]{3,2,1,0:T(8,128)S(1)}, f32[2,32,32,128]{3,2,1,0:T(8,128)S(1)}, u32[]{:S(2)}, u32[]{:S(2)}) collective-permute-start(f32[2,32,32,128]{3,2,1,0:T(8,128)S(1)} %get-tuple-element.154), channel_id=1, source_target_pairs={{0,8},{1,17},{2,10},{3,19},{4,12},{5,21},{6,14},{7,23},{8,0},{9,25... | collective-permute-start | bytes 3145736 | tf_op jit(solution)/shard_map/ppermute | solution.py:596
  107.6 25.5 %collective-permute-start.22 = (f32[1,4,128,128]{3,2,1,0:T(8,128)S(1)}, f32[1,4,128,128]{3,2,1,0:T(8,128)S(1)}, u32[]{:S(2)}, u32[]{:S(2)}) collective-permute-start(f32[1,4,128,128]{3,2,1,0:T(8,128)S(1)} %get-tuple-element.145.refs_3_), channel_id=1, source_target_pairs={{0,4},{1,5},{2,6},{3,7},{4,0},{5,1},{6,2},{7,3},{8,12},{9,13},{10,... | collective-permute-start | bytes 786440 | tf_op jit(solution)/shard_map/ppermute | solution.py:605
  129.4 15.0 %collective-permute-start.19 = (f32[2,2,8,32,128]{4,3,2,1,0:T(8,128)S(1)}, f32[2,2,8,32,128]{4,3,2,1,0:T(8,128)S(1)}, u32[]{:S(2)}, u32[]{:S(2)}) collective-permute-start(f32[2,2,8,32,128]{4,3,2,1,0:T(8,128)S(1)} %get-tuple-element.140), channel_id=1, source_target_pairs={{0,2},{1,3},{2,0},{3,1},{4,6},{5,7},{6,4},{7,5},{8,10},{9,11},{10,... | collective-permute-start | bytes 1572872 | tf_op jit(solution)/shard_map/ppermute | solution.py:605
  135.0 9.6 %collective-permute-start.26 = (f32[2,2,8,32,128]{4,3,2,1,0:T(8,128)S(1)}, f32[2,2,8,32,128]{4,3,2,1,0:T(8,128)S(1)}, u32[]{:S(2)}, u32[]{:S(2)}) collective-permute-start(f32[2,2,8,32,128]{4,3,2,1,0:T(8,128)S(1)} %get-tuple-element.156), channel_id=1, source_target_pairs={{0,1},{1,0},{2,3},{3,2},{4,5},{5,4},{6,7},{7,6},{8,9},{9,8},{10,11... | collective-permute-start | bytes 1572872 | tf_op jit(solution)/shard_map/ppermute | solution.py:605
  135.0 13.7 %collective-permute-start.24 = (f32[2,1,8,32,128]{4,3,2,1,0:T(8,128)S(1)}, f32[2,1,8,32,128]{4,3,2,1,0:T(8,128)S(1)}, u32[]{:S(2)}, u32[]{:S(2)}) collective-permute-start(f32[2,1,8,32,128]{4,3,2,1,0:T(8,128)S(1)} %get-tuple-element.153), channel_id=1, source_target_pairs={{0,2},{1,3},{2,0},{3,1},{4,6},{5,7},{6,4},{7,5},{8,10},{9,11},{10,... | collective-permute-start | bytes 786440 | tf_op jit(solution)/shard_map/ppermute | solution.py:605
  135.1 14.2 %collective-permute-start.28 = (f32[1,32,32,128]{3,2,1,0:T(8,128)S(1)}, f32[1,32,32,128]{3,2,1,0:T(8,128)S(1)}, u32[]{:S(2)}, u32[]{:S(2)}) collective-permute-start(f32[1,32,32,128]{3,2,1,0:T(8,128)S(1)} %get-tuple-element.163), channel_id=1, source_target_pairs={{0,8},{1,17},{2,10},{3,19},{4,12},{5,21},{6,14},{7,23},{8,0},{9,25... | collective-permute-start | bytes 1572872 | tf_op jit(solution)/shard_map/ppermute | solution.py:596
  144.5 8.2 %collective-permute-start.23 = (f32[2,2,8,32,128]{4,3,2,1,0:T(8,128)S(1)}, f32[2,2,8,32,128]{4,3,2,1,0:T(8,128)S(1)}, u32[]{:S(2)}, u32[]{:S(2)}) collective-permute-start(f32[2,2,8,32,128]{4,3,2,1,0:T(8,128)S(1)} %get-tuple-element.150), channel_id=1, source_target_pairs={{0,1},{1,0},{2,3},{3,2},{4,5},{5,4},{6,7},{7,6},{8,9},{9,8},{10,11... | collective-permute-start | bytes 1572872 | tf_op jit(solution)/shard_map/ppermute | solution.py:605
  (22 other events, 171.1 us)

commit v16 on v12

--- a/solution.py
+++ b/solution.py
@@ -10,17 +10,17 @@
 
 QUAD = 4
 NEAR_SIZES = (2, 2, 1)
-FAR_SIZES = (2, 2, 1)
+FAR_SIZES = (1, 2, 2)
 ORDER = (
     ("pack", 0),
+    ("pack", 5),
     ("pack", 3),
+    ("pack", 1),
+    ("local", 0),
+    ("pack", 4),
     ("pack", 2),
-    ("pack", 1),
-    ("local", 1),
     ("mix", 0),
-    ("local", 0),
     ("mix", 1),
-    ("pack", 4),
     ("spread", 0),
     ("join", 0),
     ("spread", 1),
@@ -28,23 +28,23 @@
     ("coef", 0),
     ("join", 1),
     ("spread", 2),
-    ("pack", 5),
     ("join", 2),
-    ("mix", 4),
+    ("mix", 5),
     ("coef", 1),
     ("filter", 0),
+    ("mix", 4),
+    ("coef", 2),
     ("mix", 3),
-    ("coef", 2),
-    ("mix", 5),
+    ("local", 1),
     ("filter", 1),
     ("filter", 2),
     ("back", 0),
-    ("far", 4),
+    ("far", 5),
     ("back", 1),
     ("near", 0),
+    ("far", 4),
+    ("back", 2),
     ("far", 3),
-    ("back", 2),
-    ("far", 5),
     ("near", 2),
     ("near", 1),
 )

time: 150 us -> 152 us (1.013)
  waiting for transfers between devices: 53.1 us -> 58.9 us
  local copies, waits for them, and re-layouts: 6.35 us -> 1.23 us
  Pallas kernels: 56.6 us -> 58.2 us
    ppermute x12, waiting for transfers between devices: 9.6 us -> 17.3 us  [to_partner(): return lax.ppermute(x, ('inst', 'space'), pairs)]
    unnamed x43 -> x39, local copies, waits for them, and re-layouts: 6.35 us -> 1.23 us
    ppermute x15, waiting for transfers between devices: 40.2 us -> 38.1 us  [to_sector(): return lax.ppermute(x, 'space', [(i, i ^ k) for i in range(sectors)])]
    pallas_call x29, Pallas kernels: 43.4 us -> 44.9 us  [call(): pl.pallas_call(kernel, grid=grid, in_specs=list(in_specs) + [ANY] * len(e...]
  transfers between devices with their start and end apart: 29 -> 29, of which waited for: 10 -> 11; matrix products, arithmetic and copies ran while one was open for 0% -> 0% of each run, Pallas kernels for 35% -> 35%
where the time goes in v16:
time: 152 us; the launch traced here: 151 us
  waiting for transfers between devices  58.9 us (39%)
  Pallas kernels  58.2 us (38%)
  starting transfers between devices  32.6 us (21%)
    pallas_call x29, Pallas kernels, call(): pl.pallas_call(kernel, grid=grid, in_specs=list(in_specs) + [ANY] * len(e...  44.9 us
    ppermute x15, waiting for transfers between devices, to_sector(): return lax.ppermute(x, 'space', [(i, i ^ k) for i in range(sectors)])  38.1 us
    ppermute x12, starting transfers between devices, to_partner(): return lax.ppermute(x, ('inst', 'space'), pairs)  17.3 us
    ppermute x12, waiting for transfers between devices, to_partner(): return lax.ppermute(x, ('inst', 'space'), pairs)  17.3 us
    pallas_call x6, Pallas kernels, table_call(): pl.pallas_call(kernel, grid_spec=pltpu.PrefetchScalarGridSpec(num_scalar_...  13.3 us
    ppermute x15, starting transfers between devices, to_sector(): return lax.ppermute(x, 'space', [(i, i ^ k) for i in range(sectors)])  11.8 us
    ppermute x2, starting transfers between devices, ring(): lax.ppermute(x, 'space', [(i, (i + step) % sectors) for i in range(sector...  3.54 us
    ppermute x2, waiting for transfers between devices, ring(): lax.ppermute(x, 'space', [(i, (i + step) % sectors) for i in range(sector...  3.51 us
  transfers between devices with their start and end apart: 29, of which 11 were waited for; matrix products, arithmetic and copies ran while one was open for 0% of the time, Pallas kernels for 35%

profile of v16, /device:TPU:0, one launch (start us, length us, event | category | flops | bytes accessed | tf_op | source)
XLA Modules:
  0.0 151.4 jit_solution(4845370156611707715)
XLA Ops:
  0.0 2.3 %pack.6 = (f32[2,32,32,128]{3,2,1,0:T(8,128)}, f32[6,1,64,128]{3,2,1,0:T(8,128)}, f32[6,1,64,128]{3,2,1,0:T(8,128)}, f32[8,128]{1,0:T(8,128)}) custom-call(f32[5,32,64,128]{3,2,1,0:T(8,128)} %bitcast.6, f32[5,32,64,128]{3,2,1,0:T(8,128)} %bitcast.7, f32[32,64,128]{2,1,0:T(8,128)} %refs_11_.3, f32[5,32,64,128]{3,2,1,0:T(8,128)} %bitcast.8, ...), custom_call_target="tpu_custom_call" | custom-call | tf_op jit(solution)/shard_map/pack/pallas_call | solution.py:153
  2.3 3.0 %collective-permute-start.3 = (f32[2,32,32,128]{3,2,1,0:T(8,128)}, f32[2,32,32,128]{3,2,1,0:T(8,128)}, u32[]{:S(2)}, u32[]{:S(2)}) collective-permute-start(f32[2,32,32,128]{3,2,1,0:T(8,128)} %get-tuple-element.96), channel_id=1, source_target_pairs={{0,16},{1,9},{2,18},{3,11},{4,20},{5,13},{6,22},{7,15},{8,24},{9,1... | collective-permute-start | bytes 3145736 | tf_op jit(solution)/shard_map/ppermute | solution.py:596
  9.4 2.2 %pack.9 = (f32[2,32,32,128]{3,2,1,0:T(8,128)}, f32[8,128]{1,0:T(8,128)}) custom-call(f32[5,32,64,128]{3,2,1,0:T(8,128)} %bitcast.11, f32[8,128]{1,0:T(8,128)} %get-tuple-element.90.refs_1_), custom_call_target="tpu_custom_call" | custom-call | tf_op jit(solution)/shard_map/pack/pallas_call | solution.py:153
  12.4 8.6 %local_part.2 = (f32[5,32,32,128]{3,2,1,0:T(8,128)}, f32[8,128]{1,0:T(8,128)S(1)}) custom-call(f32[5,5]{1,0:T(8,128)S(1)} %copy-done.6, f32[5]{0:T(128)S(1)} %copy-done.5, s32[5,3]{1,0:T(8,128)S(1)} %copy.23.refs_2_, f32[5,32,64,128]{3,2,1,0:T(8,128)} %bitcast.12, f32[5,32,64,128]{3,2,1,0:T(8,128)} %bitcast.13, f32[5,32,64,128]{3,2,1,0:T(8,128)} %bitcast.14, ...), custom_call_target="tpu_custom_call" | custom-call | tf_op jit(solution)/shard_map/local_part/pallas_call | solution.py:153
  25.3 8.3 %collective-permute-done.2.refs_3_.refs_12_ = f32[2,32,32,128]{3,2,1,0:T(8,128)S(1)} collective-permute-done((f32[2,32,32,128]{3,2,1,0:T(8,128)}, f32[2,32,32,128]{3,2,1,0:T(8,128)S(1)}, u32[]{:S(2)}, u32[]{:S(2)}) %collective-permute-start.2) | collective-permute-done | bytes 1048608 | tf_op jit(solution)/shard_map/ppermute | solution.py:596
  34.4 2.3 %collective-permute-start.4 = (f32[2,32,32,128]{3,2,1,0:T(8,128)S(1)}, f32[2,32,32,128]{3,2,1,0:T(8,128)S(1)}, u32[]{:S(2)}, u32[]{:S(2)}) collective-permute-start(f32[2,32,32,128]{3,2,1,0:T(8,128)S(1)} %get-tuple-element.101), channel_id=1, source_target_pairs={{0,8},{1,17},{2,10},{3,19},{4,12},{5,21},{6,14},{7,23},{8,0},{9,25... | collective-permute-start | bytes 3145736 | tf_op jit(solution)/shard_map/ppermute | solution.py:596
  36.8 3.5 %collective-permute-start.1 = (f32[6,1,64,128]{3,2,1,0:T(8,128)S(1)}, f32[6,1,64,128]{3,2,1,0:T(8,128)S(1)}, u32[]{:S(2)}, u32[]{:S(2)}) collective-permute-start(f32[6,1,64,128]{3,2,1,0:T(8,128)S(1)} %copy-done.13), channel_id=1, source_target_pairs={{0,7},{1,0},{2,1},{3,2},{4,3},{5,4},{6,5},{7,6},{8,15},{9,8},{10,9... | collective-permute-start | bytes 589832 | tf_op jit(solution)/shard_map/ppermute | solution.py:608
  40.3 3.5 %collective-permute-done.refs_5_.refs_7_ = f32[6,1,64,128]{3,2,1,0:T(8,128)S(1)} collective-permute-done((f32[6,1,64,128]{3,2,1,0:T(8,128)S(1)}, f32[6,1,64,128]{3,2,1,0:T(8,128)S(1)}, u32[]{:S(2)}, u32[]{:S(2)}) %collective-permute-start) | collective-permute-done | bytes 196640 | tf_op jit(solution)/shard_map/ppermute | solution.py:608
  43.8 2.3 %spread.3 = (f32[2,8,32,128]{3,2,1,0:T(8,128)S(1)}, f32[2,2,8,32,128]{4,3,2,1,0:T(8,128)S(1)}, f32[2,2,8,32,128]{4,3,2,1,0:T(8,128)S(1)}, f32[8,128]{1,0:T(8,128)S(1)}) custom-call(s32[22]{0:T(128)S(1)} %pad_add_fusion.refs_0_, f32[71]{0:T(128)S(1)} %copy-done.4, f32[5,32,32,128]{3,2,1,0:T(8,128)S(1)} %copy-done.1, f32[5]{0:T(128)S(1)} %copy-done.5, ...), custom_call_target="tpu_custom_call" | custom-call | tf_op jit(solution)/shard_map/spread/pallas_call | solution.py:153
  54.2 3.5 %collective-permute-done.9.refs_3_.refs_12_ = f32[1,32,32,128]{3,2,1,0:T(8,128)S(1)} collective-permute-done((f32[1,32,32,128]{3,2,1,0:T(8,128)S(1)}, f32[1,32,32,128]{3,2,1,0:T(8,128)S(1)}, u32[]{:S(2)}, u32[]{:S(2)}) %collective-permute-start.9) | collective-permute-done | bytes 524320 | tf_op jit(solution)/shard_map/ppermute | solution.py:596
  61.9 2.2 %collective-permute-done.8.refs_5_.refs_7_ = f32[2,2,8,32,128]{4,3,2,1,0:T(8,128)S(1)} collective-permute-done((f32[2,2,8,32,128]{4,3,2,1,0:T(8,128)S(1)}, f32[2,2,8,32,128]{4,3,2,1,0:T(8,128)S(1)}, u32[]{:S(2)}, u32[]{:S(2)}) %collective-permute-start.8) | collective-permute-done | bytes 524320 | tf_op jit(solution)/shard_map/ppermute | solution.py:605
  64.1 2.4 %coefficients.3 = (f32[2,4,128,128]{3,2,1,0:T(8,128)S(1)}, f32[8,128]{1,0:T(8,128)S(1)}) custom-call(s32[22]{0:T(128)S(1)} %pad_add_fusion.refs_0_, f32[71]{0:T(128)S(1)} %copy-done.4, f32[2,16,128,128]{3,2,1,0:T(8,128)S(1)} %copy-done.3, f32[2,8,32,128]{3,2,1,0:T(8,128)S(1)} %get-tuple-element.111.refs_3_.refs_5_, ...), custom_call_target="tpu_custom_call" | custom-call | tf_op jit(solution)/shard_map/coefficients/pallas_call | solution.py:432
  69.0 4.3 %collective-permute-done.12.refs_13_ = f32[1,32,32,128]{3,2,1,0:T(8,128)S(1)} collective-permute-done((f32[1,32,32,128]{3,2,1,0:T(8,128)S(1)}, f32[1,32,32,128]{3,2,1,0:T(8,128)S(1)}, u32[]{:S(2)}, u32[]{:S(2)}) %collective-permute-start.12) | collective-permute-done | bytes 524320 | tf_op jit(solution)/shard_map/ppermute | solution.py:596
  80.4 11.6 %collective-permute-done.10.refs_5_.refs_7_ = f32[2,2,8,32,128]{4,3,2,1,0:T(8,128)S(1)} collective-permute-done((f32[2,2,8,32,128]{4,3,2,1,0:T(8,128)S(1)}, f32[2,2,8,32,128]{4,3,2,1,0:T(8,128)S(1)}, u32[]{:S(2)}, u32[]{:S(2)}) %collective-permute-start.10) | collective-permute-done | bytes 524320 | tf_op jit(solution)/shard_map/ppermute | solution.py:605
  92.2 2.4 %coefficients.4 = (f32[2,4,128,128]{3,2,1,0:T(8,128)S(1)}, f32[8,128]{1,0:T(8,128)S(1)}) custom-call(s32[22]{0:T(128)S(1)} %pad_add_fusion.refs_0_, f32[71]{0:T(128)S(1)} %copy-done.4, f32[2,16,128,128]{3,2,1,0:T(8,128)S(1)} %copy-done.3, f32[2,8,32,128]{3,2,1,0:T(8,128)S(1)} %get-tuple-element.108.refs_3_.refs_5_, ...), custom_call_target="tpu_custom_call" | custom-call | tf_op jit(solution)/shard_map/coefficients/pallas_call | solution.py:432
  95.0 2.5 %filtered.3 = (f32[2,8,32,128]{3,2,1,0:T(8,128)S(1)}, f32[2,2,8,32,128]{4,3,2,1,0:T(8,128)S(1)}, f32[2,2,8,32,128]{4,3,2,1,0:T(8,128)S(1)}, f32[8,128]{1,0:T(8,128)S(1)}) custom-call(s32[22]{0:T(128)S(1)} %pad_add_fusion.refs_0_, f32[71]{0:T(128)S(1)} %copy-done.4, f32[2,16,128,128]{3,2,1,0:T(8,128)S(1)} %copy-done.2, ...), custom_call_target="tpu_custom_call" | custom-call | tf_op jit(solution)/shard_map/filtered/pallas_call | solution.py:432
  97.5 2.6 %collective-permute-start.21 = (f32[2,2,8,32,128]{4,3,2,1,0:T(8,128)S(1)}, f32[2,2,8,32,128]{4,3,2,1,0:T(8,128)S(1)}, u32[]{:S(2)}, u32[]{:S(2)}) collective-permute-start(f32[2,2,8,32,128]{4,3,2,1,0:T(8,128)S(1)} %get-tuple-element.144), channel_id=1, source_target_pairs={{0,2},{1,3},{2,0},{3,1},{4,6},{5,7},{6,4},{7,5},{8,10},{9,11},{10,... | collective-permute-start | bytes 1572872 | tf_op jit(solution)/shard_map/ppermute | solution.py:605
  105.6 5.5 %local_part.3 = (f32[5,32,32,128]{3,2,1,0:T(8,128)S(1)}, f32[8,128]{1,0:T(8,128)S(1)}) custom-call(f32[5,5]{1,0:T(8,128)S(1)} %copy-done.6, f32[5]{0:T(128)S(1)} %copy-done.5, s32[5,3]{1,0:T(8,128)S(1)} %copy.23.refs_2_, f32[5,32,64,128]{3,2,1,0:T(8,128)S(1)} %bitcast.32, f32[5,32,64,128]{3,2,1,0:T(8,128)S(1)} %bitcast.33, f32[5,32,64,128]{3,2,1,0:T(8,128)S(1)} %bitcast.34, ...), custom_call_target="tpu_custom_call" | custom-call | tf_op jit(solution)/shard_map/local_part/pallas_call | solution.py:153
  111.0 12.2 %collective-permute-done.14.refs_4_ = f32[2,4,128,128]{3,2,1,0:T(8,128)S(1)} collective-permute-done((f32[2,4,128,128]{3,2,1,0:T(8,128)S(1)}, f32[2,4,128,128]{3,2,1,0:T(8,128)S(1)}, u32[]{:S(2)}, u32[]{:S(2)}) %collective-permute-start.14) | collective-permute-done | bytes 524320 | tf_op jit(solution)/shard_map/ppermute | solution.py:605
  123.3 2.5 %filtered.4 = (f32[2,8,32,128]{3,2,1,0:T(8,128)S(1)}, f32[2,2,8,32,128]{4,3,2,1,0:T(8,128)S(1)}, f32[2,2,8,32,128]{4,3,2,1,0:T(8,128)S(1)}, f32[8,128]{1,0:T(8,128)S(1)}) custom-call(s32[22]{0:T(128)S(1)} %pad_add_fusion.refs_0_, f32[71]{0:T(128)S(1)} %copy-done.4, f32[2,16,128,128]{3,2,1,0:T(8,128)S(1)} %copy-done.2, ...), custom_call_target="tpu_custom_call" | custom-call | tf_op jit(solution)/shard_map/filtered/pallas_call | solution.py:432
  125.8 3.6 %collective-permute-done.22.refs_4_ = f32[1,4,128,128]{3,2,1,0:T(8,128)S(1)} collective-permute-done((f32[1,4,128,128]{3,2,1,0:T(8,128)S(1)}, f32[1,4,128,128]{3,2,1,0:T(8,128)S(1)}, u32[]{:S(2)}, u32[]{:S(2)}) %collective-permute-start.22) | collective-permute-done | bytes 262176 | tf_op jit(solution)/shard_map/ppermute | solution.py:605
  133.9 6.8 %collective-permute-done.19.refs_1_.refs_4_ = f32[2,2,8,32,128]{4,3,2,1,0:T(8,128)S(1)} collective-permute-done((f32[2,2,8,32,128]{4,3,2,1,0:T(8,128)S(1)}, f32[2,2,8,32,128]{4,3,2,1,0:T(8,128)S(1)}, u32[]{:S(2)}, u32[]{:S(2)}) %collective-permute-start.19) | collective-permute-done | bytes 524320 | tf_op jit(solution)/shard_map/ppermute | solution.py:605
  140.9 2.5 %place_near.3 = (f32[5,32,64,128]{3,2,1,0:T(8,128)}, f32[8,128]{1,0:T(8,128)S(1)}) custom-call(s32[22]{0:T(128)S(1)} %pad_add_fusion.refs_0_, f32[71]{0:T(128)S(1)} %copy-done.4, f32[2,8,32,128]{3,2,1,0:T(8,128)S(1)} %get-tuple-element.155.refs_2_, f32[2,2,8,32,128]{4,3,2,1,0:T(8,128)S(1)} %collective-permute-done.26.refs_3_, ...), custom_call_target="tpu_custom_call", output_to_operand_aliasing={{0}: (5, {})} | custom-call | tf_op jit(solution)/shard_map/place_near/pallas_call | solution.py:153
  149.0 2.5 %place_near.5 = (f32[5,32,64,128]{3,2,1,0:T(8,128)}, f32[8,128]{1,0:T(8,128)}) custom-call(s32[22]{0:T(128)S(1)} %pad_add_fusion.refs_0_, f32[71]{0:T(128)S(1)} %copy-done.4, f32[2,8,32,128]{3,2,1,0:T(8,128)S(1)} %get-tuple-element.138.refs_2_, f32[2,2,8,32,128]{4,3,2,1,0:T(8,128)S(1)} %collective-permute-done.23.refs_3_, ...), custom_call_target="tpu_custom_call", output_to_operand_aliasing={{0}: (5, {})} | custom-call | tf_op jit(solution)/shard_map/place_near/pallas_call | solution.py:153
  (111 shorter events, 47.8 us)
Async XLA Ops:
  2.3 19.4 %collective-permute-start.3 = (f32[2,32,32,128]{3,2,1,0:T(8,128)}, f32[2,32,32,128]{3,2,1,0:T(8,128)}, u32[]{:S(2)}, u32[]{:S(2)}) collective-permute-start(f32[2,32,32,128]{3,2,1,0:T(8,128)} %get-tuple-element.96), channel_id=1, source_target_pairs={{0,16},{1,9},{2,18},{3,11},{4,20},{5,13},{6,22},{7,15},{8,24},{9,1... | collective-permute-start | bytes 3145736 | tf_op jit(solution)/shard_map/ppermute | solution.py:596
  11.6 22.1 %collective-permute-start.2 = (f32[2,32,32,128]{3,2,1,0:T(8,128)}, f32[2,32,32,128]{3,2,1,0:T(8,128)S(1)}, u32[]{:S(2)}, u32[]{:S(2)}) collective-permute-start(f32[2,32,32,128]{3,2,1,0:T(8,128)} %get-tuple-element.95), channel_id=1, source_target_pairs={{0,16},{1,9},{2,18},{3,11},{4,20},{5,13},{6,22},{7,15},{8,24},{9,1... | collective-permute-start | bytes 3145736 | tf_op jit(solution)/shard_map/ppermute | solution.py:596
  23.3 20.5 %collective-permute-start.5 = (f32[2,32,32,128]{3,2,1,0:T(8,128)S(1)}, f32[2,32,32,128]{3,2,1,0:T(8,128)S(1)}, u32[]{:S(2)}, u32[]{:S(2)}) collective-permute-start(f32[2,32,32,128]{3,2,1,0:T(8,128)S(1)} %get-tuple-element.102), channel_id=1, source_target_pairs={{0,8},{1,17},{2,10},{3,19},{4,12},{5,21},{6,14},{7,23},{8,0},{9,25... | collective-permute-start | bytes 3145736 | tf_op jit(solution)/shard_map/ppermute | solution.py:596
  34.4 17.7 %collective-permute-start.4 = (f32[2,32,32,128]{3,2,1,0:T(8,128)S(1)}, f32[2,32,32,128]{3,2,1,0:T(8,128)S(1)}, u32[]{:S(2)}, u32[]{:S(2)}) collective-permute-start(f32[2,32,32,128]{3,2,1,0:T(8,128)S(1)} %get-tuple-element.101), channel_id=1, source_target_pairs={{0,8},{1,17},{2,10},{3,19},{4,12},{5,21},{6,14},{7,23},{8,0},{9,25... | collective-permute-start | bytes 3145736 | tf_op jit(solution)/shard_map/ppermute | solution.py:596
  48.2 9.4 %collective-permute-start.9 = (f32[1,32,32,128]{3,2,1,0:T(8,128)S(1)}, f32[1,32,32,128]{3,2,1,0:T(8,128)S(1)}, u32[]{:S(2)}, u32[]{:S(2)}) collective-permute-start(f32[1,32,32,128]{3,2,1,0:T(8,128)S(1)} %get-tuple-element.113), channel_id=1, source_target_pairs={{0,16},{1,9},{2,18},{3,11},{4,20},{5,13},{6,22},{7,15},{8,24},{9,1... | collective-permute-start | bytes 1572872 | tf_op jit(solution)/shard_map/ppermute | solution.py:596
  49.7 28.2 %collective-permute-start.11 = (f32[2,32,32,128]{3,2,1,0:T(8,128)S(1)}, f32[2,32,32,128]{3,2,1,0:T(8,128)S(1)}, u32[]{:S(2)}, u32[]{:S(2)}) collective-permute-start(f32[2,32,32,128]{3,2,1,0:T(8,128)S(1)} %copy-done.11), channel_id=1, source_target_pairs={{0,16},{1,9},{2,18},{3,11},{4,20},{5,13},{6,22},{7,15},{8,24},{9,1... | collective-permute-start | bytes 3145736 | tf_op jit(solution)/shard_map/ppermute | solution.py:596
  50.3 13.8 %collective-permute-start.8 = (f32[2,2,8,32,128]{4,3,2,1,0:T(8,128)S(1)}, f32[2,2,8,32,128]{4,3,2,1,0:T(8,128)S(1)}, u32[]{:S(2)}, u32[]{:S(2)}) collective-permute-start(f32[2,2,8,32,128]{4,3,2,1,0:T(8,128)S(1)} %get-tuple-element.112), channel_id=1, source_target_pairs={{0,2},{1,3},{2,0},{3,1},{4,6},{5,7},{6,4},{7,5},{8,10},{9,11},{10,... | collective-permute-start | bytes 1572872 | tf_op jit(solution)/shard_map/ppermute | solution.py:605
  53.8 12.8 %collective-permute-start.7 = (f32[2,2,8,32,128]{4,3,2,1,0:T(8,128)S(1)}, f32[2,2,8,32,128]{4,3,2,1,0:T(8,128)S(1)}, u32[]{:S(2)}, u32[]{:S(2)}) collective-permute-start(f32[2,2,8,32,128]{4,3,2,1,0:T(8,128)S(1)} %get-tuple-element.109), channel_id=1, source_target_pairs={{0,1},{1,0},{2,3},{3,2},{4,5},{5,4},{6,7},{7,6},{8,9},{9,8},{10,11... | collective-permute-start | bytes 1572872 | tf_op jit(solution)/shard_map/ppermute | solution.py:605
  58.3 14.9 %collective-permute-start.12 = (f32[1,32,32,128]{3,2,1,0:T(8,128)S(1)}, f32[1,32,32,128]{3,2,1,0:T(8,128)S(1)}, u32[]{:S(2)}, u32[]{:S(2)}) collective-permute-start(f32[1,32,32,128]{3,2,1,0:T(8,128)S(1)} %get-tuple-element.119), channel_id=1, source_target_pairs={{0,8},{1,17},{2,10},{3,19},{4,12},{5,21},{6,14},{7,23},{8,0},{9,25... | collective-permute-start | bytes 1572872 | tf_op jit(solution)/shard_map/ppermute | solution.py:596
  60.4 37.1 %collective-permute-start.17 = (f32[2,32,32,128]{3,2,1,0:T(8,128)S(1)}, f32[2,32,32,128]{3,2,1,0:T(8,128)S(1)}, u32[]{:S(2)}, u32[]{:S(2)}) collective-permute-start(f32[2,32,32,128]{3,2,1,0:T(8,128)S(1)} %get-tuple-element.130), channel_id=1, source_target_pairs={{0,16},{1,9},{2,18},{3,11},{4,20},{5,13},{6,22},{7,15},{8,24},{9,1... | collective-permute-start | bytes 3145736 | tf_op jit(solution)/shard_map/ppermute | solution.py:596
  66.6 25.5 %collective-permute-start.10 = (f32[2,2,8,32,128]{4,3,2,1,0:T(8,128)S(1)}, f32[2,2,8,32,128]{4,3,2,1,0:T(8,128)S(1)}, u32[]{:S(2)}, u32[]{:S(2)}) collective-permute-start(f32[2,2,8,32,128]{4,3,2,1,0:T(8,128)S(1)} %get-tuple-element.117), channel_id=1, source_target_pairs={{0,2},{1,3},{2,0},{3,1},{4,6},{5,7},{6,4},{7,5},{8,10},{9,11},{10,... | collective-permute-start | bytes 1572872 | tf_op jit(solution)/shard_map/ppermute | solution.py:605
  67.2 27.4 %collective-permute-start.18 = (f32[2,4,128,128]{3,2,1,0:T(8,128)S(1)}, f32[2,4,128,128]{3,2,1,0:T(8,128)S(1)}, u32[]{:S(2)}, u32[]{:S(2)}) collective-permute-start(f32[2,4,128,128]{3,2,1,0:T(8,128)S(1)} %get-tuple-element.131.refs_3_), channel_id=1, source_target_pairs={{0,4},{1,5},{2,6},{3,7},{4,0},{5,1},{6,2},{7,3},{8,12},{9,13},{10,... | collective-permute-start | bytes 1572872 | tf_op jit(solution)/shard_map/ppermute | solution.py:605
  75.9 28.2 %collective-permute-start.15 = (f32[1,32,32,128]{3,2,1,0:T(8,128)S(1)}, f32[1,32,32,128]{3,2,1,0:T(8,128)S(1)}, u32[]{:S(2)}, u32[]{:S(2)}) collective-permute-start(f32[1,32,32,128]{3,2,1,0:T(8,128)S(1)} %copy-done.12), channel_id=1, source_target_pairs={{0,16},{1,9},{2,18},{3,11},{4,20},{5,13},{6,22},{7,15},{8,24},{9,1... | collective-permute-start | bytes 1572872 | tf_op jit(solution)/shard_map/ppermute | solution.py:596
  77.9 23.0 %collective-permute-start.16 = (f32[2,1,8,32,128]{4,3,2,1,0:T(8,128)S(1)}, f32[2,1,8,32,128]{4,3,2,1,0:T(8,128)S(1)}, u32[]{:S(2)}, u32[]{:S(2)}) collective-permute-start(f32[2,1,8,32,128]{4,3,2,1,0:T(8,128)S(1)} %get-tuple-element.129), channel_id=1, source_target_pairs={{0,2},{1,3},{2,0},{3,1},{4,6},{5,7},{6,4},{7,5},{8,10},{9,11},{10,... | collective-permute-start | bytes 786440 | tf_op jit(solution)/shard_map/ppermute | solution.py:605
  92.1 39.3 %collective-permute-start.20 = (f32[2,32,32,128]{3,2,1,0:T(8,128)S(1)}, f32[2,32,32,128]{3,2,1,0:T(8,128)S(1)}, u32[]{:S(2)}, u32[]{:S(2)}) collective-permute-start(f32[2,32,32,128]{3,2,1,0:T(8,128)S(1)} %get-tuple-element.142), channel_id=1, source_target_pairs={{0,8},{1,17},{2,10},{3,19},{4,12},{5,21},{6,14},{7,23},{8,0},{9,25... | collective-permute-start | bytes 3145736 | tf_op jit(solution)/shard_map/ppermute | solution.py:596
  94.6 28.7 %collective-permute-start.14 = (f32[2,4,128,128]{3,2,1,0:T(8,128)S(1)}, f32[2,4,128,128]{3,2,1,0:T(8,128)S(1)}, u32[]{:S(2)}, u32[]{:S(2)}) collective-permute-start(f32[2,4,128,128]{3,2,1,0:T(8,128)S(1)} %get-tuple-element.126.refs_3_), channel_id=1, source_target_pairs={{0,4},{1,5},{2,6},{3,7},{4,0},{5,1},{6,2},{7,3},{8,12},{9,13},{10,... | collective-permute-start | bytes 1572872 | tf_op jit(solution)/shard_map/ppermute | solution.py:605
  97.5 33.7 %collective-permute-start.21 = (f32[2,2,8,32,128]{4,3,2,1,0:T(8,128)S(1)}, f32[2,2,8,32,128]{4,3,2,1,0:T(8,128)S(1)}, u32[]{:S(2)}, u32[]{:S(2)}) collective-permute-start(f32[2,2,8,32,128]{4,3,2,1,0:T(8,128)S(1)} %get-tuple-element.144), channel_id=1, source_target_pairs={{0,2},{1,3},{2,0},{3,1},{4,6},{5,7},{6,4},{7,5},{8,10},{9,11},{10,... | collective-permute-start | bytes 1572872 | tf_op jit(solution)/shard_map/ppermute | solution.py:605
  100.9 42.4 %collective-permute-start.25 = (f32[2,32,32,128]{3,2,1,0:T(8,128)S(1)}, f32[2,32,32,128]{3,2,1,0:T(8,128)S(1)}, u32[]{:S(2)}, u32[]{:S(2)}) collective-permute-start(f32[2,32,32,128]{3,2,1,0:T(8,128)S(1)} %get-tuple-element.154), channel_id=1, source_target_pairs={{0,8},{1,17},{2,10},{3,19},{4,12},{5,21},{6,14},{7,23},{8,0},{9,25... | collective-permute-start | bytes 3145736 | tf_op jit(solution)/shard_map/ppermute | solution.py:596
  104.1 25.4 %collective-permute-start.22 = (f32[1,4,128,128]{3,2,1,0:T(8,128)S(1)}, f32[1,4,128,128]{3,2,1,0:T(8,128)S(1)}, u32[]{:S(2)}, u32[]{:S(2)}) collective-permute-start(f32[1,4,128,128]{3,2,1,0:T(8,128)S(1)} %get-tuple-element.145.refs_3_), channel_id=1, source_target_pairs={{0,4},{1,5},{2,6},{3,7},{4,0},{5,1},{6,2},{7,3},{8,12},{9,13},{10,... | collective-permute-start | bytes 786440 | tf_op jit(solution)/shard_map/ppermute | solution.py:605
  125.8 15.0 %collective-permute-start.19 = (f32[2,2,8,32,128]{4,3,2,1,0:T(8,128)S(1)}, f32[2,2,8,32,128]{4,3,2,1,0:T(8,128)S(1)}, u32[]{:S(2)}, u32[]{:S(2)}) collective-permute-start(f32[2,2,8,32,128]{4,3,2,1,0:T(8,128)S(1)} %get-tuple-element.140), channel_id=1, source_target_pairs={{0,2},{1,3},{2,0},{3,1},{4,6},{5,7},{6,4},{7,5},{8,10},{9,11},{10,... | collective-permute-start | bytes 1572872 | tf_op jit(solution)/shard_map/ppermute | solution.py:605
  131.3 9.6 %collective-permute-start.26 = (f32[2,2,8,32,128]{4,3,2,1,0:T(8,128)S(1)}, f32[2,2,8,32,128]{4,3,2,1,0:T(8,128)S(1)}, u32[]{:S(2)}, u32[]{:S(2)}) collective-permute-start(f32[2,2,8,32,128]{4,3,2,1,0:T(8,128)S(1)} %get-tuple-element.156), channel_id=1, source_target_pairs={{0,1},{1,0},{2,3},{3,2},{4,5},{5,4},{6,7},{7,6},{8,9},{9,8},{10,11... | collective-permute-start | bytes 1572872 | tf_op jit(solution)/shard_map/ppermute | solution.py:605
  131.4 13.7 %collective-permute-start.24 = (f32[2,1,8,32,128]{4,3,2,1,0:T(8,128)S(1)}, f32[2,1,8,32,128]{4,3,2,1,0:T(8,128)S(1)}, u32[]{:S(2)}, u32[]{:S(2)}) collective-permute-start(f32[2,1,8,32,128]{4,3,2,1,0:T(8,128)S(1)} %get-tuple-element.153), channel_id=1, source_target_pairs={{0,2},{1,3},{2,0},{3,1},{4,6},{5,7},{6,4},{7,5},{8,10},{9,11},{10,... | collective-permute-start | bytes 786440 | tf_op jit(solution)/shard_map/ppermute | solution.py:605
  131.4 14.2 %collective-permute-start.28 = (f32[1,32,32,128]{3,2,1,0:T(8,128)S(1)}, f32[1,32,32,128]{3,2,1,0:T(8,128)S(1)}, u32[]{:S(2)}, u32[]{:S(2)}) collective-permute-start(f32[1,32,32,128]{3,2,1,0:T(8,128)S(1)} %get-tuple-element.163), channel_id=1, source_target_pairs={{0,8},{1,17},{2,10},{3,19},{4,12},{5,21},{6,14},{7,23},{8,0},{9,25... | collective-permute-start | bytes 1572872 | tf_op jit(solution)/shard_map/ppermute | solution.py:596
  140.8 8.2 %collective-permute-start.23 = (f32[2,2,8,32,128]{4,3,2,1,0:T(8,128)S(1)}, f32[2,2,8,32,128]{4,3,2,1,0:T(8,128)S(1)}, u32[]{:S(2)}, u32[]{:S(2)}) collective-permute-start(f32[2,2,8,32,128]{4,3,2,1,0:T(8,128)S(1)} %get-tuple-element.150), channel_id=1, source_target_pairs={{0,1},{1,0},{2,3},{3,2},{4,5},{5,4},{6,7},{7,6},{8,9},{9,8},{10,11... | collective-permute-start | bytes 1572872 | tf_op jit(solution)/shard_map/ppermute | solution.py:605
  (24 other events, 162.2 us)
